TPU v7x, 128 devices: a whole 4x4x4 slice. The times are simulated.
128 devices in a mesh: blk: 32 (over z, x_hi, y), freq: 4 (over x_lo, core).
Axes of the slice: x: 4 (x_hi: 2, x_lo: 2; x = x_hi * 2 + x_lo), y: 4, z: 4, core: 2. Of those that a mesh axis runs over, the one named last changes fastest.
Arguments:
- raw: bfloat16 [32768, 1024], P(('blk', 'freq')), may hold values from -6 to 6
- seg_chan: int32 [32768], P(('blk', 'freq')), may hold values from 0 to 4095, as said below
- seg_win: int32 [32768], P(('blk', 'freq')), may hold values from 0 to 3
- file_count: int32 [128], P(('blk', 'freq')), may hold values from 0 to 256, as said below
Outputs:
- stacked: float32 [32, 128, 65536], P(None, 'freq', 'blk')
Inputs may be any that keep to these rules, and one draw needn't show every extreme that they name: `seg_chan`: the live slots of all devices (those with index below the device's file_count) name each pair of channel and window exactly once together with seg_win. The segment of channel c belongs to the device at blk = c // 128 and freq = (c % 128) // 32; no device has more than 2 live slots for one such owner, and in every draw some device has exactly 2 for every owner. Dead slots hold arbitrary values. `file_count`: some device has exactly 256 live slots and some device none.
All inputs are finite; a program needn't handle non-finite values.
Results may differ from a plain program's by a relative error of at most 0.0057.
Values may be sent and summed in bfloat16 or wider, within the bound.
No kernel may reach another device: no remote copies, remote signals or barrier semaphores. Data moves between devices by JAX's collectives and lax.ppermute only.
A program may use at most 128 MiB of HBM per device.

v0:
```python
import math

import jax
import jax.numpy as jnp
from jax import lax
from jax.sharding import PartitionSpec as P

CHANNELS = 4096
LAGS = 16
HALFWIN = 64
WIN = 4


EPSILON = 1e-06


def shifted(value, axis, steps):
    count = lax.axis_size(axis)
    pairs = [(source, (source + steps) % count) for source in range(count)]
    return lax.ppermute(value, axis, pairs)


def taper_curve(samples):
    sample_pos = jnp.arange(samples, dtype=jnp.float32)
    return 0.5 - 0.5 * jnp.cos(2.0 * math.pi / samples * (sample_pos + 0.5))


def prepare(segments):
    values = segments.astype(jnp.float32)
    values = values - jnp.mean(values, axis=1, keepdims=True)
    return (values * taper_curve(segments.shape[1])[None, :]).astype(jnp.bfloat16)


def basis_table(samples, freq_total):
    sample_pos = jnp.arange(samples, dtype=jnp.int32)[:, None]
    freq_pos = jnp.arange(freq_total, dtype=jnp.int32)[None, :]
    angles = 2.0 * math.pi / samples * (sample_pos * freq_pos % samples).astype(jnp.float32)
    return jnp.concatenate([jnp.cos(angles), -jnp.sin(angles)], axis=1).astype(jnp.bfloat16)


def whiten(tapered, freq_total, half_width):
    spectrum = jnp.dot(
        tapered, basis_table(tapered.shape[1], freq_total), preferred_element_type=jnp.float32
    )
    real_part = spectrum[:, :freq_total]
    imag_part = spectrum[:, freq_total:]
    energy = real_part * real_part + imag_part * imag_part
    freq_pos = jnp.arange(freq_total, dtype=jnp.int32)
    inside = (jnp.abs(freq_pos[:, None] - freq_pos[None, :]) <= half_width).astype(jnp.float32)
    smoother = inside / jnp.sum(inside, axis=0, keepdims=True)
    smooth = jnp.dot(energy, smoother, precision=lax.Precision.HIGHEST)
    inverse = lax.rsqrt(smooth + EPSILON)
    return jnp.concatenate([real_part * inverse, imag_part * inverse], axis=1).astype(jnp.bfloat16)


def rotate(whitened, lag_count, samples, norm_factor):
    band_size = whitened.shape[3]
    freq_pos = jnp.arange(band_size, dtype=jnp.int32)
    lag_steps = jnp.arange(lag_count, dtype=jnp.int32) - lag_count // 2
    angles = (
        2.0
        * math.pi
        / samples
        * (lag_steps[:, None] * freq_pos[None, :] % samples).astype(jnp.float32)
    )
    weights = jnp.where(freq_pos == 0, 1.0, 2.0).astype(jnp.float32) * norm_factor
    cosine = (jnp.cos(angles) * weights[None, :])[None, :, None, :]
    sine_part = (jnp.sin(angles) * weights[None, :])[None, :, None, :]
    real_part = whitened[:, None, :, 0, :].astype(jnp.float32)
    imag_part = whitened[:, None, :, 1, :].astype(jnp.float32)
    turned = jnp.stack(
        [real_part * cosine - imag_part * sine_part, real_part * sine_part + imag_part * cosine],
        axis=3,
    )
    return turned.astype(jnp.bfloat16).reshape(whitened.shape[0] * lag_count, -1)


def contract(held_block, turned):
    return lax.dot_general(
        held_block, turned, (((1,), (1,)), ((), ())), preferred_element_type=jnp.float32
    )


def pass_ahead(held_block):
    return shifted(held_block, "blk", 1)


def local(raw, seg_chan, seg_win, file_count):
    blk_count = lax.axis_size("blk")
    freq_count = lax.axis_size("freq")
    dev_count = blk_count * freq_count
    slot_count, samples = raw.shape
    freq_total = samples // 2
    block_width = CHANNELS // blk_count
    quarter_width = block_width // freq_count
    seg_dev = CHANNELS * WIN // dev_count
    capacity = 2 * seg_dev // dev_count
    slot_pos = jnp.arange(slot_count, dtype=jnp.int32)
    is_live = slot_pos < file_count[0]
    owners = seg_chan // block_width * freq_count + seg_chan % block_width // quarter_width
    onehot = (owners[:, None] == jnp.arange(dev_count, dtype=jnp.int32)[None, :]).astype(jnp.int32)
    onehot = onehot * is_live.astype(jnp.int32)[:, None]
    ranks_in = jnp.sum((jnp.cumsum(onehot, axis=0) - onehot) * onehot, axis=1)
    flat_slot = jnp.where(is_live, owners * capacity + ranks_in, dev_count * capacity)
    local_spot = seg_chan % quarter_width * WIN + seg_win
    packed = (
        jnp.zeros((dev_count * capacity, samples), raw.dtype).at[flat_slot].set(raw, mode="drop")
    )
    places = (
        jnp.full((dev_count * capacity,), -1, jnp.int32).at[flat_slot].set(local_spot, mode="drop")
    )
    arrived, arrived_at = (
        lax.all_to_all(
            packed.reshape(dev_count, capacity, samples),
            ("blk", "freq"),
            split_axis=0,
            concat_axis=0,
            tiled=True,
        ),
        lax.all_to_all(
            places.reshape(dev_count, capacity),
            ("blk", "freq"),
            split_axis=0,
            concat_axis=0,
            tiled=True,
        ),
    )
    arrived = arrived.reshape(-1, samples)
    arrived_at = arrived_at.reshape(-1)
    spots = jnp.where(arrived_at >= 0, arrived_at, seg_dev)
    segments = jnp.zeros((seg_dev, samples), raw.dtype).at[spots].set(arrived, mode="drop")
    whitened = whiten(prepare(segments), freq_total, HALFWIN).reshape(
        quarter_width, WIN, 2, freq_total
    )
    norm_factor = 1.0 / math.sqrt(2.0 * WIN * freq_total)
    gathered = lax.all_gather(whitened, "freq", axis=0, tiled=True)
    turned = rotate(gathered, LAGS, samples, norm_factor)
    message = whitened.reshape(quarter_width, -1)
    own_block = lax.axis_index("blk")
    collected = jnp.zeros((blk_count,) + message.shape, message.dtype)
    collected = lax.dynamic_update_index_in_dim(collected, message, own_block, 0)

    def advance(rounds, carried):
        held_block, holding = carried
        held_block = pass_ahead(held_block)
        holding = lax.dynamic_update_index_in_dim(
            holding, held_block, (own_block - rounds) % blk_count, 0
        )
        return (held_block, holding)

    held_block, collected = lax.fori_loop(1, blk_count, advance, (message, collected))
    product = contract(collected.reshape(blk_count * quarter_width, -1), turned)
    return product.reshape(blk_count, quarter_width, -1)


def solution(mesh):
    in_specs = (
        P(("blk", "freq"), None),
        P(("blk", "freq")),
        P(("blk", "freq")),
        P(("blk", "freq")),
    )
    out_specs = P(None, "freq", "blk")
    return jax.shard_map(local, mesh=mesh, in_specs=in_specs, out_specs=out_specs, check_vma=False)
```

profile of v0, /device:TPU:0, one launch (start us, length us, event | category | flops | bytes accessed | tf_op | source)
XLA Modules:
  0.0 626.5 jit_solution(12389530750178934367)
XLA Ops:
  59.8 13.2 %all-gather.2.cloned.1.call-done = bf16[128,4,2,512]{3,1,2,0:T(4,128)(2,1)} async-done(((bf16[32,4,2,512]{3,1,2,0:T(4,128)(2,1)}), bf16[128,4,2,512]{3,1,2,0:T(4,128)(2,1)}) %all-gather.2.cloned.1.call-update) | async-done | bytes 1048592 | tf_op jit(solution)/shard_map/all_gather | solution.py:136
  74.4 36.3 %subtract_convert_fusion = (bf16[128,16,4,1,512]{4,3,2,1,0:T(2,128)(2,1)S(1)}, bf16[128,16,4,1,512]{4,3,2,1,0:T(2,128)(2,1)}) fusion(f32[16,512]{1,0:T(8,128)S(1)} %get-tuple-element.132, f32[128,4,512]{2,1,0:T(4,128)S(1)} %get-tuple-element.128, f32[16,512]{1,0:T(8,128)S(1)} %get-tuple-element.131, f32[128,4,512]{2,1,0:T(4,128)S(1)} %get-tuple-element.127), kind=kLoop, calls=%fused_computation.6 | loop fusion | flops 33554432 | bytes 18939904 | tf_op jit(solution)/shard_map/convert.2
  110.7 40.6 %pad_maximum_fusion = bf16[128,16,4,2,512]{4,3,2,1,0:T(2,128)(2,1)} fusion(bf16[128,16,4,1,512]{4,3,2,1,0:T(2,128)(2,1)} %get-tuple-element.126, bf16[128,16,4,1,512]{4,3,2,1,0:T(2,128)(2,1)S(1)} %get-tuple-element.125), kind=kLoop, calls=%fused_computation.4 | loop fusion | flops 33554432 | bytes 33554432 | tf_op jit(solution)/shard_map/stack | solution.py:71
  151.3 27.6 %reshape.267 = bf16[2048,4096,1]{1,0,2:T(8,128)(2,1)} reshape(bf16[128,16,4,2,512]{4,3,2,1,0:T(2,128)(2,1)} %pad_maximum_fusion) | data formatting | bytes 33554432 | tf_op jit(solution)/shard_map/convert_element_type | solution.py:75
  179.0 416.6 %while.17 = (s32[]{:T(128)}, bf16[32,4096]{1,0:T(8,128)(2,1)S(1)}, bf16[32,32,4096]{2,1,0:T(8,128)(2,1)}, s32[]{:T(128)}, s32[]{:T(128)}, /*index=5*/s32[]{:T(128)}, s32[]{:T(128)}, s32[]{:T(128)}) while((s32[]{:T(128)}, bf16[32,4096]{1,0:T(8,128)(2,1)S(1)}, bf16[32,32,4096]{2,1,0:T(8,128)(2,1)}, s32[]{:T(128)}, s32[]{:T(128)}, ...), condition=%wide.region_9.10_spmd, body=%wide.region_8.9_spmd.sunk | while | flops 17 | bytes 2097436 | solution.py:151
  180.5 12.7 %collective-permute-done = bf16[32,4096]{1,0:T(8,128)(2,1)S(1)} collective-permute-done((bf16[32,4096]{1,0:T(8,128)(2,1)S(1)}, bf16[32,4096]{1,0:T(8,128)(2,1)S(1)}, u32[]{:S(2)}, u32[]{:S(2)}) %collective-permute-start) | collective-permute-done | bytes 262176 | tf_op jit(solution)/shard_map/while/body/eval_jaxpr/ppermute | solution.py:20
  193.9 13.4 %collective-permute-done = bf16[32,4096]{1,0:T(8,128)(2,1)S(1)} collective-permute-done((bf16[32,4096]{1,0:T(8,128)(2,1)S(1)}, bf16[32,4096]{1,0:T(8,128)(2,1)S(1)}, u32[]{:S(2)}, u32[]{:S(2)}) %collective-permute-start) | collective-permute-done | bytes 262176 | tf_op jit(solution)/shard_map/while/body/eval_jaxpr/ppermute | solution.py:20
  208.0 12.5 %collective-permute-done = bf16[32,4096]{1,0:T(8,128)(2,1)S(1)} collective-permute-done((bf16[32,4096]{1,0:T(8,128)(2,1)S(1)}, bf16[32,4096]{1,0:T(8,128)(2,1)S(1)}, u32[]{:S(2)}, u32[]{:S(2)}) %collective-permute-start) | collective-permute-done | bytes 262176 | tf_op jit(solution)/shard_map/while/body/eval_jaxpr/ppermute | solution.py:20
  234.1 12.1 %collective-permute-done = bf16[32,4096]{1,0:T(8,128)(2,1)S(1)} collective-permute-done((bf16[32,4096]{1,0:T(8,128)(2,1)S(1)}, bf16[32,4096]{1,0:T(8,128)(2,1)S(1)}, u32[]{:S(2)}, u32[]{:S(2)}) %collective-permute-start) | collective-permute-done | bytes 262176 | tf_op jit(solution)/shard_map/while/body/eval_jaxpr/ppermute | solution.py:20
  272.6 12.1 %collective-permute-done = bf16[32,4096]{1,0:T(8,128)(2,1)S(1)} collective-permute-done((bf16[32,4096]{1,0:T(8,128)(2,1)S(1)}, bf16[32,4096]{1,0:T(8,128)(2,1)S(1)}, u32[]{:S(2)}, u32[]{:S(2)}) %collective-permute-start) | collective-permute-done | bytes 262176 | tf_op jit(solution)/shard_map/while/body/eval_jaxpr/ppermute | solution.py:20
  285.5 12.3 %collective-permute-done = bf16[32,4096]{1,0:T(8,128)(2,1)S(1)} collective-permute-done((bf16[32,4096]{1,0:T(8,128)(2,1)S(1)}, bf16[32,4096]{1,0:T(8,128)(2,1)S(1)}, u32[]{:S(2)}, u32[]{:S(2)}) %collective-permute-start) | collective-permute-done | bytes 262176 | tf_op jit(solution)/shard_map/while/body/eval_jaxpr/ppermute | solution.py:20
  298.5 13.3 %collective-permute-done = bf16[32,4096]{1,0:T(8,128)(2,1)S(1)} collective-permute-done((bf16[32,4096]{1,0:T(8,128)(2,1)S(1)}, bf16[32,4096]{1,0:T(8,128)(2,1)S(1)}, u32[]{:S(2)}, u32[]{:S(2)}) %collective-permute-start) | collective-permute-done | bytes 262176 | tf_op jit(solution)/shard_map/while/body/eval_jaxpr/ppermute | solution.py:20
  312.6 14.6 %collective-permute-done = bf16[32,4096]{1,0:T(8,128)(2,1)S(1)} collective-permute-done((bf16[32,4096]{1,0:T(8,128)(2,1)S(1)}, bf16[32,4096]{1,0:T(8,128)(2,1)S(1)}, u32[]{:S(2)}, u32[]{:S(2)}) %collective-permute-start) | collective-permute-done | bytes 262176 | tf_op jit(solution)/shard_map/while/body/eval_jaxpr/ppermute | solution.py:20
  327.9 14.1 %collective-permute-done = bf16[32,4096]{1,0:T(8,128)(2,1)S(1)} collective-permute-done((bf16[32,4096]{1,0:T(8,128)(2,1)S(1)}, bf16[32,4096]{1,0:T(8,128)(2,1)S(1)}, u32[]{:S(2)}, u32[]{:S(2)}) %collective-permute-start) | collective-permute-done | bytes 262176 | tf_op jit(solution)/shard_map/while/body/eval_jaxpr/ppermute | solution.py:20
  342.7 13.3 %collective-permute-done = bf16[32,4096]{1,0:T(8,128)(2,1)S(1)} collective-permute-done((bf16[32,4096]{1,0:T(8,128)(2,1)S(1)}, bf16[32,4096]{1,0:T(8,128)(2,1)S(1)}, u32[]{:S(2)}, u32[]{:S(2)}) %collective-permute-start) | collective-permute-done | bytes 262176 | tf_op jit(solution)/shard_map/while/body/eval_jaxpr/ppermute | solution.py:20
  356.8 12.3 %collective-permute-done = bf16[32,4096]{1,0:T(8,128)(2,1)S(1)} collective-permute-done((bf16[32,4096]{1,0:T(8,128)(2,1)S(1)}, bf16[32,4096]{1,0:T(8,128)(2,1)S(1)}, u32[]{:S(2)}, u32[]{:S(2)}) %collective-permute-start) | collective-permute-done | bytes 262176 | tf_op jit(solution)/shard_map/while/body/eval_jaxpr/ppermute | solution.py:20
  408.3 12.1 %collective-permute-done = bf16[32,4096]{1,0:T(8,128)(2,1)S(1)} collective-permute-done((bf16[32,4096]{1,0:T(8,128)(2,1)S(1)}, bf16[32,4096]{1,0:T(8,128)(2,1)S(1)}, u32[]{:S(2)}, u32[]{:S(2)}) %collective-permute-start) | collective-permute-done | bytes 262176 | tf_op jit(solution)/shard_map/while/body/eval_jaxpr/ppermute | solution.py:20
  434.0 12.4 %collective-permute-done = bf16[32,4096]{1,0:T(8,128)(2,1)S(1)} collective-permute-done((bf16[32,4096]{1,0:T(8,128)(2,1)S(1)}, bf16[32,4096]{1,0:T(8,128)(2,1)S(1)}, u32[]{:S(2)}, u32[]{:S(2)}) %collective-permute-start) | collective-permute-done | bytes 262176 | tf_op jit(solution)/shard_map/while/body/eval_jaxpr/ppermute | solution.py:20
  447.2 13.5 %collective-permute-done = bf16[32,4096]{1,0:T(8,128)(2,1)S(1)} collective-permute-done((bf16[32,4096]{1,0:T(8,128)(2,1)S(1)}, bf16[32,4096]{1,0:T(8,128)(2,1)S(1)}, u32[]{:S(2)}, u32[]{:S(2)}) %collective-permute-start) | collective-permute-done | bytes 262176 | tf_op jit(solution)/shard_map/while/body/eval_jaxpr/ppermute | solution.py:20
  461.4 14.6 %collective-permute-done = bf16[32,4096]{1,0:T(8,128)(2,1)S(1)} collective-permute-done((bf16[32,4096]{1,0:T(8,128)(2,1)S(1)}, bf16[32,4096]{1,0:T(8,128)(2,1)S(1)}, u32[]{:S(2)}, u32[]{:S(2)}) %collective-permute-start) | collective-permute-done | bytes 262176 | tf_op jit(solution)/shard_map/while/body/eval_jaxpr/ppermute | solution.py:20
  476.7 14.0 %collective-permute-done = bf16[32,4096]{1,0:T(8,128)(2,1)S(1)} collective-permute-done((bf16[32,4096]{1,0:T(8,128)(2,1)S(1)}, bf16[32,4096]{1,0:T(8,128)(2,1)S(1)}, u32[]{:S(2)}, u32[]{:S(2)}) %collective-permute-start) | collective-permute-done | bytes 262176 | tf_op jit(solution)/shard_map/while/body/eval_jaxpr/ppermute | solution.py:20
  491.6 13.2 %collective-permute-done = bf16[32,4096]{1,0:T(8,128)(2,1)S(1)} collective-permute-done((bf16[32,4096]{1,0:T(8,128)(2,1)S(1)}, bf16[32,4096]{1,0:T(8,128)(2,1)S(1)}, u32[]{:S(2)}, u32[]{:S(2)}) %collective-permute-start) | collective-permute-done | bytes 262176 | tf_op jit(solution)/shard_map/while/body/eval_jaxpr/ppermute | solution.py:20
  505.5 12.3 %collective-permute-done = bf16[32,4096]{1,0:T(8,128)(2,1)S(1)} collective-permute-done((bf16[32,4096]{1,0:T(8,128)(2,1)S(1)}, bf16[32,4096]{1,0:T(8,128)(2,1)S(1)}, u32[]{:S(2)}, u32[]{:S(2)}) %collective-permute-start) | collective-permute-done | bytes 262176 | tf_op jit(solution)/shard_map/while/body/eval_jaxpr/ppermute | solution.py:20
  595.5 24.1 %fusion.48 = f32[32,32,2048]{2,1,0:T(8,128)} fusion(bf16[32,32,4096]{2,1,0:T(8,128)(2,1)} %get-tuple-element.116, bf16[2048,4096,1]{1,0,2:T(8,128)(2,1)} %reshape.267), kind=kOutput, calls=%fused_computation.103 | convolution fusion | flops 17179869184 | bytes 33554432 | tf_op jit(solution)/shard_map/dot_general | solution.py:79
  (154 shorter events, 235.6 us)
Async XLA Ops:
  11.0 20.5 %all-to-all-start = ((s32[128,1,2]{2,1,0:T(1,128)}), s32[128,1,2]{2,1,0:T(1,128)S(1)}, u32[]{:S(2)}, u32[]{:S(2)}) async-start(s32[128,1,2]{2,1,0:T(1,128)} %bitcast.6), calls=%async_computation | async-start | bytes 131072 | tf_op jit(solution)/shard_map/all_to_all | solution.py:120
  31.5 18.2 %all-to-all-start.1 = ((bf16[128,2,1024]{2,1,0:T(2,128)(2,1)}), bf16[128,2,1024]{2,1,0:T(2,128)(2,1)S(1)}, u32[]{:S(2)}, u32[]{:S(2)}) async-start(bf16[128,2,1024]{2,1,0:T(2,128)(2,1)} %reshape.237), calls=%async_computation.1 | async-start | bytes 1048576 | tf_op jit(solution)/shard_map/all_to_all | solution.py:113
  36.1 36.8 %all-gather.2.cloned.1.call-start = ((), (), s32[]{:S(2)}) async-start(), calls=%async_computation.2 | async-start | bytes 1310720 | tf_op jit(solution)/shard_map/all_gather | solution.py:136
  179.0 14.2 %collective-permute-start = (bf16[32,4096]{1,0:T(8,128)(2,1)S(1)}, bf16[32,4096]{1,0:T(8,128)(2,1)S(1)}, u32[]{:S(2)}, u32[]{:S(2)}) collective-permute-start(bf16[32,4096]{1,0:T(8,128)(2,1)S(1)} %get-tuple-element.171), channel_id=1, source_target_pairs={{0,4},{4,8},{8,12},{12,16},{16,20},{20,24},{24,28},{28,32},{32,36}... | collective-permute-start | bytes 786440 | tf_op jit(solution)/shard_map/while/body/eval_jaxpr/ppermute | solution.py:20
  193.9 13.4 %collective-permute-start = (bf16[32,4096]{1,0:T(8,128)(2,1)S(1)}, bf16[32,4096]{1,0:T(8,128)(2,1)S(1)}, u32[]{:S(2)}, u32[]{:S(2)}) collective-permute-start(bf16[32,4096]{1,0:T(8,128)(2,1)S(1)} %get-tuple-element.171), channel_id=1, source_target_pairs={{0,4},{4,8},{8,12},{12,16},{16,20},{20,24},{24,28},{28,32},{32,36}... | collective-permute-start | bytes 786440 | tf_op jit(solution)/shard_map/while/body/eval_jaxpr/ppermute | solution.py:20
  208.0 12.5 %collective-permute-start = (bf16[32,4096]{1,0:T(8,128)(2,1)S(1)}, bf16[32,4096]{1,0:T(8,128)(2,1)S(1)}, u32[]{:S(2)}, u32[]{:S(2)}) collective-permute-start(bf16[32,4096]{1,0:T(8,128)(2,1)S(1)} %get-tuple-element.171), channel_id=1, source_target_pairs={{0,4},{4,8},{8,12},{12,16},{16,20},{20,24},{24,28},{28,32},{32,36}... | collective-permute-start | bytes 786440 | tf_op jit(solution)/shard_map/while/body/eval_jaxpr/ppermute | solution.py:20
  221.2 12.1 %collective-permute-start = (bf16[32,4096]{1,0:T(8,128)(2,1)S(1)}, bf16[32,4096]{1,0:T(8,128)(2,1)S(1)}, u32[]{:S(2)}, u32[]{:S(2)}) collective-permute-start(bf16[32,4096]{1,0:T(8,128)(2,1)S(1)} %get-tuple-element.171), channel_id=1, source_target_pairs={{0,4},{4,8},{8,12},{12,16},{16,20},{20,24},{24,28},{28,32},{32,36}... | collective-permute-start | bytes 786440 | tf_op jit(solution)/shard_map/while/body/eval_jaxpr/ppermute | solution.py:20
  234.1 12.1 %collective-permute-start = (bf16[32,4096]{1,0:T(8,128)(2,1)S(1)}, bf16[32,4096]{1,0:T(8,128)(2,1)S(1)}, u32[]{:S(2)}, u32[]{:S(2)}) collective-permute-start(bf16[32,4096]{1,0:T(8,128)(2,1)S(1)} %get-tuple-element.171), channel_id=1, source_target_pairs={{0,4},{4,8},{8,12},{12,16},{16,20},{20,24},{24,28},{28,32},{32,36}... | collective-permute-start | bytes 786440 | tf_op jit(solution)/shard_map/while/body/eval_jaxpr/ppermute | solution.py:20
  246.9 12.1 %collective-permute-start = (bf16[32,4096]{1,0:T(8,128)(2,1)S(1)}, bf16[32,4096]{1,0:T(8,128)(2,1)S(1)}, u32[]{:S(2)}, u32[]{:S(2)}) collective-permute-start(bf16[32,4096]{1,0:T(8,128)(2,1)S(1)} %get-tuple-element.171), channel_id=1, source_target_pairs={{0,4},{4,8},{8,12},{12,16},{16,20},{20,24},{24,28},{28,32},{32,36}... | collective-permute-start | bytes 786440 | tf_op jit(solution)/shard_map/while/body/eval_jaxpr/ppermute | solution.py:20
  259.7 12.1 %collective-permute-start = (bf16[32,4096]{1,0:T(8,128)(2,1)S(1)}, bf16[32,4096]{1,0:T(8,128)(2,1)S(1)}, u32[]{:S(2)}, u32[]{:S(2)}) collective-permute-start(bf16[32,4096]{1,0:T(8,128)(2,1)S(1)} %get-tuple-element.171), channel_id=1, source_target_pairs={{0,4},{4,8},{8,12},{12,16},{16,20},{20,24},{24,28},{28,32},{32,36}... | collective-permute-start | bytes 786440 | tf_op jit(solution)/shard_map/while/body/eval_jaxpr/ppermute | solution.py:20
  285.5 12.3 %collective-permute-start = (bf16[32,4096]{1,0:T(8,128)(2,1)S(1)}, bf16[32,4096]{1,0:T(8,128)(2,1)S(1)}, u32[]{:S(2)}, u32[]{:S(2)}) collective-permute-start(bf16[32,4096]{1,0:T(8,128)(2,1)S(1)} %get-tuple-element.171), channel_id=1, source_target_pairs={{0,4},{4,8},{8,12},{12,16},{16,20},{20,24},{24,28},{28,32},{32,36}... | collective-permute-start | bytes 786440 | tf_op jit(solution)/shard_map/while/body/eval_jaxpr/ppermute | solution.py:20
  298.5 13.4 %collective-permute-start = (bf16[32,4096]{1,0:T(8,128)(2,1)S(1)}, bf16[32,4096]{1,0:T(8,128)(2,1)S(1)}, u32[]{:S(2)}, u32[]{:S(2)}) collective-permute-start(bf16[32,4096]{1,0:T(8,128)(2,1)S(1)} %get-tuple-element.171), channel_id=1, source_target_pairs={{0,4},{4,8},{8,12},{12,16},{16,20},{20,24},{24,28},{28,32},{32,36}... | collective-permute-start | bytes 786440 | tf_op jit(solution)/shard_map/while/body/eval_jaxpr/ppermute | solution.py:20
  312.6 14.6 %collective-permute-start = (bf16[32,4096]{1,0:T(8,128)(2,1)S(1)}, bf16[32,4096]{1,0:T(8,128)(2,1)S(1)}, u32[]{:S(2)}, u32[]{:S(2)}) collective-permute-start(bf16[32,4096]{1,0:T(8,128)(2,1)S(1)} %get-tuple-element.171), channel_id=1, source_target_pairs={{0,4},{4,8},{8,12},{12,16},{16,20},{20,24},{24,28},{28,32},{32,36}... | collective-permute-start | bytes 786440 | tf_op jit(solution)/shard_map/while/body/eval_jaxpr/ppermute | solution.py:20
  327.9 14.1 %collective-permute-start = (bf16[32,4096]{1,0:T(8,128)(2,1)S(1)}, bf16[32,4096]{1,0:T(8,128)(2,1)S(1)}, u32[]{:S(2)}, u32[]{:S(2)}) collective-permute-start(bf16[32,4096]{1,0:T(8,128)(2,1)S(1)} %get-tuple-element.171), channel_id=1, source_target_pairs={{0,4},{4,8},{8,12},{12,16},{16,20},{20,24},{24,28},{28,32},{32,36}... | collective-permute-start | bytes 786440 | tf_op jit(solution)/shard_map/while/body/eval_jaxpr/ppermute | solution.py:20
  342.7 13.3 %collective-permute-start = (bf16[32,4096]{1,0:T(8,128)(2,1)S(1)}, bf16[32,4096]{1,0:T(8,128)(2,1)S(1)}, u32[]{:S(2)}, u32[]{:S(2)}) collective-permute-start(bf16[32,4096]{1,0:T(8,128)(2,1)S(1)} %get-tuple-element.171), channel_id=1, source_target_pairs={{0,4},{4,8},{8,12},{12,16},{16,20},{20,24},{24,28},{28,32},{32,36}... | collective-permute-start | bytes 786440 | tf_op jit(solution)/shard_map/while/body/eval_jaxpr/ppermute | solution.py:20
  356.8 12.3 %collective-permute-start = (bf16[32,4096]{1,0:T(8,128)(2,1)S(1)}, bf16[32,4096]{1,0:T(8,128)(2,1)S(1)}, u32[]{:S(2)}, u32[]{:S(2)}) collective-permute-start(bf16[32,4096]{1,0:T(8,128)(2,1)S(1)} %get-tuple-element.171), channel_id=1, source_target_pairs={{0,4},{4,8},{8,12},{12,16},{16,20},{20,24},{24,28},{28,32},{32,36}... | collective-permute-start | bytes 786440 | tf_op jit(solution)/shard_map/while/body/eval_jaxpr/ppermute | solution.py:20
  408.3 12.1 %collective-permute-start = (bf16[32,4096]{1,0:T(8,128)(2,1)S(1)}, bf16[32,4096]{1,0:T(8,128)(2,1)S(1)}, u32[]{:S(2)}, u32[]{:S(2)}) collective-permute-start(bf16[32,4096]{1,0:T(8,128)(2,1)S(1)} %get-tuple-element.171), channel_id=1, source_target_pairs={{0,4},{4,8},{8,12},{12,16},{16,20},{20,24},{24,28},{28,32},{32,36}... | collective-permute-start | bytes 786440 | tf_op jit(solution)/shard_map/while/body/eval_jaxpr/ppermute | solution.py:20
  434.0 12.4 %collective-permute-start = (bf16[32,4096]{1,0:T(8,128)(2,1)S(1)}, bf16[32,4096]{1,0:T(8,128)(2,1)S(1)}, u32[]{:S(2)}, u32[]{:S(2)}) collective-permute-start(bf16[32,4096]{1,0:T(8,128)(2,1)S(1)} %get-tuple-element.171), channel_id=1, source_target_pairs={{0,4},{4,8},{8,12},{12,16},{16,20},{20,24},{24,28},{28,32},{32,36}... | collective-permute-start | bytes 786440 | tf_op jit(solution)/shard_map/while/body/eval_jaxpr/ppermute | solution.py:20
  447.2 13.5 %collective-permute-start = (bf16[32,4096]{1,0:T(8,128)(2,1)S(1)}, bf16[32,4096]{1,0:T(8,128)(2,1)S(1)}, u32[]{:S(2)}, u32[]{:S(2)}) collective-permute-start(bf16[32,4096]{1,0:T(8,128)(2,1)S(1)} %get-tuple-element.171), channel_id=1, source_target_pairs={{0,4},{4,8},{8,12},{12,16},{16,20},{20,24},{24,28},{28,32},{32,36}... | collective-permute-start | bytes 786440 | tf_op jit(solution)/shard_map/while/body/eval_jaxpr/ppermute | solution.py:20
  461.4 14.6 %collective-permute-start = (bf16[32,4096]{1,0:T(8,128)(2,1)S(1)}, bf16[32,4096]{1,0:T(8,128)(2,1)S(1)}, u32[]{:S(2)}, u32[]{:S(2)}) collective-permute-start(bf16[32,4096]{1,0:T(8,128)(2,1)S(1)} %get-tuple-element.171), channel_id=1, source_target_pairs={{0,4},{4,8},{8,12},{12,16},{16,20},{20,24},{24,28},{28,32},{32,36}... | collective-permute-start | bytes 786440 | tf_op jit(solution)/shard_map/while/body/eval_jaxpr/ppermute | solution.py:20
  476.7 14.0 %collective-permute-start = (bf16[32,4096]{1,0:T(8,128)(2,1)S(1)}, bf16[32,4096]{1,0:T(8,128)(2,1)S(1)}, u32[]{:S(2)}, u32[]{:S(2)}) collective-permute-start(bf16[32,4096]{1,0:T(8,128)(2,1)S(1)} %get-tuple-element.171), channel_id=1, source_target_pairs={{0,4},{4,8},{8,12},{12,16},{16,20},{20,24},{24,28},{28,32},{32,36}... | collective-permute-start | bytes 786440 | tf_op jit(solution)/shard_map/while/body/eval_jaxpr/ppermute | solution.py:20
  491.6 13.2 %collective-permute-start = (bf16[32,4096]{1,0:T(8,128)(2,1)S(1)}, bf16[32,4096]{1,0:T(8,128)(2,1)S(1)}, u32[]{:S(2)}, u32[]{:S(2)}) collective-permute-start(bf16[32,4096]{1,0:T(8,128)(2,1)S(1)} %get-tuple-element.171), channel_id=1, source_target_pairs={{0,4},{4,8},{8,12},{12,16},{16,20},{20,24},{24,28},{28,32},{32,36}... | collective-permute-start | bytes 786440 | tf_op jit(solution)/shard_map/while/body/eval_jaxpr/ppermute | solution.py:20
  505.5 12.3 %collective-permute-start = (bf16[32,4096]{1,0:T(8,128)(2,1)S(1)}, bf16[32,4096]{1,0:T(8,128)(2,1)S(1)}, u32[]{:S(2)}, u32[]{:S(2)}) collective-permute-start(bf16[32,4096]{1,0:T(8,128)(2,1)S(1)} %get-tuple-element.171), channel_id=1, source_target_pairs={{0,4},{4,8},{8,12},{12,16},{16,20},{20,24},{24,28},{28,32},{32,36}... | collective-permute-start | bytes 786440 | tf_op jit(solution)/shard_map/while/body/eval_jaxpr/ppermute | solution.py:20
  518.5 12.1 %collective-permute-start = (bf16[32,4096]{1,0:T(8,128)(2,1)S(1)}, bf16[32,4096]{1,0:T(8,128)(2,1)S(1)}, u32[]{:S(2)}, u32[]{:S(2)}) collective-permute-start(bf16[32,4096]{1,0:T(8,128)(2,1)S(1)} %get-tuple-element.171), channel_id=1, source_target_pairs={{0,4},{4,8},{8,12},{12,16},{16,20},{20,24},{24,28},{28,32},{32,36}... | collective-permute-start | bytes 786440 | tf_op jit(solution)/shard_map/while/body/eval_jaxpr/ppermute | solution.py:20
  (10 other events, 121.0 us)
Sparse Core Ops, SparseCore 0:
  54.3 18.5 all-gather.1
where the time goes:
time: 627 us; the launch traced here: 626 us
  waiting for transfers between devices  414 us (66%)
  other arithmetic  89.7 us (14%)
  local copies, waits for them, and re-layouts  65.4 us (10%)
  matrix products  25.3 us (4%)
  starting transfers between devices  17.4 us (3%)
  between operations  14.2 us (2%)
    ppermute x31, waiting for transfers between devices, shifted(): return lax.ppermute(value, axis, pairs)  392 us
    another operation x5, other arithmetic  45.2 us
    another operation x1, other arithmetic, rotate(): jnp.stack([real_part * cosine - imag_part * sine_part, real_part * sine_p...  40.6 us
    convert_element_type x1, local copies, waits for them, and re-layouts, rotate(): turned.astype(jnp.bfloat16).reshape(whitened.shape[0] * lag_count, -1)  27.6 us
    dot_general x1, matrix products, contract(): lax.dot_general(held_block, turned, (((1,), (1,)), ((), ())), preferred_e...  24.1 us
    dynamic_update_slice x31, local copies, waits for them, and re-layouts, advance(): lax.dynamic_update_index_in_dim(holding, held_block, (own_block - rounds)...  22.5 us
    all_gather x1, waiting for transfers between devices, local(): gathered = lax.all_gather(whitened, 'freq', axis=0, tiled=True)  13.2 us
  transfers between devices with their start and end apart: 34, of which 34 were waited for; matrix products, arithmetic and copies ran while one was open for 3% of the time, Pallas kernels for 0%

commit v1 on v0

v1 whole, which is shorter than its diff:
```python
import functools
import math

import jax
import jax.numpy as jnp
import ml_dtypes
import numpy as np
from jax import lax
from jax.experimental import pallas as pl
from jax.experimental.pallas import tpu as pltpu
from jax.sharding import PartitionSpec as P

CHANNELS = 4096
SAMPLES = 1024
FREQS = 512
LAGS = 16
HALFWIN = 64
WIN = 4
EPSILON = 1e-06

NZ, NXH, NY = 4, 2, 4
QC = 32
HALF = QC // 2
SEG_DEV = QC * WIN
SLOTS = 256
DEVICES = 128
SPEC = WIN * 2 * FREQS
TAIL = 128
NT = 256
F32, BF16 = jnp.float32, jnp.bfloat16
VMEM_LIMIT = 48 * 1024 * 1024


def tables():
    n = np.arange(SAMPLES)[:, None]
    k = np.arange(FREQS)[None, :]
    angle = 2.0 * math.pi / SAMPLES * ((n * k) % SAMPLES)
    basis = np.concatenate([np.cos(angle), -np.sin(angle)], axis=1).astype(ml_dtypes.bfloat16)
    taper = (0.5 - 0.5 * np.cos(2.0 * math.pi / SAMPLES * (n[:, 0] + 0.5)))[None, :].astype(np.float32)
    pos = np.arange(FREQS)
    inside = (np.abs(pos[:, None] - pos[None, :]) <= HALFWIN).astype(np.float64)
    smoother = (inside / inside.sum(axis=0, keepdims=True)).astype(np.float32)
    lag = np.arange(LAGS)[:, None] - LAGS // 2
    phi = 2.0 * math.pi / SAMPLES * ((lag * pos[None, :]) % SAMPLES)
    gain = np.where(pos == 0, 1.0, 2.0)[None, :] / math.sqrt(2.0 * WIN * FREQS)
    return basis, taper, smoother, (gain * np.cos(phi)).astype(np.float32), (gain * np.sin(phi)).astype(np.float32)


def diagonal(size):
    return lax.broadcasted_iota(jnp.int32, (size, size), 0) == lax.broadcasted_iota(jnp.int32, (size, size), 1)


def pack_kernel(count_ref, chan_ref, win_ref, raw_ref, out_ref):
    chan = chan_ref[...]
    slot = lax.broadcasted_iota(jnp.int32, (1, SLOTS), 1)
    live = slot < count_ref[0]
    owner = jnp.where(live, chan // QC, -1).astype(F32)
    owner_col = jnp.sum(jnp.where(diagonal(SLOTS), owner, 0.0), axis=1, keepdims=True)
    row = lax.broadcasted_iota(jnp.int32, (SLOTS, SLOTS), 0)
    col = lax.broadcasted_iota(jnp.int32, (SLOTS, SLOTS), 1)
    earlier = jnp.where((owner_col == owner) & (row < col), 1.0, 0.0)
    rank = jnp.sum(earlier, axis=0, keepdims=True)
    flat = jnp.where(live, owner * 2.0 + rank, -1.0)
    pick = jnp.where(flat == row.astype(F32), 1.0, 0.0)
    out_ref[:, :SAMPLES] = jnp.dot(pick.astype(BF16), raw_ref[...], preferred_element_type=F32).astype(BF16)
    place = (win_ref[...] * QC + chan % QC + 1).astype(F32)
    place_col = jnp.sum(pick * place, axis=1, keepdims=True)
    out_ref[:, SAMPLES:] = jnp.broadcast_to(place_col, (SLOTS, TAIL)).astype(BF16)


def whiten_kernel(recv_ref, basis_ref, taper_ref, smoother_ref, out_ref):
    place_col = recv_ref[:, SAMPLES : SAMPLES + 1].astype(F32)
    place = jnp.sum(jnp.where(diagonal(SLOTS), place_col, 0.0), axis=0, keepdims=True)
    wanted = lax.broadcasted_iota(jnp.int32, (SEG_DEV, SLOTS), 0).astype(F32) + 1.0
    pick = jnp.where(place == wanted, 1.0, 0.0).astype(BF16)
    values = jnp.dot(pick, recv_ref[:, :SAMPLES], preferred_element_type=F32)
    values = values - jnp.sum(values, axis=1, keepdims=True) * (1.0 / SAMPLES)
    tapered = (values * taper_ref[...]).astype(BF16)
    spectrum = jnp.dot(tapered, basis_ref[...], preferred_element_type=F32)
    real, imag = spectrum[:, :FREQS], spectrum[:, FREQS:]
    energy = real * real + imag * imag
    smooth = jnp.dot(energy, smoother_ref[...], precision=lax.Precision.HIGHEST, preferred_element_type=F32)
    inverse = lax.rsqrt(smooth + EPSILON)
    real, imag = (real * inverse).astype(BF16), (imag * inverse).astype(BF16)
    for w in range(WIN):
        rows = slice(w * QC, (w + 1) * QC)
        out_ref[:, 2 * w * FREQS : (2 * w + 1) * FREQS] = real[rows]
        out_ref[:, (2 * w + 1) * FREQS : (2 * w + 2) * FREQS] = imag[rows]


def rotate_kernel(own_ref, cos_ref, sin_ref, out_ref, wide):
    wide[...] = own_ref[...].astype(F32)
    for g in range(FREQS // 128):
        cos = cos_ref[:, g * 128 : (g + 1) * 128]
        sin = sin_ref[:, g * 128 : (g + 1) * 128]
        for w in range(WIN):
            re = slice(2 * w * FREQS + g * 128, 2 * w * FREQS + (g + 1) * 128)
            im = slice((2 * w + 1) * FREQS + g * 128, (2 * w + 1) * FREQS + (g + 1) * 128)
            for i in range(16):
                a = wide[i : i + 1, re]
                b = wide[i : i + 1, im]
                out_ref[i * LAGS : (i + 1) * LAGS, re] = (a * cos - b * sin).astype(BF16)
                out_ref[i * LAGS : (i + 1) * LAGS, im] = (a * sin + b * cos).astype(BF16)


def target(out_ref, kind, part, coord, cols):
    if kind == "A":
        if part is None:
            return out_ref.at[pl.ds(2 * coord, 2), :, pl.ds(0, HALF), cols]
        return out_ref.at[2 * coord + part, :, pl.ds(0, HALF), cols]
    if part is None:
        return out_ref.at[:, coord, pl.ds(HALF, HALF), cols]
    return out_ref.at[pl.ds(4 * part, 4), coord, pl.ds(HALF, HALF), cols]


def matmul_kernel(kinds, coords_ref, *refs):
    n = len(kinds)
    pieces, rot_ref = refs[:n], refs[n]
    out_ref, left, acc, in_sem, out_sem = refs[-5:]
    step = pl.program_id(0)
    last = pl.num_programs(0) - 1
    slot = lax.rem(step, 2)
    starts = np.cumsum([0] + [p.shape[0] for p in pieces])

    def loads():
        return [
            pltpu.make_async_copy(p, left.at[pl.ds(int(starts[i]), p.shape[0])], in_sem.at[i])
            for i, p in enumerate(pieces)
        ]

    def stores(slot, step):
        cols = pl.ds(pl.multiple_of(step * NT, NT), NT)
        copies = []
        for i, (kind, part) in enumerate(kinds):
            units = pieces[i].shape[0] // HALF
            begin = int(starts[i]) // HALF
            if kind == "A" and part is None:
                src = acc.at[slot, pl.ds(begin // 4, 2)]
            elif kind == "A" or part is not None:
                src = acc.at[slot, begin // 4]
            if kind == "B" and part is None:
                for h in range(2):
                    copies.append(
                        pltpu.make_async_copy(
                            acc.at[slot, begin // 4 + h],
                            target(out_ref, kind, h, coords_ref[i], cols),
                            out_sem.at[slot, len(copies)],
                        )
                    )
            else:
                copies.append(
                    pltpu.make_async_copy(
                        src, target(out_ref, kind, part, coords_ref[i], cols), out_sem.at[slot, len(copies)]
                    )
                )
        return copies

    @pl.when(step == 0)
    def _():
        for c in loads():
            c.start()
        for c in loads():
            c.wait()

    @pl.when(step >= 2)
    def _():
        for c in stores(slot, step - 2):
            c.wait()

    product = lax.dot_general(left[...], rot_ref[...], (((1,), (1,)), ((), ())), preferred_element_type=F32)
    acc[slot] = product.reshape(acc.shape[1:])
    for c in stores(slot, step):
        c.start()

    @pl.when(step == last)
    def _():
        for c in stores(1 - slot, step - 1):
            c.wait()
        for c in stores(slot, step):
            c.wait()


def matmul(pieces, kinds, coords, rotated, out):
    rows = sum(p.shape[0] for p in pieces)
    columns = rotated.shape[0]
    operands = list(pieces) + [rotated]
    in_specs = [pl.BlockSpec(memory_space=pl.ANY)] * len(pieces) + [
        pl.BlockSpec((NT, SPEC), lambda s, c: (s, 0))
    ]
    aliases = {}
    if out is not None:
        operands.append(out)
        in_specs.append(pl.BlockSpec(memory_space=pl.ANY))
        aliases = {len(operands): 0}
    return pl.pallas_call(
        functools.partial(matmul_kernel, kinds),
        grid_spec=pltpu.PrefetchScalarGridSpec(
            num_scalar_prefetch=1,
            grid=(columns // NT,),
            in_specs=in_specs,
            out_specs=pl.BlockSpec(memory_space=pl.ANY),
            scratch_shapes=[
                pltpu.VMEM((rows, SPEC), BF16),
                pltpu.VMEM((2, rows // HALF // 4, 4, HALF, NT), F32),
                pltpu.SemaphoreType.DMA((len(pieces),)),
                pltpu.SemaphoreType.DMA((2, 2 * len(pieces))),
            ],
        ),
        out_shape=jax.ShapeDtypeStruct((NZ * NXH, NY, QC, columns), F32),
        input_output_aliases=aliases,
        compiler_params=pltpu.CompilerParams(
            dimension_semantics=("arbitrary",), vmem_limit_bytes=VMEM_LIMIT, has_side_effects=False
        ),
        cost_estimate=pl.CostEstimate(
            flops=2 * rows * columns * SPEC, bytes_accessed=2 * columns * SPEC + 4 * rows * columns, transcendentals=0
        ),
    )(jnp.stack(coords).astype(jnp.int32), *operands)


def shifted(value, dz, dxh, dy):
    pairs = []
    for z in range(NZ):
        for xh in range(NXH):
            for y in range(NY):
                to = (((z + dz) % NZ) * NXH + (xh + dxh) % NXH) * NY + (y + dy) % NY
                pairs.append(((z * NXH + xh) * NY + y, to))
    return lax.ppermute(value, "blk", pairs)


def local(raw, seg_chan, seg_win, file_count):
    basis, taper, smoother, cos, sin = (jnp.asarray(t) for t in tables())
    vmem = pl.BlockSpec(memory_space=pltpu.VMEM)
    packed = pl.pallas_call(
        pack_kernel,
        in_specs=[pl.BlockSpec(memory_space=pltpu.SMEM), vmem, vmem, vmem],
        out_specs=vmem,
        out_shape=jax.ShapeDtypeStruct((SLOTS, SAMPLES + TAIL), BF16),
        compiler_params=pltpu.CompilerParams(vmem_limit_bytes=VMEM_LIMIT),
    )(file_count, seg_chan.reshape(1, SLOTS), seg_win.reshape(1, SLOTS), raw)
    arrived = lax.all_to_all(
        packed.reshape(DEVICES, SLOTS // DEVICES, SAMPLES + TAIL),
        ("blk", "freq"),
        split_axis=0,
        concat_axis=0,
        tiled=True,
    ).reshape(SLOTS, SAMPLES + TAIL)
    white = pl.pallas_call(
        whiten_kernel,
        in_specs=[vmem] * 4,
        out_specs=vmem,
        out_shape=jax.ShapeDtypeStruct((QC, SPEC), BF16),
        compiler_params=pltpu.CompilerParams(vmem_limit_bytes=VMEM_LIMIT),
    )(arrived, basis, taper, smoother)

    own = lax.all_gather(white, "freq", axis=0, tiled=True)
    rotated = pl.pallas_call(
        rotate_kernel,
        grid=(own.shape[0] // 16,),
        in_specs=[
            pl.BlockSpec((16, SPEC), lambda s: (s, 0)),
            pl.BlockSpec((LAGS, FREQS), lambda s: (0, 0)),
            pl.BlockSpec((LAGS, FREQS), lambda s: (0, 0)),
        ],
        out_specs=pl.BlockSpec((16 * LAGS, SPEC), lambda s: (s, 0)),
        out_shape=jax.ShapeDtypeStruct((own.shape[0] * LAGS, SPEC), BF16),
        scratch_shapes=[pltpu.VMEM((16, SPEC), F32)],
        compiler_params=pltpu.CompilerParams(dimension_semantics=("arbitrary",), vmem_limit_bytes=VMEM_LIMIT),
        cost_estimate=pl.CostEstimate(flops=6 * 2048 * SPEC, bytes_accessed=2 * 2048 * SPEC, transcendentals=0),
    )(own, cos, sin)

    me = lax.axis_index("blk")
    z, xh, y = me // (NXH * NY), me // NY % NXH, me % NY
    other = shifted(white, 0, 1, 0)

    def spread(mine, theirs, step, place, count):
        held = jnp.concatenate([mine, theirs], axis=0)
        ahead = step(held, 1)
        behind = step(held, -1)
        far = [step(ahead[:HALF], 1), step(behind[HALF:], -1)]
        whole = jnp.zeros((8 * HALF, SPEC), BF16)
        parts = [
            (mine, place(0, 0)),
            (theirs, place(0, 1)),
            (ahead[:HALF], place(1, 0)),
            (ahead[HALF:], place(1, 1)),
            (behind[:HALF], place(-1, 0)),
            (behind[HALF:], place(-1, 1)),
            (far[0], place(2, 0)),
            (far[1], place(2, 1)),
        ]
        for value, spot in parts:
            whole = lax.dynamic_update_slice_in_dim(whole, value, spot * HALF, 0)
        return whole

    def along_y(value, d):
        return shifted(value, 0, 0, d)

    def along_z(value, d):
        return shifted(value, d, 0, 0)

    a8 = spread(
        white[:HALF], other[:HALF], along_y, lambda d, e: (xh + e) % NXH * NY + (y - d) % NY, NY
    )
    b8 = spread(
        white[HALF:], other[HALF:], along_z, lambda d, e: (z - d) % NZ * NXH + (xh + e) % NXH, NZ
    )
    a_ahead, a_behind = along_z(a8, 1), along_z(a8, -1)
    b_ahead, b_behind = along_y(b8, 1), along_y(b8, -1)
    cut = 4 * HALF
    a_far = [along_z(a_ahead[:cut], 1), along_z(a_behind[cut:], -1)]
    b_far = [along_y(b_ahead[:cut], 1), along_y(b_behind[cut:], -1)]

    out = matmul([a8, b8], [("A", None), ("B", None)], [z, y], rotated, None)
    out = matmul(
        [a_ahead, a_behind, b_ahead, b_behind],
        [("A", None), ("A", None), ("B", None), ("B", None)],
        [(z - 1) % NZ, (z + 1) % NZ, (y - 1) % NY, (y + 1) % NY],
        rotated,
        out,
    )
    out = matmul(
        a_far + b_far,
        [("A", 0), ("A", 1), ("B", 0), ("B", 1)],
        [(z + 2) % NZ, (z + 2) % NZ, (y + 2) % NY, (y + 2) % NY],
        rotated,
        out,
    )
    return out.reshape(NZ * NXH * NY, QC, -1)


def solution(mesh):
    in_specs = (
        P(("blk", "freq"), None),
        P(("blk", "freq")),
        P(("blk", "freq")),
        P(("blk", "freq")),
    )
    out_specs = P(None, "freq", "blk")
    return jax.shard_map(local, mesh=mesh, in_specs=in_specs, out_specs=out_specs, check_vma=False)
```

time: 627 us -> 145 us (0.23)
  waiting for transfers between devices: 414 us -> 23 us
  other arithmetic: 89.7 us -> 0.26 us
  Pallas kernels: 0 us -> 53.1 us
  local copies, waits for them, and re-layouts: 65.4 us -> 14 us
  matrix products: 25.3 us -> 0 us
  starting transfers between devices: 17.4 us -> 39.2 us
    ppermute x31 -> x17, waiting for transfers between devices: 392 us -> 9.07 us  [shifted(): return lax.ppermute(value, 'blk', pairs)]
    another operation x6 -> x3, other arithmetic: 85.8 us -> 0.23 us  [matmul(): jnp.stack(coords).astype(jnp.int32)]
    pallas_call x0 -> x6, Pallas kernels: none -> 53.1 us  [the longest x3 42.1 us: matmul(): pl.pallas_call(functools.partial(matmul_kernel, kinds), grid_spec=pltpu.P...]
    convert_element_type x6 -> x0, local copies, waits for them, and re-layouts: 29.1 us -> none  [the longest x1 27.6 us: rotate(): turned.astype(jnp.bfloat16).reshape(whitened.shape[0] * lag_count, -1)]
    ppermute x31 -> x17, starting transfers between devices: 1.57 us -> 28 us  [shifted(): return lax.ppermute(value, 'blk', pairs)]
    dot_general x3 -> x0, matrix products: 25.3 us -> none  [the longest x1 24.1 us: contract(): lax.dot_general(held_block, turned, (((1,), (1,)), ((), ())), preferred_e...]
    dynamic_update_slice x32 -> x9, local copies, waits for them, and re-layouts: 23.2 us -> 1.04 us  [spread(): whole = lax.dynamic_update_slice_in_dim(whole, value, spot * HALF, 0)]
    all_gather x1, waiting for transfers between devices: 13.2 us -> 0.01 us  [local(): own = lax.all_gather(white, 'freq', axis=0, tiled=True)]
  transfers between devices with their start and end apart: 34 -> 19, of which waited for: 34 -> 4; matrix products, arithmetic and copies ran while one was open for 3% -> 4% of each run, Pallas kernels for 0% -> 26%
where the time goes in v1:
time: 145 us; the launch traced here: 144 us
  Pallas kernels  53.1 us (37%)
  starting transfers between devices  39.2 us (27%)
  waiting for transfers between devices  23 us (16%)
  between operations  14.7 us (10%)
  local copies, waits for them, and re-layouts  14 us (10%)
    pallas_call x3, Pallas kernels, matmul(): pl.pallas_call(functools.partial(matmul_kernel, kinds), grid_spec=pltpu.P...  42.1 us
    ppermute x17, starting transfers between devices, shifted(): return lax.ppermute(value, 'blk', pairs)  28 us
    all_to_all x1, waiting for transfers between devices, local(): lax.all_to_all(packed.reshape(DEVICES, SLOTS // DEVICES, SAMPLES + TAIL),...  13.9 us
    all_to_all x1, starting transfers between devices, local(): lax.all_to_all(packed.reshape(DEVICES, SLOTS // DEVICES, SAMPLES + TAIL),...  11.1 us
    ppermute x17, waiting for transfers between devices, shifted(): return lax.ppermute(value, 'blk', pairs)  9.07 us
    pallas_call x1, Pallas kernels, local(): pl.pallas_call(rotate_kernel, grid=(own.shape[0] // 16,), in_specs=[pl.Bl...  8.42 us
    unnamed x18, local copies, waits for them, and re-layouts  7.12 us
  transfers between devices with their start and end apart: 19, of which 4 were waited for; matrix products, arithmetic and copies ran while one was open for 4% of the time, Pallas kernels for 26%

profile of v1, /device:TPU:0, one launch (start us, length us, event | category | flops | bytes accessed | tf_op | source)
XLA Modules:
  0.0 144.2 jit_solution(13050157378037572880)
XLA Ops:
  11.1 11.1 %all-to-all-start = ((bf16[128,2,1152]{2,1,0:T(2,128)(2,1)}), bf16[128,2,1152]{2,1,0:T(2,128)(2,1)S(1)}, u32[]{:S(2)}, u32[]{:S(2)}) async-start(bf16[128,2,1152]{2,1,0:T(2,128)(2,1)} %reshape.17), calls=%async_computation | async-start | bytes 1179648 | tf_op jit(solution)/shard_map/all_to_all | solution.py:240
  22.6 13.9 %all-to-all-done = bf16[128,2,1152]{2,1,0:T(2,128)(2,1)S(1)} async-done(((bf16[128,2,1152]{2,1,0:T(2,128)(2,1)}), bf16[128,2,1152]{2,1,0:T(2,128)(2,1)S(1)}, u32[]{:S(2)}, u32[]{:S(2)}) %all-to-all-start) | async-done | bytes 589856 | tf_op jit(solution)/shard_map/all_to_all | solution.py:240
  36.7 1.6 %copy-done = bf16[1024,1024]{1,0:T(8,128)(2,1)S(1)} copy-done((bf16[1024,1024]{1,0:T(8,128)(2,1)S(1)}, bf16[1024,1024]{1,0:T(8,128)(2,1)}, u32[]{:S(2)}) %copy-start) | copy-done | bytes 2097176
  38.3 1.2 copy-done.1
  40.2 2.1 %shard_map.92 = bf16[32,4096]{1,0:T(8,128)(2,1)} custom-call(bf16[256,1152]{1,0:T(8,128)(2,1)S(1)} %reshape.18.recv_ref, bf16[1024,1024]{1,0:T(8,128)(2,1)S(1)} %copy-done, f32[1,1024]{1,0:T(1,128)S(1)} %copy-done.6, f32[512,512]{1,0:T(8,128)S(1)} %copy-done.1), custom_call_target="tpu_custom_call" | custom-call | tf_op jit(solution)/shard_map/pallas_call | solution.py:247
  42.3 1.1 collective-permute-start
  45.6 6.4 %collective-permute-done = bf16[32,4096]{1,0:T(8,128)(2,1)S(1)} collective-permute-done((bf16[32,4096]{1,0:T(8,128)(2,1)}, bf16[32,4096]{1,0:T(8,128)(2,1)S(1)}, u32[]{:S(2)}, u32[]{:S(2)}) %collective-permute-start) | collective-permute-done | bytes 262176 | tf_op jit(solution)/shard_map/ppermute | solution.py:227
  53.0 2.4 %collective-permute-start.10 = (bf16[32,4096]{1,0:T(8,128)(2,1)S(1)}, bf16[32,4096]{1,0:T(8,128)(2,1)S(1)}, u32[]{:S(2)}, u32[]{:S(2)}) collective-permute-start(bf16[32,4096]{1,0:T(8,128)(2,1)S(1)} %pad_maximum_fusion.1), channel_id=1, source_target_pairs={{0,96},{4,100},{8,104},{12,108},{16,112},{20,116},{24,120},{28,124... | collective-permute-start | bytes 786440 | tf_op jit(solution)/shard_map/ppermute | solution.py:227
  56.0 2.8 %collective-permute-start.2 = (bf16[32,4096]{1,0:T(8,128)(2,1)S(1)}, bf16[32,4096]{1,0:T(8,128)(2,1)S(1)}, u32[]{:S(2)}, u32[]{:S(2)}) collective-permute-start(bf16[32,4096]{1,0:T(8,128)(2,1)S(1)} %pad_maximum_fusion), channel_id=1, source_target_pairs={{0,12},{4,0},{8,4},{12,8},{16,28},{20,16},{24,20},{28,24},{32,44},... | collective-permute-start | bytes 786440 | tf_op jit(solution)/shard_map/ppermute | solution.py:227
  58.8 1.8 %collective-permute-done.9 = bf16[32,4096]{1,0:T(8,128)(2,1)S(1)} collective-permute-done((bf16[32,4096]{1,0:T(8,128)(2,1)S(1)}, bf16[32,4096]{1,0:T(8,128)(2,1)S(1)}, u32[]{:S(2)}, u32[]{:S(2)}) %collective-permute-start.9) | collective-permute-done | bytes 262176 | tf_op jit(solution)/shard_map/ppermute | solution.py:227
  60.9 3.2 %collective-permute-start.12 = (bf16[16,4096]{1,0:T(8,128)(2,1)S(1)}, bf16[16,4096]{1,0:T(8,128)(2,1)S(1)}, u32[]{:S(2)}, u32[]{:S(2)}) collective-permute-start(bf16[16,4096]{1,0:T(8,128)(2,1)S(1)} %get-tuple-element.5), channel_id=1, source_target_pairs={{0,96},{4,100},{8,104},{12,108},{16,112},{20,116},{24,120},{28,124... | collective-permute-start | bytes 393224 | tf_op jit(solution)/shard_map/ppermute | solution.py:227
  65.1 2.4 %collective-permute-start.4 = (bf16[16,4096]{1,0:T(8,128)(2,1)S(1)}, bf16[16,4096]{1,0:T(8,128)(2,1)S(1)}, u32[]{:S(2)}, u32[]{:S(2)}) collective-permute-start(bf16[16,4096]{1,0:T(8,128)(2,1)S(1)} %get-tuple-element.16), channel_id=1, source_target_pairs={{0,12},{4,0},{8,4},{12,8},{16,28},{20,16},{24,20},{28,24},{32,44},... | collective-permute-start | bytes 393224 | tf_op jit(solution)/shard_map/ppermute | solution.py:227
  67.9 3.0 %collective-permute-start.15 = (bf16[128,4096]{1,0:T(8,128)(2,1)S(1)}, bf16[128,4096]{1,0:T(8,128)(2,1)}, u32[]{:S(2)}, u32[]{:S(2)}) collective-permute-start(bf16[128,4096]{1,0:T(8,128)(2,1)S(1)} %constant_dynamic-update-slice_fusion.refs_1_), channel_id=1, source_target_pairs={{0,12},{4,0},{8,4},{12,8},{16,28},{20,16},{24,20},{28,24},{32,44},... | collective-permute-start | bytes 3145736 | tf_op jit(solution)/shard_map/ppermute | solution.py:227
  71.8 3.2 %collective-permute-start.7 = (bf16[128,4096]{1,0:T(8,128)(2,1)S(1)}, bf16[128,4096]{1,0:T(8,128)(2,1)}, u32[]{:S(2)}, u32[]{:S(2)}) collective-permute-start(bf16[128,4096]{1,0:T(8,128)(2,1)S(1)} %constant_dynamic-update-slice_fusion.6.refs_0_), channel_id=1, source_target_pairs={{0,96},{4,100},{8,104},{12,108},{16,112},{20,116},{24,120},{28,124... | collective-permute-start | bytes 3145736 | tf_op jit(solution)/shard_map/ppermute | solution.py:227
  75.3 1.2 copy-done.2
  76.5 8.4 %shard_map.93.refs_2_.refs_4_ = bf16[2048,4096]{1,0:T(8,128)(2,1)} custom-call(bf16[128,4096]{1,0:T(8,128)(2,1)S(1)} %copy-done.2, f32[16,512]{1,0:T(8,128)S(1)} %copy-done.4, f32[16,512]{1,0:T(8,128)S(1)} %copy-done.5), custom_call_target="tpu_custom_call" | custom-call | flops 50331648 | bytes 16777216 | tf_op jit(solution)/shard_map/pallas_call | solution.py:256
  84.9 12.4 %shard_map.94.refs_5_ = f32[8,4,32,2048]{3,2,1,0:T(8,128)} custom-call(s32[2]{0:T(128)S(1)} %pad_add_fusion.2.coords_ref, bf16[128,4096]{1,0:T(8,128)(2,1)S(1)} %constant_dynamic-update-slice_fusion.6.refs_0_, bf16[128,4096]{1,0:T(8,128)(2,1)S(1)} %constant_dynamic-update-slice_fusion.refs_1_, bf16[2048,4096]{1,0:T(8,128)(2,1)} %shard_map.93.refs_2_.refs_4_), custom_call_target="tpu_custom_call" | custom-call | flops 4294967296 | bytes 18874368 | tf_op jit(solution)/shard_map/pallas_call | solution.py:195
  97.5 1.1 slice.83
  98.6 3.5 %collective-permute-start.16 = (bf16[64,4096]{1,0:T(8,128)(2,1)S(1)}, bf16[64,4096]{1,0:T(8,128)(2,1)S(1)}, u32[]{:S(2)}, u32[]{:S(2)}) collective-permute-start(bf16[64,4096]{1,0:T(8,128)(2,1)S(1)} %slice.83), channel_id=1, source_target_pairs={{0,12},{4,0},{8,4},{12,8},{16,28},{20,16},{24,20},{28,24},{32,44},... | collective-permute-start | bytes 1572872 | tf_op jit(solution)/shard_map/ppermute | solution.py:227
  102.0 1.1 slice.74
  103.2 1.1 slice.75
  104.3 3.3 %collective-permute-start.8 = (bf16[64,4096]{1,0:T(8,128)(2,1)S(1)}, bf16[64,4096]{1,0:T(8,128)(2,1)S(1)}, u32[]{:S(2)}, u32[]{:S(2)}) collective-permute-start(bf16[64,4096]{1,0:T(8,128)(2,1)S(1)} %slice.75), channel_id=1, source_target_pairs={{0,96},{4,100},{8,104},{12,108},{16,112},{20,116},{24,120},{28,124... | collective-permute-start | bytes 1572872 | tf_op jit(solution)/shard_map/ppermute | solution.py:227
  107.6 17.2 %shard_map.95.refs_5_ = f32[8,4,32,2048]{3,2,1,0:T(8,128)} custom-call(s32[4]{0:T(128)S(1)} %pad_add_fusion.1.coords_ref, bf16[128,4096]{1,0:T(8,128)(2,1)} %collective-permute-done.5.refs_0_, bf16[128,4096]{1,0:T(8,128)(2,1)} %collective-permute-done.7.refs_1_, ...), custom_call_target="tpu_custom_call", output_to_operand_aliasing={{}: (6, {})} | custom-call | flops 8589934592 | bytes 20971520 | tf_op jit(solution)/shard_map/pallas_call | solution.py:195
  124.8 12.5 %shard_map.96 = f32[8,4,32,2048]{3,2,1,0:T(8,128)} custom-call(s32[4]{0:T(128)S(1)} %pad_add_fusion.coords_ref, bf16[64,4096]{1,0:T(8,128)(2,1)S(1)} %collective-permute-done.6.refs_0_, bf16[64,4096]{1,0:T(8,128)(2,1)S(1)} %collective-permute-done.8.refs_1_, bf16[64,4096]{1,0:T(8,128)(2,1)S(1)} %collective-permute-done.14.refs_2_, ...), custom_call_target="tpu_custom_call", output_to_operand_aliasing={{}: (6, {})} | custom-call | flops 4294967296 | bytes 18874368 | tf_op jit(solution)/shard_map/pallas_call | solution.py:195
  (67 shorter events, 11.3 us)
Async XLA Ops:
  10.0 65.3 %copy-start.4 = (f32[16,512]{1,0:T(8,128)S(1)}, f32[16,512]{1,0:T(8,128)}, u32[]{:S(2)}) copy-start(f32[16,512]{1,0:T(8,128)} %constant.183.clone.cos_ref) | copy-start | bytes 98308
  10.0 65.2 %copy-start.5 = (f32[16,512]{1,0:T(8,128)S(1)}, f32[16,512]{1,0:T(8,128)}, u32[]{:S(2)}) copy-start(f32[16,512]{1,0:T(8,128)} %constant.184.clone.sin_ref) | copy-start | bytes 98308
  11.1 25.4 %all-to-all-start = ((bf16[128,2,1152]{2,1,0:T(2,128)(2,1)}), bf16[128,2,1152]{2,1,0:T(2,128)(2,1)S(1)}, u32[]{:S(2)}, u32[]{:S(2)}) async-start(bf16[128,2,1152]{2,1,0:T(2,128)(2,1)} %reshape.17), calls=%async_computation | async-start | bytes 1179648 | tf_op jit(solution)/shard_map/all_to_all | solution.py:240
  22.2 53.1 %all-gather.2.cloned.1.call-start = ((), (), s32[]{:S(2)}) async-start(), calls=%async_computation.1 | async-start | bytes 1310720 | tf_op jit(solution)/shard_map/all_gather | solution.py:255
  36.7 1.6 %copy-start = (bf16[1024,1024]{1,0:T(8,128)(2,1)S(1)}, bf16[1024,1024]{1,0:T(8,128)(2,1)}, u32[]{:S(2)}) copy-start(bf16[1024,1024]{1,0:T(8,128)(2,1)} %constant.180.clone.basis_ref) | copy-start | bytes 6291460
  38.3 1.2 copy-start.1
  42.3 9.8 %collective-permute-start = (bf16[32,4096]{1,0:T(8,128)(2,1)}, bf16[32,4096]{1,0:T(8,128)(2,1)S(1)}, u32[]{:S(2)}, u32[]{:S(2)}) collective-permute-start(bf16[32,4096]{1,0:T(8,128)(2,1)} %shard_map.92), channel_id=1, source_target_pairs={{0,16},{4,20},{8,24},{12,28},{16,0},{20,4},{24,8},{28,12},{32,48},... | collective-permute-start | bytes 786440 | tf_op jit(solution)/shard_map/ppermute | solution.py:227
  52.1 8.4 %collective-permute-start.9 = (bf16[32,4096]{1,0:T(8,128)(2,1)S(1)}, bf16[32,4096]{1,0:T(8,128)(2,1)S(1)}, u32[]{:S(2)}, u32[]{:S(2)}) collective-permute-start(bf16[32,4096]{1,0:T(8,128)(2,1)S(1)} %pad_maximum_fusion.1), channel_id=1, source_target_pairs={{0,32},{4,36},{8,40},{12,44},{16,48},{20,52},{24,56},{28,60},{32,6... | collective-permute-start | bytes 786440 | tf_op jit(solution)/shard_map/ppermute | solution.py:227
  53.0 7.8 %collective-permute-start.10 = (bf16[32,4096]{1,0:T(8,128)(2,1)S(1)}, bf16[32,4096]{1,0:T(8,128)(2,1)S(1)}, u32[]{:S(2)}, u32[]{:S(2)}) collective-permute-start(bf16[32,4096]{1,0:T(8,128)(2,1)S(1)} %pad_maximum_fusion.1), channel_id=1, source_target_pairs={{0,96},{4,100},{8,104},{12,108},{16,112},{20,116},{24,120},{28,124... | collective-permute-start | bytes 786440 | tf_op jit(solution)/shard_map/ppermute | solution.py:227
  55.5 8.6 %collective-permute-start.1 = (bf16[32,4096]{1,0:T(8,128)(2,1)S(1)}, bf16[32,4096]{1,0:T(8,128)(2,1)S(1)}, u32[]{:S(2)}, u32[]{:S(2)}) collective-permute-start(bf16[32,4096]{1,0:T(8,128)(2,1)S(1)} %pad_maximum_fusion), channel_id=1, source_target_pairs={{0,4},{4,8},{8,12},{12,0},{16,20},{20,24},{24,28},{28,16},{32,36},... | collective-permute-start | bytes 786440 | tf_op jit(solution)/shard_map/ppermute | solution.py:227
  56.0 9.1 %collective-permute-start.2 = (bf16[32,4096]{1,0:T(8,128)(2,1)S(1)}, bf16[32,4096]{1,0:T(8,128)(2,1)S(1)}, u32[]{:S(2)}, u32[]{:S(2)}) collective-permute-start(bf16[32,4096]{1,0:T(8,128)(2,1)S(1)} %pad_maximum_fusion), channel_id=1, source_target_pairs={{0,12},{4,0},{8,4},{12,8},{16,28},{20,16},{24,20},{28,24},{32,44},... | collective-permute-start | bytes 786440 | tf_op jit(solution)/shard_map/ppermute | solution.py:227
  60.6 6.9 %collective-permute-start.11 = (bf16[16,4096]{1,0:T(8,128)(2,1)S(1)}, bf16[16,4096]{1,0:T(8,128)(2,1)S(1)}, u32[]{:S(2)}, u32[]{:S(2)}) collective-permute-start(bf16[16,4096]{1,0:T(8,128)(2,1)S(1)} %get-tuple-element.7), channel_id=1, source_target_pairs={{0,32},{4,36},{8,40},{12,44},{16,48},{20,52},{24,56},{28,60},{32,6... | collective-permute-start | bytes 393224 | tf_op jit(solution)/shard_map/ppermute | solution.py:227
  60.9 6.7 %collective-permute-start.12 = (bf16[16,4096]{1,0:T(8,128)(2,1)S(1)}, bf16[16,4096]{1,0:T(8,128)(2,1)S(1)}, u32[]{:S(2)}, u32[]{:S(2)}) collective-permute-start(bf16[16,4096]{1,0:T(8,128)(2,1)S(1)} %get-tuple-element.5), channel_id=1, source_target_pairs={{0,96},{4,100},{8,104},{12,108},{16,112},{20,116},{24,120},{28,124... | collective-permute-start | bytes 393224 | tf_op jit(solution)/shard_map/ppermute | solution.py:227
  64.1 7.6 %collective-permute-start.3 = (bf16[16,4096]{1,0:T(8,128)(2,1)S(1)}, bf16[16,4096]{1,0:T(8,128)(2,1)S(1)}, u32[]{:S(2)}, u32[]{:S(2)}) collective-permute-start(bf16[16,4096]{1,0:T(8,128)(2,1)S(1)} %get-tuple-element.18), channel_id=1, source_target_pairs={{0,4},{4,8},{8,12},{12,0},{16,20},{20,24},{24,28},{28,16},{32,36},... | collective-permute-start | bytes 393224 | tf_op jit(solution)/shard_map/ppermute | solution.py:227
  65.1 6.6 %collective-permute-start.4 = (bf16[16,4096]{1,0:T(8,128)(2,1)S(1)}, bf16[16,4096]{1,0:T(8,128)(2,1)S(1)}, u32[]{:S(2)}, u32[]{:S(2)}) collective-permute-start(bf16[16,4096]{1,0:T(8,128)(2,1)S(1)} %get-tuple-element.16), channel_id=1, source_target_pairs={{0,12},{4,0},{8,4},{12,8},{16,28},{20,16},{24,20},{28,24},{32,44},... | collective-permute-start | bytes 393224 | tf_op jit(solution)/shard_map/ppermute | solution.py:227
  67.6 29.7 %collective-permute-start.13 = (bf16[128,4096]{1,0:T(8,128)(2,1)S(1)}, bf16[128,4096]{1,0:T(8,128)(2,1)S(1)}, u32[]{:S(2)}, u32[]{:S(2)}) collective-permute-start(bf16[128,4096]{1,0:T(8,128)(2,1)S(1)} %constant_dynamic-update-slice_fusion.refs_1_), channel_id=1, source_target_pairs={{0,4},{4,8},{8,12},{12,0},{16,20},{20,24},{24,28},{28,16},{32,36},... | collective-permute-start | bytes 3145736 | tf_op jit(solution)/shard_map/ppermute | solution.py:227
  67.9 29.6 %collective-permute-start.15 = (bf16[128,4096]{1,0:T(8,128)(2,1)S(1)}, bf16[128,4096]{1,0:T(8,128)(2,1)}, u32[]{:S(2)}, u32[]{:S(2)}) collective-permute-start(bf16[128,4096]{1,0:T(8,128)(2,1)S(1)} %constant_dynamic-update-slice_fusion.refs_1_), channel_id=1, source_target_pairs={{0,12},{4,0},{8,4},{12,8},{16,28},{20,16},{24,20},{28,24},{32,44},... | collective-permute-start | bytes 3145736 | tf_op jit(solution)/shard_map/ppermute | solution.py:227
  71.7 30.3 %collective-permute-start.5 = (bf16[128,4096]{1,0:T(8,128)(2,1)S(1)}, bf16[128,4096]{1,0:T(8,128)(2,1)}, u32[]{:S(2)}, u32[]{:S(2)}) collective-permute-start(bf16[128,4096]{1,0:T(8,128)(2,1)S(1)} %constant_dynamic-update-slice_fusion.6.refs_0_), channel_id=1, source_target_pairs={{0,32},{4,36},{8,40},{12,44},{16,48},{20,52},{24,56},{28,60},{32,6... | collective-permute-start | bytes 3145736 | tf_op jit(solution)/shard_map/ppermute | solution.py:227
  71.8 31.4 %collective-permute-start.7 = (bf16[128,4096]{1,0:T(8,128)(2,1)S(1)}, bf16[128,4096]{1,0:T(8,128)(2,1)}, u32[]{:S(2)}, u32[]{:S(2)}) collective-permute-start(bf16[128,4096]{1,0:T(8,128)(2,1)S(1)} %constant_dynamic-update-slice_fusion.6.refs_0_), channel_id=1, source_target_pairs={{0,96},{4,100},{8,104},{12,108},{16,112},{20,116},{24,120},{28,124... | collective-permute-start | bytes 3145736 | tf_op jit(solution)/shard_map/ppermute | solution.py:227
  75.3 1.2 copy-start.2
  97.4 27.4 %collective-permute-start.14 = (bf16[64,4096]{1,0:T(8,128)(2,1)S(1)}, bf16[64,4096]{1,0:T(8,128)(2,1)S(1)}, u32[]{:S(2)}, u32[]{:S(2)}) collective-permute-start(bf16[64,4096]{1,0:T(8,128)(2,1)S(1)} %slice.82), channel_id=1, source_target_pairs={{0,4},{4,8},{8,12},{12,0},{16,20},{20,24},{24,28},{28,16},{32,36},... | collective-permute-start | bytes 1572872 | tf_op jit(solution)/shard_map/ppermute | solution.py:227
  98.6 26.3 %collective-permute-start.16 = (bf16[64,4096]{1,0:T(8,128)(2,1)S(1)}, bf16[64,4096]{1,0:T(8,128)(2,1)S(1)}, u32[]{:S(2)}, u32[]{:S(2)}) collective-permute-start(bf16[64,4096]{1,0:T(8,128)(2,1)S(1)} %slice.83), channel_id=1, source_target_pairs={{0,12},{4,0},{8,4},{12,8},{16,28},{20,16},{24,20},{28,24},{32,44},... | collective-permute-start | bytes 1572872 | tf_op jit(solution)/shard_map/ppermute | solution.py:227
  103.1 21.7 %collective-permute-start.6 = (bf16[64,4096]{1,0:T(8,128)(2,1)S(1)}, bf16[64,4096]{1,0:T(8,128)(2,1)S(1)}, u32[]{:S(2)}, u32[]{:S(2)}) collective-permute-start(bf16[64,4096]{1,0:T(8,128)(2,1)S(1)} %slice.74), channel_id=1, source_target_pairs={{0,32},{4,36},{8,40},{12,44},{16,48},{20,52},{24,56},{28,60},{32,6... | collective-permute-start | bytes 1572872 | tf_op jit(solution)/shard_map/ppermute | solution.py:227
  104.3 20.5 %collective-permute-start.8 = (bf16[64,4096]{1,0:T(8,128)(2,1)S(1)}, bf16[64,4096]{1,0:T(8,128)(2,1)S(1)}, u32[]{:S(2)}, u32[]{:S(2)}) collective-permute-start(bf16[64,4096]{1,0:T(8,128)(2,1)S(1)} %slice.75), channel_id=1, source_target_pairs={{0,96},{4,100},{8,104},{12,108},{16,112},{20,116},{24,120},{28,124... | collective-permute-start | bytes 1572872 | tf_op jit(solution)/shard_map/ppermute | solution.py:227
  (4 other events, 3.1 us)
Sparse Core Ops, SparseCore 0:
  43.6 17.4 all-gather.1

commit v2 on v1

v2 whole, which is shorter than its diff:
```python
import functools
import math

import jax
import jax.numpy as jnp
import ml_dtypes
import numpy as np
from jax import lax
from jax.experimental import pallas as pl
from jax.experimental.pallas import tpu as pltpu
from jax.sharding import PartitionSpec as P

SAMPLES = 1024
FREQS = 512
LAGS = 16
HALFWIN = 64
WIN = 4
EPSILON = 1e-06

NZ, NXH, NY = 4, 2, 4
NXL, NCORE = 2, 2
QC = 32
HALF = QC // 2
CB = QC * NXL * NCORE
SEG_DEV = QC * WIN
SLOTS = 256
DEVICES = 128
SPEC = WIN * 2 * FREQS
COLS = CB * LAGS
TAIL = 128
NT = 512
GROUP = 4
F32, BF16 = jnp.float32, jnp.bfloat16
MIB = 1024 * 1024
ANY = pl.BlockSpec(memory_space=pl.ANY)
VMEM = pl.BlockSpec(memory_space=pltpu.VMEM)
SMEM = pl.BlockSpec(memory_space=pltpu.SMEM)


def tables():
    n = np.arange(SAMPLES)[:, None]
    k = np.arange(FREQS)[None, :]
    angle = 2.0 * math.pi / SAMPLES * ((n * k) % SAMPLES)
    basis = np.concatenate([np.cos(angle), -np.sin(angle)], axis=1).astype(ml_dtypes.bfloat16)
    taper = (0.5 - 0.5 * np.cos(2.0 * math.pi / SAMPLES * (n[:, 0] + 0.5)))[None, :].astype(np.float32)
    pos = np.arange(FREQS)
    inside = (np.abs(pos[:, None] - pos[None, :]) <= HALFWIN).astype(np.float64)
    smoother = (inside / inside.sum(axis=0, keepdims=True)).astype(np.float32)
    lag = np.arange(128)[None, :] % LAGS - LAGS // 2
    phi = 2.0 * math.pi / SAMPLES * ((lag * pos[:, None]) % SAMPLES)
    gain = np.where(pos == 0, 1.0, 2.0)[:, None] / math.sqrt(2.0 * WIN * FREQS)
    turn = np.concatenate([gain * np.cos(phi), gain * np.sin(phi)], axis=0).astype(np.float32)
    return basis, taper, smoother, turn


def diagonal(size):
    return lax.broadcasted_iota(jnp.int32, (size, size), 0) == lax.broadcasted_iota(jnp.int32, (size, size), 1)


def pack_kernel(count_ref, chan_hbm, win_hbm, raw_hbm, out_ref, chan_ref, win_ref, raw_ref, sem):
    loads = [
        pltpu.make_async_copy(chan_hbm, chan_ref, sem.at[0]),
        pltpu.make_async_copy(win_hbm, win_ref, sem.at[1]),
        pltpu.make_async_copy(raw_hbm, raw_ref, sem.at[2]),
    ]
    for c in loads:
        c.start()
    loads[0].wait()
    loads[1].wait()
    chan = chan_ref[...]
    slot = lax.broadcasted_iota(jnp.int32, (1, SLOTS), 1)
    live = slot < count_ref[0]
    owner = jnp.where(live, chan // QC, -1).astype(F32)
    owner_col = jnp.sum(jnp.where(diagonal(SLOTS), owner, 0.0), axis=1, keepdims=True)
    row = lax.broadcasted_iota(jnp.int32, (SLOTS, SLOTS), 0)
    col = lax.broadcasted_iota(jnp.int32, (SLOTS, SLOTS), 1)
    earlier = jnp.where((owner_col == owner) & (row < col), 1.0, 0.0)
    rank = jnp.sum(earlier, axis=0, keepdims=True)
    flat = jnp.where(live, owner * 2.0 + rank, -1.0)
    pick = jnp.where(flat == row.astype(F32), 1.0, 0.0)
    place = (win_ref[...] * QC + chan % QC + 1).astype(F32)
    place_col = jnp.sum(pick * place, axis=1, keepdims=True)
    out_ref[:, SAMPLES:] = jnp.broadcast_to(place_col, (SLOTS, TAIL)).astype(BF16)
    loads[2].wait()
    out_ref[:, :SAMPLES] = jnp.dot(pick.astype(BF16), raw_ref[...], preferred_element_type=F32).astype(BF16)


def fetch_kernel(after_hbm, basis_hbm, taper_hbm, smoother_hbm, turn_hbm, basis_ref, taper_ref, smoother_ref, turn_ref, sem):
    del after_hbm
    pairs = [(basis_hbm, basis_ref), (taper_hbm, taper_ref), (smoother_hbm, smoother_ref), (turn_hbm, turn_ref)]
    loads = [pltpu.make_async_copy(s, d, sem.at[i]) for i, (s, d) in enumerate(pairs)]
    for c in loads:
        c.start()
    for c in loads:
        c.wait()


def whiten_kernel(core_ref, recv_ref, basis_ref, taper_ref, smoother_ref, out_ref):
    place_col = recv_ref[:, SAMPLES : SAMPLES + 1].astype(F32)
    place = jnp.sum(jnp.where(diagonal(SLOTS), place_col, 0.0), axis=0, keepdims=True)
    row = lax.broadcasted_iota(jnp.int32, (SEG_DEV, SLOTS), 0)
    wanted = row // QC * QC + (row + core_ref[0] * HALF) % QC + 1
    pick = jnp.where(place == wanted.astype(F32), 1.0, 0.0).astype(BF16)
    values = jnp.dot(pick, recv_ref[:, :SAMPLES], preferred_element_type=F32)
    values = values - jnp.sum(values, axis=1, keepdims=True) * (1.0 / SAMPLES)
    tapered = (values * taper_ref[...]).astype(BF16)
    spectrum = jnp.dot(tapered, basis_ref[...], preferred_element_type=F32)
    real, imag = spectrum[:, :FREQS], spectrum[:, FREQS:]
    energy = real * real + imag * imag
    smooth = jnp.dot(energy, smoother_ref[...], precision=lax.Precision.HIGHEST, preferred_element_type=F32)
    inverse = lax.rsqrt(smooth + EPSILON)
    real, imag = (real * inverse).astype(BF16), (imag * inverse).astype(BF16)
    for w in range(WIN):
        rows = slice(w * QC, (w + 1) * QC)
        out_ref[:, 2 * w * FREQS : (2 * w + 1) * FREQS] = real[rows]
        out_ref[:, (2 * w + 1) * FREQS : (2 * w + 2) * FREQS] = imag[rows]


def rotate_kernel(quarter_ref, own0, own1, own2, own3, turn_ref, out_ref, turned, expand):
    col = lax.broadcasted_iota(jnp.int32, (QC, COLS), 1) // LAGS
    row = lax.broadcasted_iota(jnp.int32, (QC, COLS), 0)
    for g, own in enumerate((own0, own1, own2, own3)):
        turned[:, g * QC : (g + 1) * QC] = own[...].T
        q = quarter_ref[g]
        channel = q * QC + (row + (q % NCORE) * HALF) % QC
        expand[g * QC : (g + 1) * QC, :] = jnp.where(col == channel, 1.0, 0.0).astype(BF16)
    step = 64
    per = FREQS // step

    def body(s, carry):
        w, k0 = s // per, pl.multiple_of(lax.rem(s, per) * step, step)
        re = pl.ds(pl.multiple_of(w * 2 * FREQS + k0, step), step)
        im = pl.ds(pl.multiple_of((w * 2 + 1) * FREQS + k0, step), step)
        cos = turn_ref[pl.ds(k0, step), :]
        sin = turn_ref[pl.ds(FREQS + k0, step), :]
        for n in range(COLS // 256):
            a2 = jnp.dot(turned[re, :], expand[:, n * 256 : (n + 1) * 256], preferred_element_type=F32)
            b2 = jnp.dot(turned[im, :], expand[:, n * 256 : (n + 1) * 256], preferred_element_type=F32)
            for h in range(2):
                a, b = a2[:, h * 128 : (h + 1) * 128], b2[:, h * 128 : (h + 1) * 128]
                cols = slice(n * 256 + h * 128, n * 256 + (h + 1) * 128)
                out_ref[re, cols] = (a * cos - b * sin).astype(BF16)
                out_ref[im, cols] = (a * sin + b * cos).astype(BF16)
        return carry

    lax.fori_loop(0, WIN * per, body, 0)


def matmul_kernel(count, ids_ref, *refs):
    mine, theirs, rot_ref = refs[:count], refs[count : 2 * count], refs[2 * count]
    out_ref, left, acc, in_sem, out_sem = refs[-5:]
    rows = GROUP * HALF
    units = 2 * count * GROUP
    loads = []
    for i in range(count):
        loads.append(
            pltpu.make_async_copy(mine[i].at[pl.ds(0, rows)], left.at[pl.ds(2 * i * rows, rows)], in_sem.at[2 * i])
        )
        loads.append(
            pltpu.make_async_copy(
                theirs[i].at[pl.ds(rows, rows)], left.at[pl.ds((2 * i + 1) * rows, rows)], in_sem.at[2 * i + 1]
            )
        )
    for c in loads:
        c.start()
    for c in loads:
        c.wait()

    def stores(slot, step):
        cols = pl.ds(pl.multiple_of(step * NT, NT), NT)
        return [
            pltpu.make_async_copy(acc.at[slot, u], out_ref.at[ids_ref[u], :, cols], out_sem.at[slot, u])
            for u in range(units)
        ]

    for step in range(COLS // NT):
        slot = step % 2
        if step >= 2:
            for c in stores(slot, step - 2):
                c.wait()
        product = jnp.dot(left[...], rot_ref[:, step * NT : (step + 1) * NT], preferred_element_type=F32)
        acc[slot] = product.reshape(units, HALF, NT)
        for c in stores(slot, step):
            c.start()
    for step in range(COLS // NT - 2, COLS // NT):
        for c in stores(step % 2, step):
            c.wait()


def matmul(mine, theirs, ids, rotated, out):
    count = len(mine)
    rows = 2 * count * GROUP * HALF
    operands = [jnp.concatenate(ids), *mine, *theirs, rotated]
    in_specs = [SMEM] + [ANY] * (2 * count) + [VMEM]
    aliases = {}
    if out is not None:
        aliases = {len(operands): 0}
        operands.append(out)
        in_specs.append(ANY)
    return pl.pallas_call(
        functools.partial(matmul_kernel, count),
        in_specs=in_specs,
        out_specs=ANY,
        scratch_shapes=[
            pltpu.VMEM((rows, SPEC), BF16),
            pltpu.VMEM((2, rows // HALF, HALF, NT), F32),
            pltpu.SemaphoreType.DMA((2 * count,)),
            pltpu.SemaphoreType.DMA((2, rows // HALF)),
        ],
        out_shape=jax.ShapeDtypeStruct((NZ * NXH * NY * 2, HALF, COLS), F32),
        input_output_aliases=aliases,
        compiler_params=pltpu.CompilerParams(vmem_limit_bytes=20 * MIB),
        cost_estimate=pl.CostEstimate(
            flops=2 * rows * COLS * SPEC, bytes_accessed=2 * rows * SPEC + 4 * rows * COLS, transcendentals=0
        ),
    )(*operands)


def permuted(value, move):
    sizes = (NZ, NXH, NY, NXL, NCORE)
    pairs = []
    for source in range(DEVICES):
        place = np.unravel_index(source, sizes)
        to = [int(t) % s for t, s in zip(move(*(int(p) for p in place)), sizes, strict=True)]
        pairs.append((source, int(np.ravel_multi_index(to, sizes))))
    return lax.ppermute(value, ("blk", "freq"), pairs)


def first(value, d):
    return permuted(value, lambda z, xh, y, xl, c: (z + d * c, xh, y + d * (1 - c), xl, c))


def second(value, d):
    return permuted(value, lambda z, xh, y, xl, c: (z + d * (1 - c), xh, y + d * c, xl, c))


def across(value):
    return permuted(value, lambda z, xh, y, xl, c: (z, xh + 1, y, xl, c))


def sibling(value):
    return permuted(value, lambda z, xh, y, xl, c: (z, xh, y, xl, c + 1))


def neighbour(value):
    return permuted(value, lambda z, xh, y, xl, c: (z, xh, y, xl + 1, c))


def grouped(units):
    return jnp.concatenate([u[:HALF] for u in units] + [u[HALF:] for u in units], axis=0)


def local(raw, seg_chan, seg_win, file_count):
    basis, taper, smoother, turn = (jnp.asarray(t) for t in tables())
    blk, freq = lax.axis_index("blk"), lax.axis_index("freq")
    z, xh, y = blk // (NXH * NY), blk // NY % NXH, blk % NY
    xl, core = freq // NCORE, freq % NCORE

    packed = pl.pallas_call(
        pack_kernel,
        in_specs=[SMEM, ANY, ANY, ANY],
        out_specs=VMEM,
        out_shape=jax.ShapeDtypeStruct((SLOTS, SAMPLES + TAIL), BF16),
        scratch_shapes=[
            pltpu.VMEM((1, SLOTS), jnp.int32),
            pltpu.VMEM((1, SLOTS), jnp.int32),
            pltpu.VMEM((SLOTS, SAMPLES), BF16),
            pltpu.SemaphoreType.DMA((3,)),
        ],
        compiler_params=pltpu.CompilerParams(vmem_limit_bytes=8 * MIB),
    )(file_count, seg_chan.reshape(1, SLOTS), seg_win.reshape(1, SLOTS), raw)
    arrived = lax.all_to_all(
        packed.reshape(DEVICES, SLOTS // DEVICES, SAMPLES + TAIL),
        ("blk", "freq"),
        split_axis=0,
        concat_axis=0,
        tiled=True,
    ).reshape(SLOTS, SAMPLES + TAIL)
    tabled = (basis, taper, smoother, turn)
    basis, taper, smoother, turn = pl.pallas_call(
        fetch_kernel,
        in_specs=[ANY] * 5,
        out_specs=[VMEM] * 4,
        out_shape=[jax.ShapeDtypeStruct(t.shape, t.dtype) for t in tabled],
        scratch_shapes=[pltpu.SemaphoreType.DMA((4,))],
        compiler_params=pltpu.CompilerParams(vmem_limit_bytes=8 * MIB),
        cost_estimate=pl.CostEstimate(flops=0, bytes_accessed=8 * MIB, transcendentals=0),
    )(packed, *tabled)
    white = pl.pallas_call(
        whiten_kernel,
        in_specs=[SMEM] + [VMEM] * 4,
        out_specs=VMEM,
        out_shape=jax.ShapeDtypeStruct((QC, SPEC), BF16),
        compiler_params=pltpu.CompilerParams(vmem_limit_bytes=8 * MIB),
    )(core.reshape(1), arrived, basis, taper, smoother)

    sib = sibling(white)
    unit = jnp.concatenate([white[:HALF], sib[HALF:]], axis=0)
    beyond = across(unit)
    ahead, behind = first(unit, 1), first(unit, -1)
    facing = neighbour(white)
    facing_sib = sibling(facing)

    quarters = jnp.stack([(xl ^ (g // 2)) * NCORE + (core ^ (g % 2)) for g in range(4)]).astype(jnp.int32)
    rotated = pl.pallas_call(
        rotate_kernel,
        in_specs=[SMEM] + [VMEM] * 5,
        out_specs=VMEM,
        out_shape=jax.ShapeDtypeStruct((SPEC, COLS), BF16),
        scratch_shapes=[pltpu.VMEM((SPEC, CB), BF16), pltpu.VMEM((CB, COLS), BF16)],
        compiler_params=pltpu.CompilerParams(vmem_limit_bytes=8 * MIB),
        cost_estimate=pl.CostEstimate(flops=2 * CB * SPEC * COLS * 4, bytes_accessed=MIB, transcendentals=0),
    )(quarters, white, sib, facing, facing_sib, turn)

    pair = first(jnp.concatenate([beyond, ahead], axis=0), 1)
    beyond_behind = first(beyond, -1)
    beyond_far = first(beyond_behind, -1)
    near = grouped([unit, beyond, ahead, behind])
    rest = grouped([pair[:QC], pair[QC:], beyond_behind, beyond_far])
    near_up, near_down = second(near, 1), second(near, -1)
    rest_up, rest_down = second(rest, 1), second(rest, -1)
    near_far, rest_far = second(near_up, 1), second(rest_down, -1)

    def ids(offsets, dq):
        found = []
        for c in (core, 1 - core):
            for dp, dx in offsets:
                p0, q0 = jnp.where(c == 0, y, z), jnp.where(c == 0, z, y)
                p1, q1 = (p0 + dp) % 4, (q0 + dq) % 4
                zz, yy = jnp.where(c == 0, q1, p1), jnp.where(c == 0, p1, q1)
                found.append(((zz * NXH + (xh + dx) % NXH) * NY + yy) * 2 + c)
        return jnp.stack(found).astype(jnp.int32)

    near_at = [(0, 0), (0, 1), (-1, 0), (1, 0)]
    rest_at = [(-1, 1), (-2, 0), (1, 1), (2, 1)]
    out = None
    for arrays in (
        [(near, near_at, 0), (rest, rest_at, 0)],
        [(near_up, near_at, -1), (near_down, near_at, 1)],
        [(rest_up, rest_at, -1), (rest_down, rest_at, 1)],
        [(near_far, near_at, -2), (rest_far, rest_at, 2)],
    ):
        out = matmul(
            [a for a, _, _ in arrays],
            [sibling(a) for a, _, _ in arrays],
            [ids(at, dq) for _, at, dq in arrays],
            rotated,
            out,
        )
    return out.reshape(NZ * NXH * NY, QC, COLS)


def solution(mesh):
    in_specs = (
        P(("blk", "freq"), None),
        P(("blk", "freq")),
        P(("blk", "freq")),
        P(("blk", "freq")),
    )
    out_specs = P(None, "freq", "blk")
    return jax.shard_map(local, mesh=mesh, in_specs=in_specs, out_specs=out_specs, check_vma=False)
```

time: 145 us -> 143 us (0.986)
  waiting for transfers between devices: 23 us -> 43.3 us
  between operations: 14.7 us -> 1.26 us
  starting transfers between devices: 39.2 us -> 29.8 us
  Pallas kernels: 53.1 us -> 47.2 us
  local copies, waits for them, and re-layouts: 14 us -> 19.2 us
    ppermute x17 -> x23, waiting for transfers between devices: 9.07 us -> 36.1 us  [permuted(): return lax.ppermute(value, ('blk', 'freq'), pairs)]
    ppermute x17 -> x23, starting transfers between devices: 28 us -> 18.2 us  [permuted(): return lax.ppermute(value, ('blk', 'freq'), pairs)]
    unnamed x18 -> x55, local copies, waits for them, and re-layouts: 7.12 us -> 15.7 us
    all_to_all x1, waiting for transfers between devices: 13.9 us -> 7.24 us  [local(): lax.all_to_all(packed.reshape(DEVICES, SLOTS // DEVICES, SAMPLES + TAIL),...]
    pallas_call x6 -> x8, Pallas kernels: 53.1 us -> 47.2 us  [the longest x4 30.8 us: matmul(): pl.pallas_call(functools.partial(matmul_kernel, count), in_specs=in_specs...]
    slice x10 -> x2, local copies, waits for them, and re-layouts: 4.38 us -> 0.03 us  [local(): unit = jnp.concatenate([white[:HALF], sib[HALF:]], axis=0)]
    reshape x1, local copies, waits for them, and re-layouts: 0.22 us -> 1.98 us  [local(): arrived = lax.all_to_all(packed.reshape(DEVICES, SLOTS // DEVICES, SAMPLE...]
  transfers between devices with their start and end apart: 19 -> 24, of which waited for: 4 -> 9; matrix products, arithmetic and copies ran while one was open for 4% -> 1% of each run, Pallas kernels for 26% -> 27%
where the time goes in v2:
time: 143 us; the launch traced here: 141 us
  Pallas kernels  47.2 us (33%)
  waiting for transfers between devices  43.3 us (30%)
  starting transfers between devices  29.8 us (21%)
  local copies, waits for them, and re-layouts  19.2 us (13%)
    ppermute x23, waiting for transfers between devices, permuted(): return lax.ppermute(value, ('blk', 'freq'), pairs)  36.1 us
    pallas_call x4, Pallas kernels, matmul(): pl.pallas_call(functools.partial(matmul_kernel, count), in_specs=in_specs...  30.8 us
    ppermute x23, starting transfers between devices, permuted(): return lax.ppermute(value, ('blk', 'freq'), pairs)  18.2 us
    unnamed x55, local copies, waits for them, and re-layouts  15.7 us
    pallas_call x1, Pallas kernels, local(): pl.pallas_call(rotate_kernel, in_specs=[SMEM] + [VMEM] * 5, out_specs=VME...  14.2 us
    all_to_all x1, starting transfers between devices, local(): lax.all_to_all(packed.reshape(DEVICES, SLOTS // DEVICES, SAMPLES + TAIL),...  11.6 us
    all_to_all x1, waiting for transfers between devices, local(): lax.all_to_all(packed.reshape(DEVICES, SLOTS // DEVICES, SAMPLES + TAIL),...  7.24 us
  transfers between devices with their start and end apart: 24, of which 9 were waited for; matrix products, arithmetic and copies ran while one was open for 1% of the time, Pallas kernels for 27%

profile of v2, /device:TPU:0, one launch (start us, length us, event | category | flops | bytes accessed | tf_op | source)
XLA Modules:
  0.0 140.9 jit_solution(17003036588328822267)
XLA Ops:
  4.7 11.6 %all-to-all-start = ((bf16[128,2,1152]{2,1,0:T(2,128)(2,1)}), bf16[128,2,1152]{2,1,0:T(2,128)(2,1)}, u32[]{:S(2)}, u32[]{:S(2)}) async-start(bf16[128,2,1152]{2,1,0:T(2,128)(2,1)} %reshape.21), calls=%async_computation | async-start | bytes 1179648 | tf_op jit(solution)/shard_map/all_to_all | solution.py:272
  16.4 1.6 %copy-done = bf16[1024,1024]{1,0:T(8,128)(2,1)S(1)} copy-done((bf16[1024,1024]{1,0:T(8,128)(2,1)S(1)}, bf16[1024,1024]{1,0:T(8,128)(2,1)}, u32[]{:S(2)}) %copy-start) | copy-done | bytes 2097176
  18.0 1.2 copy-done.5
  23.0 7.2 %all-to-all-done = bf16[128,2,1152]{2,1,0:T(2,128)(2,1)} async-done(((bf16[128,2,1152]{2,1,0:T(2,128)(2,1)}), bf16[128,2,1152]{2,1,0:T(2,128)(2,1)}, u32[]{:S(2)}, u32[]{:S(2)}) %all-to-all-start) | async-done | bytes 589856 | tf_op jit(solution)/shard_map/all_to_all | solution.py:272
  30.3 2.0 %reshape.22.recv_ref = bf16[256,1152]{1,0:T(8,128)(2,1)S(1)} reshape(bf16[128,2,1152]{2,1,0:T(2,128)(2,1)} %all-to-all-done) | data formatting | bytes 1179648 | tf_op jit(solution)/shard_map/reshape | solution.py:278
  32.3 1.2 copy-done.7
  33.5 1.4 shard_map.84.own0
  36.5 1.2 collective-permute-start.1
  38.4 2.6 %collective-permute-start.3 = (bf16[32,4096]{1,0:T(8,128)(2,1)S(1)}, bf16[32,4096]{1,0:T(8,128)(2,1)S(1)}, u32[]{:S(2)}, u32[]{:S(2)}) collective-permute-start(bf16[32,4096]{1,0:T(8,128)(2,1)S(1)} %pad_maximum_fusion.1), channel_id=1, source_target_pairs={{0,12},{1,97},{2,14},{3,99},{4,0},{5,101},{6,2},{7,103},{8,4},{9,1... | collective-permute-start | bytes 786440 | tf_op jit(solution)/shard_map/ppermute | solution.py:226
  41.0 3.2 %collective-permute-done.13.own2 = bf16[32,4096]{1,0:T(8,128)(2,1)S(1)} collective-permute-done((bf16[32,4096]{1,0:T(8,128)(2,1)S(1)}, bf16[32,4096]{1,0:T(8,128)(2,1)S(1)}, u32[]{:S(2)}, u32[]{:S(2)}) %collective-permute-start.13) | collective-permute-done | bytes 262176 | tf_op jit(solution)/shard_map/ppermute | solution.py:226
  44.2 5.0 %collective-permute-done.1 = bf16[32,4096]{1,0:T(8,128)(2,1)S(1)} collective-permute-done((bf16[32,4096]{1,0:T(8,128)(2,1)S(1)}, bf16[32,4096]{1,0:T(8,128)(2,1)S(1)}, u32[]{:S(2)}, u32[]{:S(2)}) %collective-permute-start.1) | collective-permute-done | bytes 262176 | tf_op jit(solution)/shard_map/ppermute | solution.py:226
  50.4 2.1 %collective-permute-start.7 = (bf16[32,4096]{1,0:T(8,128)(2,1)S(1)}, bf16[32,4096]{1,0:T(8,128)(2,1)S(1)}, u32[]{:S(2)}, u32[]{:S(2)}) collective-permute-start(bf16[32,4096]{1,0:T(8,128)(2,1)S(1)} %collective-permute-done.1), channel_id=1, source_target_pairs={{0,12},{1,97},{2,14},{3,99},{4,0},{5,101},{6,2},{7,103},{8,4},{9,1... | collective-permute-start | bytes 786440 | tf_op jit(solution)/shard_map/ppermute | solution.py:226
  53.5 3.2 %collective-permute-done.7 = bf16[32,4096]{1,0:T(8,128)(2,1)S(1)} collective-permute-done((bf16[32,4096]{1,0:T(8,128)(2,1)S(1)}, bf16[32,4096]{1,0:T(8,128)(2,1)S(1)}, u32[]{:S(2)}, u32[]{:S(2)}) %collective-permute-start.7) | collective-permute-done | bytes 262176 | tf_op jit(solution)/shard_map/ppermute | solution.py:226
  57.7 4.6 %collective-permute-done.6 = bf16[64,4096]{1,0:T(8,128)(2,1)S(1)} collective-permute-done((bf16[64,4096]{1,0:T(8,128)(2,1)S(1)}, bf16[64,4096]{1,0:T(8,128)(2,1)S(1)}, u32[]{:S(2)}, u32[]{:S(2)}) %collective-permute-start.6) | collective-permute-done | bytes 524320 | tf_op jit(solution)/shard_map/ppermute | solution.py:226
  62.2 1.4 %collective-permute-start.8 = (bf16[32,4096]{1,0:T(8,128)(2,1)S(1)}, bf16[32,4096]{1,0:T(8,128)(2,1)S(1)}, u32[]{:S(2)}, u32[]{:S(2)}) collective-permute-start(bf16[32,4096]{1,0:T(8,128)(2,1)S(1)} %collective-permute-done.7), channel_id=1, source_target_pairs={{0,12},{1,97},{2,14},{3,99},{4,0},{5,101},{6,2},{7,103},{8,4},{9,1... | collective-permute-start | bytes 786440 | tf_op jit(solution)/shard_map/ppermute | solution.py:226
  63.7 7.8 %collective-permute-done.8 = bf16[32,4096]{1,0:T(8,128)(2,1)S(1)} collective-permute-done((bf16[32,4096]{1,0:T(8,128)(2,1)S(1)}, bf16[32,4096]{1,0:T(8,128)(2,1)S(1)}, u32[]{:S(2)}, u32[]{:S(2)}) %collective-permute-start.8) | collective-permute-done | bytes 262176 | tf_op jit(solution)/shard_map/ppermute | solution.py:226
  71.6 1.3 collective-permute-start.9
  76.3 10.2 %collective-permute-done.9.refs_1_ = bf16[128,4096]{1,0:T(8,128)(2,1)} collective-permute-done((bf16[128,4096]{1,0:T(8,128)(2,1)S(1)}, bf16[128,4096]{1,0:T(8,128)(2,1)}, u32[]{:S(2)}, u32[]{:S(2)}) %collective-permute-start.9) | collective-permute-done | bytes 1048608 | tf_op jit(solution)/shard_map/ppermute | solution.py:226
  86.5 2.4 %collective-permute-start.10 = (bf16[128,4096]{1,0:T(8,128)(2,1)}, bf16[128,4096]{1,0:T(8,128)(2,1)}, u32[]{:S(2)}, u32[]{:S(2)}) collective-permute-start(bf16[128,4096]{1,0:T(8,128)(2,1)} %collective-permute-done.9.refs_1_), channel_id=1, source_target_pairs={{0,96},{1,13},{2,98},{3,15},{4,100},{5,1},{6,102},{7,3},{8,104},{9... | collective-permute-start | bytes 3145736 | tf_op jit(solution)/shard_map/ppermute | solution.py:226
  95.1 14.2 %shard_map.85.refs_4_ = bf16[4096,2048]{1,0:T(8,128)(2,1)S(1)} custom-call(s32[4]{0:T(128)S(1)} %pad_add_fusion.quarter_ref, bf16[32,4096]{1,0:T(8,128)(2,1)S(1)} %shard_map.84.own0, bf16[32,4096]{1,0:T(8,128)(2,1)S(1)} %copy-done.11, bf16[32,4096]{1,0:T(8,128)(2,1)S(1)} %copy-done.18, bf16[32,4096]{1,0:T(8,128)(2,1)S(1)} %copy-done.20, ...), custom_call_target="tpu_custom_call" | custom-call | flops 8589934592 | bytes 1048576 | tf_op jit(solution)/shard_map/pallas_call | solution.py:305
  109.9 7.7 %shard_map.86.refs_5_ = f32[64,16,2048]{2,1,0:T(8,128)} custom-call(s32[16]{0:T(128)S(1)} %concatenate.31.ids_ref, bf16[128,4096]{1,0:T(8,128)(2,1)S(1)} %slice_dynamic-update-slice_fusion.8.refs_0_, bf16[128,4096]{1,0:T(8,128)(2,1)S(1)} %slice_dynamic-update-slice_fusion.refs_1_, bf16[128,4096]{1,0:T(8,128)(2,1)S(1)} %copy-done.2, ...), custom_call_target="tpu_custom_call" | custom-call | flops 4294967296 | bytes 4194304 | tf_op jit(solution)/shard_map/pallas_call | solution.py:200
  117.6 7.6 %shard_map.87.refs_5_ = f32[64,16,2048]{2,1,0:T(8,128)} custom-call(s32[16]{0:T(128)S(1)} %concatenate.30.ids_ref, bf16[128,4096]{1,0:T(8,128)(2,1)S(1)} %collective-permute-done.4.refs_0_, bf16[128,4096]{1,0:T(8,128)(2,1)S(1)} %copy-done.4, bf16[128,4096]{1,0:T(8,128)(2,1)} %collective-permute-done.19.refs_2_, ...), custom_call_target="tpu_custom_call", output_to_operand_aliasing={{}: (6, {})} | custom-call | flops 4294967296 | bytes 4194304 | tf_op jit(solution)/shard_map/pallas_call | solution.py:200
  125.2 7.7 %shard_map.88.refs_5_ = f32[64,16,2048]{2,1,0:T(8,128)} custom-call(s32[16]{0:T(128)S(1)} %concatenate.29.ids_ref, bf16[128,4096]{1,0:T(8,128)(2,1)} %collective-permute-done.15.refs_0_, bf16[128,4096]{1,0:T(8,128)(2,1)} %collective-permute-done.9.refs_1_, bf16[128,4096]{1,0:T(8,128)(2,1)S(1)} %collective-permute-done.16.refs_2_, ...), custom_call_target="tpu_custom_call", output_to_operand_aliasing={{}: (6, {})} | custom-call | flops 4294967296 | bytes 4194304 | tf_op jit(solution)/shard_map/pallas_call | solution.py:200
  133.0 7.7 %shard_map.89 = f32[64,16,2048]{2,1,0:T(8,128)} custom-call(s32[16]{0:T(128)S(1)} %concatenate.24.ids_ref, bf16[128,4096]{1,0:T(8,128)(2,1)} %collective-permute-done.5.refs_0_, bf16[128,4096]{1,0:T(8,128)(2,1)} %collective-permute-done.10.refs_1_, bf16[128,4096]{1,0:T(8,128)(2,1)S(1)} %collective-permute-done.11.refs_2_, ...), custom_call_target="tpu_custom_call", output_to_operand_aliasing={{}: (6, {})} | custom-call | flops 4294967296 | bytes 4194304 | tf_op jit(solution)/shard_map/pallas_call | solution.py:200
  (100 shorter events, 23.4 us)
Async XLA Ops:
  4.7 25.5 %all-to-all-start = ((bf16[128,2,1152]{2,1,0:T(2,128)(2,1)}), bf16[128,2,1152]{2,1,0:T(2,128)(2,1)}, u32[]{:S(2)}, u32[]{:S(2)}) async-start(bf16[128,2,1152]{2,1,0:T(2,128)(2,1)} %reshape.21), calls=%async_computation | async-start | bytes 1179648 | tf_op jit(solution)/shard_map/all_to_all | solution.py:272
  34.9 1.6 %collective-permute-start = (bf16[32,4096]{1,0:T(8,128)(2,1)S(1)}, bf16[32,4096]{1,0:T(8,128)(2,1)S(1)}, u32[]{:S(2)}, u32[]{:S(2)}) collective-permute-start(bf16[32,4096]{1,0:T(8,128)(2,1)S(1)} %shard_map.84.own0), channel_id=1, source_target_pairs={{0,1},{1,0},{2,3},{3,2},{4,5},{5,4},{6,7},{7,6},{8,9},{9,8},{10,11... | collective-permute-start | bytes 786440 | tf_op jit(solution)/shard_map/ppermute | solution.py:226
  35.0 9.2 %collective-permute-start.13 = (bf16[32,4096]{1,0:T(8,128)(2,1)S(1)}, bf16[32,4096]{1,0:T(8,128)(2,1)S(1)}, u32[]{:S(2)}, u32[]{:S(2)}) collective-permute-start(bf16[32,4096]{1,0:T(8,128)(2,1)S(1)} %shard_map.84.own0), channel_id=1, source_target_pairs={{0,2},{1,3},{2,0},{3,1},{4,6},{5,7},{6,4},{7,5},{8,10},{9,11},{10,... | collective-permute-start | bytes 786440 | tf_op jit(solution)/shard_map/ppermute | solution.py:226
  36.5 12.6 %collective-permute-start.1 = (bf16[32,4096]{1,0:T(8,128)(2,1)S(1)}, bf16[32,4096]{1,0:T(8,128)(2,1)S(1)}, u32[]{:S(2)}, u32[]{:S(2)}) collective-permute-start(bf16[32,4096]{1,0:T(8,128)(2,1)S(1)} %pad_maximum_fusion.1), channel_id=1, source_target_pairs={{0,16},{1,17},{2,18},{3,19},{4,20},{5,21},{6,22},{7,23},{8,24},{9,... | collective-permute-start | bytes 786440 | tf_op jit(solution)/shard_map/ppermute | solution.py:226
  37.8 11.4 %collective-permute-start.2 = (bf16[32,4096]{1,0:T(8,128)(2,1)S(1)}, bf16[32,4096]{1,0:T(8,128)(2,1)S(1)}, u32[]{:S(2)}, u32[]{:S(2)}) collective-permute-start(bf16[32,4096]{1,0:T(8,128)(2,1)S(1)} %pad_maximum_fusion.1), channel_id=1, source_target_pairs={{0,4},{1,33},{2,6},{3,35},{4,8},{5,37},{6,10},{7,39},{8,12},{9,41}... | collective-permute-start | bytes 786440 | tf_op jit(solution)/shard_map/ppermute | solution.py:226
  38.4 14.2 %collective-permute-start.3 = (bf16[32,4096]{1,0:T(8,128)(2,1)S(1)}, bf16[32,4096]{1,0:T(8,128)(2,1)S(1)}, u32[]{:S(2)}, u32[]{:S(2)}) collective-permute-start(bf16[32,4096]{1,0:T(8,128)(2,1)S(1)} %pad_maximum_fusion.1), channel_id=1, source_target_pairs={{0,12},{1,97},{2,14},{3,99},{4,0},{5,101},{6,2},{7,103},{8,4},{9,1... | collective-permute-start | bytes 786440 | tf_op jit(solution)/shard_map/ppermute | solution.py:226
  44.2 28.7 %collective-permute-start.14 = (bf16[32,4096]{1,0:T(8,128)(2,1)S(1)}, bf16[32,4096]{1,0:T(8,128)(2,1)S(1)}, u32[]{:S(2)}, u32[]{:S(2)}) collective-permute-start(bf16[32,4096]{1,0:T(8,128)(2,1)S(1)} %collective-permute-done.13.own2), channel_id=1, source_target_pairs={{0,1},{1,0},{2,3},{3,2},{4,5},{5,4},{6,7},{7,6},{8,9},{9,8},{10,11... | collective-permute-start | bytes 786440 | tf_op jit(solution)/shard_map/ppermute | solution.py:226
  49.2 13.0 %collective-permute-start.6 = (bf16[64,4096]{1,0:T(8,128)(2,1)S(1)}, bf16[64,4096]{1,0:T(8,128)(2,1)S(1)}, u32[]{:S(2)}, u32[]{:S(2)}) collective-permute-start(bf16[64,4096]{1,0:T(8,128)(2,1)S(1)} %pad_maximum_fusion), channel_id=1, source_target_pairs={{0,4},{1,33},{2,6},{3,35},{4,8},{5,37},{6,10},{7,39},{8,12},{9,41}... | collective-permute-start | bytes 1572872 | tf_op jit(solution)/shard_map/ppermute | solution.py:226
  50.4 6.4 %collective-permute-start.7 = (bf16[32,4096]{1,0:T(8,128)(2,1)S(1)}, bf16[32,4096]{1,0:T(8,128)(2,1)S(1)}, u32[]{:S(2)}, u32[]{:S(2)}) collective-permute-start(bf16[32,4096]{1,0:T(8,128)(2,1)S(1)} %collective-permute-done.1), channel_id=1, source_target_pairs={{0,12},{1,97},{2,14},{3,99},{4,0},{5,101},{6,2},{7,103},{8,4},{9,1... | collective-permute-start | bytes 786440 | tf_op jit(solution)/shard_map/ppermute | solution.py:226
  52.7 20.9 %collective-permute-start.21 = (bf16[128,4096]{1,0:T(8,128)(2,1)S(1)}, bf16[128,4096]{1,0:T(8,128)(2,1)S(1)}, u32[]{:S(2)}, u32[]{:S(2)}) collective-permute-start(bf16[128,4096]{1,0:T(8,128)(2,1)S(1)} %slice_dynamic-update-slice_fusion.8.refs_0_), channel_id=1, source_target_pairs={{0,1},{1,0},{2,3},{3,2},{4,5},{5,4},{6,7},{7,6},{8,9},{9,8},{10,11... | collective-permute-start | bytes 3145736 | tf_op jit(solution)/shard_map/ppermute | solution.py:226
  52.8 22.6 %collective-permute-start.4 = (bf16[128,4096]{1,0:T(8,128)(2,1)S(1)}, bf16[128,4096]{1,0:T(8,128)(2,1)S(1)}, u32[]{:S(2)}, u32[]{:S(2)}) collective-permute-start(bf16[128,4096]{1,0:T(8,128)(2,1)S(1)} %slice_dynamic-update-slice_fusion.8.refs_0_), channel_id=1, source_target_pairs={{0,32},{1,5},{2,34},{3,7},{4,36},{5,9},{6,38},{7,11},{8,40},{9,13}... | collective-permute-start | bytes 3145736 | tf_op jit(solution)/shard_map/ppermute | solution.py:226
  56.8 18.6 %collective-permute-start.18 = (bf16[128,4096]{1,0:T(8,128)(2,1)S(1)}, bf16[128,4096]{1,0:T(8,128)(2,1)S(1)}, u32[]{:S(2)}, u32[]{:S(2)}) collective-permute-start(bf16[128,4096]{1,0:T(8,128)(2,1)S(1)} %slice_dynamic-update-slice_fusion.8.refs_0_), channel_id=1, source_target_pairs={{0,96},{1,13},{2,98},{3,15},{4,100},{5,1},{6,102},{7,3},{8,104},{9... | collective-permute-start | bytes 3145736 | tf_op jit(solution)/shard_map/ppermute | solution.py:226
  62.2 9.2 %collective-permute-start.8 = (bf16[32,4096]{1,0:T(8,128)(2,1)S(1)}, bf16[32,4096]{1,0:T(8,128)(2,1)S(1)}, u32[]{:S(2)}, u32[]{:S(2)}) collective-permute-start(bf16[32,4096]{1,0:T(8,128)(2,1)S(1)} %collective-permute-done.7), channel_id=1, source_target_pairs={{0,12},{1,97},{2,14},{3,99},{4,0},{5,101},{6,2},{7,103},{8,4},{9,1... | collective-permute-start | bytes 786440 | tf_op jit(solution)/shard_map/ppermute | solution.py:226
  71.6 15.0 %collective-permute-start.9 = (bf16[128,4096]{1,0:T(8,128)(2,1)S(1)}, bf16[128,4096]{1,0:T(8,128)(2,1)}, u32[]{:S(2)}, u32[]{:S(2)}) collective-permute-start(bf16[128,4096]{1,0:T(8,128)(2,1)S(1)} %slice_dynamic-update-slice_fusion.refs_1_), channel_id=1, source_target_pairs={{0,96},{1,13},{2,98},{3,15},{4,100},{5,1},{6,102},{7,3},{8,104},{9... | collective-permute-start | bytes 3145736 | tf_op jit(solution)/shard_map/ppermute | solution.py:226
  73.6 15.9 %collective-permute-start.22 = (bf16[128,4096]{1,0:T(8,128)(2,1)S(1)}, bf16[128,4096]{1,0:T(8,128)(2,1)}, u32[]{:S(2)}, u32[]{:S(2)}) collective-permute-start(bf16[128,4096]{1,0:T(8,128)(2,1)S(1)} %slice_dynamic-update-slice_fusion.refs_1_), channel_id=1, source_target_pairs={{0,1},{1,0},{2,3},{3,2},{4,5},{5,4},{6,7},{7,6},{8,9},{9,8},{10,11... | collective-permute-start | bytes 3145736 | tf_op jit(solution)/shard_map/ppermute | solution.py:226
  74.6 16.1 %collective-permute-start.15 = (bf16[128,4096]{1,0:T(8,128)(2,1)S(1)}, bf16[128,4096]{1,0:T(8,128)(2,1)}, u32[]{:S(2)}, u32[]{:S(2)}) collective-permute-start(bf16[128,4096]{1,0:T(8,128)(2,1)S(1)} %slice_dynamic-update-slice_fusion.refs_1_), channel_id=1, source_target_pairs={{0,32},{1,5},{2,34},{3,7},{4,36},{5,9},{6,38},{7,11},{8,40},{9,13}... | collective-permute-start | bytes 3145736 | tf_op jit(solution)/shard_map/ppermute | solution.py:226
  75.4 15.3 %collective-permute-start.19 = (bf16[128,4096]{1,0:T(8,128)(2,1)S(1)}, bf16[128,4096]{1,0:T(8,128)(2,1)}, u32[]{:S(2)}, u32[]{:S(2)}) collective-permute-start(bf16[128,4096]{1,0:T(8,128)(2,1)S(1)} %collective-permute-done.4.refs_0_), channel_id=1, source_target_pairs={{0,1},{1,0},{2,3},{3,2},{4,5},{5,4},{6,7},{7,6},{8,9},{9,8},{10,11... | collective-permute-start | bytes 3145736 | tf_op jit(solution)/shard_map/ppermute | solution.py:226
  75.4 33.9 %collective-permute-start.5 = (bf16[128,4096]{1,0:T(8,128)(2,1)S(1)}, bf16[128,4096]{1,0:T(8,128)(2,1)}, u32[]{:S(2)}, u32[]{:S(2)}) collective-permute-start(bf16[128,4096]{1,0:T(8,128)(2,1)S(1)} %collective-permute-done.4.refs_0_), channel_id=1, source_target_pairs={{0,32},{1,5},{2,34},{3,7},{4,36},{5,9},{6,38},{7,11},{8,40},{9,13}... | collective-permute-start | bytes 3145736 | tf_op jit(solution)/shard_map/ppermute | solution.py:226
  86.5 22.8 %collective-permute-start.10 = (bf16[128,4096]{1,0:T(8,128)(2,1)}, bf16[128,4096]{1,0:T(8,128)(2,1)}, u32[]{:S(2)}, u32[]{:S(2)}) collective-permute-start(bf16[128,4096]{1,0:T(8,128)(2,1)} %collective-permute-done.9.refs_1_), channel_id=1, source_target_pairs={{0,96},{1,13},{2,98},{3,15},{4,100},{5,1},{6,102},{7,3},{8,104},{9... | collective-permute-start | bytes 3145736 | tf_op jit(solution)/shard_map/ppermute | solution.py:226
  89.5 28.1 %collective-permute-start.20 = (bf16[128,4096]{1,0:T(8,128)(2,1)}, bf16[128,4096]{1,0:T(8,128)(2,1)S(1)}, u32[]{:S(2)}, u32[]{:S(2)}) collective-permute-start(bf16[128,4096]{1,0:T(8,128)(2,1)} %copy-done.3), channel_id=1, source_target_pairs={{0,1},{1,0},{2,3},{3,2},{4,5},{5,4},{6,7},{7,6},{8,9},{9,8},{10,11... | collective-permute-start | bytes 3145736 | tf_op jit(solution)/shard_map/ppermute | solution.py:226
  90.7 34.5 %collective-permute-start.17 = (bf16[128,4096]{1,0:T(8,128)(2,1)}, bf16[128,4096]{1,0:T(8,128)(2,1)S(1)}, u32[]{:S(2)}, u32[]{:S(2)}) collective-permute-start(bf16[128,4096]{1,0:T(8,128)(2,1)} %collective-permute-done.9.refs_1_), channel_id=1, source_target_pairs={{0,1},{1,0},{2,3},{3,2},{4,5},{5,4},{6,7},{7,6},{8,9},{9,8},{10,11... | collective-permute-start | bytes 3145736 | tf_op jit(solution)/shard_map/ppermute | solution.py:226
  90.7 34.5 %collective-permute-start.16 = (bf16[128,4096]{1,0:T(8,128)(2,1)}, bf16[128,4096]{1,0:T(8,128)(2,1)S(1)}, u32[]{:S(2)}, u32[]{:S(2)}) collective-permute-start(bf16[128,4096]{1,0:T(8,128)(2,1)} %collective-permute-done.15.refs_0_), channel_id=1, source_target_pairs={{0,1},{1,0},{2,3},{3,2},{4,5},{5,4},{6,7},{7,6},{8,9},{9,8},{10,11... | collective-permute-start | bytes 3145736 | tf_op jit(solution)/shard_map/ppermute | solution.py:226
  109.3 23.7 %collective-permute-start.11 = (bf16[128,4096]{1,0:T(8,128)(2,1)}, bf16[128,4096]{1,0:T(8,128)(2,1)S(1)}, u32[]{:S(2)}, u32[]{:S(2)}) collective-permute-start(bf16[128,4096]{1,0:T(8,128)(2,1)} %collective-permute-done.5.refs_0_), channel_id=1, source_target_pairs={{0,1},{1,0},{2,3},{3,2},{4,5},{5,4},{6,7},{7,6},{8,9},{9,8},{10,11... | collective-permute-start | bytes 3145736 | tf_op jit(solution)/shard_map/ppermute | solution.py:226
  109.4 23.6 %collective-permute-start.12 = (bf16[128,4096]{1,0:T(8,128)(2,1)}, bf16[128,4096]{1,0:T(8,128)(2,1)S(1)}, u32[]{:S(2)}, u32[]{:S(2)}) collective-permute-start(bf16[128,4096]{1,0:T(8,128)(2,1)} %collective-permute-done.10.refs_1_), channel_id=1, source_target_pairs={{0,1},{1,0},{2,3},{3,2},{4,5},{5,4},{6,7},{7,6},{8,9},{9,8},{10,11... | collective-permute-start | bytes 3145736 | tf_op jit(solution)/shard_map/ppermute | solution.py:226
  (21 other events, 108.4 us)

commit v3 on v2

v3 whole, which is shorter than its diff:
```python
import functools
import math

import jax
import jax.numpy as jnp
import ml_dtypes
import numpy as np
from jax import lax
from jax.experimental import pallas as pl
from jax.experimental.pallas import tpu as pltpu
from jax.sharding import PartitionSpec as P

SAMPLES = 1024
FREQS = 512
LAGS = 16
HALFWIN = 64
WIN = 4
EPSILON = 1e-06

NZ, NXH, NY = 4, 2, 4
NXL, NCORE = 2, 2
QC = 32
HALF = QC // 2
CB = QC * NXL * NCORE
SEG_DEV = QC * WIN
SLOTS = 256
DEVICES = 128
SPEC = WIN * 2 * FREQS
COLS = CB * LAGS
TAIL = 128
NT = 512
TILES = COLS // NT
GROUP = 4
F32, BF16 = jnp.float32, jnp.bfloat16
MIB = 1024 * 1024
SMALL = pl.CostEstimate(flops=1024, bytes_accessed=1024, transcendentals=0)
TOKEN = jax.ShapeDtypeStruct((8, 128), F32)
ANY = pl.BlockSpec(memory_space=pl.ANY)
HBM = pl.BlockSpec(memory_space=pltpu.HBM)
VMEM = pl.BlockSpec(memory_space=pltpu.VMEM)
SMEM = pl.BlockSpec(memory_space=pltpu.SMEM)


def tables():
    n = np.arange(SAMPLES)[:, None]
    k = np.arange(FREQS)[None, :]
    angle = 2.0 * math.pi / SAMPLES * ((n * k) % SAMPLES)
    basis = np.concatenate([np.cos(angle), -np.sin(angle)], axis=1).astype(ml_dtypes.bfloat16)
    taper = (0.5 - 0.5 * np.cos(2.0 * math.pi / SAMPLES * (n[:, 0] + 0.5)))[None, :].astype(np.float32)
    pos = np.arange(FREQS)[:, None]
    lag = np.arange(128)[None, :] % LAGS - LAGS // 2
    phi = 2.0 * math.pi / SAMPLES * ((lag * pos) % SAMPLES)
    gain = np.where(pos == 0, 1.0, 2.0) / math.sqrt(2.0 * WIN * FREQS)
    turn = np.concatenate([gain * np.cos(phi), gain * np.sin(phi)], axis=0).astype(np.float32)
    return basis, taper, turn


def diagonal(size):
    return lax.broadcasted_iota(jnp.int32, (size, size), 0) == lax.broadcasted_iota(jnp.int32, (size, size), 1)


def pack_kernel(count_ref, chan_hbm, win_hbm, raw_hbm, out_ref, chan_ref, win_ref, raw_ref, sem):
    loads = [
        pltpu.make_async_copy(chan_hbm, chan_ref, sem.at[0]),
        pltpu.make_async_copy(win_hbm, win_ref, sem.at[1]),
        pltpu.make_async_copy(raw_hbm, raw_ref, sem.at[2]),
    ]
    for c in loads:
        c.start()
    loads[0].wait()
    loads[1].wait()
    chan = chan_ref[...]
    slot = lax.broadcasted_iota(jnp.int32, (1, SLOTS), 1)
    live = slot < count_ref[0]
    owner = jnp.where(live, chan // QC, -1).astype(F32)
    owner_col = jnp.sum(jnp.where(diagonal(SLOTS), owner, 0.0), axis=1, keepdims=True)
    row = lax.broadcasted_iota(jnp.int32, (SLOTS, SLOTS), 0)
    col = lax.broadcasted_iota(jnp.int32, (SLOTS, SLOTS), 1)
    earlier = jnp.where((owner_col == owner) & (row < col), 1.0, 0.0)
    rank = jnp.sum(earlier, axis=0, keepdims=True)
    flat = jnp.where(live, owner * 2.0 + rank, -1.0)
    pick = jnp.where(flat == row.astype(F32), 1.0, 0.0)
    place = (win_ref[...] * QC + chan % QC + 1).astype(F32)
    place_col = jnp.sum(pick * place, axis=1, keepdims=True)
    out_ref[:, SAMPLES:] = jnp.broadcast_to(place_col, (SLOTS, TAIL)).astype(BF16)
    loads[2].wait()
    out_ref[:, :SAMPLES] = jnp.dot(pick.astype(BF16), raw_ref[...], preferred_element_type=F32).astype(BF16)


def fetch_kernel(after_hbm, basis_hbm, taper_hbm, basis_ref, taper_ref, sem):
    del after_hbm
    loads = [
        pltpu.make_async_copy(basis_hbm, basis_ref, sem.at[0]),
        pltpu.make_async_copy(taper_hbm, taper_ref, sem.at[1]),
    ]
    for c in loads:
        c.start()
    for c in loads:
        c.wait()


def band_mean(energy):
    row = lax.broadcasted_iota(jnp.int32, (FREQS, FREQS), 0)
    col = lax.broadcasted_iota(jnp.int32, (FREQS, FREQS), 1)
    inside = jnp.where(jnp.abs(row - col) <= HALFWIN, 1.0, 0.0).astype(BF16)
    high = energy.astype(BF16)
    left = energy - high.astype(F32)
    middle = left.astype(BF16)
    low = (left - middle.astype(F32)).astype(BF16)
    total = jnp.dot(low, inside, preferred_element_type=F32)
    total = total + jnp.dot(middle, inside, preferred_element_type=F32)
    total = total + jnp.dot(high, inside, preferred_element_type=F32)
    pos = lax.broadcasted_iota(jnp.int32, (1, FREQS), 1)
    count = jnp.minimum(pos, HALFWIN) + jnp.minimum(FREQS - 1 - pos, HALFWIN) + 1
    return total / count.astype(F32)


def whiten_kernel(place_ref, recv_ref, basis_ref, taper_ref, out_ref):
    place_col = recv_ref[:, SAMPLES : SAMPLES + 1].astype(F32)
    place = jnp.sum(jnp.where(diagonal(SLOTS), place_col, 0.0), axis=0, keepdims=True)
    row = lax.broadcasted_iota(jnp.int32, (SEG_DEV, SLOTS), 0)
    wanted = row // QC * QC + (row + place_ref[4] * HALF) % QC + 1
    pick = jnp.where(place == wanted.astype(F32), 1.0, 0.0).astype(BF16)
    values = jnp.dot(pick, recv_ref[:, :SAMPLES], preferred_element_type=F32)
    values = values - jnp.sum(values, axis=1, keepdims=True) * (1.0 / SAMPLES)
    tapered = (values * taper_ref[...]).astype(BF16)
    spectrum = jnp.dot(tapered, basis_ref[...], preferred_element_type=F32)
    real, imag = spectrum[:, :FREQS], spectrum[:, FREQS:]
    inverse = lax.rsqrt(band_mean(real * real + imag * imag) + EPSILON)
    real, imag = (real * inverse).astype(BF16), (imag * inverse).astype(BF16)
    for w in range(WIN):
        rows = slice(w * QC, (w + 1) * QC)
        out_ref[:, 2 * w * FREQS : (2 * w + 1) * FREQS] = real[rows]
        out_ref[:, (2 * w + 1) * FREQS : (2 * w + 2) * FREQS] = imag[rows]


def group_kernel(moves, n_in, *refs):
    outs, sem = refs[n_in:-1], refs[-1]
    copies = [
        pltpu.make_async_copy(
            refs[i].at[pl.ds(h * HALF, HALF)], outs[o].at[pl.ds(p * HALF, HALF)], sem.at[n]
        )
        for n, (i, h, o, p) in enumerate(moves)
    ]
    for c in copies:
        c.start()
    for c in copies:
        c.wait()


def grouped(moves, halves, arrays, after):
    return pl.pallas_call(
        functools.partial(group_kernel, moves, len(arrays) + len(after)),
        in_specs=[ANY] * (len(arrays) + len(after)),
        out_specs=[ANY] * len(halves),
        out_shape=[jax.ShapeDtypeStruct((n * HALF, SPEC), BF16) for n in halves],
        scratch_shapes=[pltpu.SemaphoreType.DMA((len(moves),))],
        compiler_params=pltpu.CompilerParams(vmem_limit_bytes=MIB),
        cost_estimate=SMALL,
    )(*arrays, *after)


def gate_kernel(*refs):
    del refs


def gated(value, after):
    return pl.pallas_call(
        gate_kernel,
        in_specs=[ANY] * (1 + len(after)),
        out_specs=ANY,
        out_shape=jax.ShapeDtypeStruct(value.shape, value.dtype),
        input_output_aliases={0: 0},
        compiler_params=pltpu.CompilerParams(vmem_limit_bytes=MIB),
        cost_estimate=SMALL,
    )(value, *after)


def rotate_kernel(place_ref, own0, own1, own2, own3, turn_hbm, out_ref, token_ref, turn_ref, whole, turned, expand, sem):
    load = pltpu.make_async_copy(turn_hbm, turn_ref, sem.at[0])
    load.start()
    col = lax.broadcasted_iota(jnp.int32, (HALF, COLS), 1) // LAGS
    row = lax.broadcasted_iota(jnp.int32, (HALF, COLS), 0)
    for g, own in enumerate((own0, own1, own2, own3)):
        whole[g * QC : (g + 1) * QC, :] = own[...]
    for k in range(0, SPEC, FREQS):
        turned[k : k + FREQS, :] = whole[:, k : k + FREQS].T
    xl, core = place_ref[3], place_ref[4]
    halves = [(0, 0, 0), (0, 0, 1), (0, 1, 1), (0, 1, 0), (1, 0, 0), (1, 1, 0), (1, 1, 1), (1, 0, 1)]
    for g, (chip, other, flip) in enumerate(halves):
        quarter = (1 - xl if chip else xl) * NCORE + (1 - core if other else core)
        base = quarter * QC + (1 - core if flip else core) * HALF
        expand[g * HALF : (g + 1) * HALF, :] = jnp.where(col == base + row, 1.0, 0.0).astype(BF16)
    load.wait()
    token_ref[...] = jnp.zeros_like(token_ref)
    step = 256
    per = FREQS // step

    def body(s, carry):
        w, k0 = s // per, pl.multiple_of(lax.rem(s, per) * step, step)
        re = pl.ds(pl.multiple_of(w * 2 * FREQS + k0, step), step)
        im = pl.ds(pl.multiple_of((w * 2 + 1) * FREQS + k0, step), step)
        cos = turn_ref[pl.ds(k0, step), :]
        sin = turn_ref[pl.ds(FREQS + k0, step), :]
        for n in range(COLS // 256):
            a2 = jnp.dot(turned[re, :], expand[:, n * 256 : (n + 1) * 256], preferred_element_type=F32)
            b2 = jnp.dot(turned[im, :], expand[:, n * 256 : (n + 1) * 256], preferred_element_type=F32)
            for h in range(2):
                a, b = a2[:, h * 128 : (h + 1) * 128], b2[:, h * 128 : (h + 1) * 128]
                cols = slice(n * 256 + h * 128, n * 256 + (h + 1) * 128)
                out_ref[re, cols] = (a * cos - b * sin).astype(BF16)
                out_ref[im, cols] = (a * sin + b * cos).astype(BF16)
        return carry

    lax.fori_loop(0, WIN * per, body, 0)


def matmul_kernel(sources, n_in, place_ref, *refs):
    rot_ref = refs[n_in]
    out_ref, token_ref, left, acc, in_sem, out_sem = refs[-6:]
    rows = GROUP * HALF
    z, xh, y, core = place_ref[0], place_ref[1], place_ref[2], place_ref[4]
    loads = [
        pltpu.make_async_copy(refs[i].at[pl.ds(row, rows)], left.at[pl.ds(n * rows, rows)], in_sem.at[n])
        for n, (i, row, _, _, _) in enumerate(sources)
    ]
    for c in loads:
        c.start()
    token_ref[...] = jnp.zeros_like(token_ref)
    ids = []
    for _, _, other, offsets, dq in sources:
        c = 1 - core if other else core
        for dp, dx in offsets:
            p = lax.rem(jnp.where(c == 0, y, z) + dp + 4, 4)
            q = lax.rem(jnp.where(c == 0, z, y) + dq + 4, 4)
            block = (jnp.where(c == 0, q, p) * NXH + lax.rem(xh + dx, NXH)) * NY + jnp.where(c == 0, p, q)
            ids.append(block * 2 + c)
    for c in loads:
        c.wait()

    def stores(step):
        cols = pl.ds(step * NT, NT)
        slot = step % 2
        return [
            pltpu.make_async_copy(acc.at[slot, u], out_ref.at[i, :, cols], out_sem.at[slot, u])
            for u, i in enumerate(ids)
        ]

    for step in range(TILES):
        if step >= 2:
            for c in stores(step - 2):
                c.wait()
        product = jnp.dot(left[...], rot_ref[:, step * NT : (step + 1) * NT], preferred_element_type=F32)
        acc[step % 2] = product.reshape(acc.shape[1:])
        for c in stores(step):
            c.start()
    for step in range(TILES - 2, TILES):
        for c in stores(step):
            c.wait()


def matmul(place, carried, rotated, out):
    arrays, sources = [], []
    for value, theirs, at, dq in carried:
        n = len(arrays)
        arrays += [value, theirs]
        sources += [(n, 0, False, at, dq), (n + 1, GROUP * HALF, True, at, dq)]
    rows = len(sources) * GROUP * HALF
    operands = [place, *arrays, rotated]
    in_specs = [SMEM] + [ANY] * len(arrays) + [VMEM]
    aliases = {}
    if out is not None:
        aliases = {len(operands): 0}
        operands.append(out)
        in_specs.append(ANY)
    return pl.pallas_call(
        functools.partial(matmul_kernel, sources, len(arrays)),
        in_specs=in_specs,
        out_specs=[ANY, VMEM],
        scratch_shapes=[
            pltpu.VMEM((rows, SPEC), BF16),
            pltpu.VMEM((2, rows // HALF, HALF, NT), F32),
            pltpu.SemaphoreType.DMA((len(sources),)),
            pltpu.SemaphoreType.DMA((2, rows // HALF)),
        ],
        out_shape=[jax.ShapeDtypeStruct((NZ * NXH * NY * 2, HALF, COLS), F32), TOKEN],
        input_output_aliases=aliases,
        compiler_params=pltpu.CompilerParams(vmem_limit_bytes=12 * MIB),
        cost_estimate=pl.CostEstimate(
            flops=3 * rows * COLS * SPEC, bytes_accessed=2 * rows * SPEC + 4 * rows * COLS, transcendentals=0
        ),
    )(*operands)


def permuted(value, move):
    sizes = (NZ, NXH, NY, NXL, NCORE)
    pairs = []
    for source in range(DEVICES):
        place = np.unravel_index(source, sizes)
        to = [int(t) % s for t, s in zip(move(*(int(p) for p in place)), sizes, strict=True)]
        pairs.append((source, int(np.ravel_multi_index(to, sizes))))
    return lax.ppermute(value, ("blk", "freq"), pairs)


def first(value, d):
    return permuted(value, lambda z, xh, y, xl, c: (z + d * c, xh, y + d * (1 - c), xl, c))


def second(value, d):
    return permuted(value, lambda z, xh, y, xl, c: (z + d * (1 - c), xh, y + d * c, xl, c))


def across(value):
    return permuted(value, lambda z, xh, y, xl, c: (z, xh + 1, y, xl, c))


def sibling(value):
    return permuted(value, lambda z, xh, y, xl, c: (z, xh, y, xl, c + 1))


def neighbour(value):
    return permuted(value, lambda z, xh, y, xl, c: (z, xh, y, xl + 1, c))


def local(raw, seg_chan, seg_win, file_count):
    basis, taper, turn = (jnp.asarray(t) for t in tables())
    blk, freq = lax.axis_index("blk"), lax.axis_index("freq")
    z, xh, y = blk // (NXH * NY), blk // NY % NXH, blk % NY
    place = jnp.stack([z, xh, y, freq // NCORE, freq % NCORE]).astype(jnp.int32)

    packed = pl.pallas_call(
        pack_kernel,
        in_specs=[SMEM, HBM, HBM, HBM],
        out_specs=VMEM,
        out_shape=jax.ShapeDtypeStruct((SLOTS, SAMPLES + TAIL), BF16),
        scratch_shapes=[
            pltpu.VMEM((1, SLOTS), jnp.int32),
            pltpu.VMEM((1, SLOTS), jnp.int32),
            pltpu.VMEM((SLOTS, SAMPLES), BF16),
            pltpu.SemaphoreType.DMA((3,)),
        ],
        compiler_params=pltpu.CompilerParams(vmem_limit_bytes=8 * MIB),
    )(file_count, seg_chan.reshape(1, SLOTS), seg_win.reshape(1, SLOTS), raw)
    arrived = lax.all_to_all(
        packed.reshape(DEVICES, SLOTS // DEVICES, SAMPLES + TAIL),
        ("blk", "freq"),
        split_axis=0,
        concat_axis=0,
        tiled=True,
    ).reshape(SLOTS, SAMPLES + TAIL)
    basis, taper = pl.pallas_call(
        fetch_kernel,
        in_specs=[ANY, HBM, HBM],
        out_specs=[VMEM] * 2,
        out_shape=[jax.ShapeDtypeStruct(t.shape, t.dtype) for t in (basis, taper)],
        scratch_shapes=[pltpu.SemaphoreType.DMA((2,))],
        compiler_params=pltpu.CompilerParams(vmem_limit_bytes=MIB),
        cost_estimate=SMALL,
    )(packed, basis, taper)
    white = pl.pallas_call(
        whiten_kernel,
        in_specs=[SMEM] + [VMEM] * 3,
        out_specs=VMEM,
        out_shape=jax.ShapeDtypeStruct((QC, SPEC), BF16),
        compiler_params=pltpu.CompilerParams(vmem_limit_bytes=8 * MIB),
    )(place, arrived, basis, taper)

    sib = sibling(white)
    unit = jnp.concatenate([white[:HALF], sib[HALF:]], axis=0)
    beyond = across(unit)
    ahead, behind = first(unit, 1), first(unit, -1)
    facing = neighbour(gated(unit, [ahead, behind]))
    facing_sib = sibling(facing)
    two = [(i, h, 0, 2 * i + h) for i in range(2) for h in range(2)]
    pair = first(grouped(two, [4], [beyond, ahead], [])[0], 1)
    beyond_behind = first(beyond, -1)
    beyond_far = first(beyond, 2)
    moves = [(i, h, 0, h * GROUP + i) for i in range(GROUP) for h in range(2)]
    (near,) = grouped(moves, [8], [unit, beyond, ahead, behind], [])
    near_up, near_down = second(near, 1), second(near, -1)
    moves = [(0, 0, 0, 0), (0, 1, 0, 4), (0, 2, 0, 1), (0, 3, 0, 5)]
    moves += [(i, h, 0, h * GROUP + i + 1) for i in (1, 2) for h in range(2)]
    (rest,) = grouped(moves, [8], [pair, beyond_behind, beyond_far], [])
    rest_up, rest_down = second(rest, 1), second(rest, -1)
    rotated, _ = pl.pallas_call(
        rotate_kernel,
        in_specs=[SMEM] + [VMEM] * 4 + [HBM],
        out_specs=[VMEM, VMEM],
        out_shape=[jax.ShapeDtypeStruct((SPEC, COLS), BF16), TOKEN],
        scratch_shapes=[
            pltpu.VMEM((2 * FREQS, 128), F32),
            pltpu.VMEM((CB, SPEC), BF16),
            pltpu.VMEM((SPEC, CB), BF16),
            pltpu.VMEM((CB, COLS), BF16),
            pltpu.SemaphoreType.DMA((1,)),
        ],
        compiler_params=pltpu.CompilerParams(vmem_limit_bytes=8 * MIB),
        cost_estimate=pl.CostEstimate(flops=2 * CB * SPEC * COLS * 5, bytes_accessed=MIB, transcendentals=0),
    )(place, white, sib, facing, facing_sib, turn)

    near_at = [(0, 0), (0, 1), (-1, 0), (1, 0)]
    rest_at = [(-1, 1), (-2, 0), (1, 1), (2, 1)]

    def product(out, *carried):
        return matmul(place, [(value, sibling(value), at, dq) for value, at, dq in carried], rotated, out)

    out, done = product(None, (near, near_at, 0), (near_down, near_at, 1))
    near_up = gated(near_up, [done])
    near_far = second(near_up, 1)
    out, done = product(out, (rest, rest_at, 0))
    rest_down = gated(rest_down, [done, rest_up])
    rest_far = second(rest_down, -1)
    out, _ = product(out, (near_up, near_at, -1), (rest_up, rest_at, -1))
    out, done = product(out, (rest_down, rest_at, 1), (near_far, near_at, -2))
    out, _ = product(out, (gated(rest_far, [done]), rest_at, 2))
    return out.reshape(NZ * NXH * NY, QC, COLS)


def solution(mesh):
    in_specs = (
        P(("blk", "freq"), None),
        P(("blk", "freq")),
        P(("blk", "freq")),
        P(("blk", "freq")),
    )
    out_specs = P(None, "freq", "blk")
    return jax.shard_map(local, mesh=mesh, in_specs=in_specs, out_specs=out_specs, check_vma=False)
```

time: 143 us -> 132 us (0.923)
  local copies, waits for them, and re-layouts: 19.2 us -> 7.79 us
  waiting for transfers between devices: 43.3 us -> 46.3 us
    unnamed x55 -> x12, local copies, waits for them, and re-layouts: 15.7 us -> 4.67 us
    all_to_all x1, waiting for transfers between devices: 7.24 us -> 11.3 us  [local(): lax.all_to_all(packed.reshape(DEVICES, SLOTS // DEVICES, SAMPLES + TAIL),...]
    pallas_call x8 -> x16, Pallas kernels: 47.2 us -> 46.4 us  [the longest x5 30.6 us: matmul(): pl.pallas_call(functools.partial(matmul_kernel, sources, len(arrays)), in...]
  transfers between devices with their start and end apart: 24 -> 24, of which waited for: 9 -> 9; matrix products, arithmetic and copies ran while one was open for 1% -> 0% of each run, Pallas kernels for 27% -> 29%
where the time goes in v3:
time: 132 us; the launch traced here: 131 us
  Pallas kernels  46.4 us (35%)
  waiting for transfers between devices  46.3 us (35%)
  starting transfers between devices  29.1 us (22%)
  local copies, waits for them, and re-layouts  7.79 us (6%)
    ppermute x23, waiting for transfers between devices, permuted(): return lax.ppermute(value, ('blk', 'freq'), pairs)  35 us
    pallas_call x5, Pallas kernels, matmul(): pl.pallas_call(functools.partial(matmul_kernel, sources, len(arrays)), in...  30.6 us
    ppermute x23, starting transfers between devices, permuted(): return lax.ppermute(value, ('blk', 'freq'), pairs)  17.5 us
    all_to_all x1, starting transfers between devices, local(): lax.all_to_all(packed.reshape(DEVICES, SLOTS // DEVICES, SAMPLES + TAIL),...  11.6 us
    all_to_all x1, waiting for transfers between devices, local(): lax.all_to_all(packed.reshape(DEVICES, SLOTS // DEVICES, SAMPLES + TAIL),...  11.3 us
    pallas_call x1, Pallas kernels, local(): pl.pallas_call(rotate_kernel, in_specs=[SMEM] + [VMEM] * 4 + [HBM], out_s...  9.78 us
    unnamed x12, local copies, waits for them, and re-layouts  4.67 us
    pallas_call x3, Pallas kernels, grouped(): pl.pallas_call(functools.partial(group_kernel, moves, len(arrays) + len(a...  3.53 us
  transfers between devices with their start and end apart: 24, of which 9 were waited for; matrix products, arithmetic and copies ran while one was open for 0% of the time, Pallas kernels for 29%

profile of v3, /device:TPU:0, one launch (start us, length us, event | category | flops | bytes accessed | tf_op | source)
XLA Modules:
  0.0 130.8 jit_solution(10088853834180705355)
XLA Ops:
  4.7 11.6 %all-to-all-start = ((bf16[128,2,1152]{2,1,0:T(2,128)(2,1)}), bf16[128,2,1152]{2,1,0:T(2,128)(2,1)}, u32[]{:S(2)}, u32[]{:S(2)}) async-start(bf16[128,2,1152]{2,1,0:T(2,128)(2,1)} %reshape.17), calls=%async_computation | async-start | bytes 1179648 | tf_op jit(solution)/shard_map/all_to_all | solution.py:344
  16.4 1.6 %copy-done = bf16[1024,1024]{1,0:T(8,128)(2,1)S(1)} copy-done((bf16[1024,1024]{1,0:T(8,128)(2,1)S(1)}, bf16[1024,1024]{1,0:T(8,128)(2,1)}, u32[]{:S(2)}) %copy-start) | copy-done | bytes 2097176
  18.9 11.3 %all-to-all-done = bf16[128,2,1152]{2,1,0:T(2,128)(2,1)} async-done(((bf16[128,2,1152]{2,1,0:T(2,128)(2,1)}), bf16[128,2,1152]{2,1,0:T(2,128)(2,1)}, u32[]{:S(2)}, u32[]{:S(2)}) %all-to-all-start) | async-done | bytes 589856 | tf_op jit(solution)/shard_map/all_to_all | solution.py:344
  30.3 2.0 %reshape.18.recv_ref = bf16[256,1152]{1,0:T(8,128)(2,1)S(1)} reshape(bf16[128,2,1152]{2,1,0:T(2,128)(2,1)} %all-to-all-done) | data formatting | bytes 1179648 | tf_op jit(solution)/shard_map/reshape | solution.py:350
  32.2 1.7 %shard_map.75.own0 = bf16[32,4096]{1,0:T(8,128)(2,1)S(1)} custom-call(s32[5]{0:T(128)S(1)} %stack.23.place_ref, bf16[256,1152]{1,0:T(8,128)(2,1)S(1)} %reshape.18.recv_ref, bf16[1024,1024]{1,0:T(8,128)(2,1)S(1)} %get-tuple-element.16.basis_ref, f32[1,1024]{1,0:T(1,128)S(1)} %get-tuple-element.17.taper_ref), custom_call_target="tpu_custom_call" | custom-call | tf_op jit(solution)/shard_map/pallas_call | solution.py:360
  34.0 1.5 %collective-permute-done.own1 = bf16[32,4096]{1,0:T(8,128)(2,1)S(1)} collective-permute-done((bf16[32,4096]{1,0:T(8,128)(2,1)S(1)}, bf16[32,4096]{1,0:T(8,128)(2,1)S(1)}, u32[]{:S(2)}, u32[]{:S(2)}) %collective-permute-start) | collective-permute-done | bytes 262176 | tf_op jit(solution)/shard_map/ppermute | solution.py:302
  37.4 2.6 %collective-permute-start.8 = (bf16[32,4096]{1,0:T(8,128)(2,1)S(1)}, bf16[32,4096]{1,0:T(8,128)(2,1)S(1)}, u32[]{:S(2)}, u32[]{:S(2)}) collective-permute-start(bf16[32,4096]{1,0:T(8,128)(2,1)S(1)} %pad_maximum_fusion.refs_0_), channel_id=1, source_target_pairs={{0,12},{1,97},{2,14},{3,99},{4,0},{5,101},{6,2},{7,103},{8,4},{9,1... | collective-permute-start | bytes 786440 | tf_op jit(solution)/shard_map/ppermute | solution.py:302
  40.0 5.5 %collective-permute-done.1.refs_0_.refs_1_ = bf16[32,4096]{1,0:T(8,128)(2,1)S(1)} collective-permute-done((bf16[32,4096]{1,0:T(8,128)(2,1)S(1)}, bf16[32,4096]{1,0:T(8,128)(2,1)S(1)}, u32[]{:S(2)}, u32[]{:S(2)}) %collective-permute-start.1) | collective-permute-done | bytes 262176 | tf_op jit(solution)/shard_map/ppermute | solution.py:302
  45.5 1.4 %shard_map.80.refs_0_ = bf16[128,4096]{1,0:T(8,128)(2,1)S(1)} custom-call(bf16[32,4096]{1,0:T(8,128)(2,1)S(1)} %pad_maximum_fusion.refs_0_, bf16[32,4096]{1,0:T(8,128)(2,1)S(1)} %collective-permute-done.1.refs_0_.refs_1_, bf16[32,4096]{1,0:T(8,128)(2,1)S(1)} %collective-permute-done.2.refs_1_.refs_2_, bf16[32,4096]{1,0:T(8,128)(2,1)S(1)} %collective-permute-done.8.refs_2_.refs_3_), custom_call_target="tpu_custom_call" | custom-call | flops 1024 | bytes 1024 | tf_op jit(solution)/shard_map/pallas_call | solution.py:152
  49.7 2.5 %collective-permute-start.4 = (bf16[32,4096]{1,0:T(8,128)(2,1)S(1)}, bf16[32,4096]{1,0:T(8,128)(2,1)S(1)}, u32[]{:S(2)}, u32[]{:S(2)}) collective-permute-start(bf16[32,4096]{1,0:T(8,128)(2,1)S(1)} %collective-permute-done.1.refs_0_.refs_1_), channel_id=1, source_target_pairs={{0,12},{1,97},{2,14},{3,99},{4,0},{5,101},{6,2},{7,103},{8,4},{9,1... | collective-permute-start | bytes 786440 | tf_op jit(solution)/shard_map/ppermute | solution.py:302
  52.7 3.4 %collective-permute-done.9.own2 = bf16[32,4096]{1,0:T(8,128)(2,1)S(1)} collective-permute-done((bf16[32,4096]{1,0:T(8,128)(2,1)S(1)}, bf16[32,4096]{1,0:T(8,128)(2,1)S(1)}, u32[]{:S(2)}, u32[]{:S(2)}) %collective-permute-start.9) | collective-permute-done | bytes 262176 | tf_op jit(solution)/shard_map/ppermute | solution.py:302
  56.2 3.3 %collective-permute-done.4.refs_1_ = bf16[32,4096]{1,0:T(8,128)(2,1)S(1)} collective-permute-done((bf16[32,4096]{1,0:T(8,128)(2,1)S(1)}, bf16[32,4096]{1,0:T(8,128)(2,1)S(1)}, u32[]{:S(2)}, u32[]{:S(2)}) %collective-permute-start.4) | collective-permute-done | bytes 262176 | tf_op jit(solution)/shard_map/ppermute | solution.py:302
  59.4 8.0 %collective-permute-done.12.refs_2_ = bf16[128,4096]{1,0:T(8,128)(2,1)S(1)} collective-permute-done((bf16[128,4096]{1,0:T(8,128)(2,1)S(1)}, bf16[128,4096]{1,0:T(8,128)(2,1)S(1)}, u32[]{:S(2)}, u32[]{:S(2)}) %collective-permute-start.12) | collective-permute-done | bytes 1048608 | tf_op jit(solution)/shard_map/ppermute | solution.py:302
  70.1 9.8 %shard_map.79 = (bf16[4096,2048]{1,0:T(8,128)(2,1)S(1)}, f32[8,128]{1,0:T(8,128)}) custom-call(s32[5]{0:T(128)S(1)} %stack.23.place_ref, bf16[32,4096]{1,0:T(8,128)(2,1)S(1)} %shard_map.75.own0, bf16[32,4096]{1,0:T(8,128)(2,1)S(1)} %collective-permute-done.own1, bf16[32,4096]{1,0:T(8,128)(2,1)S(1)} %collective-permute-done.9.own2, ...), custom_call_target="tpu_custom_call" | custom-call | flops 10737418240 | bytes 1048576 | tf_op jit(solution)/shard_map/pallas_call | solution.py:385
  79.9 2.9 %collective-permute-start.6 = (bf16[128,4096]{1,0:T(8,128)(2,1)S(1)}, bf16[128,4096]{1,0:T(8,128)(2,1)S(1)}, u32[]{:S(2)}, u32[]{:S(2)}) collective-permute-start(bf16[128,4096]{1,0:T(8,128)(2,1)S(1)} %shard_map.77.refs_0_), channel_id=1, source_target_pairs={{0,96},{1,13},{2,98},{3,15},{4,100},{5,1},{6,102},{7,3},{8,104},{9... | collective-permute-start | bytes 3145736 | tf_op jit(solution)/shard_map/ppermute | solution.py:302
  82.8 6.9 %shard_map.81 = (f32[64,16,2048]{2,1,0:T(8,128)}, f32[8,128]{1,0:T(8,128)S(1)}) custom-call(s32[5]{0:T(128)S(1)} %stack.23.place_ref, bf16[128,4096]{1,0:T(8,128)(2,1)S(1)} %shard_map.80.refs_0_, bf16[128,4096]{1,0:T(8,128)(2,1)S(1)} %collective-permute-done.11.refs_1_, bf16[128,4096]{1,0:T(8,128)(2,1)S(1)} %collective-permute-done.12.refs_2_, ...), custom_call_target="tpu_custom_call" | custom-call | flops 6442450944 | bytes 4194304 | tf_op jit(solution)/shard_map/pallas_call | solution.py:276
  89.8 4.8 %collective-permute-done.14.refs_2_ = bf16[128,4096]{1,0:T(8,128)(2,1)S(1)} collective-permute-done((bf16[128,4096]{1,0:T(8,128)(2,1)S(1)}, bf16[128,4096]{1,0:T(8,128)(2,1)S(1)}, u32[]{:S(2)}, u32[]{:S(2)}) %collective-permute-start.14) | collective-permute-done | bytes 1048608 | tf_op jit(solution)/shard_map/ppermute | solution.py:302
  95.2 4.4 %shard_map.82 = (f32[64,16,2048]{2,1,0:T(8,128)}, f32[8,128]{1,0:T(8,128)S(1)}) custom-call(s32[5]{0:T(128)S(1)} %stack.23.place_ref, bf16[128,4096]{1,0:T(8,128)(2,1)S(1)} %shard_map.77.refs_0_, bf16[128,4096]{1,0:T(8,128)(2,1)S(1)} %collective-permute-done.7.refs_1_, ...), custom_call_target="tpu_custom_call", output_to_operand_aliasing={{0}: (4, {})} | custom-call | flops 3221225472 | bytes 2097152 | tf_op jit(solution)/shard_map/pallas_call | solution.py:276
  99.7 6.2 %collective-permute-done.18.refs_2_ = bf16[128,4096]{1,0:T(8,128)(2,1)S(1)} collective-permute-done((bf16[128,4096]{1,0:T(8,128)(2,1)S(1)}, bf16[128,4096]{1,0:T(8,128)(2,1)S(1)}, u32[]{:S(2)}, u32[]{:S(2)}) %collective-permute-start.18) | collective-permute-done | bytes 1048608 | tf_op jit(solution)/shard_map/ppermute | solution.py:302
  107.2 7.4 %shard_map.85 = (f32[64,16,2048]{2,1,0:T(8,128)}, f32[8,128]{1,0:T(8,128)}) custom-call(s32[5]{0:T(128)S(1)} %stack.23.place_ref, bf16[128,4096]{1,0:T(8,128)(2,1)S(1)} %shard_map.84.refs_0_, bf16[128,4096]{1,0:T(8,128)(2,1)S(1)} %collective-permute-done.20.refs_1_, ...), custom_call_target="tpu_custom_call", output_to_operand_aliasing={{0}: (6, {})} | custom-call | flops 6442450944 | bytes 4194304 | tf_op jit(solution)/shard_map/pallas_call | solution.py:276
  114.7 6.9 %shard_map.86 = (f32[64,16,2048]{2,1,0:T(8,128)}, f32[8,128]{1,0:T(8,128)S(1)}) custom-call(s32[5]{0:T(128)S(1)} %stack.23.place_ref, bf16[128,4096]{1,0:T(8,128)(2,1)S(1)} %shard_map.83.refs_0_, bf16[128,4096]{1,0:T(8,128)(2,1)S(1)} %collective-permute-done.16.refs_1_, ...), custom_call_target="tpu_custom_call", output_to_operand_aliasing={{0}: (6, {})} | custom-call | flops 6442450944 | bytes 4194304 | tf_op jit(solution)/shard_map/pallas_call | solution.py:276
  121.6 1.7 %collective-permute-start.22 = (bf16[128,4096]{1,0:T(8,128)(2,1)S(1)}, bf16[128,4096]{1,0:T(8,128)(2,1)S(1)}, u32[]{:S(2)}, u32[]{:S(2)}) collective-permute-start(bf16[128,4096]{1,0:T(8,128)(2,1)S(1)} %shard_map.87.refs_0_), channel_id=1, source_target_pairs={{0,1},{1,0},{2,3},{3,2},{4,5},{5,4},{6,7},{7,6},{8,9},{9,8},{10,11... | collective-permute-start | bytes 3145736 | tf_op jit(solution)/shard_map/ppermute | solution.py:302
  123.3 2.3 %collective-permute-done.22.refs_1_ = bf16[128,4096]{1,0:T(8,128)(2,1)S(1)} collective-permute-done((bf16[128,4096]{1,0:T(8,128)(2,1)S(1)}, bf16[128,4096]{1,0:T(8,128)(2,1)S(1)}, u32[]{:S(2)}, u32[]{:S(2)}) %collective-permute-start.22) | collective-permute-done | bytes 1048608 | tf_op jit(solution)/shard_map/ppermute | solution.py:302
  125.6 5.0 %shard_map.88 = (f32[64,16,2048]{2,1,0:T(8,128)}, f32[8,128]{1,0:T(8,128)}) custom-call(s32[5]{0:T(128)S(1)} %stack.23.place_ref, bf16[128,4096]{1,0:T(8,128)(2,1)S(1)} %shard_map.87.refs_0_, bf16[128,4096]{1,0:T(8,128)(2,1)S(1)} %collective-permute-done.22.refs_1_, ...), custom_call_target="tpu_custom_call", output_to_operand_aliasing={{0}: (4, {})} | custom-call | flops 3221225472 | bytes 2097152 | tf_op jit(solution)/shard_map/pallas_call | solution.py:276
  (58 shorter events, 15.0 us)
Async XLA Ops:
  4.7 25.5 %all-to-all-start = ((bf16[128,2,1152]{2,1,0:T(2,128)(2,1)}), bf16[128,2,1152]{2,1,0:T(2,128)(2,1)}, u32[]{:S(2)}, u32[]{:S(2)}) async-start(bf16[128,2,1152]{2,1,0:T(2,128)(2,1)} %reshape.17), calls=%async_computation | async-start | bytes 1179648 | tf_op jit(solution)/shard_map/all_to_all | solution.py:344
  33.9 1.6 %collective-permute-start = (bf16[32,4096]{1,0:T(8,128)(2,1)S(1)}, bf16[32,4096]{1,0:T(8,128)(2,1)S(1)}, u32[]{:S(2)}, u32[]{:S(2)}) collective-permute-start(bf16[32,4096]{1,0:T(8,128)(2,1)S(1)} %shard_map.75.own0), channel_id=1, source_target_pairs={{0,1},{1,0},{2,3},{3,2},{4,5},{5,4},{6,7},{7,6},{8,9},{9,8},{10,11... | collective-permute-start | bytes 786440 | tf_op jit(solution)/shard_map/ppermute | solution.py:302
  35.6 9.9 %collective-permute-start.1 = (bf16[32,4096]{1,0:T(8,128)(2,1)S(1)}, bf16[32,4096]{1,0:T(8,128)(2,1)S(1)}, u32[]{:S(2)}, u32[]{:S(2)}) collective-permute-start(bf16[32,4096]{1,0:T(8,128)(2,1)S(1)} %pad_maximum_fusion.refs_0_), channel_id=1, source_target_pairs={{0,16},{1,17},{2,18},{3,19},{4,20},{5,21},{6,22},{7,23},{8,24},{9,... | collective-permute-start | bytes 786440 | tf_op jit(solution)/shard_map/ppermute | solution.py:302
  36.8 8.7 %collective-permute-start.2 = (bf16[32,4096]{1,0:T(8,128)(2,1)S(1)}, bf16[32,4096]{1,0:T(8,128)(2,1)S(1)}, u32[]{:S(2)}, u32[]{:S(2)}) collective-permute-start(bf16[32,4096]{1,0:T(8,128)(2,1)S(1)} %pad_maximum_fusion.refs_0_), channel_id=1, source_target_pairs={{0,4},{1,33},{2,6},{3,35},{4,8},{5,37},{6,10},{7,39},{8,12},{9,41}... | collective-permute-start | bytes 786440 | tf_op jit(solution)/shard_map/ppermute | solution.py:302
  37.4 8.1 %collective-permute-start.8 = (bf16[32,4096]{1,0:T(8,128)(2,1)S(1)}, bf16[32,4096]{1,0:T(8,128)(2,1)S(1)}, u32[]{:S(2)}, u32[]{:S(2)}) collective-permute-start(bf16[32,4096]{1,0:T(8,128)(2,1)S(1)} %pad_maximum_fusion.refs_0_), channel_id=1, source_target_pairs={{0,12},{1,97},{2,14},{3,99},{4,0},{5,101},{6,2},{7,103},{8,4},{9,1... | collective-permute-start | bytes 786440 | tf_op jit(solution)/shard_map/ppermute | solution.py:302
  46.9 20.4 %collective-permute-start.12 = (bf16[128,4096]{1,0:T(8,128)(2,1)S(1)}, bf16[128,4096]{1,0:T(8,128)(2,1)S(1)}, u32[]{:S(2)}, u32[]{:S(2)}) collective-permute-start(bf16[128,4096]{1,0:T(8,128)(2,1)S(1)} %shard_map.80.refs_0_), channel_id=1, source_target_pairs={{0,96},{1,13},{2,98},{3,15},{4,100},{5,1},{6,102},{7,3},{8,104},{9... | collective-permute-start | bytes 3145736 | tf_op jit(solution)/shard_map/ppermute | solution.py:302
  48.3 19.7 %collective-permute-start.3 = (bf16[64,4096]{1,0:T(8,128)(2,1)S(1)}, bf16[64,4096]{1,0:T(8,128)(2,1)S(1)}, u32[]{:S(2)}, u32[]{:S(2)}) collective-permute-start(bf16[64,4096]{1,0:T(8,128)(2,1)S(1)} %shard_map.76), channel_id=1, source_target_pairs={{0,4},{1,33},{2,6},{3,35},{4,8},{5,37},{6,10},{7,39},{8,12},{9,41}... | collective-permute-start | bytes 1572872 | tf_op jit(solution)/shard_map/ppermute | solution.py:302
  48.8 7.4 %collective-permute-start.9 = (bf16[32,4096]{1,0:T(8,128)(2,1)S(1)}, bf16[32,4096]{1,0:T(8,128)(2,1)S(1)}, u32[]{:S(2)}, u32[]{:S(2)}) collective-permute-start(bf16[32,4096]{1,0:T(8,128)(2,1)S(1)} %shard_map.78), channel_id=1, source_target_pairs={{0,2},{1,3},{2,0},{3,1},{4,6},{5,7},{6,4},{7,5},{8,10},{9,11},{10,... | collective-permute-start | bytes 786440 | tf_op jit(solution)/shard_map/ppermute | solution.py:302
  49.7 9.8 %collective-permute-start.4 = (bf16[32,4096]{1,0:T(8,128)(2,1)S(1)}, bf16[32,4096]{1,0:T(8,128)(2,1)S(1)}, u32[]{:S(2)}, u32[]{:S(2)}) collective-permute-start(bf16[32,4096]{1,0:T(8,128)(2,1)S(1)} %collective-permute-done.1.refs_0_.refs_1_), channel_id=1, source_target_pairs={{0,12},{1,97},{2,14},{3,99},{4,0},{5,101},{6,2},{7,103},{8,4},{9,1... | collective-permute-start | bytes 786440 | tf_op jit(solution)/shard_map/ppermute | solution.py:302
  52.1 15.3 %collective-permute-start.5 = (bf16[32,4096]{1,0:T(8,128)(2,1)S(1)}, bf16[32,4096]{1,0:T(8,128)(2,1)S(1)}, u32[]{:S(2)}, u32[]{:S(2)}) collective-permute-start(bf16[32,4096]{1,0:T(8,128)(2,1)S(1)} %collective-permute-done.1.refs_0_.refs_1_), channel_id=1, source_target_pairs={{0,8},{1,65},{2,10},{3,67},{4,12},{5,69},{6,14},{7,71},{8,0},{9,73... | collective-permute-start | bytes 786440 | tf_op jit(solution)/shard_map/ppermute | solution.py:302
  56.2 13.3 %collective-permute-start.10 = (bf16[32,4096]{1,0:T(8,128)(2,1)S(1)}, bf16[32,4096]{1,0:T(8,128)(2,1)S(1)}, u32[]{:S(2)}, u32[]{:S(2)}) collective-permute-start(bf16[32,4096]{1,0:T(8,128)(2,1)S(1)} %collective-permute-done.9.own2), channel_id=1, source_target_pairs={{0,1},{1,0},{2,3},{3,2},{4,5},{5,4},{6,7},{7,6},{8,9},{9,8},{10,11... | collective-permute-start | bytes 786440 | tf_op jit(solution)/shard_map/ppermute | solution.py:302
  59.4 20.5 %collective-permute-start.11 = (bf16[128,4096]{1,0:T(8,128)(2,1)S(1)}, bf16[128,4096]{1,0:T(8,128)(2,1)S(1)}, u32[]{:S(2)}, u32[]{:S(2)}) collective-permute-start(bf16[128,4096]{1,0:T(8,128)(2,1)S(1)} %shard_map.80.refs_0_), channel_id=1, source_target_pairs={{0,1},{1,0},{2,3},{3,2},{4,5},{5,4},{6,7},{7,6},{8,9},{9,8},{10,11... | collective-permute-start | bytes 3145736 | tf_op jit(solution)/shard_map/ppermute | solution.py:302
  67.4 15.4 %collective-permute-start.13 = (bf16[128,4096]{1,0:T(8,128)(2,1)S(1)}, bf16[128,4096]{1,0:T(8,128)(2,1)S(1)}, u32[]{:S(2)}, u32[]{:S(2)}) collective-permute-start(bf16[128,4096]{1,0:T(8,128)(2,1)S(1)} %collective-permute-done.12.refs_2_), channel_id=1, source_target_pairs={{0,1},{1,0},{2,3},{3,2},{4,5},{5,4},{6,7},{7,6},{8,9},{9,8},{10,11... | collective-permute-start | bytes 3145736 | tf_op jit(solution)/shard_map/ppermute | solution.py:302
  67.4 22.3 %collective-permute-start.17 = (bf16[128,4096]{1,0:T(8,128)(2,1)S(1)}, bf16[128,4096]{1,0:T(8,128)(2,1)S(1)}, u32[]{:S(2)}, u32[]{:S(2)}) collective-permute-start(bf16[128,4096]{1,0:T(8,128)(2,1)S(1)} %shard_map.80.refs_0_), channel_id=1, source_target_pairs={{0,32},{1,5},{2,34},{3,7},{4,36},{5,9},{6,38},{7,11},{8,40},{9,13}... | collective-permute-start | bytes 3145736 | tf_op jit(solution)/shard_map/ppermute | solution.py:302
  69.4 25.8 %collective-permute-start.7 = (bf16[128,4096]{1,0:T(8,128)(2,1)S(1)}, bf16[128,4096]{1,0:T(8,128)(2,1)S(1)}, u32[]{:S(2)}, u32[]{:S(2)}) collective-permute-start(bf16[128,4096]{1,0:T(8,128)(2,1)S(1)} %shard_map.77.refs_0_), channel_id=1, source_target_pairs={{0,1},{1,0},{2,3},{3,2},{4,5},{5,4},{6,7},{7,6},{8,9},{9,8},{10,11... | collective-permute-start | bytes 3145736 | tf_op jit(solution)/shard_map/ppermute | solution.py:302
  69.5 25.2 %collective-permute-start.14 = (bf16[128,4096]{1,0:T(8,128)(2,1)S(1)}, bf16[128,4096]{1,0:T(8,128)(2,1)S(1)}, u32[]{:S(2)}, u32[]{:S(2)}) collective-permute-start(bf16[128,4096]{1,0:T(8,128)(2,1)S(1)} %shard_map.77.refs_0_), channel_id=1, source_target_pairs={{0,32},{1,5},{2,34},{3,7},{4,36},{5,9},{6,38},{7,11},{8,40},{9,13}... | collective-permute-start | bytes 3145736 | tf_op jit(solution)/shard_map/ppermute | solution.py:302
  79.9 19.7 %collective-permute-start.6 = (bf16[128,4096]{1,0:T(8,128)(2,1)S(1)}, bf16[128,4096]{1,0:T(8,128)(2,1)S(1)}, u32[]{:S(2)}, u32[]{:S(2)}) collective-permute-start(bf16[128,4096]{1,0:T(8,128)(2,1)S(1)} %shard_map.77.refs_0_), channel_id=1, source_target_pairs={{0,96},{1,13},{2,98},{3,15},{4,100},{5,1},{6,102},{7,3},{8,104},{9... | collective-permute-start | bytes 3145736 | tf_op jit(solution)/shard_map/ppermute | solution.py:302
  89.7 16.2 %collective-permute-start.18 = (bf16[128,4096]{1,0:T(8,128)(2,1)S(1)}, bf16[128,4096]{1,0:T(8,128)(2,1)S(1)}, u32[]{:S(2)}, u32[]{:S(2)}) collective-permute-start(bf16[128,4096]{1,0:T(8,128)(2,1)S(1)} %shard_map.84.refs_0_), channel_id=1, source_target_pairs={{0,32},{1,5},{2,34},{3,7},{4,36},{5,9},{6,38},{7,11},{8,40},{9,13}... | collective-permute-start | bytes 3145736 | tf_op jit(solution)/shard_map/ppermute | solution.py:302
  94.6 12.6 %collective-permute-start.21 = (bf16[128,4096]{1,0:T(8,128)(2,1)S(1)}, bf16[128,4096]{1,0:T(8,128)(2,1)S(1)}, u32[]{:S(2)}, u32[]{:S(2)}) collective-permute-start(bf16[128,4096]{1,0:T(8,128)(2,1)S(1)} %collective-permute-done.14.refs_2_), channel_id=1, source_target_pairs={{0,1},{1,0},{2,3},{3,2},{4,5},{5,4},{6,7},{7,6},{8,9},{9,8},{10,11... | collective-permute-start | bytes 3145736 | tf_op jit(solution)/shard_map/ppermute | solution.py:302
  94.7 12.6 %collective-permute-start.20 = (bf16[128,4096]{1,0:T(8,128)(2,1)S(1)}, bf16[128,4096]{1,0:T(8,128)(2,1)S(1)}, u32[]{:S(2)}, u32[]{:S(2)}) collective-permute-start(bf16[128,4096]{1,0:T(8,128)(2,1)S(1)} %shard_map.84.refs_0_), channel_id=1, source_target_pairs={{0,1},{1,0},{2,3},{3,2},{4,5},{5,4},{6,7},{7,6},{8,9},{9,8},{10,11... | collective-permute-start | bytes 3145736 | tf_op jit(solution)/shard_map/ppermute | solution.py:302
  99.6 15.0 %collective-permute-start.16 = (bf16[128,4096]{1,0:T(8,128)(2,1)S(1)}, bf16[128,4096]{1,0:T(8,128)(2,1)S(1)}, u32[]{:S(2)}, u32[]{:S(2)}) collective-permute-start(bf16[128,4096]{1,0:T(8,128)(2,1)S(1)} %shard_map.83.refs_0_), channel_id=1, source_target_pairs={{0,1},{1,0},{2,3},{3,2},{4,5},{5,4},{6,7},{7,6},{8,9},{9,8},{10,11... | collective-permute-start | bytes 3145736 | tf_op jit(solution)/shard_map/ppermute | solution.py:302
  105.9 8.8 %collective-permute-start.19 = (bf16[128,4096]{1,0:T(8,128)(2,1)S(1)}, bf16[128,4096]{1,0:T(8,128)(2,1)S(1)}, u32[]{:S(2)}, u32[]{:S(2)}) collective-permute-start(bf16[128,4096]{1,0:T(8,128)(2,1)S(1)} %collective-permute-done.18.refs_2_), channel_id=1, source_target_pairs={{0,1},{1,0},{2,3},{3,2},{4,5},{5,4},{6,7},{7,6},{8,9},{9,8},{10,11... | collective-permute-start | bytes 3145736 | tf_op jit(solution)/shard_map/ppermute | solution.py:302
  105.9 15.7 %collective-permute-start.15 = (bf16[128,4096]{1,0:T(8,128)(2,1)S(1)}, bf16[128,4096]{1,0:T(8,128)(2,1)S(1)}, u32[]{:S(2)}, u32[]{:S(2)}) collective-permute-start(bf16[128,4096]{1,0:T(8,128)(2,1)S(1)} %shard_map.83.refs_0_), channel_id=1, source_target_pairs={{0,96},{1,13},{2,98},{3,15},{4,100},{5,1},{6,102},{7,3},{8,104},{9... | collective-permute-start | bytes 3145736 | tf_op jit(solution)/shard_map/ppermute | solution.py:302
  121.6 4.0 %collective-permute-start.22 = (bf16[128,4096]{1,0:T(8,128)(2,1)S(1)}, bf16[128,4096]{1,0:T(8,128)(2,1)S(1)}, u32[]{:S(2)}, u32[]{:S(2)}) collective-permute-start(bf16[128,4096]{1,0:T(8,128)(2,1)S(1)} %shard_map.87.refs_0_), channel_id=1, source_target_pairs={{0,1},{1,0},{2,3},{3,2},{4,5},{5,4},{6,7},{7,6},{8,9},{9,8},{10,11... | collective-permute-start | bytes 3145736 | tf_op jit(solution)/shard_map/ppermute | solution.py:302
  (6 other events, 71.1 us)

commit v4 on v3

--- a/solution.py
+++ b/solution.py
@@ -218,12 +218,14 @@
 def matmul_kernel(sources, n_in, place_ref, *refs):
     rot_ref = refs[n_in]
     out_ref, token_ref, left, acc, in_sem, out_sem = refs[-6:]
-    rows = GROUP * HALF
     z, xh, y, core = place_ref[0], place_ref[1], place_ref[2], place_ref[4]
-    loads = [
-        pltpu.make_async_copy(refs[i].at[pl.ds(row, rows)], left.at[pl.ds(n * rows, rows)], in_sem.at[n])
-        for n, (i, row, _, _, _) in enumerate(sources)
-    ]
+    loads, begin = [], 0
+    for n, (i, row, _, offsets, _) in enumerate(sources):
+        rows = len(offsets) * HALF
+        loads.append(
+            pltpu.make_async_copy(refs[i].at[pl.ds(row, rows)], left.at[pl.ds(begin, rows)], in_sem.at[n])
+        )
+        begin += rows
     for c in loads:
         c.start()
     token_ref[...] = jnp.zeros_like(token_ref)
@@ -260,12 +262,9 @@
 
 
 def matmul(place, carried, rotated, out):
-    arrays, sources = [], []
-    for value, theirs, at, dq in carried:
-        n = len(arrays)
-        arrays += [value, theirs]
-        sources += [(n, 0, False, at, dq), (n + 1, GROUP * HALF, True, at, dq)]
-    rows = len(sources) * GROUP * HALF
+    arrays = [value for value, _, _, _ in carried]
+    sources = [(n, len(at) * HALF if other else 0, other, at, dq) for n, (_, other, at, dq) in enumerate(carried)]
+    rows = sum(len(at) for _, _, at, _ in carried) * HALF
     operands = [place, *arrays, rotated]
     in_specs = [SMEM] + [ANY] * len(arrays) + [VMEM]
     aliases = {}
@@ -369,19 +368,18 @@
     unit = jnp.concatenate([white[:HALF], sib[HALF:]], axis=0)
     beyond = across(unit)
     ahead, behind = first(unit, 1), first(unit, -1)
-    facing = neighbour(gated(unit, [ahead, behind]))
+    facing = neighbour(unit)
     facing_sib = sibling(facing)
     two = [(i, h, 0, 2 * i + h) for i in range(2) for h in range(2)]
     pair = first(grouped(two, [4], [beyond, ahead], [])[0], 1)
     beyond_behind = first(beyond, -1)
     beyond_far = first(beyond, 2)
-    moves = [(i, h, 0, h * GROUP + i) for i in range(GROUP) for h in range(2)]
-    (near,) = grouped(moves, [8], [unit, beyond, ahead, behind], [])
-    near_up, near_down = second(near, 1), second(near, -1)
-    moves = [(0, 0, 0, 0), (0, 1, 0, 4), (0, 2, 0, 1), (0, 3, 0, 5)]
-    moves += [(i, h, 0, h * GROUP + i + 1) for i in (1, 2) for h in range(2)]
-    (rest,) = grouped(moves, [8], [pair, beyond_behind, beyond_far], [])
-    rest_up, rest_down = second(rest, 1), second(rest, -1)
+    arrays = [unit, beyond, ahead, behind, beyond_behind, beyond_far, pair]
+    moves = [(i, h, 0, 8 * h + i) for i in range(6) for h in range(2)]
+    moves += [(6, 2 * i + h, 0, 8 * h + 6 + i) for i in range(2) for h in range(2)]
+    line_at = [(0, 0), (0, 1), (-1, 0), (1, 0), (1, 1), (2, 1), (-1, 1), (-2, 0)]
+    (line,) = grouped(moves, [16], arrays, [facing_sib])
+    up, down = second(line, 1), second(line, -1)
     rotated, _ = pl.pallas_call(
         rotate_kernel,
         in_specs=[SMEM] + [VMEM] * 4 + [HBM],
@@ -398,21 +396,17 @@
         cost_estimate=pl.CostEstimate(flops=2 * CB * SPEC * COLS * 5, bytes_accessed=MIB, transcendentals=0),
     )(place, white, sib, facing, facing_sib, turn)
 
-    near_at = [(0, 0), (0, 1), (-1, 0), (1, 0)]
-    rest_at = [(-1, 1), (-2, 0), (1, 1), (2, 1)]
-
-    def product(out, *carried):
-        return matmul(place, [(value, sibling(value), at, dq) for value, at, dq in carried], rotated, out)
-
-    out, done = product(None, (near, near_at, 0), (near_down, near_at, 1))
-    near_up = gated(near_up, [done])
-    near_far = second(near_up, 1)
-    out, done = product(out, (rest, rest_at, 0))
-    rest_down = gated(rest_down, [done, rest_up])
-    rest_far = second(rest_down, -1)
-    out, _ = product(out, (near_up, near_at, -1), (rest_up, rest_at, -1))
-    out, done = product(out, (rest_down, rest_at, 1), (near_far, near_at, -2))
-    out, _ = product(out, (gated(rest_far, [done]), rest_at, 2))
+    out, done = matmul(place, [(line, False, line_at, 0), (sibling(line), True, line_at, 0)], rotated, None)
+    up, down = gated(up, [done]), gated(down, [done])
+    parts = [[(i, 8 * h + 4 * i + u, i, 4 * h + u) for h in range(2) for u in range(4)] for i in range(2)]
+    turn_up, turn_down = grouped(parts[0] + parts[1], [8, 8], [up, down], [])
+    far_up, far_down = second(turn_up, 1), second(turn_down, -1)
+    out, _ = matmul(place, [(up, False, line_at, -1), (down, False, line_at, 1)], rotated, out)
+    out, done = matmul(place, [(sibling(up), True, line_at, -1), (sibling(down), True, line_at, 1)], rotated, out)
+    far_up, far_down = gated(far_up, [done]), gated(far_down, [done])
+    halves = [(far_up, line_at[:4], -2), (far_down, line_at[4:], 2)]
+    out, _ = matmul(place, [(value, False, at, dq) for value, at, dq in halves], rotated, out)
+    out, _ = matmul(place, [(sibling(value), True, at, dq) for value, at, dq in halves], rotated, out)
     return out.reshape(NZ * NXH * NY, QC, COLS)
 
 

time: 132 us -> 123 us (0.932)
  waiting for transfers between devices: 46.3 us -> 38.5 us
  Pallas kernels: 46.4 us -> 49.8 us
  local copies, waits for them, and re-layouts: 7.79 us -> 5.35 us
  starting transfers between devices: 29.1 us -> 27.1 us
    ppermute x23 -> x18, waiting for transfers between devices: 35 us -> 26.2 us  [permuted(): return lax.ppermute(value, ('blk', 'freq'), pairs)]
    pallas_call x3, Pallas kernels: 3.53 us -> 6.39 us  [grouped(): pl.pallas_call(functools.partial(group_kernel, moves, len(arrays) + len(a...]
    reshape x1, local copies, waits for them, and re-layouts: 1.98 us -> 0.22 us  [local(): arrived = lax.all_to_all(packed.reshape(DEVICES, SLOTS // DEVICES, SAMPLE...]
    ppermute x23 -> x18, starting transfers between devices: 17.5 us -> 15.9 us  [permuted(): return lax.ppermute(value, ('blk', 'freq'), pairs)]
  transfers between devices with their start and end apart: 24 -> 19, of which waited for: 9 -> 7; matrix products, arithmetic and copies ran while one was open for 0% -> 0% of each run, Pallas kernels for 29% -> 32%
where the time goes in v4:
time: 123 us; the launch traced here: 122 us
  Pallas kernels  49.8 us (40%)
  waiting for transfers between devices  38.5 us (31%)
  starting transfers between devices  27.1 us (22%)
  local copies, waits for them, and re-layouts  5.35 us (4%)
    pallas_call x5, Pallas kernels, matmul(): pl.pallas_call(functools.partial(matmul_kernel, sources, len(arrays)), in...  31.2 us
    ppermute x18, waiting for transfers between devices, permuted(): return lax.ppermute(value, ('blk', 'freq'), pairs)  26.2 us
    ppermute x18, starting transfers between devices, permuted(): return lax.ppermute(value, ('blk', 'freq'), pairs)  15.9 us
    all_to_all x1, waiting for transfers between devices, local(): lax.all_to_all(packed.reshape(DEVICES, SLOTS // DEVICES, SAMPLES + TAIL),...  12.4 us
    all_to_all x1, starting transfers between devices, local(): lax.all_to_all(packed.reshape(DEVICES, SLOTS // DEVICES, SAMPLES + TAIL),...  11.1 us
    pallas_call x1, Pallas kernels, local(): pl.pallas_call(rotate_kernel, in_specs=[SMEM] + [VMEM] * 4 + [HBM], out_s...  9.78 us
    pallas_call x3, Pallas kernels, grouped(): pl.pallas_call(functools.partial(group_kernel, moves, len(arrays) + len(a...  6.39 us
    unnamed x12, local copies, waits for them, and re-layouts  3.99 us
  transfers between devices with their start and end apart: 19, of which 7 were waited for; matrix products, arithmetic and copies ran while one was open for 0% of the time, Pallas kernels for 32%

profile of v4, /device:TPU:0, one launch (start us, length us, event | category | flops | bytes accessed | tf_op | source)
XLA Modules:
  0.0 121.9 jit_solution(14513540985459053316)
XLA Ops:
  3.7 1.0 reshape.17
  4.7 11.1 %all-to-all-start = ((bf16[128,2,1152]{2,1,0:T(2,128)(2,1)}), bf16[128,2,1152]{2,1,0:T(2,128)(2,1)S(1)}, u32[]{:S(2)}, u32[]{:S(2)}) async-start(bf16[128,2,1152]{2,1,0:T(2,128)(2,1)} %reshape.17), calls=%async_computation | async-start | bytes 1179648 | tf_op jit(solution)/shard_map/all_to_all | solution.py:343
  15.9 1.6 %copy-done = bf16[1024,1024]{1,0:T(8,128)(2,1)S(1)} copy-done((bf16[1024,1024]{1,0:T(8,128)(2,1)S(1)}, bf16[1024,1024]{1,0:T(8,128)(2,1)}, u32[]{:S(2)}) %copy-start) | copy-done | bytes 2097176
  17.8 12.4 %all-to-all-done = bf16[128,2,1152]{2,1,0:T(2,128)(2,1)S(1)} async-done(((bf16[128,2,1152]{2,1,0:T(2,128)(2,1)}), bf16[128,2,1152]{2,1,0:T(2,128)(2,1)S(1)}, u32[]{:S(2)}, u32[]{:S(2)}) %all-to-all-start) | async-done | bytes 589856 | tf_op jit(solution)/shard_map/all_to_all | solution.py:343
  30.4 1.7 %shard_map.75.own0 = bf16[32,4096]{1,0:T(8,128)(2,1)S(1)} custom-call(s32[5]{0:T(128)S(1)} %stack.23.place_ref, bf16[256,1152]{1,0:T(8,128)(2,1)S(1)} %reshape.18.recv_ref, bf16[1024,1024]{1,0:T(8,128)(2,1)S(1)} %get-tuple-element.17.basis_ref, f32[1,1024]{1,0:T(1,128)S(1)} %get-tuple-element.18.taper_ref), custom_call_target="tpu_custom_call" | custom-call | tf_op jit(solution)/shard_map/pallas_call | solution.py:359
  32.2 1.5 %collective-permute-done.own1 = bf16[32,4096]{1,0:T(8,128)(2,1)S(1)} collective-permute-done((bf16[32,4096]{1,0:T(8,128)(2,1)S(1)}, bf16[32,4096]{1,0:T(8,128)(2,1)S(1)}, u32[]{:S(2)}, u32[]{:S(2)}) %collective-permute-start) | collective-permute-done | bytes 262176 | tf_op jit(solution)/shard_map/ppermute | solution.py:301
  33.8 1.7 %collective-permute-start.1 = (bf16[32,4096]{1,0:T(8,128)(2,1)S(1)}, bf16[32,4096]{1,0:T(8,128)(2,1)S(1)}, u32[]{:S(2)}, u32[]{:S(2)}) collective-permute-start(bf16[32,4096]{1,0:T(8,128)(2,1)S(1)} %pad_maximum_fusion.refs_0_), channel_id=1, source_target_pairs={{0,16},{1,17},{2,18},{3,19},{4,20},{5,21},{6,22},{7,23},{8,24},{9,... | collective-permute-start | bytes 786440 | tf_op jit(solution)/shard_map/ppermute | solution.py:301
  36.2 5.2 %collective-permute-done.2.refs_1_.refs_2_ = bf16[32,4096]{1,0:T(8,128)(2,1)S(1)} collective-permute-done((bf16[32,4096]{1,0:T(8,128)(2,1)S(1)}, bf16[32,4096]{1,0:T(8,128)(2,1)S(1)}, u32[]{:S(2)}, u32[]{:S(2)}) %collective-permute-start.2) | collective-permute-done | bytes 262176 | tf_op jit(solution)/shard_map/ppermute | solution.py:301
  41.4 3.1 %collective-permute-done.1.refs_0_.refs_1_ = bf16[32,4096]{1,0:T(8,128)(2,1)S(1)} collective-permute-done((bf16[32,4096]{1,0:T(8,128)(2,1)S(1)}, bf16[32,4096]{1,0:T(8,128)(2,1)S(1)}, u32[]{:S(2)}, u32[]{:S(2)}) %collective-permute-start.1) | collective-permute-done | bytes 262176 | tf_op jit(solution)/shard_map/ppermute | solution.py:301
  46.0 2.6 %collective-permute-start.3 = (bf16[32,4096]{1,0:T(8,128)(2,1)S(1)}, bf16[32,4096]{1,0:T(8,128)(2,1)S(1)}, u32[]{:S(2)}, u32[]{:S(2)}) collective-permute-start(bf16[32,4096]{1,0:T(8,128)(2,1)S(1)} %pad_maximum_fusion.refs_0_), channel_id=1, source_target_pairs={{0,12},{1,97},{2,14},{3,99},{4,0},{5,101},{6,2},{7,103},{8,4},{9,1... | collective-permute-start | bytes 786440 | tf_op jit(solution)/shard_map/ppermute | solution.py:301
  48.5 1.4 %collective-permute-start.5 = (bf16[32,4096]{1,0:T(8,128)(2,1)S(1)}, bf16[32,4096]{1,0:T(8,128)(2,1)S(1)}, u32[]{:S(2)}, u32[]{:S(2)}) collective-permute-start(bf16[32,4096]{1,0:T(8,128)(2,1)S(1)} %collective-permute-done.1.refs_0_.refs_1_), channel_id=1, source_target_pairs={{0,8},{1,65},{2,10},{3,67},{4,12},{5,69},{6,14},{7,71},{8,0},{9,73... | collective-permute-start | bytes 786440 | tf_op jit(solution)/shard_map/ppermute | solution.py:301
  50.9 4.4 %collective-permute-done.3.refs_3_ = bf16[32,4096]{1,0:T(8,128)(2,1)S(1)} collective-permute-done((bf16[32,4096]{1,0:T(8,128)(2,1)S(1)}, bf16[32,4096]{1,0:T(8,128)(2,1)S(1)}, u32[]{:S(2)}, u32[]{:S(2)}) %collective-permute-start.3) | collective-permute-done | bytes 262176 | tf_op jit(solution)/shard_map/ppermute | solution.py:301
  55.3 4.5 %collective-permute-done.5.refs_5_ = bf16[32,4096]{1,0:T(8,128)(2,1)S(1)} collective-permute-done((bf16[32,4096]{1,0:T(8,128)(2,1)S(1)}, bf16[32,4096]{1,0:T(8,128)(2,1)S(1)}, u32[]{:S(2)}, u32[]{:S(2)}) %collective-permute-start.5) | collective-permute-done | bytes 262176 | tf_op jit(solution)/shard_map/ppermute | solution.py:301
  59.8 2.9 %shard_map.77.refs_0_ = bf16[256,4096]{1,0:T(8,128)(2,1)S(1)} custom-call(bf16[32,4096]{1,0:T(8,128)(2,1)S(1)} %pad_maximum_fusion.refs_0_, bf16[32,4096]{1,0:T(8,128)(2,1)S(1)} %collective-permute-done.1.refs_0_.refs_1_, bf16[32,4096]{1,0:T(8,128)(2,1)S(1)} %collective-permute-done.2.refs_1_.refs_2_, bf16[32,4096]{1,0:T(8,128)(2,1)S(1)} %collective-permute-done.3.refs_3_, ...), custom_call_target="tpu_custom_call" | custom-call | flops 1024 | bytes 1024 | tf_op jit(solution)/shard_map/pallas_call | solution.py:152
  63.3 2.8 %collective-permute-start.11 = (bf16[256,4096]{1,0:T(8,128)(2,1)S(1)}, bf16[256,4096]{1,0:T(8,128)(2,1)S(1)}, u32[]{:S(2)}, u32[]{:S(2)}) collective-permute-start(bf16[256,4096]{1,0:T(8,128)(2,1)S(1)} %shard_map.77.refs_0_), channel_id=1, source_target_pairs={{0,96},{1,13},{2,98},{3,15},{4,100},{5,1},{6,102},{7,3},{8,104},{9... | collective-permute-start | bytes 6291464 | tf_op jit(solution)/shard_map/ppermute | solution.py:301
  66.1 9.8 %shard_map.78 = (bf16[4096,2048]{1,0:T(8,128)(2,1)S(1)}, f32[8,128]{1,0:T(8,128)}) custom-call(s32[5]{0:T(128)S(1)} %stack.23.place_ref, bf16[32,4096]{1,0:T(8,128)(2,1)S(1)} %shard_map.75.own0, bf16[32,4096]{1,0:T(8,128)(2,1)S(1)} %collective-permute-done.own1, bf16[32,4096]{1,0:T(8,128)(2,1)S(1)} %collective-permute-done.7.own2, ...), custom_call_target="tpu_custom_call" | custom-call | flops 10737418240 | bytes 1048576 | tf_op jit(solution)/shard_map/pallas_call | solution.py:383
  75.9 6.8 %shard_map.79 = (f32[64,16,2048]{2,1,0:T(8,128)}, f32[8,128]{1,0:T(8,128)S(1)}) custom-call(s32[5]{0:T(128)S(1)} %stack.23.place_ref, bf16[256,4096]{1,0:T(8,128)(2,1)S(1)} %shard_map.77.refs_0_, bf16[256,4096]{1,0:T(8,128)(2,1)S(1)} %collective-permute-done.10.refs_1_, bf16[4096,2048]{1,0:T(8,128)(2,1)S(1)} %get-tuple-element.19.refs_2_), custom_call_target="tpu_custom_call" | custom-call | flops 6442450944 | bytes 4194304 | tf_op jit(solution)/shard_map/pallas_call | solution.py:275
  82.7 7.4 %collective-permute-done.9.refs_0_ = bf16[256,4096]{1,0:T(8,128)(2,1)S(1)} collective-permute-done((bf16[256,4096]{1,0:T(8,128)(2,1)S(1)}, bf16[256,4096]{1,0:T(8,128)(2,1)S(1)}, u32[]{:S(2)}, u32[]{:S(2)}) %collective-permute-start.9) | collective-permute-done | bytes 2097184 | tf_op jit(solution)/shard_map/ppermute | solution.py:301
  90.6 2.8 %shard_map.82 = (bf16[128,4096]{1,0:T(8,128)(2,1)S(1)}, bf16[128,4096]{1,0:T(8,128)(2,1)S(1)}) custom-call(bf16[256,4096]{1,0:T(8,128)(2,1)S(1)} %shard_map.80.refs_0_, bf16[256,4096]{1,0:T(8,128)(2,1)S(1)} %shard_map.81.refs_1_), custom_call_target="tpu_custom_call" | custom-call | flops 1024 | bytes 1024 | tf_op jit(solution)/shard_map/pallas_call | solution.py:152
  93.5 3.2 %collective-permute-start.16 = (bf16[128,4096]{1,0:T(8,128)(2,1)S(1)}, bf16[128,4096]{1,0:T(8,128)(2,1)S(1)}, u32[]{:S(2)}, u32[]{:S(2)}) collective-permute-start(bf16[128,4096]{1,0:T(8,128)(2,1)S(1)} %get-tuple-element.25), channel_id=1, source_target_pairs={{0,96},{1,13},{2,98},{3,15},{4,100},{5,1},{6,102},{7,3},{8,104},{9... | collective-permute-start | bytes 3145736 | tf_op jit(solution)/shard_map/ppermute | solution.py:301
  96.7 7.4 %shard_map.83 = (f32[64,16,2048]{2,1,0:T(8,128)}, f32[8,128]{1,0:T(8,128)}) custom-call(s32[5]{0:T(128)S(1)} %stack.23.place_ref, bf16[256,4096]{1,0:T(8,128)(2,1)S(1)} %shard_map.80.refs_0_, bf16[256,4096]{1,0:T(8,128)(2,1)S(1)} %shard_map.81.refs_1_, bf16[4096,2048]{1,0:T(8,128)(2,1)S(1)} %get-tuple-element.19.refs_2_, ...), custom_call_target="tpu_custom_call", output_to_operand_aliasing={{0}: (4, {})} | custom-call | flops 6442450944 | bytes 4194304 | tf_op jit(solution)/shard_map/pallas_call | solution.py:275
  104.2 6.8 %shard_map.84 = (f32[64,16,2048]{2,1,0:T(8,128)}, f32[8,128]{1,0:T(8,128)S(1)}) custom-call(s32[5]{0:T(128)S(1)} %stack.23.place_ref, bf16[256,4096]{1,0:T(8,128)(2,1)S(1)} %collective-permute-done.13.refs_0_, bf16[256,4096]{1,0:T(8,128)(2,1)S(1)} %collective-permute-done.14.refs_1_, ...), custom_call_target="tpu_custom_call", output_to_operand_aliasing={{0}: (4, {})} | custom-call | flops 6442450944 | bytes 4194304 | tf_op jit(solution)/shard_map/pallas_call | solution.py:275
  111.7 5.0 %shard_map.87 = (f32[64,16,2048]{2,1,0:T(8,128)}, f32[8,128]{1,0:T(8,128)}) custom-call(s32[5]{0:T(128)S(1)} %stack.23.place_ref, bf16[128,4096]{1,0:T(8,128)(2,1)S(1)} %shard_map.85.refs_0_, bf16[128,4096]{1,0:T(8,128)(2,1)S(1)} %shard_map.86.refs_1_, bf16[4096,2048]{1,0:T(8,128)(2,1)S(1)} %get-tuple-element.19.refs_2_, ...), custom_call_target="tpu_custom_call", output_to_operand_aliasing={{0}: (4, {})} | custom-call | flops 3221225472 | bytes 2097152 | tf_op jit(solution)/shard_map/pallas_call | solution.py:275
  116.7 5.0 %shard_map.88 = (f32[64,16,2048]{2,1,0:T(8,128)}, f32[8,128]{1,0:T(8,128)}) custom-call(s32[5]{0:T(128)S(1)} %stack.23.place_ref, bf16[128,4096]{1,0:T(8,128)(2,1)S(1)} %collective-permute-done.15.refs_0_, bf16[128,4096]{1,0:T(8,128)(2,1)S(1)} %collective-permute-done.17.refs_1_, ...), custom_call_target="tpu_custom_call", output_to_operand_aliasing={{0}: (4, {})} | custom-call | flops 3221225472 | bytes 2097152 | tf_op jit(solution)/shard_map/pallas_call | solution.py:275
  (48 shorter events, 8.5 us)
Async XLA Ops:
  0.0 15.9 %copy-start.2 = (f32[1,1024]{1,0:T(1,128)S(1)}, f32[1,1024]{1,0:T(1,128)}, u32[]{:S(2)}) copy-start(f32[1,1024]{1,0:T(1,128)} %constant.72.clone.taper_hbm) | copy-start | bytes 12292
  0.7 1.0 copy-start.1
  1.7 0.7 copy-start.3
  4.7 25.4 %all-to-all-start = ((bf16[128,2,1152]{2,1,0:T(2,128)(2,1)}), bf16[128,2,1152]{2,1,0:T(2,128)(2,1)S(1)}, u32[]{:S(2)}, u32[]{:S(2)}) async-start(bf16[128,2,1152]{2,1,0:T(2,128)(2,1)} %reshape.17), calls=%async_computation | async-start | bytes 1179648 | tf_op jit(solution)/shard_map/all_to_all | solution.py:343
  15.9 1.6 %copy-start = (bf16[1024,1024]{1,0:T(8,128)(2,1)S(1)}, bf16[1024,1024]{1,0:T(8,128)(2,1)}, u32[]{:S(2)}) copy-start(bf16[1024,1024]{1,0:T(8,128)(2,1)} %constant.71.clone.basis_hbm) | copy-start | bytes 6291460
  32.1 1.6 %collective-permute-start = (bf16[32,4096]{1,0:T(8,128)(2,1)S(1)}, bf16[32,4096]{1,0:T(8,128)(2,1)S(1)}, u32[]{:S(2)}, u32[]{:S(2)}) collective-permute-start(bf16[32,4096]{1,0:T(8,128)(2,1)S(1)} %shard_map.75.own0), channel_id=1, source_target_pairs={{0,1},{1,0},{2,3},{3,2},{4,5},{5,4},{6,7},{7,6},{8,9},{9,8},{10,11... | collective-permute-start | bytes 786440 | tf_op jit(solution)/shard_map/ppermute | solution.py:301
  33.7 7.7 %collective-permute-start.2 = (bf16[32,4096]{1,0:T(8,128)(2,1)S(1)}, bf16[32,4096]{1,0:T(8,128)(2,1)S(1)}, u32[]{:S(2)}, u32[]{:S(2)}) collective-permute-start(bf16[32,4096]{1,0:T(8,128)(2,1)S(1)} %pad_maximum_fusion.refs_0_), channel_id=1, source_target_pairs={{0,4},{1,33},{2,6},{3,35},{4,8},{5,37},{6,10},{7,39},{8,12},{9,41}... | collective-permute-start | bytes 786440 | tf_op jit(solution)/shard_map/ppermute | solution.py:301
  33.8 10.7 %collective-permute-start.1 = (bf16[32,4096]{1,0:T(8,128)(2,1)S(1)}, bf16[32,4096]{1,0:T(8,128)(2,1)S(1)}, u32[]{:S(2)}, u32[]{:S(2)}) collective-permute-start(bf16[32,4096]{1,0:T(8,128)(2,1)S(1)} %pad_maximum_fusion.refs_0_), channel_id=1, source_target_pairs={{0,16},{1,17},{2,18},{3,19},{4,20},{5,21},{6,22},{7,23},{8,24},{9,... | collective-permute-start | bytes 786440 | tf_op jit(solution)/shard_map/ppermute | solution.py:301
  35.6 13.0 %collective-permute-start.7 = (bf16[32,4096]{1,0:T(8,128)(2,1)S(1)}, bf16[32,4096]{1,0:T(8,128)(2,1)S(1)}, u32[]{:S(2)}, u32[]{:S(2)}) collective-permute-start(bf16[32,4096]{1,0:T(8,128)(2,1)S(1)} %pad_maximum_fusion.refs_0_), channel_id=1, source_target_pairs={{0,2},{1,3},{2,0},{3,1},{4,6},{5,7},{6,4},{7,5},{8,10},{9,11},{10,... | collective-permute-start | bytes 786440 | tf_op jit(solution)/shard_map/ppermute | solution.py:301
  45.2 20.9 %copy-start.5 = (f32[1024,128]{1,0:T(8,128)S(1)}, f32[1024,128]{1,0:T(8,128)}, u32[]{:S(2)}) copy-start(f32[1024,128]{1,0:T(8,128)} %constant.73.clone.turn_hbm) | copy-start | bytes 1572868
  45.2 14.6 %collective-permute-start.6 = (bf16[64,4096]{1,0:T(8,128)(2,1)S(1)}, bf16[64,4096]{1,0:T(8,128)(2,1)S(1)}, u32[]{:S(2)}, u32[]{:S(2)}) collective-permute-start(bf16[64,4096]{1,0:T(8,128)(2,1)S(1)} %shard_map.76), channel_id=1, source_target_pairs={{0,4},{1,33},{2,6},{3,35},{4,8},{5,37},{6,10},{7,39},{8,12},{9,41}... | collective-permute-start | bytes 1572872 | tf_op jit(solution)/shard_map/ppermute | solution.py:301
  46.0 9.3 %collective-permute-start.3 = (bf16[32,4096]{1,0:T(8,128)(2,1)S(1)}, bf16[32,4096]{1,0:T(8,128)(2,1)S(1)}, u32[]{:S(2)}, u32[]{:S(2)}) collective-permute-start(bf16[32,4096]{1,0:T(8,128)(2,1)S(1)} %pad_maximum_fusion.refs_0_), channel_id=1, source_target_pairs={{0,12},{1,97},{2,14},{3,99},{4,0},{5,101},{6,2},{7,103},{8,4},{9,1... | collective-permute-start | bytes 786440 | tf_op jit(solution)/shard_map/ppermute | solution.py:301
  48.5 6.7 %collective-permute-start.8 = (bf16[32,4096]{1,0:T(8,128)(2,1)S(1)}, bf16[32,4096]{1,0:T(8,128)(2,1)S(1)}, u32[]{:S(2)}, u32[]{:S(2)}) collective-permute-start(bf16[32,4096]{1,0:T(8,128)(2,1)S(1)} %collective-permute-done.7.own2), channel_id=1, source_target_pairs={{0,1},{1,0},{2,3},{3,2},{4,5},{5,4},{6,7},{7,6},{8,9},{9,8},{10,11... | collective-permute-start | bytes 786440 | tf_op jit(solution)/shard_map/ppermute | solution.py:301
  48.5 11.2 %collective-permute-start.5 = (bf16[32,4096]{1,0:T(8,128)(2,1)S(1)}, bf16[32,4096]{1,0:T(8,128)(2,1)S(1)}, u32[]{:S(2)}, u32[]{:S(2)}) collective-permute-start(bf16[32,4096]{1,0:T(8,128)(2,1)S(1)} %collective-permute-done.1.refs_0_.refs_1_), channel_id=1, source_target_pairs={{0,8},{1,65},{2,10},{3,67},{4,12},{5,69},{6,14},{7,71},{8,0},{9,73... | collective-permute-start | bytes 786440 | tf_op jit(solution)/shard_map/ppermute | solution.py:301
  49.9 9.9 %collective-permute-start.4 = (bf16[32,4096]{1,0:T(8,128)(2,1)S(1)}, bf16[32,4096]{1,0:T(8,128)(2,1)S(1)}, u32[]{:S(2)}, u32[]{:S(2)}) collective-permute-start(bf16[32,4096]{1,0:T(8,128)(2,1)S(1)} %collective-permute-done.1.refs_0_.refs_1_), channel_id=1, source_target_pairs={{0,12},{1,97},{2,14},{3,99},{4,0},{5,101},{6,2},{7,103},{8,4},{9,1... | collective-permute-start | bytes 786440 | tf_op jit(solution)/shard_map/ppermute | solution.py:301
  62.7 13.2 %collective-permute-start.10 = (bf16[256,4096]{1,0:T(8,128)(2,1)S(1)}, bf16[256,4096]{1,0:T(8,128)(2,1)S(1)}, u32[]{:S(2)}, u32[]{:S(2)}) collective-permute-start(bf16[256,4096]{1,0:T(8,128)(2,1)S(1)} %shard_map.77.refs_0_), channel_id=1, source_target_pairs={{0,1},{1,0},{2,3},{3,2},{4,5},{5,4},{6,7},{7,6},{8,9},{9,8},{10,11... | collective-permute-start | bytes 6291464 | tf_op jit(solution)/shard_map/ppermute | solution.py:301
  62.8 27.3 %collective-permute-start.9 = (bf16[256,4096]{1,0:T(8,128)(2,1)S(1)}, bf16[256,4096]{1,0:T(8,128)(2,1)S(1)}, u32[]{:S(2)}, u32[]{:S(2)}) collective-permute-start(bf16[256,4096]{1,0:T(8,128)(2,1)S(1)} %shard_map.77.refs_0_), channel_id=1, source_target_pairs={{0,32},{1,5},{2,34},{3,7},{4,36},{5,9},{6,38},{7,11},{8,40},{9,13}... | collective-permute-start | bytes 6291464 | tf_op jit(solution)/shard_map/ppermute | solution.py:301
  63.3 26.8 %collective-permute-start.11 = (bf16[256,4096]{1,0:T(8,128)(2,1)S(1)}, bf16[256,4096]{1,0:T(8,128)(2,1)S(1)}, u32[]{:S(2)}, u32[]{:S(2)}) collective-permute-start(bf16[256,4096]{1,0:T(8,128)(2,1)S(1)} %shard_map.77.refs_0_), channel_id=1, source_target_pairs={{0,96},{1,13},{2,98},{3,15},{4,100},{5,1},{6,102},{7,3},{8,104},{9... | collective-permute-start | bytes 6291464 | tf_op jit(solution)/shard_map/ppermute | solution.py:301
  90.1 14.1 %collective-permute-start.13 = (bf16[256,4096]{1,0:T(8,128)(2,1)S(1)}, bf16[256,4096]{1,0:T(8,128)(2,1)S(1)}, u32[]{:S(2)}, u32[]{:S(2)}) collective-permute-start(bf16[256,4096]{1,0:T(8,128)(2,1)S(1)} %shard_map.80.refs_0_), channel_id=1, source_target_pairs={{0,1},{1,0},{2,3},{3,2},{4,5},{5,4},{6,7},{7,6},{8,9},{9,8},{10,11... | collective-permute-start | bytes 6291464 | tf_op jit(solution)/shard_map/ppermute | solution.py:301
  90.1 14.1 %collective-permute-start.14 = (bf16[256,4096]{1,0:T(8,128)(2,1)S(1)}, bf16[256,4096]{1,0:T(8,128)(2,1)S(1)}, u32[]{:S(2)}, u32[]{:S(2)}) collective-permute-start(bf16[256,4096]{1,0:T(8,128)(2,1)S(1)} %shard_map.81.refs_1_), channel_id=1, source_target_pairs={{0,1},{1,0},{2,3},{3,2},{4,5},{5,4},{6,7},{7,6},{8,9},{9,8},{10,11... | collective-permute-start | bytes 6291464 | tf_op jit(solution)/shard_map/ppermute | solution.py:301
  93.4 17.6 %collective-permute-start.12 = (bf16[128,4096]{1,0:T(8,128)(2,1)S(1)}, bf16[128,4096]{1,0:T(8,128)(2,1)S(1)}, u32[]{:S(2)}, u32[]{:S(2)}) collective-permute-start(bf16[128,4096]{1,0:T(8,128)(2,1)S(1)} %get-tuple-element.21), channel_id=1, source_target_pairs={{0,32},{1,5},{2,34},{3,7},{4,36},{5,9},{6,38},{7,11},{8,40},{9,13}... | collective-permute-start | bytes 3145736 | tf_op jit(solution)/shard_map/ppermute | solution.py:301
  93.5 17.6 %collective-permute-start.16 = (bf16[128,4096]{1,0:T(8,128)(2,1)S(1)}, bf16[128,4096]{1,0:T(8,128)(2,1)S(1)}, u32[]{:S(2)}, u32[]{:S(2)}) collective-permute-start(bf16[128,4096]{1,0:T(8,128)(2,1)S(1)} %get-tuple-element.25), channel_id=1, source_target_pairs={{0,96},{1,13},{2,98},{3,15},{4,100},{5,1},{6,102},{7,3},{8,104},{9... | collective-permute-start | bytes 3145736 | tf_op jit(solution)/shard_map/ppermute | solution.py:301
  111.1 5.6 %collective-permute-start.15 = (bf16[128,4096]{1,0:T(8,128)(2,1)S(1)}, bf16[128,4096]{1,0:T(8,128)(2,1)S(1)}, u32[]{:S(2)}, u32[]{:S(2)}) collective-permute-start(bf16[128,4096]{1,0:T(8,128)(2,1)S(1)} %shard_map.85.refs_0_), channel_id=1, source_target_pairs={{0,1},{1,0},{2,3},{3,2},{4,5},{5,4},{6,7},{7,6},{8,9},{9,8},{10,11... | collective-permute-start | bytes 3145736 | tf_op jit(solution)/shard_map/ppermute | solution.py:301
  111.2 5.5 %collective-permute-start.17 = (bf16[128,4096]{1,0:T(8,128)(2,1)S(1)}, bf16[128,4096]{1,0:T(8,128)(2,1)S(1)}, u32[]{:S(2)}, u32[]{:S(2)}) collective-permute-start(bf16[128,4096]{1,0:T(8,128)(2,1)S(1)} %shard_map.86.refs_1_), channel_id=1, source_target_pairs={{0,1},{1,0},{2,3},{3,2},{4,5},{5,4},{6,7},{7,6},{8,9},{9,8},{10,11... | collective-permute-start | bytes 3145736 | tf_op jit(solution)/shard_map/ppermute | solution.py:301
  (1 other events, 0.7 us)

commit v5 on v4

--- a/solution.py
+++ b/solution.py
@@ -27,6 +27,7 @@
 DEVICES = 128
 SPEC = WIN * 2 * FREQS
 COLS = CB * LAGS
+SIDE = COLS // NXL
 TAIL = 128
 NT = 512
 TILES = COLS // NT
@@ -135,28 +136,19 @@
 
 
 def group_kernel(moves, n_in, *refs):
-    outs, sem = refs[n_in:-1], refs[-1]
-    copies = [
-        pltpu.make_async_copy(
-            refs[i].at[pl.ds(h * HALF, HALF)], outs[o].at[pl.ds(p * HALF, HALF)], sem.at[n]
-        )
-        for n, (i, h, o, p) in enumerate(moves)
-    ]
-    for c in copies:
-        c.start()
-    for c in copies:
-        c.wait()
+    outs = refs[n_in:]
+    for i, h, o, p in moves:
+        outs[o][p * HALF : (p + 1) * HALF, :] = refs[i][h * HALF : (h + 1) * HALF, :]
 
 
 def grouped(moves, halves, arrays, after):
     return pl.pallas_call(
         functools.partial(group_kernel, moves, len(arrays) + len(after)),
-        in_specs=[ANY] * (len(arrays) + len(after)),
-        out_specs=[ANY] * len(halves),
+        in_specs=[VMEM] * len(arrays) + [ANY] * len(after),
+        out_specs=[VMEM] * len(halves),
         out_shape=[jax.ShapeDtypeStruct((n * HALF, SPEC), BF16) for n in halves],
-        scratch_shapes=[pltpu.SemaphoreType.DMA((len(moves),))],
         compiler_params=pltpu.CompilerParams(vmem_limit_bytes=MIB),
-        cost_estimate=SMALL,
+        cost_estimate=pl.CostEstimate(flops=0, bytes_accessed=2 * MIB, transcendentals=0),
     )(*arrays, *after)
 
 
@@ -176,20 +168,18 @@
     )(value, *after)
 
 
-def rotate_kernel(place_ref, own0, own1, own2, own3, turn_hbm, out_ref, token_ref, turn_ref, whole, turned, expand, sem):
+def rotate_kernel(halves, place_ref, own0, own1, turn_hbm, out_ref, token_ref, turn_ref, whole, turned, expand, sem):
     load = pltpu.make_async_copy(turn_hbm, turn_ref, sem.at[0])
     load.start()
-    col = lax.broadcasted_iota(jnp.int32, (HALF, COLS), 1) // LAGS
-    row = lax.broadcasted_iota(jnp.int32, (HALF, COLS), 0)
-    for g, own in enumerate((own0, own1, own2, own3)):
+    col = lax.broadcasted_iota(jnp.int32, (HALF, SIDE), 1) // LAGS
+    row = lax.broadcasted_iota(jnp.int32, (HALF, SIDE), 0)
+    for g, own in enumerate((own0, own1)):
         whole[g * QC : (g + 1) * QC, :] = own[...]
     for k in range(0, SPEC, FREQS):
         turned[k : k + FREQS, :] = whole[:, k : k + FREQS].T
-    xl, core = place_ref[3], place_ref[4]
-    halves = [(0, 0, 0), (0, 0, 1), (0, 1, 1), (0, 1, 0), (1, 0, 0), (1, 1, 0), (1, 1, 1), (1, 0, 1)]
-    for g, (chip, other, flip) in enumerate(halves):
-        quarter = (1 - xl if chip else xl) * NCORE + (1 - core if other else core)
-        base = quarter * QC + (1 - core if flip else core) * HALF
+    core = place_ref[4]
+    for g, (other, flip) in enumerate(halves):
+        base = (1 - core if other else core) * QC + (1 - core if flip else core) * HALF
         expand[g * HALF : (g + 1) * HALF, :] = jnp.where(col == base + row, 1.0, 0.0).astype(BF16)
     load.wait()
     token_ref[...] = jnp.zeros_like(token_ref)
@@ -202,7 +192,7 @@
         im = pl.ds(pl.multiple_of((w * 2 + 1) * FREQS + k0, step), step)
         cos = turn_ref[pl.ds(k0, step), :]
         sin = turn_ref[pl.ds(FREQS + k0, step), :]
-        for n in range(COLS // 256):
+        for n in range(SIDE // 256):
             a2 = jnp.dot(turned[re, :], expand[:, n * 256 : (n + 1) * 256], preferred_element_type=F32)
             b2 = jnp.dot(turned[im, :], expand[:, n * 256 : (n + 1) * 256], preferred_element_type=F32)
             for h in range(2):
@@ -215,22 +205,38 @@
     lax.fori_loop(0, WIN * per, body, 0)
 
 
+def rotate(place, halves, own0, own1, turn):
+    return pl.pallas_call(
+        functools.partial(rotate_kernel, halves),
+        in_specs=[SMEM, VMEM, VMEM, HBM],
+        out_specs=[VMEM, VMEM],
+        out_shape=[jax.ShapeDtypeStruct((SPEC, SIDE), BF16), TOKEN],
+        scratch_shapes=[
+            pltpu.VMEM((2 * FREQS, 128), F32),
+            pltpu.VMEM((2 * QC, SPEC), BF16),
+            pltpu.VMEM((SPEC, 2 * QC), BF16),
+            pltpu.VMEM((2 * QC, SIDE), BF16),
+            pltpu.SemaphoreType.DMA((1,)),
+        ],
+        compiler_params=pltpu.CompilerParams(vmem_limit_bytes=8 * MIB),
+        cost_estimate=SMALL,
+    )(place, own0, own1, turn)
+
+
 def matmul_kernel(sources, n_in, place_ref, *refs):
-    rot_ref = refs[n_in]
+    rot_refs = refs[n_in : n_in + 2]
     out_ref, token_ref, left, acc, in_sem, out_sem = refs[-6:]
-    z, xh, y, core = place_ref[0], place_ref[1], place_ref[2], place_ref[4]
+    z, xh, y, xl, core = (place_ref[i] for i in range(5))
     loads, begin = [], 0
-    for n, (i, row, _, offsets, _) in enumerate(sources):
-        rows = len(offsets) * HALF
-        loads.append(
-            pltpu.make_async_copy(refs[i].at[pl.ds(row, rows)], left.at[pl.ds(begin, rows)], in_sem.at[n])
-        )
+    for n in range(n_in):
+        rows = refs[n].shape[0]
+        loads.append(pltpu.make_async_copy(refs[n], left.at[pl.ds(begin, rows)], in_sem.at[n]))
         begin += rows
     for c in loads:
         c.start()
     token_ref[...] = jnp.zeros_like(token_ref)
     ids = []
-    for _, _, other, offsets, dq in sources:
+    for other, offsets, dq in sources:
         c = 1 - core if other else core
         for dp, dx in offsets:
             p = lax.rem(jnp.where(c == 0, y, z) + dp + 4, 4)
@@ -241,7 +247,8 @@
         c.wait()
 
     def stores(step):
-        cols = pl.ds(step * NT, NT)
+        chip, part = divmod(step, SIDE // NT)
+        cols = pl.ds(pl.multiple_of((1 - xl if chip else xl) * SIDE + part * NT, NT), NT)
         slot = step % 2
         return [
             pltpu.make_async_copy(acc.at[slot, u], out_ref.at[i, :, cols], out_sem.at[slot, u])
@@ -252,7 +259,9 @@
         if step >= 2:
             for c in stores(step - 2):
                 c.wait()
-        product = jnp.dot(left[...], rot_ref[:, step * NT : (step + 1) * NT], preferred_element_type=F32)
+        chip, part = divmod(step, SIDE // NT)
+        tile = rot_refs[chip][:, part * NT : (part + 1) * NT]
+        product = jnp.dot(left[...], tile, preferred_element_type=F32)
         acc[step % 2] = product.reshape(acc.shape[1:])
         for c in stores(step):
             c.start()
@@ -263,10 +272,10 @@
 
 def matmul(place, carried, rotated, out):
     arrays = [value for value, _, _, _ in carried]
-    sources = [(n, len(at) * HALF if other else 0, other, at, dq) for n, (_, other, at, dq) in enumerate(carried)]
+    sources = [(other, at, dq) for _, other, at, dq in carried]
     rows = sum(len(at) for _, _, at, _ in carried) * HALF
-    operands = [place, *arrays, rotated]
-    in_specs = [SMEM] + [ANY] * len(arrays) + [VMEM]
+    operands = [place, *arrays, *rotated]
+    in_specs = [SMEM] + [ANY] * len(arrays) + [VMEM] * 2
     aliases = {}
     if out is not None:
         aliases = {len(operands): 0}
@@ -285,9 +294,7 @@
         out_shape=[jax.ShapeDtypeStruct((NZ * NXH * NY * 2, HALF, COLS), F32), TOKEN],
         input_output_aliases=aliases,
         compiler_params=pltpu.CompilerParams(vmem_limit_bytes=12 * MIB),
-        cost_estimate=pl.CostEstimate(
-            flops=3 * rows * COLS * SPEC, bytes_accessed=2 * rows * SPEC + 4 * rows * COLS, transcendentals=0
-        ),
+        cost_estimate=SMALL,
     )(*operands)
 
 
@@ -305,8 +312,8 @@
     return permuted(value, lambda z, xh, y, xl, c: (z + d * c, xh, y + d * (1 - c), xl, c))
 
 
-def second(value, d):
-    return permuted(value, lambda z, xh, y, xl, c: (z + d * (1 - c), xh, y + d * c, xl, c))
+def second(value, d, swap=0):
+    return permuted(value, lambda z, xh, y, xl, c: (z + d * (1 - c), xh, y + d * c, xl, c + swap))
 
 
 def across(value):
@@ -368,45 +375,32 @@
     unit = jnp.concatenate([white[:HALF], sib[HALF:]], axis=0)
     beyond = across(unit)
     ahead, behind = first(unit, 1), first(unit, -1)
-    facing = neighbour(unit)
+    opposite = first(unit, 2)
+    near_side, token = rotate(place, [(0, 0), (0, 1), (1, 1), (1, 0)], white, sib, turn)
+    beyond_ahead, beyond_behind, beyond_opposite = first(beyond, 1), first(beyond, -1), first(beyond, 2)
+    (turned,) = grouped([(0, h, 0, h) for h in range(2)], [2], [unit], [ahead, behind, opposite, token])
+    facing = neighbour(turned)
     facing_sib = sibling(facing)
-    two = [(i, h, 0, 2 * i + h) for i in range(2) for h in range(2)]
-    pair = first(grouped(two, [4], [beyond, ahead], [])[0], 1)
-    beyond_behind = first(beyond, -1)
-    beyond_far = first(beyond, 2)
-    arrays = [unit, beyond, ahead, behind, beyond_behind, beyond_far, pair]
-    moves = [(i, h, 0, 8 * h + i) for i in range(6) for h in range(2)]
-    moves += [(6, 2 * i + h, 0, 8 * h + 6 + i) for i in range(2) for h in range(2)]
-    line_at = [(0, 0), (0, 1), (-1, 0), (1, 0), (1, 1), (2, 1), (-1, 1), (-2, 0)]
-    (line,) = grouped(moves, [16], arrays, [facing_sib])
-    up, down = second(line, 1), second(line, -1)
-    rotated, _ = pl.pallas_call(
-        rotate_kernel,
-        in_specs=[SMEM] + [VMEM] * 4 + [HBM],
-        out_specs=[VMEM, VMEM],
-        out_shape=[jax.ShapeDtypeStruct((SPEC, COLS), BF16), TOKEN],
-        scratch_shapes=[
-            pltpu.VMEM((2 * FREQS, 128), F32),
-            pltpu.VMEM((CB, SPEC), BF16),
-            pltpu.VMEM((SPEC, CB), BF16),
-            pltpu.VMEM((CB, COLS), BF16),
-            pltpu.SemaphoreType.DMA((1,)),
-        ],
-        compiler_params=pltpu.CompilerParams(vmem_limit_bytes=8 * MIB),
-        cost_estimate=pl.CostEstimate(flops=2 * CB * SPEC * COLS * 5, bytes_accessed=MIB, transcendentals=0),
-    )(place, white, sib, facing, facing_sib, turn)
-
-    out, done = matmul(place, [(line, False, line_at, 0), (sibling(line), True, line_at, 0)], rotated, None)
-    up, down = gated(up, [done]), gated(down, [done])
-    parts = [[(i, 8 * h + 4 * i + u, i, 4 * h + u) for h in range(2) for u in range(4)] for i in range(2)]
-    turn_up, turn_down = grouped(parts[0] + parts[1], [8, 8], [up, down], [])
-    far_up, far_down = second(turn_up, 1), second(turn_down, -1)
-    out, _ = matmul(place, [(up, False, line_at, -1), (down, False, line_at, 1)], rotated, out)
-    out, done = matmul(place, [(sibling(up), True, line_at, -1), (sibling(down), True, line_at, 1)], rotated, out)
-    far_up, far_down = gated(far_up, [done]), gated(far_down, [done])
-    halves = [(far_up, line_at[:4], -2), (far_down, line_at[4:], 2)]
-    out, _ = matmul(place, [(value, False, at, dq) for value, at, dq in halves], rotated, out)
-    out, _ = matmul(place, [(sibling(value), True, at, dq) for value, at, dq in halves], rotated, out)
+    arrays = [unit, ahead, behind, opposite, beyond, beyond_ahead, beyond_behind, beyond_opposite]
+    line_at = [(0, 0), (-1, 0), (1, 0), (2, 0), (0, 1), (-1, 1), (1, 1), (2, 1)]
+    moves = [(i, h, h, i) for i in range(8) for h in range(2)]
+    moves += [(i, h, h + 2, p) for i, h, _, p in moves]
+    kept, given, later_kept, later_given = grouped(moves, [8] * 4, arrays, [facing])
+    far_side, _ = rotate(place, [(0, 0), (1, 0), (1, 1), (0, 1)], facing, facing_sib, turn)
+    rotated = (near_side, far_side)
+    kept_up, given_down = second(kept, 1), second(given, -1, swap=1)
+    later_kept, later_given = gated(later_kept, [facing_sib]), gated(later_given, [facing_sib])
+    kept_down, given_up = second(later_kept, -1), second(later_given, 1, swap=1)
+
+    def product(out, *carried):
+        return matmul(place, [(value, other, line_at, dq) for value, other, dq in carried], rotated, out)
+
+    out, done = product(None, (kept, False, 0), (sibling(given), True, 0))
+    kept_up, given_down = gated(kept_up, [done]), gated(given_down, [done])
+    kept_far, given_far = second(kept_up, 1), first(given_down, -1)
+    out, _ = product(out, (kept_up, False, -1), (given_down, True, 1))
+    out, _ = product(out, (kept_down, False, 1), (given_up, True, -1))
+    out, _ = product(out, (kept_far, False, -2), (given_far, True, 2))
     return out.reshape(NZ * NXH * NY, QC, COLS)
 
 

time: 123 us -> 106 us (0.86)
  waiting for transfers between devices: 38.5 us -> 20.5 us
  Pallas kernels: 49.8 us -> 45.4 us
  starting transfers between devices: 27.1 us -> 30 us
  local copies, waits for them, and re-layouts: 5.35 us -> 7.79 us
    ppermute x18 -> x17, waiting for transfers between devices: 26.2 us -> 9.17 us  [permuted(): return lax.ppermute(value, ('blk', 'freq'), pairs)]
    pallas_call x3 -> x2, Pallas kernels: 6.39 us -> 0.29 us  [grouped(): pl.pallas_call(functools.partial(group_kernel, moves, len(arrays) + len(a...]
    ppermute x18 -> x17, starting transfers between devices: 15.9 us -> 18.4 us  [permuted(): return lax.ppermute(value, ('blk', 'freq'), pairs)]
    reshape x1, local copies, waits for them, and re-layouts: 0.22 us -> 1.98 us  [local(): arrived = lax.all_to_all(packed.reshape(DEVICES, SLOTS // DEVICES, SAMPLE...]
    pallas_call x1 -> x2, Pallas kernels: 9.78 us -> 11.5 us  [rotate(): pl.pallas_call(functools.partial(rotate_kernel, halves), in_specs=[SMEM,...]
    pallas_call x5 -> x4, Pallas kernels: 31.2 us -> 31.1 us  [matmul(): pl.pallas_call(functools.partial(matmul_kernel, sources, len(arrays)), in...]
  transfers between devices with their start and end apart: 19 -> 18, of which waited for: 7 -> 5; matrix products, arithmetic and copies ran while one was open for 0% -> 0% of each run, Pallas kernels for 32% -> 33%
where the time goes in v5:
time: 106 us; the launch traced here: 105 us
  Pallas kernels  45.4 us (43%)
  starting transfers between devices  30 us (28%)
  waiting for transfers between devices  20.5 us (19%)
  local copies, waits for them, and re-layouts  7.79 us (7%)
  between operations  1.18 us (1%)
    pallas_call x4, Pallas kernels, matmul(): pl.pallas_call(functools.partial(matmul_kernel, sources, len(arrays)), in...  31.1 us
    ppermute x17, starting transfers between devices, permuted(): return lax.ppermute(value, ('blk', 'freq'), pairs)  18.4 us
    all_to_all x1, starting transfers between devices, local(): lax.all_to_all(packed.reshape(DEVICES, SLOTS // DEVICES, SAMPLES + TAIL),...  11.6 us
    pallas_call x2, Pallas kernels, rotate(): pl.pallas_call(functools.partial(rotate_kernel, halves), in_specs=[SMEM,...  11.5 us
    all_to_all x1, waiting for transfers between devices, local(): lax.all_to_all(packed.reshape(DEVICES, SLOTS // DEVICES, SAMPLES + TAIL),...  11.3 us
    ppermute x17, waiting for transfers between devices, permuted(): return lax.ppermute(value, ('blk', 'freq'), pairs)  9.17 us
    unnamed x12, local copies, waits for them, and re-layouts  4.67 us
  transfers between devices with their start and end apart: 18, of which 5 were waited for; matrix products, arithmetic and copies ran while one was open for 0% of the time, Pallas kernels for 33%

profile of v5, /device:TPU:0, one launch (start us, length us, event | category | flops | bytes accessed | tf_op | source)
XLA Modules:
  0.0 104.8 jit_solution(6966882441610555396)
XLA Ops:
  3.7 1.0 reshape.17
  4.8 11.6 %all-to-all-start = ((bf16[128,2,1152]{2,1,0:T(2,128)(2,1)}), bf16[128,2,1152]{2,1,0:T(2,128)(2,1)}, u32[]{:S(2)}, u32[]{:S(2)}) async-start(bf16[128,2,1152]{2,1,0:T(2,128)(2,1)} %reshape.17), calls=%async_computation | async-start | bytes 1179648 | tf_op jit(solution)/shard_map/all_to_all | solution.py:350
  16.4 1.6 %copy-done = bf16[1024,1024]{1,0:T(8,128)(2,1)S(1)} copy-done((bf16[1024,1024]{1,0:T(8,128)(2,1)S(1)}, bf16[1024,1024]{1,0:T(8,128)(2,1)}, u32[]{:S(2)}) %copy-start) | copy-done | bytes 2097176
  19.0 11.3 %all-to-all-done = bf16[128,2,1152]{2,1,0:T(2,128)(2,1)} async-done(((bf16[128,2,1152]{2,1,0:T(2,128)(2,1)}), bf16[128,2,1152]{2,1,0:T(2,128)(2,1)}, u32[]{:S(2)}, u32[]{:S(2)}) %all-to-all-start) | async-done | bytes 589856 | tf_op jit(solution)/shard_map/all_to_all | solution.py:350
  30.3 2.0 %reshape.18.recv_ref = bf16[256,1152]{1,0:T(8,128)(2,1)S(1)} reshape(bf16[128,2,1152]{2,1,0:T(2,128)(2,1)} %all-to-all-done) | data formatting | bytes 1179648 | tf_op jit(solution)/shard_map/reshape | solution.py:356
  32.3 1.7 %shard_map.75.own0 = bf16[32,4096]{1,0:T(8,128)(2,1)S(1)} custom-call(s32[5]{0:T(128)S(1)} %stack.23.place_ref, bf16[256,1152]{1,0:T(8,128)(2,1)S(1)} %reshape.18.recv_ref, bf16[1024,1024]{1,0:T(8,128)(2,1)S(1)} %get-tuple-element.19.basis_ref, f32[1,1024]{1,0:T(1,128)S(1)} %get-tuple-element.20.taper_ref), custom_call_target="tpu_custom_call" | custom-call | tf_op jit(solution)/shard_map/pallas_call | solution.py:366
  34.1 1.5 %collective-permute-done.own1 = bf16[32,4096]{1,0:T(8,128)(2,1)S(1)} collective-permute-done((bf16[32,4096]{1,0:T(8,128)(2,1)S(1)}, bf16[32,4096]{1,0:T(8,128)(2,1)S(1)}, u32[]{:S(2)}, u32[]{:S(2)}) %collective-permute-start) | collective-permute-done | bytes 262176 | tf_op jit(solution)/shard_map/ppermute | solution.py:308
  35.6 1.2 %collective-permute-start.4 = (bf16[32,4096]{1,0:T(8,128)(2,1)S(1)}, bf16[32,4096]{1,0:T(8,128)(2,1)S(1)}, u32[]{:S(2)}, u32[]{:S(2)}) collective-permute-start(bf16[32,4096]{1,0:T(8,128)(2,1)S(1)} %pad_maximum_fusion.refs_0_), channel_id=1, source_target_pairs={{0,16},{1,17},{2,18},{3,19},{4,20},{5,21},{6,22},{7,23},{8,24},{9,... | collective-permute-start | bytes 786440 | tf_op jit(solution)/shard_map/ppermute | solution.py:308
  37.7 2.5 %collective-permute-start.2 = (bf16[32,4096]{1,0:T(8,128)(2,1)S(1)}, bf16[32,4096]{1,0:T(8,128)(2,1)S(1)}, u32[]{:S(2)}, u32[]{:S(2)}) collective-permute-start(bf16[32,4096]{1,0:T(8,128)(2,1)S(1)} %pad_maximum_fusion.refs_0_), channel_id=1, source_target_pairs={{0,12},{1,97},{2,14},{3,99},{4,0},{5,101},{6,2},{7,103},{8,4},{9,1... | collective-permute-start | bytes 786440 | tf_op jit(solution)/shard_map/ppermute | solution.py:308
  40.2 5.8 %shard_map.76 = (bf16[4096,1024]{1,0:T(8,128)(2,1)S(1)}, f32[8,128]{1,0:T(8,128)S(1)}) custom-call(s32[5]{0:T(128)S(1)} %stack.23.place_ref, bf16[32,4096]{1,0:T(8,128)(2,1)S(1)} %shard_map.75.own0, bf16[32,4096]{1,0:T(8,128)(2,1)S(1)} %collective-permute-done.own1, f32[1024,128]{1,0:T(8,128)S(1)} %copy-done.1), custom_call_target="tpu_custom_call" | custom-call | flops 1024 | bytes 1024 | tf_op jit(solution)/shard_map/pallas_call | solution.py:209
  46.0 2.3 %collective-permute-start.7 = (bf16[32,4096]{1,0:T(8,128)(2,1)S(1)}, bf16[32,4096]{1,0:T(8,128)(2,1)S(1)}, u32[]{:S(2)}, u32[]{:S(2)}) collective-permute-start(bf16[32,4096]{1,0:T(8,128)(2,1)S(1)} %collective-permute-done.4.refs_4_), channel_id=1, source_target_pairs={{0,8},{1,65},{2,10},{3,67},{4,12},{5,69},{6,14},{7,71},{8,0},{9,73... | collective-permute-start | bytes 786440 | tf_op jit(solution)/shard_map/ppermute | solution.py:308
  48.3 1.1 %collective-permute-start.6 = (bf16[32,4096]{1,0:T(8,128)(2,1)S(1)}, bf16[32,4096]{1,0:T(8,128)(2,1)S(1)}, u32[]{:S(2)}, u32[]{:S(2)}) collective-permute-start(bf16[32,4096]{1,0:T(8,128)(2,1)S(1)} %collective-permute-done.4.refs_4_), channel_id=1, source_target_pairs={{0,12},{1,97},{2,14},{3,99},{4,0},{5,101},{6,2},{7,103},{8,4},{9,1... | collective-permute-start | bytes 786440 | tf_op jit(solution)/shard_map/ppermute | solution.py:308
  50.9 3.1 %collective-permute-done.7.refs_7_ = bf16[32,4096]{1,0:T(8,128)(2,1)S(1)} collective-permute-done((bf16[32,4096]{1,0:T(8,128)(2,1)S(1)}, bf16[32,4096]{1,0:T(8,128)(2,1)S(1)}, u32[]{:S(2)}, u32[]{:S(2)}) %collective-permute-start.7) | collective-permute-done | bytes 262176 | tf_op jit(solution)/shard_map/ppermute | solution.py:308
  53.9 3.4 %collective-permute-done.6.refs_6_ = bf16[32,4096]{1,0:T(8,128)(2,1)S(1)} collective-permute-done((bf16[32,4096]{1,0:T(8,128)(2,1)S(1)}, bf16[32,4096]{1,0:T(8,128)(2,1)S(1)}, u32[]{:S(2)}, u32[]{:S(2)}) %collective-permute-start.6) | collective-permute-done | bytes 262176 | tf_op jit(solution)/shard_map/ppermute | solution.py:308
  57.7 1.6 %collective-permute-start.9 = (bf16[128,4096]{1,0:T(8,128)(2,1)S(1)}, bf16[128,4096]{1,0:T(8,128)(2,1)S(1)}, u32[]{:S(2)}, u32[]{:S(2)}) collective-permute-start(bf16[128,4096]{1,0:T(8,128)(2,1)S(1)} %get-tuple-element.22.refs_0_), channel_id=1, source_target_pairs={{0,32},{1,5},{2,34},{3,7},{4,36},{5,9},{6,38},{7,11},{8,40},{9,13}... | collective-permute-start | bytes 3145736 | tf_op jit(solution)/shard_map/ppermute | solution.py:308
  59.3 1.1 %collective-permute-start.13 = (bf16[128,4096]{1,0:T(8,128)(2,1)S(1)}, bf16[128,4096]{1,0:T(8,128)(2,1)S(1)}, u32[]{:S(2)}, u32[]{:S(2)}) collective-permute-start(bf16[128,4096]{1,0:T(8,128)(2,1)S(1)} %get-tuple-element.23), channel_id=1, source_target_pairs={{0,97},{1,12},{2,99},{3,14},{4,101},{5,0},{6,103},{7,2},{8,105},{9... | collective-permute-start | bytes 3145736 | tf_op jit(solution)/shard_map/ppermute | solution.py:308
  61.1 1.2 %collective-permute-done.11.own1.refs_1_ = bf16[32,4096]{1,0:T(8,128)(2,1)S(1)} collective-permute-done((bf16[32,4096]{1,0:T(8,128)(2,1)S(1)}, bf16[32,4096]{1,0:T(8,128)(2,1)S(1)}, u32[]{:S(2)}, u32[]{:S(2)}) %collective-permute-start.11) | collective-permute-done | bytes 262176 | tf_op jit(solution)/shard_map/ppermute | solution.py:308
  62.4 3.2 %collective-permute-start.15 = (bf16[128,4096]{1,0:T(8,128)(2,1)S(1)}, bf16[128,4096]{1,0:T(8,128)(2,1)S(1)}, u32[]{:S(2)}, u32[]{:S(2)}) collective-permute-start(bf16[128,4096]{1,0:T(8,128)(2,1)S(1)} %shard_map.83), channel_id=1, source_target_pairs={{0,96},{1,13},{2,98},{3,15},{4,100},{5,1},{6,102},{7,3},{8,104},{9... | collective-permute-start | bytes 3145736 | tf_op jit(solution)/shard_map/ppermute | solution.py:308
  65.5 5.7 %shard_map.79 = (bf16[4096,1024]{1,0:T(8,128)(2,1)S(1)}, f32[8,128]{1,0:T(8,128)}) custom-call(s32[5]{0:T(128)S(1)} %stack.23.place_ref, bf16[32,4096]{1,0:T(8,128)(2,1)S(1)} %collective-permute-done.8.refs_8_.own0, bf16[32,4096]{1,0:T(8,128)(2,1)S(1)} %collective-permute-done.11.own1.refs_1_, f32[1024,128]{1,0:T(8,128)S(1)} %copy-done.1), custom_call_target="tpu_custom_call" | custom-call | flops 1024 | bytes 1024 | tf_op jit(solution)/shard_map/pallas_call | solution.py:209
  71.3 7.3 %shard_map.80 = (f32[64,16,2048]{2,1,0:T(8,128)}, f32[8,128]{1,0:T(8,128)S(1)}) custom-call(s32[5]{0:T(128)S(1)} %stack.23.place_ref, bf16[128,4096]{1,0:T(8,128)(2,1)S(1)} %get-tuple-element.22.refs_0_, bf16[128,4096]{1,0:T(8,128)(2,1)S(1)} %collective-permute-done.10.refs_1_, bf16[4096,1024]{1,0:T(8,128)(2,1)S(1)} %get-tuple-element.24.refs_2_, ...), custom_call_target="tpu_custom_call" | custom-call | flops 1024 | bytes 1024 | tf_op jit(solution)/shard_map/pallas_call | solution.py:284
  78.7 2.1 %collective-permute-start.14 = (bf16[128,4096]{1,0:T(8,128)(2,1)S(1)}, bf16[128,4096]{1,0:T(8,128)(2,1)S(1)}, u32[]{:S(2)}, u32[]{:S(2)}) collective-permute-start(bf16[128,4096]{1,0:T(8,128)(2,1)S(1)} %shard_map.82.refs_1_), channel_id=1, source_target_pairs={{0,12},{1,97},{2,14},{3,99},{4,0},{5,101},{6,2},{7,103},{8,4},{9,1... | collective-permute-start | bytes 3145736 | tf_op jit(solution)/shard_map/ppermute | solution.py:308
  80.8 7.9 %shard_map.85 = (f32[64,16,2048]{2,1,0:T(8,128)}, f32[8,128]{1,0:T(8,128)}) custom-call(s32[5]{0:T(128)S(1)} %stack.23.place_ref, bf16[128,4096]{1,0:T(8,128)(2,1)S(1)} %shard_map.81.refs_0_, bf16[128,4096]{1,0:T(8,128)(2,1)S(1)} %shard_map.82.refs_1_, bf16[4096,1024]{1,0:T(8,128)(2,1)S(1)} %get-tuple-element.24.refs_2_, ...), custom_call_target="tpu_custom_call", output_to_operand_aliasing={{0}: (5, {})} | custom-call | flops 1024 | bytes 1024 | tf_op jit(solution)/shard_map/pallas_call | solution.py:284
  88.8 7.9 %shard_map.86 = (f32[64,16,2048]{2,1,0:T(8,128)}, f32[8,128]{1,0:T(8,128)}) custom-call(s32[5]{0:T(128)S(1)} %stack.23.place_ref, bf16[128,4096]{1,0:T(8,128)(2,1)S(1)} %collective-permute-done.15.refs_0_, bf16[128,4096]{1,0:T(8,128)(2,1)S(1)} %collective-permute-done.16.refs_1_, ...), custom_call_target="tpu_custom_call", output_to_operand_aliasing={{0}: (5, {})} | custom-call | flops 1024 | bytes 1024 | tf_op jit(solution)/shard_map/pallas_call | solution.py:284
  96.7 7.9 %shard_map.87 = (f32[64,16,2048]{2,1,0:T(8,128)}, f32[8,128]{1,0:T(8,128)}) custom-call(s32[5]{0:T(128)S(1)} %stack.23.place_ref, bf16[128,4096]{1,0:T(8,128)(2,1)S(1)} %collective-permute-done.12.refs_0_, bf16[128,4096]{1,0:T(8,128)(2,1)S(1)} %collective-permute-done.14.refs_1_, ...), custom_call_target="tpu_custom_call", output_to_operand_aliasing={{0}: (5, {})} | custom-call | flops 1024 | bytes 1024 | tf_op jit(solution)/shard_map/pallas_call | solution.py:284
  (45 shorter events, 7.7 us)
Async XLA Ops:
  0.0 40.2 %copy-start.1 = (f32[1024,128]{1,0:T(8,128)S(1)}, f32[1024,128]{1,0:T(8,128)}, u32[]{:S(2)}) copy-start(f32[1024,128]{1,0:T(8,128)} %constant.73.clone.turn_hbm) | copy-start | bytes 1572868
  0.7 1.0 copy-start.2
  1.8 0.7 copy-start.4
  2.4 0.7 copy-start.5
  4.8 25.5 %all-to-all-start = ((bf16[128,2,1152]{2,1,0:T(2,128)(2,1)}), bf16[128,2,1152]{2,1,0:T(2,128)(2,1)}, u32[]{:S(2)}, u32[]{:S(2)}) async-start(bf16[128,2,1152]{2,1,0:T(2,128)(2,1)} %reshape.17), calls=%async_computation | async-start | bytes 1179648 | tf_op jit(solution)/shard_map/all_to_all | solution.py:350
  16.4 1.6 %copy-start = (bf16[1024,1024]{1,0:T(8,128)(2,1)S(1)}, bf16[1024,1024]{1,0:T(8,128)(2,1)}, u32[]{:S(2)}) copy-start(bf16[1024,1024]{1,0:T(8,128)(2,1)} %constant.71.clone.basis_hbm) | copy-start | bytes 6291460
  18.0 0.7 copy-start.3
  34.0 1.6 %collective-permute-start = (bf16[32,4096]{1,0:T(8,128)(2,1)S(1)}, bf16[32,4096]{1,0:T(8,128)(2,1)S(1)}, u32[]{:S(2)}, u32[]{:S(2)}) collective-permute-start(bf16[32,4096]{1,0:T(8,128)(2,1)S(1)} %shard_map.75.own0), channel_id=1, source_target_pairs={{0,1},{1,0},{2,3},{3,2},{4,5},{5,4},{6,7},{7,6},{8,9},{9,8},{10,11... | collective-permute-start | bytes 786440 | tf_op jit(solution)/shard_map/ppermute | solution.py:308
  35.6 10.3 %collective-permute-start.4 = (bf16[32,4096]{1,0:T(8,128)(2,1)S(1)}, bf16[32,4096]{1,0:T(8,128)(2,1)S(1)}, u32[]{:S(2)}, u32[]{:S(2)}) collective-permute-start(bf16[32,4096]{1,0:T(8,128)(2,1)S(1)} %pad_maximum_fusion.refs_0_), channel_id=1, source_target_pairs={{0,16},{1,17},{2,18},{3,19},{4,20},{5,21},{6,22},{7,23},{8,24},{9,... | collective-permute-start | bytes 786440 | tf_op jit(solution)/shard_map/ppermute | solution.py:308
  36.8 12.5 %collective-permute-start.3 = (bf16[32,4096]{1,0:T(8,128)(2,1)S(1)}, bf16[32,4096]{1,0:T(8,128)(2,1)S(1)}, u32[]{:S(2)}, u32[]{:S(2)}) collective-permute-start(bf16[32,4096]{1,0:T(8,128)(2,1)S(1)} %pad_maximum_fusion.refs_0_), channel_id=1, source_target_pairs={{0,8},{1,65},{2,10},{3,67},{4,12},{5,69},{6,14},{7,71},{8,0},{9,73... | collective-permute-start | bytes 786440 | tf_op jit(solution)/shard_map/ppermute | solution.py:308
  37.7 12.6 %collective-permute-start.2 = (bf16[32,4096]{1,0:T(8,128)(2,1)S(1)}, bf16[32,4096]{1,0:T(8,128)(2,1)S(1)}, u32[]{:S(2)}, u32[]{:S(2)}) collective-permute-start(bf16[32,4096]{1,0:T(8,128)(2,1)S(1)} %pad_maximum_fusion.refs_0_), channel_id=1, source_target_pairs={{0,12},{1,97},{2,14},{3,99},{4,0},{5,101},{6,2},{7,103},{8,4},{9,1... | collective-permute-start | bytes 786440 | tf_op jit(solution)/shard_map/ppermute | solution.py:308
  40.1 10.2 %collective-permute-start.1 = (bf16[32,4096]{1,0:T(8,128)(2,1)S(1)}, bf16[32,4096]{1,0:T(8,128)(2,1)S(1)}, u32[]{:S(2)}, u32[]{:S(2)}) collective-permute-start(bf16[32,4096]{1,0:T(8,128)(2,1)S(1)} %pad_maximum_fusion.refs_0_), channel_id=1, source_target_pairs={{0,4},{1,33},{2,6},{3,35},{4,8},{5,37},{6,10},{7,39},{8,12},{9,41}... | collective-permute-start | bytes 786440 | tf_op jit(solution)/shard_map/ppermute | solution.py:308
  46.0 8.0 %collective-permute-start.7 = (bf16[32,4096]{1,0:T(8,128)(2,1)S(1)}, bf16[32,4096]{1,0:T(8,128)(2,1)S(1)}, u32[]{:S(2)}, u32[]{:S(2)}) collective-permute-start(bf16[32,4096]{1,0:T(8,128)(2,1)S(1)} %collective-permute-done.4.refs_4_), channel_id=1, source_target_pairs={{0,8},{1,65},{2,10},{3,67},{4,12},{5,69},{6,14},{7,71},{8,0},{9,73... | collective-permute-start | bytes 786440 | tf_op jit(solution)/shard_map/ppermute | solution.py:308
  48.3 9.0 %collective-permute-start.6 = (bf16[32,4096]{1,0:T(8,128)(2,1)S(1)}, bf16[32,4096]{1,0:T(8,128)(2,1)S(1)}, u32[]{:S(2)}, u32[]{:S(2)}) collective-permute-start(bf16[32,4096]{1,0:T(8,128)(2,1)S(1)} %collective-permute-done.4.refs_4_), channel_id=1, source_target_pairs={{0,12},{1,97},{2,14},{3,99},{4,0},{5,101},{6,2},{7,103},{8,4},{9,1... | collective-permute-start | bytes 786440 | tf_op jit(solution)/shard_map/ppermute | solution.py:308
  49.4 8.0 %collective-permute-start.5 = (bf16[32,4096]{1,0:T(8,128)(2,1)S(1)}, bf16[32,4096]{1,0:T(8,128)(2,1)S(1)}, u32[]{:S(2)}, u32[]{:S(2)}) collective-permute-start(bf16[32,4096]{1,0:T(8,128)(2,1)S(1)} %collective-permute-done.4.refs_4_), channel_id=1, source_target_pairs={{0,4},{1,33},{2,6},{3,35},{4,8},{5,37},{6,10},{7,39},{8,12},{9,41}... | collective-permute-start | bytes 786440 | tf_op jit(solution)/shard_map/ppermute | solution.py:308
  50.3 7.0 %collective-permute-start.8 = (bf16[32,4096]{1,0:T(8,128)(2,1)S(1)}, bf16[32,4096]{1,0:T(8,128)(2,1)S(1)}, u32[]{:S(2)}, u32[]{:S(2)}) collective-permute-start(bf16[32,4096]{1,0:T(8,128)(2,1)S(1)} %shard_map.77), channel_id=1, source_target_pairs={{0,2},{1,3},{2,0},{3,1},{4,6},{5,7},{6,4},{7,5},{8,10},{9,11},{10,... | collective-permute-start | bytes 786440 | tf_op jit(solution)/shard_map/ppermute | solution.py:308
  57.6 13.7 %collective-permute-start.10 = (bf16[128,4096]{1,0:T(8,128)(2,1)S(1)}, bf16[128,4096]{1,0:T(8,128)(2,1)S(1)}, u32[]{:S(2)}, u32[]{:S(2)}) collective-permute-start(bf16[128,4096]{1,0:T(8,128)(2,1)S(1)} %get-tuple-element.23), channel_id=1, source_target_pairs={{0,1},{1,0},{2,3},{3,2},{4,5},{5,4},{6,7},{7,6},{8,9},{9,8},{10,11... | collective-permute-start | bytes 3145736 | tf_op jit(solution)/shard_map/ppermute | solution.py:308
  57.7 20.9 %collective-permute-start.9 = (bf16[128,4096]{1,0:T(8,128)(2,1)S(1)}, bf16[128,4096]{1,0:T(8,128)(2,1)S(1)}, u32[]{:S(2)}, u32[]{:S(2)}) collective-permute-start(bf16[128,4096]{1,0:T(8,128)(2,1)S(1)} %get-tuple-element.22.refs_0_), channel_id=1, source_target_pairs={{0,32},{1,5},{2,34},{3,7},{4,36},{5,9},{6,38},{7,11},{8,40},{9,13}... | collective-permute-start | bytes 3145736 | tf_op jit(solution)/shard_map/ppermute | solution.py:308
  59.3 19.4 %collective-permute-start.13 = (bf16[128,4096]{1,0:T(8,128)(2,1)S(1)}, bf16[128,4096]{1,0:T(8,128)(2,1)S(1)}, u32[]{:S(2)}, u32[]{:S(2)}) collective-permute-start(bf16[128,4096]{1,0:T(8,128)(2,1)S(1)} %get-tuple-element.23), channel_id=1, source_target_pairs={{0,97},{1,12},{2,99},{3,14},{4,101},{5,0},{6,103},{7,2},{8,105},{9... | collective-permute-start | bytes 3145736 | tf_op jit(solution)/shard_map/ppermute | solution.py:308
  60.4 1.9 %collective-permute-start.11 = (bf16[32,4096]{1,0:T(8,128)(2,1)S(1)}, bf16[32,4096]{1,0:T(8,128)(2,1)S(1)}, u32[]{:S(2)}, u32[]{:S(2)}) collective-permute-start(bf16[32,4096]{1,0:T(8,128)(2,1)S(1)} %collective-permute-done.8.refs_8_.own0), channel_id=1, source_target_pairs={{0,1},{1,0},{2,3},{3,2},{4,5},{5,4},{6,7},{7,6},{8,9},{9,8},{10,11... | collective-permute-start | bytes 786440 | tf_op jit(solution)/shard_map/ppermute | solution.py:308
  62.3 26.4 %collective-permute-start.16 = (bf16[128,4096]{1,0:T(8,128)(2,1)S(1)}, bf16[128,4096]{1,0:T(8,128)(2,1)S(1)}, u32[]{:S(2)}, u32[]{:S(2)}) collective-permute-start(bf16[128,4096]{1,0:T(8,128)(2,1)S(1)} %shard_map.84), channel_id=1, source_target_pairs={{0,33},{1,4},{2,35},{3,6},{4,37},{5,8},{6,39},{7,10},{8,41},{9,12}... | collective-permute-start | bytes 3145736 | tf_op jit(solution)/shard_map/ppermute | solution.py:308
  62.4 26.4 %collective-permute-start.15 = (bf16[128,4096]{1,0:T(8,128)(2,1)S(1)}, bf16[128,4096]{1,0:T(8,128)(2,1)S(1)}, u32[]{:S(2)}, u32[]{:S(2)}) collective-permute-start(bf16[128,4096]{1,0:T(8,128)(2,1)S(1)} %shard_map.83), channel_id=1, source_target_pairs={{0,96},{1,13},{2,98},{3,15},{4,100},{5,1},{6,102},{7,3},{8,104},{9... | collective-permute-start | bytes 3145736 | tf_op jit(solution)/shard_map/ppermute | solution.py:308
  78.6 18.1 %collective-permute-start.12 = (bf16[128,4096]{1,0:T(8,128)(2,1)S(1)}, bf16[128,4096]{1,0:T(8,128)(2,1)S(1)}, u32[]{:S(2)}, u32[]{:S(2)}) collective-permute-start(bf16[128,4096]{1,0:T(8,128)(2,1)S(1)} %shard_map.81.refs_0_), channel_id=1, source_target_pairs={{0,32},{1,5},{2,34},{3,7},{4,36},{5,9},{6,38},{7,11},{8,40},{9,13}... | collective-permute-start | bytes 3145736 | tf_op jit(solution)/shard_map/ppermute | solution.py:308
  78.7 18.0 %collective-permute-start.14 = (bf16[128,4096]{1,0:T(8,128)(2,1)S(1)}, bf16[128,4096]{1,0:T(8,128)(2,1)S(1)}, u32[]{:S(2)}, u32[]{:S(2)}) collective-permute-start(bf16[128,4096]{1,0:T(8,128)(2,1)S(1)} %shard_map.82.refs_1_), channel_id=1, source_target_pairs={{0,12},{1,97},{2,14},{3,99},{4,0},{5,101},{6,2},{7,103},{8,4},{9,1... | collective-permute-start | bytes 3145736 | tf_op jit(solution)/shard_map/ppermute | solution.py:308

commit v6 on v5

--- a/solution.py
+++ b/solution.py
@@ -12,6 +12,7 @@
 
 SAMPLES = 1024
 FREQS = 512
+FINE = 64
 LAGS = 16
 HALFWIN = 64
 WIN = 4
@@ -29,7 +30,7 @@
 COLS = CB * LAGS
 SIDE = COLS // NXL
 TAIL = 128
-NT = 512
+NT = 1024
 TILES = COLS // NT
 GROUP = 4
 F32, BF16 = jnp.float32, jnp.bfloat16
@@ -48,11 +49,12 @@
     angle = 2.0 * math.pi / SAMPLES * ((n * k) % SAMPLES)
     basis = np.concatenate([np.cos(angle), -np.sin(angle)], axis=1).astype(ml_dtypes.bfloat16)
     taper = (0.5 - 0.5 * np.cos(2.0 * math.pi / SAMPLES * (n[:, 0] + 0.5)))[None, :].astype(np.float32)
-    pos = np.arange(FREQS)[:, None]
     lag = np.arange(128)[None, :] % LAGS - LAGS // 2
-    phi = 2.0 * math.pi / SAMPLES * ((lag * pos) % SAMPLES)
-    gain = np.where(pos == 0, 1.0, 2.0) / math.sqrt(2.0 * WIN * FREQS)
-    turn = np.concatenate([gain * np.cos(phi), gain * np.sin(phi)], axis=0).astype(np.float32)
+    coarse = 2.0 * math.pi / SAMPLES * ((lag * FINE * np.arange(FREQS // FINE)[:, None]) % SAMPLES)
+    fine = 2.0 * math.pi / SAMPLES * ((lag * np.arange(FINE)[:, None]) % SAMPLES)
+    gain = 2.0 / math.sqrt(2.0 * WIN * FREQS)
+    turn = np.concatenate([np.cos(coarse), np.sin(coarse), gain * np.cos(fine), gain * np.sin(fine)], axis=0)
+    turn = turn.astype(np.float32)
     return basis, taper, turn
 
 
@@ -60,17 +62,9 @@
     return lax.broadcasted_iota(jnp.int32, (size, size), 0) == lax.broadcasted_iota(jnp.int32, (size, size), 1)
 
 
-def pack_kernel(count_ref, chan_hbm, win_hbm, raw_hbm, out_ref, chan_ref, win_ref, raw_ref, sem):
-    loads = [
-        pltpu.make_async_copy(chan_hbm, chan_ref, sem.at[0]),
-        pltpu.make_async_copy(win_hbm, win_ref, sem.at[1]),
-        pltpu.make_async_copy(raw_hbm, raw_ref, sem.at[2]),
-    ]
-    for c in loads:
-        c.start()
-    loads[0].wait()
-    loads[1].wait()
-    chan = chan_ref[...]
+def pack_kernel(count_ref, key_ref, raw_ref, out_ref):
+    key = key_ref[...]
+    chan = key // WIN
     slot = lax.broadcasted_iota(jnp.int32, (1, SLOTS), 1)
     live = slot < count_ref[0]
     owner = jnp.where(live, chan // QC, -1).astype(F32)
@@ -81,18 +75,18 @@
     rank = jnp.sum(earlier, axis=0, keepdims=True)
     flat = jnp.where(live, owner * 2.0 + rank, -1.0)
     pick = jnp.where(flat == row.astype(F32), 1.0, 0.0)
-    place = (win_ref[...] * QC + chan % QC + 1).astype(F32)
+    place = (key % WIN * QC + chan % QC + 1).astype(F32)
     place_col = jnp.sum(pick * place, axis=1, keepdims=True)
     out_ref[:, SAMPLES:] = jnp.broadcast_to(place_col, (SLOTS, TAIL)).astype(BF16)
-    loads[2].wait()
     out_ref[:, :SAMPLES] = jnp.dot(pick.astype(BF16), raw_ref[...], preferred_element_type=F32).astype(BF16)
 
 
-def fetch_kernel(after_hbm, basis_hbm, taper_hbm, basis_ref, taper_ref, sem):
+def fetch_kernel(after_hbm, basis_hbm, taper_hbm, turn_hbm, basis_ref, taper_ref, turn_ref, sem):
     del after_hbm
     loads = [
         pltpu.make_async_copy(basis_hbm, basis_ref, sem.at[0]),
         pltpu.make_async_copy(taper_hbm, taper_ref, sem.at[1]),
+        pltpu.make_async_copy(turn_hbm, turn_ref, sem.at[2]),
     ]
     for c in loads:
         c.start()
@@ -168,9 +162,7 @@
     )(value, *after)
 
 
-def rotate_kernel(halves, place_ref, own0, own1, turn_hbm, out_ref, token_ref, turn_ref, whole, turned, expand, sem):
-    load = pltpu.make_async_copy(turn_hbm, turn_ref, sem.at[0])
-    load.start()
+def rotate_kernel(halves, place_ref, own0, own1, small_ref, out_ref, token_ref, turn_ref, whole, turned, expand):
     col = lax.broadcasted_iota(jnp.int32, (HALF, SIDE), 1) // LAGS
     row = lax.broadcasted_iota(jnp.int32, (HALF, SIDE), 0)
     for g, own in enumerate((own0, own1)):
@@ -181,7 +173,15 @@
     for g, (other, flip) in enumerate(halves):
         base = (1 - core if other else core) * QC + (1 - core if flip else core) * HALF
         expand[g * HALF : (g + 1) * HALF, :] = jnp.where(col == base + row, 1.0, 0.0).astype(BF16)
-    load.wait()
+    many = FREQS // FINE
+    fine_cos = small_ref[2 * many : 2 * many + FINE, :]
+    fine_sin = small_ref[2 * many + FINE :, :]
+    first_half = jnp.where(lax.broadcasted_iota(jnp.int32, (FINE, 128), 0) == 0, 0.5, 1.0)
+    for a in range(many):
+        cos, sin = small_ref[a : a + 1, :], small_ref[many + a : many + a + 1, :]
+        weight = first_half if a == 0 else 1.0
+        turn_ref[a * FINE : (a + 1) * FINE, :] = (cos * fine_cos - sin * fine_sin) * weight
+        turn_ref[FREQS + a * FINE : FREQS + (a + 1) * FINE, :] = (sin * fine_cos + cos * fine_sin) * weight
     token_ref[...] = jnp.zeros_like(token_ref)
     step = 256
     per = FREQS // step
@@ -208,7 +208,7 @@
 def rotate(place, halves, own0, own1, turn):
     return pl.pallas_call(
         functools.partial(rotate_kernel, halves),
-        in_specs=[SMEM, VMEM, VMEM, HBM],
+        in_specs=[SMEM, VMEM, VMEM, VMEM],
         out_specs=[VMEM, VMEM],
         out_shape=[jax.ShapeDtypeStruct((SPEC, SIDE), BF16), TOKEN],
         scratch_shapes=[
@@ -216,7 +216,6 @@
             pltpu.VMEM((2 * QC, SPEC), BF16),
             pltpu.VMEM((SPEC, 2 * QC), BF16),
             pltpu.VMEM((2 * QC, SIDE), BF16),
-            pltpu.SemaphoreType.DMA((1,)),
         ],
         compiler_params=pltpu.CompilerParams(vmem_limit_bytes=8 * MIB),
         cost_estimate=SMALL,
@@ -336,17 +335,11 @@
 
     packed = pl.pallas_call(
         pack_kernel,
-        in_specs=[SMEM, HBM, HBM, HBM],
+        in_specs=[SMEM, VMEM, VMEM],
         out_specs=VMEM,
         out_shape=jax.ShapeDtypeStruct((SLOTS, SAMPLES + TAIL), BF16),
-        scratch_shapes=[
-            pltpu.VMEM((1, SLOTS), jnp.int32),
-            pltpu.VMEM((1, SLOTS), jnp.int32),
-            pltpu.VMEM((SLOTS, SAMPLES), BF16),
-            pltpu.SemaphoreType.DMA((3,)),
-        ],
         compiler_params=pltpu.CompilerParams(vmem_limit_bytes=8 * MIB),
-    )(file_count, seg_chan.reshape(1, SLOTS), seg_win.reshape(1, SLOTS), raw)
+    )(file_count, (seg_chan * WIN + seg_win).reshape(1, SLOTS), raw)
     arrived = lax.all_to_all(
         packed.reshape(DEVICES, SLOTS // DEVICES, SAMPLES + TAIL),
         ("blk", "freq"),
@@ -354,15 +347,15 @@
         concat_axis=0,
         tiled=True,
     ).reshape(SLOTS, SAMPLES + TAIL)
-    basis, taper = pl.pallas_call(
+    basis, taper, turn = pl.pallas_call(
         fetch_kernel,
-        in_specs=[ANY, HBM, HBM],
-        out_specs=[VMEM] * 2,
-        out_shape=[jax.ShapeDtypeStruct(t.shape, t.dtype) for t in (basis, taper)],
-        scratch_shapes=[pltpu.SemaphoreType.DMA((2,))],
+        in_specs=[ANY, HBM, HBM, HBM],
+        out_specs=[VMEM] * 3,
+        out_shape=[jax.ShapeDtypeStruct(t.shape, t.dtype) for t in (basis, taper, turn)],
+        scratch_shapes=[pltpu.SemaphoreType.DMA((3,))],
         compiler_params=pltpu.CompilerParams(vmem_limit_bytes=MIB),
         cost_estimate=SMALL,
-    )(packed, basis, taper)
+    )(packed, basis, taper, turn)
     white = pl.pallas_call(
         whiten_kernel,
         in_specs=[SMEM] + [VMEM] * 3,

time: 106 us -> 102 us (0.962)
  Pallas kernels: 45.4 us -> 42.2 us
  local copies, waits for them, and re-layouts: 7.79 us -> 5.56 us
  waiting for transfers between devices: 20.5 us -> 21.8 us
    pallas_call x4, Pallas kernels: 31.1 us -> 28.1 us  [matmul(): pl.pallas_call(functools.partial(matmul_kernel, sources, len(arrays)), in...]
    ppermute x17, waiting for transfers between devices: 9.17 us -> 11.1 us  [permuted(): return lax.ppermute(value, ('blk', 'freq'), pairs)]
    reshape x1, local copies, waits for them, and re-layouts: 1.98 us -> 0.22 us  [local(): arrived = lax.all_to_all(packed.reshape(DEVICES, SLOTS // DEVICES, SAMPLE...]
    unnamed x12 -> x8, local copies, waits for them, and re-layouts: 4.67 us -> 4.2 us
  transfers between devices with their start and end apart: 18 -> 18, of which waited for: 5 -> 6; matrix products, arithmetic and copies ran while one was open for 0% -> 0% of each run, Pallas kernels for 33% -> 32%
where the time goes in v6:
time: 102 us; the launch traced here: 101 us
  Pallas kernels  42.2 us (41%)
  starting transfers between devices  29.5 us (29%)
  waiting for transfers between devices  21.8 us (21%)
  local copies, waits for them, and re-layouts  5.56 us (5%)
  between operations  1.08 us (1%)
    pallas_call x4, Pallas kernels, matmul(): pl.pallas_call(functools.partial(matmul_kernel, sources, len(arrays)), in...  28.1 us
    ppermute x17, starting transfers between devices, permuted(): return lax.ppermute(value, ('blk', 'freq'), pairs)  18.3 us
    pallas_call x2, Pallas kernels, rotate(): pl.pallas_call(functools.partial(rotate_kernel, halves), in_specs=[SMEM,...  11.5 us
    all_to_all x1, starting transfers between devices, local(): lax.all_to_all(packed.reshape(DEVICES, SLOTS // DEVICES, SAMPLES + TAIL),...  11.2 us
    ppermute x17, waiting for transfers between devices, permuted(): return lax.ppermute(value, ('blk', 'freq'), pairs)  11.1 us
    all_to_all x1, waiting for transfers between devices, local(): lax.all_to_all(packed.reshape(DEVICES, SLOTS // DEVICES, SAMPLES + TAIL),...  10.7 us
    unnamed x8, local copies, waits for them, and re-layouts  4.2 us
  transfers between devices with their start and end apart: 18, of which 6 were waited for; matrix products, arithmetic and copies ran while one was open for 0% of the time, Pallas kernels for 32%

profile of v6, /device:TPU:0, one launch (start us, length us, event | category | flops | bytes accessed | tf_op | source)
XLA Modules:
  0.0 100.9 jit_solution(13221562238679923206)
XLA Ops:
  1.4 1.0 %copy-done.1 = bf16[256,1024]{1,0:T(8,128)(2,1)S(1)} copy-done((bf16[256,1024]{1,0:T(8,128)(2,1)S(1)}, bf16[256,1024]{1,0:T(8,128)(2,1)}, u32[]{:S(2)}) %copy-start.1) | copy-done | bytes 524312
  3.9 11.2 %all-to-all-start = ((bf16[128,2,1152]{2,1,0:T(2,128)(2,1)}), bf16[128,2,1152]{2,1,0:T(2,128)(2,1)S(1)}, u32[]{:S(2)}, u32[]{:S(2)}) async-start(bf16[128,2,1152]{2,1,0:T(2,128)(2,1)} %reshape.13), calls=%async_computation | async-start | bytes 1179648 | tf_op jit(solution)/shard_map/all_to_all | solution.py:343
  15.0 1.6 %copy-done = bf16[1024,1024]{1,0:T(8,128)(2,1)S(1)} copy-done((bf16[1024,1024]{1,0:T(8,128)(2,1)S(1)}, bf16[1024,1024]{1,0:T(8,128)(2,1)}, u32[]{:S(2)}) %copy-start) | copy-done | bytes 2097176
  18.6 10.7 %all-to-all-done = bf16[128,2,1152]{2,1,0:T(2,128)(2,1)S(1)} async-done(((bf16[128,2,1152]{2,1,0:T(2,128)(2,1)}), bf16[128,2,1152]{2,1,0:T(2,128)(2,1)S(1)}, u32[]{:S(2)}, u32[]{:S(2)}) %all-to-all-start) | async-done | bytes 589856 | tf_op jit(solution)/shard_map/all_to_all | solution.py:343
  29.5 1.7 %shard_map.75.own0 = bf16[32,4096]{1,0:T(8,128)(2,1)S(1)} custom-call(s32[5]{0:T(128)S(1)} %stack.23.place_ref, bf16[256,1152]{1,0:T(8,128)(2,1)S(1)} %reshape.14.recv_ref, bf16[1024,1024]{1,0:T(8,128)(2,1)S(1)} %get-tuple-element.20.basis_ref, f32[1,1024]{1,0:T(1,128)S(1)} %get-tuple-element.21.taper_ref), custom_call_target="tpu_custom_call" | custom-call | tf_op jit(solution)/shard_map/pallas_call | solution.py:359
  31.3 1.5 %collective-permute-done.own1 = bf16[32,4096]{1,0:T(8,128)(2,1)S(1)} collective-permute-done((bf16[32,4096]{1,0:T(8,128)(2,1)S(1)}, bf16[32,4096]{1,0:T(8,128)(2,1)S(1)}, u32[]{:S(2)}, u32[]{:S(2)}) %collective-permute-start) | collective-permute-done | bytes 262176 | tf_op jit(solution)/shard_map/ppermute | solution.py:307
  32.8 1.2 %collective-permute-start.4 = (bf16[32,4096]{1,0:T(8,128)(2,1)S(1)}, bf16[32,4096]{1,0:T(8,128)(2,1)S(1)}, u32[]{:S(2)}, u32[]{:S(2)}) collective-permute-start(bf16[32,4096]{1,0:T(8,128)(2,1)S(1)} %pad_maximum_fusion.refs_0_), channel_id=1, source_target_pairs={{0,16},{1,17},{2,18},{3,19},{4,20},{5,21},{6,22},{7,23},{8,24},{9,... | collective-permute-start | bytes 786440 | tf_op jit(solution)/shard_map/ppermute | solution.py:307
  34.9 2.5 %collective-permute-start.2 = (bf16[32,4096]{1,0:T(8,128)(2,1)S(1)}, bf16[32,4096]{1,0:T(8,128)(2,1)S(1)}, u32[]{:S(2)}, u32[]{:S(2)}) collective-permute-start(bf16[32,4096]{1,0:T(8,128)(2,1)S(1)} %pad_maximum_fusion.refs_0_), channel_id=1, source_target_pairs={{0,12},{1,97},{2,14},{3,99},{4,0},{5,101},{6,2},{7,103},{8,4},{9,1... | collective-permute-start | bytes 786440 | tf_op jit(solution)/shard_map/ppermute | solution.py:307
  37.4 5.8 %shard_map.76 = (bf16[4096,1024]{1,0:T(8,128)(2,1)S(1)}, f32[8,128]{1,0:T(8,128)S(1)}) custom-call(s32[5]{0:T(128)S(1)} %stack.23.place_ref, bf16[32,4096]{1,0:T(8,128)(2,1)S(1)} %shard_map.75.own0, bf16[32,4096]{1,0:T(8,128)(2,1)S(1)} %collective-permute-done.own1, f32[144,128]{1,0:T(8,128)S(1)} %get-tuple-element.22.small_ref), custom_call_target="tpu_custom_call" | custom-call | flops 1024 | bytes 1024 | tf_op jit(solution)/shard_map/pallas_call | solution.py:209
  43.2 2.3 %collective-permute-start.7 = (bf16[32,4096]{1,0:T(8,128)(2,1)S(1)}, bf16[32,4096]{1,0:T(8,128)(2,1)S(1)}, u32[]{:S(2)}, u32[]{:S(2)}) collective-permute-start(bf16[32,4096]{1,0:T(8,128)(2,1)S(1)} %collective-permute-done.4.refs_4_), channel_id=1, source_target_pairs={{0,8},{1,65},{2,10},{3,67},{4,12},{5,69},{6,14},{7,71},{8,0},{9,73... | collective-permute-start | bytes 786440 | tf_op jit(solution)/shard_map/ppermute | solution.py:307
  45.5 1.1 %collective-permute-start.6 = (bf16[32,4096]{1,0:T(8,128)(2,1)S(1)}, bf16[32,4096]{1,0:T(8,128)(2,1)S(1)}, u32[]{:S(2)}, u32[]{:S(2)}) collective-permute-start(bf16[32,4096]{1,0:T(8,128)(2,1)S(1)} %collective-permute-done.4.refs_4_), channel_id=1, source_target_pairs={{0,12},{1,97},{2,14},{3,99},{4,0},{5,101},{6,2},{7,103},{8,4},{9,1... | collective-permute-start | bytes 786440 | tf_op jit(solution)/shard_map/ppermute | solution.py:307
  48.0 3.1 %collective-permute-done.7.refs_7_ = bf16[32,4096]{1,0:T(8,128)(2,1)S(1)} collective-permute-done((bf16[32,4096]{1,0:T(8,128)(2,1)S(1)}, bf16[32,4096]{1,0:T(8,128)(2,1)S(1)}, u32[]{:S(2)}, u32[]{:S(2)}) %collective-permute-start.7) | collective-permute-done | bytes 262176 | tf_op jit(solution)/shard_map/ppermute | solution.py:307
  51.1 3.4 %collective-permute-done.6.refs_6_ = bf16[32,4096]{1,0:T(8,128)(2,1)S(1)} collective-permute-done((bf16[32,4096]{1,0:T(8,128)(2,1)S(1)}, bf16[32,4096]{1,0:T(8,128)(2,1)S(1)}, u32[]{:S(2)}, u32[]{:S(2)}) %collective-permute-start.6) | collective-permute-done | bytes 262176 | tf_op jit(solution)/shard_map/ppermute | solution.py:307
  54.9 1.6 %collective-permute-start.9 = (bf16[128,4096]{1,0:T(8,128)(2,1)S(1)}, bf16[128,4096]{1,0:T(8,128)(2,1)S(1)}, u32[]{:S(2)}, u32[]{:S(2)}) collective-permute-start(bf16[128,4096]{1,0:T(8,128)(2,1)S(1)} %get-tuple-element.24.refs_0_), channel_id=1, source_target_pairs={{0,32},{1,5},{2,34},{3,7},{4,36},{5,9},{6,38},{7,11},{8,40},{9,13}... | collective-permute-start | bytes 3145736 | tf_op jit(solution)/shard_map/ppermute | solution.py:307
  56.5 1.1 %collective-permute-start.13 = (bf16[128,4096]{1,0:T(8,128)(2,1)S(1)}, bf16[128,4096]{1,0:T(8,128)(2,1)S(1)}, u32[]{:S(2)}, u32[]{:S(2)}) collective-permute-start(bf16[128,4096]{1,0:T(8,128)(2,1)S(1)} %get-tuple-element.25), channel_id=1, source_target_pairs={{0,97},{1,12},{2,99},{3,14},{4,101},{5,0},{6,103},{7,2},{8,105},{9... | collective-permute-start | bytes 3145736 | tf_op jit(solution)/shard_map/ppermute | solution.py:307
  58.3 1.2 %collective-permute-done.11.own1.refs_1_ = bf16[32,4096]{1,0:T(8,128)(2,1)S(1)} collective-permute-done((bf16[32,4096]{1,0:T(8,128)(2,1)S(1)}, bf16[32,4096]{1,0:T(8,128)(2,1)S(1)}, u32[]{:S(2)}, u32[]{:S(2)}) %collective-permute-start.11) | collective-permute-done | bytes 262176 | tf_op jit(solution)/shard_map/ppermute | solution.py:307
  59.6 3.2 %collective-permute-start.15 = (bf16[128,4096]{1,0:T(8,128)(2,1)S(1)}, bf16[128,4096]{1,0:T(8,128)(2,1)S(1)}, u32[]{:S(2)}, u32[]{:S(2)}) collective-permute-start(bf16[128,4096]{1,0:T(8,128)(2,1)S(1)} %shard_map.83), channel_id=1, source_target_pairs={{0,96},{1,13},{2,98},{3,15},{4,100},{5,1},{6,102},{7,3},{8,104},{9... | collective-permute-start | bytes 3145736 | tf_op jit(solution)/shard_map/ppermute | solution.py:307
  62.7 5.7 %shard_map.79 = (bf16[4096,1024]{1,0:T(8,128)(2,1)S(1)}, f32[8,128]{1,0:T(8,128)}) custom-call(s32[5]{0:T(128)S(1)} %stack.23.place_ref, bf16[32,4096]{1,0:T(8,128)(2,1)S(1)} %collective-permute-done.8.refs_8_.own0, bf16[32,4096]{1,0:T(8,128)(2,1)S(1)} %collective-permute-done.11.own1.refs_1_, f32[144,128]{1,0:T(8,128)S(1)} %get-tuple-element.22.small_ref), custom_call_target="tpu_custom_call" | custom-call | flops 1024 | bytes 1024 | tf_op jit(solution)/shard_map/pallas_call | solution.py:209
  68.4 6.6 %shard_map.80 = (f32[64,16,2048]{2,1,0:T(8,128)}, f32[8,128]{1,0:T(8,128)S(1)}) custom-call(s32[5]{0:T(128)S(1)} %stack.23.place_ref, bf16[128,4096]{1,0:T(8,128)(2,1)S(1)} %get-tuple-element.24.refs_0_, bf16[128,4096]{1,0:T(8,128)(2,1)S(1)} %collective-permute-done.10.refs_1_, bf16[4096,1024]{1,0:T(8,128)(2,1)S(1)} %get-tuple-element.26.refs_2_, ...), custom_call_target="tpu_custom_call" | custom-call | flops 1024 | bytes 1024 | tf_op jit(solution)/shard_map/pallas_call | solution.py:283
  75.2 2.1 %collective-permute-start.14 = (bf16[128,4096]{1,0:T(8,128)(2,1)S(1)}, bf16[128,4096]{1,0:T(8,128)(2,1)S(1)}, u32[]{:S(2)}, u32[]{:S(2)}) collective-permute-start(bf16[128,4096]{1,0:T(8,128)(2,1)S(1)} %shard_map.82.refs_1_), channel_id=1, source_target_pairs={{0,12},{1,97},{2,14},{3,99},{4,0},{5,101},{6,2},{7,103},{8,4},{9,1... | collective-permute-start | bytes 3145736 | tf_op jit(solution)/shard_map/ppermute | solution.py:307
  77.2 7.2 %shard_map.85 = (f32[64,16,2048]{2,1,0:T(8,128)}, f32[8,128]{1,0:T(8,128)}) custom-call(s32[5]{0:T(128)S(1)} %stack.23.place_ref, bf16[128,4096]{1,0:T(8,128)(2,1)S(1)} %shard_map.81.refs_0_, bf16[128,4096]{1,0:T(8,128)(2,1)S(1)} %shard_map.82.refs_1_, bf16[4096,1024]{1,0:T(8,128)(2,1)S(1)} %get-tuple-element.26.refs_2_, ...), custom_call_target="tpu_custom_call", output_to_operand_aliasing={{0}: (5, {})} | custom-call | flops 1024 | bytes 1024 | tf_op jit(solution)/shard_map/pallas_call | solution.py:283
  84.4 2.0 %collective-permute-done.15.refs_0_ = bf16[128,4096]{1,0:T(8,128)(2,1)S(1)} collective-permute-done((bf16[128,4096]{1,0:T(8,128)(2,1)S(1)}, bf16[128,4096]{1,0:T(8,128)(2,1)S(1)}, u32[]{:S(2)}, u32[]{:S(2)}) %collective-permute-start.15) | collective-permute-done | bytes 1048608 | tf_op jit(solution)/shard_map/ppermute | solution.py:307
  86.4 7.2 %shard_map.86 = (f32[64,16,2048]{2,1,0:T(8,128)}, f32[8,128]{1,0:T(8,128)}) custom-call(s32[5]{0:T(128)S(1)} %stack.23.place_ref, bf16[128,4096]{1,0:T(8,128)(2,1)S(1)} %collective-permute-done.15.refs_0_, bf16[128,4096]{1,0:T(8,128)(2,1)S(1)} %collective-permute-done.16.refs_1_, ...), custom_call_target="tpu_custom_call", output_to_operand_aliasing={{0}: (5, {})} | custom-call | flops 1024 | bytes 1024 | tf_op jit(solution)/shard_map/pallas_call | solution.py:283
  93.6 7.2 %shard_map.87 = (f32[64,16,2048]{2,1,0:T(8,128)}, f32[8,128]{1,0:T(8,128)}) custom-call(s32[5]{0:T(128)S(1)} %stack.23.place_ref, bf16[128,4096]{1,0:T(8,128)(2,1)S(1)} %collective-permute-done.12.refs_0_, bf16[128,4096]{1,0:T(8,128)(2,1)S(1)} %collective-permute-done.14.refs_1_, ...), custom_call_target="tpu_custom_call", output_to_operand_aliasing={{0}: (5, {})} | custom-call | flops 1024 | bytes 1024 | tf_op jit(solution)/shard_map/pallas_call | solution.py:283
  (42 shorter events, 8.0 us)
Async XLA Ops:
  1.4 1.0 %copy-start.1 = (bf16[256,1024]{1,0:T(8,128)(2,1)S(1)}, bf16[256,1024]{1,0:T(8,128)(2,1)}, u32[]{:S(2)}) copy-start(bf16[256,1024]{1,0:T(8,128)(2,1)} %raw_ref.1) | copy-start | bytes 1572868
  3.9 25.4 %all-to-all-start = ((bf16[128,2,1152]{2,1,0:T(2,128)(2,1)}), bf16[128,2,1152]{2,1,0:T(2,128)(2,1)S(1)}, u32[]{:S(2)}, u32[]{:S(2)}) async-start(bf16[128,2,1152]{2,1,0:T(2,128)(2,1)} %reshape.13), calls=%async_computation | async-start | bytes 1179648 | tf_op jit(solution)/shard_map/all_to_all | solution.py:343
  15.0 1.6 %copy-start = (bf16[1024,1024]{1,0:T(8,128)(2,1)S(1)}, bf16[1024,1024]{1,0:T(8,128)(2,1)}, u32[]{:S(2)}) copy-start(bf16[1024,1024]{1,0:T(8,128)(2,1)} %constant.72.clone.basis_hbm) | copy-start | bytes 6291460
  16.6 0.9 copy-start.2
  17.5 0.7 copy-start.3
  31.2 1.6 %collective-permute-start = (bf16[32,4096]{1,0:T(8,128)(2,1)S(1)}, bf16[32,4096]{1,0:T(8,128)(2,1)S(1)}, u32[]{:S(2)}, u32[]{:S(2)}) collective-permute-start(bf16[32,4096]{1,0:T(8,128)(2,1)S(1)} %shard_map.75.own0), channel_id=1, source_target_pairs={{0,1},{1,0},{2,3},{3,2},{4,5},{5,4},{6,7},{7,6},{8,9},{9,8},{10,11... | collective-permute-start | bytes 786440 | tf_op jit(solution)/shard_map/ppermute | solution.py:307
  32.8 10.3 %collective-permute-start.4 = (bf16[32,4096]{1,0:T(8,128)(2,1)S(1)}, bf16[32,4096]{1,0:T(8,128)(2,1)S(1)}, u32[]{:S(2)}, u32[]{:S(2)}) collective-permute-start(bf16[32,4096]{1,0:T(8,128)(2,1)S(1)} %pad_maximum_fusion.refs_0_), channel_id=1, source_target_pairs={{0,16},{1,17},{2,18},{3,19},{4,20},{5,21},{6,22},{7,23},{8,24},{9,... | collective-permute-start | bytes 786440 | tf_op jit(solution)/shard_map/ppermute | solution.py:307
  34.1 12.5 %collective-permute-start.3 = (bf16[32,4096]{1,0:T(8,128)(2,1)S(1)}, bf16[32,4096]{1,0:T(8,128)(2,1)S(1)}, u32[]{:S(2)}, u32[]{:S(2)}) collective-permute-start(bf16[32,4096]{1,0:T(8,128)(2,1)S(1)} %pad_maximum_fusion.refs_0_), channel_id=1, source_target_pairs={{0,8},{1,65},{2,10},{3,67},{4,12},{5,69},{6,14},{7,71},{8,0},{9,73... | collective-permute-start | bytes 786440 | tf_op jit(solution)/shard_map/ppermute | solution.py:307
  34.9 12.6 %collective-permute-start.2 = (bf16[32,4096]{1,0:T(8,128)(2,1)S(1)}, bf16[32,4096]{1,0:T(8,128)(2,1)S(1)}, u32[]{:S(2)}, u32[]{:S(2)}) collective-permute-start(bf16[32,4096]{1,0:T(8,128)(2,1)S(1)} %pad_maximum_fusion.refs_0_), channel_id=1, source_target_pairs={{0,12},{1,97},{2,14},{3,99},{4,0},{5,101},{6,2},{7,103},{8,4},{9,1... | collective-permute-start | bytes 786440 | tf_op jit(solution)/shard_map/ppermute | solution.py:307
  37.4 10.2 %collective-permute-start.1 = (bf16[32,4096]{1,0:T(8,128)(2,1)S(1)}, bf16[32,4096]{1,0:T(8,128)(2,1)S(1)}, u32[]{:S(2)}, u32[]{:S(2)}) collective-permute-start(bf16[32,4096]{1,0:T(8,128)(2,1)S(1)} %pad_maximum_fusion.refs_0_), channel_id=1, source_target_pairs={{0,4},{1,33},{2,6},{3,35},{4,8},{5,37},{6,10},{7,39},{8,12},{9,41}... | collective-permute-start | bytes 786440 | tf_op jit(solution)/shard_map/ppermute | solution.py:307
  43.2 8.0 %collective-permute-start.7 = (bf16[32,4096]{1,0:T(8,128)(2,1)S(1)}, bf16[32,4096]{1,0:T(8,128)(2,1)S(1)}, u32[]{:S(2)}, u32[]{:S(2)}) collective-permute-start(bf16[32,4096]{1,0:T(8,128)(2,1)S(1)} %collective-permute-done.4.refs_4_), channel_id=1, source_target_pairs={{0,8},{1,65},{2,10},{3,67},{4,12},{5,69},{6,14},{7,71},{8,0},{9,73... | collective-permute-start | bytes 786440 | tf_op jit(solution)/shard_map/ppermute | solution.py:307
  45.5 9.0 %collective-permute-start.6 = (bf16[32,4096]{1,0:T(8,128)(2,1)S(1)}, bf16[32,4096]{1,0:T(8,128)(2,1)S(1)}, u32[]{:S(2)}, u32[]{:S(2)}) collective-permute-start(bf16[32,4096]{1,0:T(8,128)(2,1)S(1)} %collective-permute-done.4.refs_4_), channel_id=1, source_target_pairs={{0,12},{1,97},{2,14},{3,99},{4,0},{5,101},{6,2},{7,103},{8,4},{9,1... | collective-permute-start | bytes 786440 | tf_op jit(solution)/shard_map/ppermute | solution.py:307
  46.6 8.0 %collective-permute-start.5 = (bf16[32,4096]{1,0:T(8,128)(2,1)S(1)}, bf16[32,4096]{1,0:T(8,128)(2,1)S(1)}, u32[]{:S(2)}, u32[]{:S(2)}) collective-permute-start(bf16[32,4096]{1,0:T(8,128)(2,1)S(1)} %collective-permute-done.4.refs_4_), channel_id=1, source_target_pairs={{0,4},{1,33},{2,6},{3,35},{4,8},{5,37},{6,10},{7,39},{8,12},{9,41}... | collective-permute-start | bytes 786440 | tf_op jit(solution)/shard_map/ppermute | solution.py:307
  47.5 7.0 %collective-permute-start.8 = (bf16[32,4096]{1,0:T(8,128)(2,1)S(1)}, bf16[32,4096]{1,0:T(8,128)(2,1)S(1)}, u32[]{:S(2)}, u32[]{:S(2)}) collective-permute-start(bf16[32,4096]{1,0:T(8,128)(2,1)S(1)} %shard_map.77), channel_id=1, source_target_pairs={{0,2},{1,3},{2,0},{3,1},{4,6},{5,7},{6,4},{7,5},{8,10},{9,11},{10,... | collective-permute-start | bytes 786440 | tf_op jit(solution)/shard_map/ppermute | solution.py:307
  54.8 13.6 %collective-permute-start.10 = (bf16[128,4096]{1,0:T(8,128)(2,1)S(1)}, bf16[128,4096]{1,0:T(8,128)(2,1)S(1)}, u32[]{:S(2)}, u32[]{:S(2)}) collective-permute-start(bf16[128,4096]{1,0:T(8,128)(2,1)S(1)} %get-tuple-element.25), channel_id=1, source_target_pairs={{0,1},{1,0},{2,3},{3,2},{4,5},{5,4},{6,7},{7,6},{8,9},{9,8},{10,11... | collective-permute-start | bytes 3145736 | tf_op jit(solution)/shard_map/ppermute | solution.py:307
  54.9 20.1 %collective-permute-start.9 = (bf16[128,4096]{1,0:T(8,128)(2,1)S(1)}, bf16[128,4096]{1,0:T(8,128)(2,1)S(1)}, u32[]{:S(2)}, u32[]{:S(2)}) collective-permute-start(bf16[128,4096]{1,0:T(8,128)(2,1)S(1)} %get-tuple-element.24.refs_0_), channel_id=1, source_target_pairs={{0,32},{1,5},{2,34},{3,7},{4,36},{5,9},{6,38},{7,11},{8,40},{9,13}... | collective-permute-start | bytes 3145736 | tf_op jit(solution)/shard_map/ppermute | solution.py:307
  56.5 18.7 %collective-permute-start.13 = (bf16[128,4096]{1,0:T(8,128)(2,1)S(1)}, bf16[128,4096]{1,0:T(8,128)(2,1)S(1)}, u32[]{:S(2)}, u32[]{:S(2)}) collective-permute-start(bf16[128,4096]{1,0:T(8,128)(2,1)S(1)} %get-tuple-element.25), channel_id=1, source_target_pairs={{0,97},{1,12},{2,99},{3,14},{4,101},{5,0},{6,103},{7,2},{8,105},{9... | collective-permute-start | bytes 3145736 | tf_op jit(solution)/shard_map/ppermute | solution.py:307
  57.6 1.9 %collective-permute-start.11 = (bf16[32,4096]{1,0:T(8,128)(2,1)S(1)}, bf16[32,4096]{1,0:T(8,128)(2,1)S(1)}, u32[]{:S(2)}, u32[]{:S(2)}) collective-permute-start(bf16[32,4096]{1,0:T(8,128)(2,1)S(1)} %collective-permute-done.8.refs_8_.own0), channel_id=1, source_target_pairs={{0,1},{1,0},{2,3},{3,2},{4,5},{5,4},{6,7},{7,6},{8,9},{9,8},{10,11... | collective-permute-start | bytes 786440 | tf_op jit(solution)/shard_map/ppermute | solution.py:307
  59.5 24.9 %collective-permute-start.16 = (bf16[128,4096]{1,0:T(8,128)(2,1)S(1)}, bf16[128,4096]{1,0:T(8,128)(2,1)S(1)}, u32[]{:S(2)}, u32[]{:S(2)}) collective-permute-start(bf16[128,4096]{1,0:T(8,128)(2,1)S(1)} %shard_map.84), channel_id=1, source_target_pairs={{0,33},{1,4},{2,35},{3,6},{4,37},{5,8},{6,39},{7,10},{8,41},{9,12}... | collective-permute-start | bytes 3145736 | tf_op jit(solution)/shard_map/ppermute | solution.py:307
  59.6 26.8 %collective-permute-start.15 = (bf16[128,4096]{1,0:T(8,128)(2,1)S(1)}, bf16[128,4096]{1,0:T(8,128)(2,1)S(1)}, u32[]{:S(2)}, u32[]{:S(2)}) collective-permute-start(bf16[128,4096]{1,0:T(8,128)(2,1)S(1)} %shard_map.83), channel_id=1, source_target_pairs={{0,96},{1,13},{2,98},{3,15},{4,100},{5,1},{6,102},{7,3},{8,104},{9... | collective-permute-start | bytes 3145736 | tf_op jit(solution)/shard_map/ppermute | solution.py:307
  75.1 18.5 %collective-permute-start.12 = (bf16[128,4096]{1,0:T(8,128)(2,1)S(1)}, bf16[128,4096]{1,0:T(8,128)(2,1)S(1)}, u32[]{:S(2)}, u32[]{:S(2)}) collective-permute-start(bf16[128,4096]{1,0:T(8,128)(2,1)S(1)} %shard_map.81.refs_0_), channel_id=1, source_target_pairs={{0,32},{1,5},{2,34},{3,7},{4,36},{5,9},{6,38},{7,11},{8,40},{9,13}... | collective-permute-start | bytes 3145736 | tf_op jit(solution)/shard_map/ppermute | solution.py:307
  75.2 18.4 %collective-permute-start.14 = (bf16[128,4096]{1,0:T(8,128)(2,1)S(1)}, bf16[128,4096]{1,0:T(8,128)(2,1)S(1)}, u32[]{:S(2)}, u32[]{:S(2)}) collective-permute-start(bf16[128,4096]{1,0:T(8,128)(2,1)S(1)} %shard_map.82.refs_1_), channel_id=1, source_target_pairs={{0,12},{1,97},{2,14},{3,99},{4,0},{5,101},{6,2},{7,103},{8,4},{9,1... | collective-permute-start | bytes 3145736 | tf_op jit(solution)/shard_map/ppermute | solution.py:307

commit v7 on v6

--- a/solution.py
+++ b/solution.py
@@ -77,8 +77,10 @@
     pick = jnp.where(flat == row.astype(F32), 1.0, 0.0)
     place = (key % WIN * QC + chan % QC + 1).astype(F32)
     place_col = jnp.sum(pick * place, axis=1, keepdims=True)
-    out_ref[:, SAMPLES:] = jnp.broadcast_to(place_col, (SLOTS, TAIL)).astype(BF16)
-    out_ref[:, :SAMPLES] = jnp.dot(pick.astype(BF16), raw_ref[...], preferred_element_type=F32).astype(BF16)
+    place_all = jnp.broadcast_to(place_col, (SLOTS, TAIL)).astype(BF16)
+    out_ref[:, :, SAMPLES:] = place_all.reshape(DEVICES, SLOTS // DEVICES, TAIL)
+    sent = jnp.dot(pick.astype(BF16), raw_ref[...], preferred_element_type=F32).astype(BF16)
+    out_ref[:, :, :SAMPLES] = sent.reshape(DEVICES, SLOTS // DEVICES, SAMPLES)
 
 
 def fetch_kernel(after_hbm, basis_hbm, taper_hbm, turn_hbm, basis_ref, taper_ref, turn_ref, sem):
@@ -102,9 +104,9 @@
     left = energy - high.astype(F32)
     middle = left.astype(BF16)
     low = (left - middle.astype(F32)).astype(BF16)
-    total = jnp.dot(low, inside, preferred_element_type=F32)
-    total = total + jnp.dot(middle, inside, preferred_element_type=F32)
-    total = total + jnp.dot(high, inside, preferred_element_type=F32)
+    rows = energy.shape[0]
+    sums = jnp.dot(jnp.concatenate([low, middle, high], axis=0), inside, preferred_element_type=F32)
+    total = sums[:rows] + sums[rows : 2 * rows] + sums[2 * rows :]
     pos = lax.broadcasted_iota(jnp.int32, (1, FREQS), 1)
     count = jnp.minimum(pos, HALFWIN) + jnp.minimum(FREQS - 1 - pos, HALFWIN) + 1
     return total / count.astype(F32)
@@ -337,11 +339,11 @@
         pack_kernel,
         in_specs=[SMEM, VMEM, VMEM],
         out_specs=VMEM,
-        out_shape=jax.ShapeDtypeStruct((SLOTS, SAMPLES + TAIL), BF16),
+        out_shape=jax.ShapeDtypeStruct((DEVICES, SLOTS // DEVICES, SAMPLES + TAIL), BF16),
         compiler_params=pltpu.CompilerParams(vmem_limit_bytes=8 * MIB),
     )(file_count, (seg_chan * WIN + seg_win).reshape(1, SLOTS), raw)
     arrived = lax.all_to_all(
-        packed.reshape(DEVICES, SLOTS // DEVICES, SAMPLES + TAIL),
+        packed,
         ("blk", "freq"),
         split_axis=0,
         concat_axis=0,
@@ -371,14 +373,14 @@
     opposite = first(unit, 2)
     near_side, token = rotate(place, [(0, 0), (0, 1), (1, 1), (1, 0)], white, sib, turn)
     beyond_ahead, beyond_behind, beyond_opposite = first(beyond, 1), first(beyond, -1), first(beyond, 2)
-    (turned,) = grouped([(0, h, 0, h) for h in range(2)], [2], [unit], [ahead, behind, opposite, token])
+    (turned,) = grouped([(0, h, 0, h) for h in range(2)], [2], [unit], [ahead, behind, opposite])
     facing = neighbour(turned)
     facing_sib = sibling(facing)
     arrays = [unit, ahead, behind, opposite, beyond, beyond_ahead, beyond_behind, beyond_opposite]
     line_at = [(0, 0), (-1, 0), (1, 0), (2, 0), (0, 1), (-1, 1), (1, 1), (2, 1)]
     moves = [(i, h, h, i) for i in range(8) for h in range(2)]
     moves += [(i, h, h + 2, p) for i, h, _, p in moves]
-    kept, given, later_kept, later_given = grouped(moves, [8] * 4, arrays, [facing])
+    kept, given, later_kept, later_given = grouped(moves, [8] * 4, arrays, [facing, token])
     far_side, _ = rotate(place, [(0, 0), (1, 0), (1, 1), (0, 1)], facing, facing_sib, turn)
     rotated = (near_side, far_side)
     kept_up, given_down = second(kept, 1), second(given, -1, swap=1)

time: 102 us -> 100 us (0.980)
  starting transfers between devices: 29.5 us -> 28.3 us
  local copies, waits for them, and re-layouts: 5.56 us -> 4.52 us
    ppermute x17, starting transfers between devices: 18.3 us -> 17.1 us  [permuted(): return lax.ppermute(value, ('blk', 'freq'), pairs)]
    reshape x2 -> x1, local copies, waits for them, and re-layouts: 1.26 us -> 0.22 us  [local(): arrived = lax.all_to_all(packed, ('blk', 'freq'), split_axis=0, concat_ax...]
  transfers between devices with their start and end apart: 18 -> 18, of which waited for: 6 -> 7; matrix products, arithmetic and copies ran while one was open for 0% -> 0% of each run, Pallas kernels for 32% -> 33%
where the time goes in v7:
time: 100 us; the launch traced here: 99.5 us
  Pallas kernels  43 us (43%)
  starting transfers between devices  28.3 us (28%)
  waiting for transfers between devices  21.9 us (22%)
  local copies, waits for them, and re-layouts  4.52 us (5%)
  between operations  1.08 us (1%)
    pallas_call x4, Pallas kernels, matmul(): pl.pallas_call(functools.partial(matmul_kernel, sources, len(arrays)), in...  28.1 us
    ppermute x17, starting transfers between devices, permuted(): return lax.ppermute(value, ('blk', 'freq'), pairs)  17.1 us
    pallas_call x2, Pallas kernels, rotate(): pl.pallas_call(functools.partial(rotate_kernel, halves), in_specs=[SMEM,...  11.5 us
    ppermute x17, waiting for transfers between devices, permuted(): return lax.ppermute(value, ('blk', 'freq'), pairs)  11.2 us
    all_to_all x1, starting transfers between devices, local(): lax.all_to_all(packed, ('blk', 'freq'), split_axis=0, concat_axis=0, tile...  11.2 us
    all_to_all x1, waiting for transfers between devices, local(): lax.all_to_all(packed, ('blk', 'freq'), split_axis=0, concat_axis=0, tile...  10.7 us
    unnamed x8, local copies, waits for them, and re-layouts  4.2 us
  transfers between devices with their start and end apart: 18, of which 7 were waited for; matrix products, arithmetic and copies ran while one was open for 0% of the time, Pallas kernels for 33%

profile of v7, /device:TPU:0, one launch (start us, length us, event | category | flops | bytes accessed | tf_op | source)
XLA Modules:
  0.0 99.5 jit_solution(965017257304032291)
XLA Ops:
  1.4 1.0 %copy-done.1 = bf16[256,1024]{1,0:T(8,128)(2,1)S(1)} copy-done((bf16[256,1024]{1,0:T(8,128)(2,1)S(1)}, bf16[256,1024]{1,0:T(8,128)(2,1)}, u32[]{:S(2)}) %copy-start.1) | copy-done | bytes 524312
  2.4 1.2 %shard_map.73.after_hbm = bf16[128,2,1152]{2,1,0:T(2,128)(2,1)} custom-call(s32[1]{0:T(128)S(6)} %copy.22.count_ref, s32[1,256]{1,0:T(1,128)S(1)} %bitcast.7, bf16[256,1024]{1,0:T(8,128)(2,1)S(1)} %copy-done.1), custom_call_target="tpu_custom_call" | custom-call | tf_op jit(solution)/shard_map/pallas_call | solution.py:338
  3.6 11.2 %all-to-all-start = ((bf16[128,2,1152]{2,1,0:T(2,128)(2,1)}), bf16[128,2,1152]{2,1,0:T(2,128)(2,1)S(1)}, u32[]{:S(2)}, u32[]{:S(2)}) async-start(bf16[128,2,1152]{2,1,0:T(2,128)(2,1)} %shard_map.73.after_hbm), calls=%async_computation | async-start | bytes 1179648 | tf_op jit(solution)/shard_map/all_to_all | solution.py:345
  14.8 1.6 %copy-done = bf16[1024,1024]{1,0:T(8,128)(2,1)S(1)} copy-done((bf16[1024,1024]{1,0:T(8,128)(2,1)S(1)}, bf16[1024,1024]{1,0:T(8,128)(2,1)}, u32[]{:S(2)}) %copy-start) | copy-done | bytes 2097176
  18.4 10.7 %all-to-all-done = bf16[128,2,1152]{2,1,0:T(2,128)(2,1)S(1)} async-done(((bf16[128,2,1152]{2,1,0:T(2,128)(2,1)}), bf16[128,2,1152]{2,1,0:T(2,128)(2,1)S(1)}, u32[]{:S(2)}, u32[]{:S(2)}) %all-to-all-start) | async-done | bytes 589856 | tf_op jit(solution)/shard_map/all_to_all | solution.py:345
  29.3 1.7 %shard_map.75.own0 = bf16[32,4096]{1,0:T(8,128)(2,1)S(1)} custom-call(s32[5]{0:T(128)S(1)} %stack.23.place_ref, bf16[256,1152]{1,0:T(8,128)(2,1)S(1)} %reshape.10.recv_ref, bf16[1024,1024]{1,0:T(8,128)(2,1)S(1)} %get-tuple-element.20.basis_ref, f32[1,1024]{1,0:T(1,128)S(1)} %get-tuple-element.21.taper_ref), custom_call_target="tpu_custom_call" | custom-call | tf_op jit(solution)/shard_map/pallas_call | solution.py:361
  31.1 1.5 %collective-permute-done.own1 = bf16[32,4096]{1,0:T(8,128)(2,1)S(1)} collective-permute-done((bf16[32,4096]{1,0:T(8,128)(2,1)S(1)}, bf16[32,4096]{1,0:T(8,128)(2,1)S(1)}, u32[]{:S(2)}, u32[]{:S(2)}) %collective-permute-start) | collective-permute-done | bytes 262176 | tf_op jit(solution)/shard_map/ppermute | solution.py:309
  32.6 1.2 %collective-permute-start.4 = (bf16[32,4096]{1,0:T(8,128)(2,1)S(1)}, bf16[32,4096]{1,0:T(8,128)(2,1)S(1)}, u32[]{:S(2)}, u32[]{:S(2)}) collective-permute-start(bf16[32,4096]{1,0:T(8,128)(2,1)S(1)} %pad_maximum_fusion.refs_0_), channel_id=1, source_target_pairs={{0,16},{1,17},{2,18},{3,19},{4,20},{5,21},{6,22},{7,23},{8,24},{9,... | collective-permute-start | bytes 786440 | tf_op jit(solution)/shard_map/ppermute | solution.py:309
  34.7 2.5 %collective-permute-start.2 = (bf16[32,4096]{1,0:T(8,128)(2,1)S(1)}, bf16[32,4096]{1,0:T(8,128)(2,1)S(1)}, u32[]{:S(2)}, u32[]{:S(2)}) collective-permute-start(bf16[32,4096]{1,0:T(8,128)(2,1)S(1)} %pad_maximum_fusion.refs_0_), channel_id=1, source_target_pairs={{0,12},{1,97},{2,14},{3,99},{4,0},{5,101},{6,2},{7,103},{8,4},{9,1... | collective-permute-start | bytes 786440 | tf_op jit(solution)/shard_map/ppermute | solution.py:309
  37.2 5.4 %collective-permute-done.4.refs_4_ = bf16[32,4096]{1,0:T(8,128)(2,1)S(1)} collective-permute-done((bf16[32,4096]{1,0:T(8,128)(2,1)S(1)}, bf16[32,4096]{1,0:T(8,128)(2,1)S(1)}, u32[]{:S(2)}, u32[]{:S(2)}) %collective-permute-start.4) | collective-permute-done | bytes 262176 | tf_op jit(solution)/shard_map/ppermute | solution.py:309
  43.3 2.0 %collective-permute-start.6 = (bf16[32,4096]{1,0:T(8,128)(2,1)S(1)}, bf16[32,4096]{1,0:T(8,128)(2,1)S(1)}, u32[]{:S(2)}, u32[]{:S(2)}) collective-permute-start(bf16[32,4096]{1,0:T(8,128)(2,1)S(1)} %collective-permute-done.4.refs_4_), channel_id=1, source_target_pairs={{0,12},{1,97},{2,14},{3,99},{4,0},{5,101},{6,2},{7,103},{8,4},{9,1... | collective-permute-start | bytes 786440 | tf_op jit(solution)/shard_map/ppermute | solution.py:309
  45.4 0.9 collective-permute-start.8
  46.3 5.8 %shard_map.77 = (bf16[4096,1024]{1,0:T(8,128)(2,1)S(1)}, f32[8,128]{1,0:T(8,128)S(1)}) custom-call(s32[5]{0:T(128)S(1)} %stack.23.place_ref, bf16[32,4096]{1,0:T(8,128)(2,1)S(1)} %shard_map.75.own0, bf16[32,4096]{1,0:T(8,128)(2,1)S(1)} %collective-permute-done.own1, f32[144,128]{1,0:T(8,128)S(1)} %get-tuple-element.22.small_ref), custom_call_target="tpu_custom_call" | custom-call | flops 1024 | bytes 1024 | tf_op jit(solution)/shard_map/pallas_call | solution.py:211
  52.1 1.1 %collective-permute-done.5.refs_5_ = bf16[32,4096]{1,0:T(8,128)(2,1)S(1)} collective-permute-done((bf16[32,4096]{1,0:T(8,128)(2,1)S(1)}, bf16[32,4096]{1,0:T(8,128)(2,1)S(1)}, u32[]{:S(2)}, u32[]{:S(2)}) %collective-permute-start.5) | collective-permute-done | bytes 262176 | tf_op jit(solution)/shard_map/ppermute | solution.py:309
  54.2 2.1 %collective-permute-start.13 = (bf16[128,4096]{1,0:T(8,128)(2,1)S(1)}, bf16[128,4096]{1,0:T(8,128)(2,1)S(1)}, u32[]{:S(2)}, u32[]{:S(2)}) collective-permute-start(bf16[128,4096]{1,0:T(8,128)(2,1)S(1)} %get-tuple-element.25), channel_id=1, source_target_pairs={{0,97},{1,12},{2,99},{3,14},{4,101},{5,0},{6,103},{7,2},{8,105},{9... | collective-permute-start | bytes 3145736 | tf_op jit(solution)/shard_map/ppermute | solution.py:309
  56.8 1.2 %collective-permute-done.11.own1.refs_1_ = bf16[32,4096]{1,0:T(8,128)(2,1)S(1)} collective-permute-done((bf16[32,4096]{1,0:T(8,128)(2,1)S(1)}, bf16[32,4096]{1,0:T(8,128)(2,1)S(1)}, u32[]{:S(2)}, u32[]{:S(2)}) %collective-permute-start.11) | collective-permute-done | bytes 262176 | tf_op jit(solution)/shard_map/ppermute | solution.py:309
  58.0 3.2 %collective-permute-start.15 = (bf16[128,4096]{1,0:T(8,128)(2,1)S(1)}, bf16[128,4096]{1,0:T(8,128)(2,1)S(1)}, u32[]{:S(2)}, u32[]{:S(2)}) collective-permute-start(bf16[128,4096]{1,0:T(8,128)(2,1)S(1)} %shard_map.83), channel_id=1, source_target_pairs={{0,96},{1,13},{2,98},{3,15},{4,100},{5,1},{6,102},{7,3},{8,104},{9... | collective-permute-start | bytes 3145736 | tf_op jit(solution)/shard_map/ppermute | solution.py:309
  61.1 5.7 %shard_map.79 = (bf16[4096,1024]{1,0:T(8,128)(2,1)S(1)}, f32[8,128]{1,0:T(8,128)}) custom-call(s32[5]{0:T(128)S(1)} %stack.23.place_ref, bf16[32,4096]{1,0:T(8,128)(2,1)S(1)} %collective-permute-done.8.refs_8_.own0, bf16[32,4096]{1,0:T(8,128)(2,1)S(1)} %collective-permute-done.11.own1.refs_1_, f32[144,128]{1,0:T(8,128)S(1)} %get-tuple-element.22.small_ref), custom_call_target="tpu_custom_call" | custom-call | flops 1024 | bytes 1024 | tf_op jit(solution)/shard_map/pallas_call | solution.py:211
  66.9 6.6 %shard_map.80 = (f32[64,16,2048]{2,1,0:T(8,128)}, f32[8,128]{1,0:T(8,128)S(1)}) custom-call(s32[5]{0:T(128)S(1)} %stack.23.place_ref, bf16[128,4096]{1,0:T(8,128)(2,1)S(1)} %get-tuple-element.24.refs_0_, bf16[128,4096]{1,0:T(8,128)(2,1)S(1)} %collective-permute-done.10.refs_1_, bf16[4096,1024]{1,0:T(8,128)(2,1)S(1)} %get-tuple-element.26.refs_2_, ...), custom_call_target="tpu_custom_call" | custom-call | flops 1024 | bytes 1024 | tf_op jit(solution)/shard_map/pallas_call | solution.py:285
  73.6 2.2 %collective-permute-start.14 = (bf16[128,4096]{1,0:T(8,128)(2,1)S(1)}, bf16[128,4096]{1,0:T(8,128)(2,1)S(1)}, u32[]{:S(2)}, u32[]{:S(2)}) collective-permute-start(bf16[128,4096]{1,0:T(8,128)(2,1)S(1)} %shard_map.82.refs_1_), channel_id=1, source_target_pairs={{0,12},{1,97},{2,14},{3,99},{4,0},{5,101},{6,2},{7,103},{8,4},{9,1... | collective-permute-start | bytes 3145736 | tf_op jit(solution)/shard_map/ppermute | solution.py:309
  75.8 7.2 %shard_map.85 = (f32[64,16,2048]{2,1,0:T(8,128)}, f32[8,128]{1,0:T(8,128)}) custom-call(s32[5]{0:T(128)S(1)} %stack.23.place_ref, bf16[128,4096]{1,0:T(8,128)(2,1)S(1)} %shard_map.81.refs_0_, bf16[128,4096]{1,0:T(8,128)(2,1)S(1)} %shard_map.82.refs_1_, bf16[4096,1024]{1,0:T(8,128)(2,1)S(1)} %get-tuple-element.26.refs_2_, ...), custom_call_target="tpu_custom_call", output_to_operand_aliasing={{0}: (5, {})} | custom-call | flops 1024 | bytes 1024 | tf_op jit(solution)/shard_map/pallas_call | solution.py:285
  83.6 7.2 %shard_map.86 = (f32[64,16,2048]{2,1,0:T(8,128)}, f32[8,128]{1,0:T(8,128)}) custom-call(s32[5]{0:T(128)S(1)} %stack.23.place_ref, bf16[128,4096]{1,0:T(8,128)(2,1)S(1)} %collective-permute-done.15.refs_0_, bf16[128,4096]{1,0:T(8,128)(2,1)S(1)} %collective-permute-done.16.refs_1_, ...), custom_call_target="tpu_custom_call", output_to_operand_aliasing={{0}: (5, {})} | custom-call | flops 1024 | bytes 1024 | tf_op jit(solution)/shard_map/pallas_call | solution.py:285
  90.8 1.4 %collective-permute-done.12.refs_0_ = bf16[128,4096]{1,0:T(8,128)(2,1)S(1)} collective-permute-done((bf16[128,4096]{1,0:T(8,128)(2,1)S(1)}, bf16[128,4096]{1,0:T(8,128)(2,1)S(1)}, u32[]{:S(2)}, u32[]{:S(2)}) %collective-permute-start.12) | collective-permute-done | bytes 1048608 | tf_op jit(solution)/shard_map/ppermute | solution.py:309
  92.2 7.2 %shard_map.87 = (f32[64,16,2048]{2,1,0:T(8,128)}, f32[8,128]{1,0:T(8,128)}) custom-call(s32[5]{0:T(128)S(1)} %stack.23.place_ref, bf16[128,4096]{1,0:T(8,128)(2,1)S(1)} %collective-permute-done.12.refs_0_, bf16[128,4096]{1,0:T(8,128)(2,1)S(1)} %collective-permute-done.14.refs_1_, ...), custom_call_target="tpu_custom_call", output_to_operand_aliasing={{0}: (5, {})} | custom-call | flops 1024 | bytes 1024 | tf_op jit(solution)/shard_map/pallas_call | solution.py:285
  (41 shorter events, 6.8 us)
Async XLA Ops:
  1.4 1.0 %copy-start.1 = (bf16[256,1024]{1,0:T(8,128)(2,1)S(1)}, bf16[256,1024]{1,0:T(8,128)(2,1)}, u32[]{:S(2)}) copy-start(bf16[256,1024]{1,0:T(8,128)(2,1)} %raw_ref.1) | copy-start | bytes 1572868
  3.6 25.4 %all-to-all-start = ((bf16[128,2,1152]{2,1,0:T(2,128)(2,1)}), bf16[128,2,1152]{2,1,0:T(2,128)(2,1)S(1)}, u32[]{:S(2)}, u32[]{:S(2)}) async-start(bf16[128,2,1152]{2,1,0:T(2,128)(2,1)} %shard_map.73.after_hbm), calls=%async_computation | async-start | bytes 1179648 | tf_op jit(solution)/shard_map/all_to_all | solution.py:345
  14.8 1.6 %copy-start = (bf16[1024,1024]{1,0:T(8,128)(2,1)S(1)}, bf16[1024,1024]{1,0:T(8,128)(2,1)}, u32[]{:S(2)}) copy-start(bf16[1024,1024]{1,0:T(8,128)(2,1)} %constant.72.clone.basis_hbm) | copy-start | bytes 6291460
  16.4 0.9 copy-start.2
  17.3 0.7 copy-start.3
  31.0 1.6 %collective-permute-start = (bf16[32,4096]{1,0:T(8,128)(2,1)S(1)}, bf16[32,4096]{1,0:T(8,128)(2,1)S(1)}, u32[]{:S(2)}, u32[]{:S(2)}) collective-permute-start(bf16[32,4096]{1,0:T(8,128)(2,1)S(1)} %shard_map.75.own0), channel_id=1, source_target_pairs={{0,1},{1,0},{2,3},{3,2},{4,5},{5,4},{6,7},{7,6},{8,9},{9,8},{10,11... | collective-permute-start | bytes 786440 | tf_op jit(solution)/shard_map/ppermute | solution.py:309
  32.6 9.9 %collective-permute-start.4 = (bf16[32,4096]{1,0:T(8,128)(2,1)S(1)}, bf16[32,4096]{1,0:T(8,128)(2,1)S(1)}, u32[]{:S(2)}, u32[]{:S(2)}) collective-permute-start(bf16[32,4096]{1,0:T(8,128)(2,1)S(1)} %pad_maximum_fusion.refs_0_), channel_id=1, source_target_pairs={{0,16},{1,17},{2,18},{3,19},{4,20},{5,21},{6,22},{7,23},{8,24},{9,... | collective-permute-start | bytes 786440 | tf_op jit(solution)/shard_map/ppermute | solution.py:309
  33.9 11.5 %collective-permute-start.3 = (bf16[32,4096]{1,0:T(8,128)(2,1)S(1)}, bf16[32,4096]{1,0:T(8,128)(2,1)S(1)}, u32[]{:S(2)}, u32[]{:S(2)}) collective-permute-start(bf16[32,4096]{1,0:T(8,128)(2,1)S(1)} %pad_maximum_fusion.refs_0_), channel_id=1, source_target_pairs={{0,8},{1,65},{2,10},{3,67},{4,12},{5,69},{6,14},{7,71},{8,0},{9,73... | collective-permute-start | bytes 786440 | tf_op jit(solution)/shard_map/ppermute | solution.py:309
  34.7 10.7 %collective-permute-start.2 = (bf16[32,4096]{1,0:T(8,128)(2,1)S(1)}, bf16[32,4096]{1,0:T(8,128)(2,1)S(1)}, u32[]{:S(2)}, u32[]{:S(2)}) collective-permute-start(bf16[32,4096]{1,0:T(8,128)(2,1)S(1)} %pad_maximum_fusion.refs_0_), channel_id=1, source_target_pairs={{0,12},{1,97},{2,14},{3,99},{4,0},{5,101},{6,2},{7,103},{8,4},{9,1... | collective-permute-start | bytes 786440 | tf_op jit(solution)/shard_map/ppermute | solution.py:309
  37.2 8.2 %collective-permute-start.1 = (bf16[32,4096]{1,0:T(8,128)(2,1)S(1)}, bf16[32,4096]{1,0:T(8,128)(2,1)S(1)}, u32[]{:S(2)}, u32[]{:S(2)}) collective-permute-start(bf16[32,4096]{1,0:T(8,128)(2,1)S(1)} %pad_maximum_fusion.refs_0_), channel_id=1, source_target_pairs={{0,4},{1,33},{2,6},{3,35},{4,8},{5,37},{6,10},{7,39},{8,12},{9,41}... | collective-permute-start | bytes 786440 | tf_op jit(solution)/shard_map/ppermute | solution.py:309
  42.6 9.5 %collective-permute-start.7 = (bf16[32,4096]{1,0:T(8,128)(2,1)S(1)}, bf16[32,4096]{1,0:T(8,128)(2,1)S(1)}, u32[]{:S(2)}, u32[]{:S(2)}) collective-permute-start(bf16[32,4096]{1,0:T(8,128)(2,1)S(1)} %collective-permute-done.4.refs_4_), channel_id=1, source_target_pairs={{0,8},{1,65},{2,10},{3,67},{4,12},{5,69},{6,14},{7,71},{8,0},{9,73... | collective-permute-start | bytes 786440 | tf_op jit(solution)/shard_map/ppermute | solution.py:309
  43.3 8.8 %collective-permute-start.6 = (bf16[32,4096]{1,0:T(8,128)(2,1)S(1)}, bf16[32,4096]{1,0:T(8,128)(2,1)S(1)}, u32[]{:S(2)}, u32[]{:S(2)}) collective-permute-start(bf16[32,4096]{1,0:T(8,128)(2,1)S(1)} %collective-permute-done.4.refs_4_), channel_id=1, source_target_pairs={{0,12},{1,97},{2,14},{3,99},{4,0},{5,101},{6,2},{7,103},{8,4},{9,1... | collective-permute-start | bytes 786440 | tf_op jit(solution)/shard_map/ppermute | solution.py:309
  45.4 7.9 %collective-permute-start.5 = (bf16[32,4096]{1,0:T(8,128)(2,1)S(1)}, bf16[32,4096]{1,0:T(8,128)(2,1)S(1)}, u32[]{:S(2)}, u32[]{:S(2)}) collective-permute-start(bf16[32,4096]{1,0:T(8,128)(2,1)S(1)} %collective-permute-done.4.refs_4_), channel_id=1, source_target_pairs={{0,4},{1,33},{2,6},{3,35},{4,8},{5,37},{6,10},{7,39},{8,12},{9,41}... | collective-permute-start | bytes 786440 | tf_op jit(solution)/shard_map/ppermute | solution.py:309
  45.4 7.8 %collective-permute-start.8 = (bf16[32,4096]{1,0:T(8,128)(2,1)S(1)}, bf16[32,4096]{1,0:T(8,128)(2,1)S(1)}, u32[]{:S(2)}, u32[]{:S(2)}) collective-permute-start(bf16[32,4096]{1,0:T(8,128)(2,1)S(1)} %shard_map.76), channel_id=1, source_target_pairs={{0,2},{1,3},{2,0},{3,1},{4,6},{5,7},{6,4},{7,5},{8,10},{9,11},{10,... | collective-permute-start | bytes 786440 | tf_op jit(solution)/shard_map/ppermute | solution.py:309
  53.5 13.3 %collective-permute-start.10 = (bf16[128,4096]{1,0:T(8,128)(2,1)S(1)}, bf16[128,4096]{1,0:T(8,128)(2,1)S(1)}, u32[]{:S(2)}, u32[]{:S(2)}) collective-permute-start(bf16[128,4096]{1,0:T(8,128)(2,1)S(1)} %get-tuple-element.25), channel_id=1, source_target_pairs={{0,1},{1,0},{2,3},{3,2},{4,5},{5,4},{6,7},{7,6},{8,9},{9,8},{10,11... | collective-permute-start | bytes 3145736 | tf_op jit(solution)/shard_map/ppermute | solution.py:309
  53.6 19.8 %collective-permute-start.9 = (bf16[128,4096]{1,0:T(8,128)(2,1)S(1)}, bf16[128,4096]{1,0:T(8,128)(2,1)S(1)}, u32[]{:S(2)}, u32[]{:S(2)}) collective-permute-start(bf16[128,4096]{1,0:T(8,128)(2,1)S(1)} %get-tuple-element.24.refs_0_), channel_id=1, source_target_pairs={{0,32},{1,5},{2,34},{3,7},{4,36},{5,9},{6,38},{7,11},{8,40},{9,13}... | collective-permute-start | bytes 3145736 | tf_op jit(solution)/shard_map/ppermute | solution.py:309
  54.2 19.3 %collective-permute-start.13 = (bf16[128,4096]{1,0:T(8,128)(2,1)S(1)}, bf16[128,4096]{1,0:T(8,128)(2,1)S(1)}, u32[]{:S(2)}, u32[]{:S(2)}) collective-permute-start(bf16[128,4096]{1,0:T(8,128)(2,1)S(1)} %get-tuple-element.25), channel_id=1, source_target_pairs={{0,97},{1,12},{2,99},{3,14},{4,101},{5,0},{6,103},{7,2},{8,105},{9... | collective-permute-start | bytes 3145736 | tf_op jit(solution)/shard_map/ppermute | solution.py:309
  56.3 1.6 %collective-permute-start.11 = (bf16[32,4096]{1,0:T(8,128)(2,1)S(1)}, bf16[32,4096]{1,0:T(8,128)(2,1)S(1)}, u32[]{:S(2)}, u32[]{:S(2)}) collective-permute-start(bf16[32,4096]{1,0:T(8,128)(2,1)S(1)} %collective-permute-done.8.refs_8_.own0), channel_id=1, source_target_pairs={{0,1},{1,0},{2,3},{3,2},{4,5},{5,4},{6,7},{7,6},{8,9},{9,8},{10,11... | collective-permute-start | bytes 786440 | tf_op jit(solution)/shard_map/ppermute | solution.py:309
  57.9 25.1 %collective-permute-start.16 = (bf16[128,4096]{1,0:T(8,128)(2,1)S(1)}, bf16[128,4096]{1,0:T(8,128)(2,1)S(1)}, u32[]{:S(2)}, u32[]{:S(2)}) collective-permute-start(bf16[128,4096]{1,0:T(8,128)(2,1)S(1)} %shard_map.84), channel_id=1, source_target_pairs={{0,33},{1,4},{2,35},{3,6},{4,37},{5,8},{6,39},{7,10},{8,41},{9,12}... | collective-permute-start | bytes 3145736 | tf_op jit(solution)/shard_map/ppermute | solution.py:309
  58.0 25.7 %collective-permute-start.15 = (bf16[128,4096]{1,0:T(8,128)(2,1)S(1)}, bf16[128,4096]{1,0:T(8,128)(2,1)S(1)}, u32[]{:S(2)}, u32[]{:S(2)}) collective-permute-start(bf16[128,4096]{1,0:T(8,128)(2,1)S(1)} %shard_map.83), channel_id=1, source_target_pairs={{0,96},{1,13},{2,98},{3,15},{4,100},{5,1},{6,102},{7,3},{8,104},{9... | collective-permute-start | bytes 3145736 | tf_op jit(solution)/shard_map/ppermute | solution.py:309
  73.5 18.7 %collective-permute-start.12 = (bf16[128,4096]{1,0:T(8,128)(2,1)S(1)}, bf16[128,4096]{1,0:T(8,128)(2,1)S(1)}, u32[]{:S(2)}, u32[]{:S(2)}) collective-permute-start(bf16[128,4096]{1,0:T(8,128)(2,1)S(1)} %shard_map.81.refs_0_), channel_id=1, source_target_pairs={{0,32},{1,5},{2,34},{3,7},{4,36},{5,9},{6,38},{7,11},{8,40},{9,13}... | collective-permute-start | bytes 3145736 | tf_op jit(solution)/shard_map/ppermute | solution.py:309
  73.6 18.6 %collective-permute-start.14 = (bf16[128,4096]{1,0:T(8,128)(2,1)S(1)}, bf16[128,4096]{1,0:T(8,128)(2,1)S(1)}, u32[]{:S(2)}, u32[]{:S(2)}) collective-permute-start(bf16[128,4096]{1,0:T(8,128)(2,1)S(1)} %shard_map.82.refs_1_), channel_id=1, source_target_pairs={{0,12},{1,97},{2,14},{3,99},{4,0},{5,101},{6,2},{7,103},{8,4},{9,1... | collective-permute-start | bytes 3145736 | tf_op jit(solution)/shard_map/ppermute | solution.py:309

commit v8 on v7

--- a/solution.py
+++ b/solution.py
@@ -77,10 +77,8 @@
     pick = jnp.where(flat == row.astype(F32), 1.0, 0.0)
     place = (key % WIN * QC + chan % QC + 1).astype(F32)
     place_col = jnp.sum(pick * place, axis=1, keepdims=True)
-    place_all = jnp.broadcast_to(place_col, (SLOTS, TAIL)).astype(BF16)
-    out_ref[:, :, SAMPLES:] = place_all.reshape(DEVICES, SLOTS // DEVICES, TAIL)
-    sent = jnp.dot(pick.astype(BF16), raw_ref[...], preferred_element_type=F32).astype(BF16)
-    out_ref[:, :, :SAMPLES] = sent.reshape(DEVICES, SLOTS // DEVICES, SAMPLES)
+    out_ref[:, SAMPLES:] = jnp.broadcast_to(place_col, (SLOTS, TAIL)).astype(BF16)
+    out_ref[:, :SAMPLES] = jnp.dot(pick.astype(BF16), raw_ref[...], preferred_element_type=F32).astype(BF16)
 
 
 def fetch_kernel(after_hbm, basis_hbm, taper_hbm, turn_hbm, basis_ref, taper_ref, turn_ref, sem):
@@ -339,11 +337,11 @@
         pack_kernel,
         in_specs=[SMEM, VMEM, VMEM],
         out_specs=VMEM,
-        out_shape=jax.ShapeDtypeStruct((DEVICES, SLOTS // DEVICES, SAMPLES + TAIL), BF16),
+        out_shape=jax.ShapeDtypeStruct((SLOTS, SAMPLES + TAIL), BF16),
         compiler_params=pltpu.CompilerParams(vmem_limit_bytes=8 * MIB),
     )(file_count, (seg_chan * WIN + seg_win).reshape(1, SLOTS), raw)
     arrived = lax.all_to_all(
-        packed,
+        packed.reshape(DEVICES, SLOTS // DEVICES, SAMPLES + TAIL),
         ("blk", "freq"),
         split_axis=0,
         concat_axis=0,

time: 100 us -> 101 us (1.010)
  local copies, waits for them, and re-layouts: 4.52 us -> 5.56 us
    reshape x1 -> x2, local copies, waits for them, and re-layouts: 0.22 us -> 1.26 us  [the longest x1 1.04 us: local(): packed.reshape(DEVICES, SLOTS // DEVICES, SAMPLES + TAIL)]
where the time goes in v8:
time: 101 us; the launch traced here: 99.7 us
  Pallas kernels  42.2 us (42%)
  starting transfers between devices  28.2 us (28%)
  waiting for transfers between devices  21.9 us (22%)
  local copies, waits for them, and re-layouts  5.56 us (6%)
  between operations  1.09 us (1%)
    pallas_call x4, Pallas kernels, matmul(): pl.pallas_call(functools.partial(matmul_kernel, sources, len(arrays)), in...  28.1 us
    ppermute x17, starting transfers between devices, permuted(): return lax.ppermute(value, ('blk', 'freq'), pairs)  17 us
    pallas_call x2, Pallas kernels, rotate(): pl.pallas_call(functools.partial(rotate_kernel, halves), in_specs=[SMEM,...  11.5 us
    ppermute x17, waiting for transfers between devices, permuted(): return lax.ppermute(value, ('blk', 'freq'), pairs)  11.2 us
    all_to_all x1, starting transfers between devices, local(): lax.all_to_all(packed.reshape(DEVICES, SLOTS // DEVICES, SAMPLES + TAIL),...  11.2 us
    all_to_all x1, waiting for transfers between devices, local(): lax.all_to_all(packed.reshape(DEVICES, SLOTS // DEVICES, SAMPLES + TAIL),...  10.7 us
    unnamed x8, local copies, waits for them, and re-layouts  4.2 us
  transfers between devices with their start and end apart: 18, of which 7 were waited for; matrix products, arithmetic and copies ran while one was open for 0% of the time, Pallas kernels for 33%

profile of v8, /device:TPU:0, one launch (start us, length us, event | category | flops | bytes accessed | tf_op | source)
XLA Modules:
  0.0 99.7 jit_solution(3711545512418461906)
XLA Ops:
  1.4 1.0 %copy-done.1 = bf16[256,1024]{1,0:T(8,128)(2,1)S(1)} copy-done((bf16[256,1024]{1,0:T(8,128)(2,1)S(1)}, bf16[256,1024]{1,0:T(8,128)(2,1)}, u32[]{:S(2)}) %copy-start.1) | copy-done | bytes 524312
  2.8 1.0 %reshape.13 = bf16[128,2,1152]{2,1,0:T(2,128)(2,1)} reshape(bf16[256,1152]{1,0:T(8,128)(2,1)S(1)} %shard_map.73.after_hbm) | data formatting | bytes 1179648 | tf_op jit(solution)/shard_map/reshape | solution.py:344
  3.9 11.2 %all-to-all-start = ((bf16[128,2,1152]{2,1,0:T(2,128)(2,1)}), bf16[128,2,1152]{2,1,0:T(2,128)(2,1)S(1)}, u32[]{:S(2)}, u32[]{:S(2)}) async-start(bf16[128,2,1152]{2,1,0:T(2,128)(2,1)} %reshape.13), calls=%async_computation | async-start | bytes 1179648 | tf_op jit(solution)/shard_map/all_to_all | solution.py:343
  15.0 1.6 %copy-done = bf16[1024,1024]{1,0:T(8,128)(2,1)S(1)} copy-done((bf16[1024,1024]{1,0:T(8,128)(2,1)S(1)}, bf16[1024,1024]{1,0:T(8,128)(2,1)}, u32[]{:S(2)}) %copy-start) | copy-done | bytes 2097176
  18.6 10.7 %all-to-all-done = bf16[128,2,1152]{2,1,0:T(2,128)(2,1)S(1)} async-done(((bf16[128,2,1152]{2,1,0:T(2,128)(2,1)}), bf16[128,2,1152]{2,1,0:T(2,128)(2,1)S(1)}, u32[]{:S(2)}, u32[]{:S(2)}) %all-to-all-start) | async-done | bytes 589856 | tf_op jit(solution)/shard_map/all_to_all | solution.py:343
  29.5 1.7 %shard_map.75.own0 = bf16[32,4096]{1,0:T(8,128)(2,1)S(1)} custom-call(s32[5]{0:T(128)S(1)} %stack.23.place_ref, bf16[256,1152]{1,0:T(8,128)(2,1)S(1)} %reshape.14.recv_ref, bf16[1024,1024]{1,0:T(8,128)(2,1)S(1)} %get-tuple-element.20.basis_ref, f32[1,1024]{1,0:T(1,128)S(1)} %get-tuple-element.21.taper_ref), custom_call_target="tpu_custom_call" | custom-call | tf_op jit(solution)/shard_map/pallas_call | solution.py:359
  31.3 1.5 %collective-permute-done.own1 = bf16[32,4096]{1,0:T(8,128)(2,1)S(1)} collective-permute-done((bf16[32,4096]{1,0:T(8,128)(2,1)S(1)}, bf16[32,4096]{1,0:T(8,128)(2,1)S(1)}, u32[]{:S(2)}, u32[]{:S(2)}) %collective-permute-start) | collective-permute-done | bytes 262176 | tf_op jit(solution)/shard_map/ppermute | solution.py:307
  32.9 1.2 %collective-permute-start.4 = (bf16[32,4096]{1,0:T(8,128)(2,1)S(1)}, bf16[32,4096]{1,0:T(8,128)(2,1)S(1)}, u32[]{:S(2)}, u32[]{:S(2)}) collective-permute-start(bf16[32,4096]{1,0:T(8,128)(2,1)S(1)} %pad_maximum_fusion.refs_0_), channel_id=1, source_target_pairs={{0,16},{1,17},{2,18},{3,19},{4,20},{5,21},{6,22},{7,23},{8,24},{9,... | collective-permute-start | bytes 786440 | tf_op jit(solution)/shard_map/ppermute | solution.py:307
  34.9 2.5 %collective-permute-start.2 = (bf16[32,4096]{1,0:T(8,128)(2,1)S(1)}, bf16[32,4096]{1,0:T(8,128)(2,1)S(1)}, u32[]{:S(2)}, u32[]{:S(2)}) collective-permute-start(bf16[32,4096]{1,0:T(8,128)(2,1)S(1)} %pad_maximum_fusion.refs_0_), channel_id=1, source_target_pairs={{0,12},{1,97},{2,14},{3,99},{4,0},{5,101},{6,2},{7,103},{8,4},{9,1... | collective-permute-start | bytes 786440 | tf_op jit(solution)/shard_map/ppermute | solution.py:307
  37.4 5.4 %collective-permute-done.4.refs_4_ = bf16[32,4096]{1,0:T(8,128)(2,1)S(1)} collective-permute-done((bf16[32,4096]{1,0:T(8,128)(2,1)S(1)}, bf16[32,4096]{1,0:T(8,128)(2,1)S(1)}, u32[]{:S(2)}, u32[]{:S(2)}) %collective-permute-start.4) | collective-permute-done | bytes 262176 | tf_op jit(solution)/shard_map/ppermute | solution.py:307
  43.6 2.0 %collective-permute-start.6 = (bf16[32,4096]{1,0:T(8,128)(2,1)S(1)}, bf16[32,4096]{1,0:T(8,128)(2,1)S(1)}, u32[]{:S(2)}, u32[]{:S(2)}) collective-permute-start(bf16[32,4096]{1,0:T(8,128)(2,1)S(1)} %collective-permute-done.4.refs_4_), channel_id=1, source_target_pairs={{0,12},{1,97},{2,14},{3,99},{4,0},{5,101},{6,2},{7,103},{8,4},{9,1... | collective-permute-start | bytes 786440 | tf_op jit(solution)/shard_map/ppermute | solution.py:307
  45.6 0.9 collective-permute-start.8
  46.6 5.8 %shard_map.77 = (bf16[4096,1024]{1,0:T(8,128)(2,1)S(1)}, f32[8,128]{1,0:T(8,128)S(1)}) custom-call(s32[5]{0:T(128)S(1)} %stack.23.place_ref, bf16[32,4096]{1,0:T(8,128)(2,1)S(1)} %shard_map.75.own0, bf16[32,4096]{1,0:T(8,128)(2,1)S(1)} %collective-permute-done.own1, f32[144,128]{1,0:T(8,128)S(1)} %get-tuple-element.22.small_ref), custom_call_target="tpu_custom_call" | custom-call | flops 1024 | bytes 1024 | tf_op jit(solution)/shard_map/pallas_call | solution.py:209
  52.3 1.1 %collective-permute-done.5.refs_5_ = bf16[32,4096]{1,0:T(8,128)(2,1)S(1)} collective-permute-done((bf16[32,4096]{1,0:T(8,128)(2,1)S(1)}, bf16[32,4096]{1,0:T(8,128)(2,1)S(1)}, u32[]{:S(2)}, u32[]{:S(2)}) %collective-permute-start.5) | collective-permute-done | bytes 262176 | tf_op jit(solution)/shard_map/ppermute | solution.py:307
  54.4 2.1 %collective-permute-start.13 = (bf16[128,4096]{1,0:T(8,128)(2,1)S(1)}, bf16[128,4096]{1,0:T(8,128)(2,1)S(1)}, u32[]{:S(2)}, u32[]{:S(2)}) collective-permute-start(bf16[128,4096]{1,0:T(8,128)(2,1)S(1)} %get-tuple-element.25), channel_id=1, source_target_pairs={{0,97},{1,12},{2,99},{3,14},{4,101},{5,0},{6,103},{7,2},{8,105},{9... | collective-permute-start | bytes 3145736 | tf_op jit(solution)/shard_map/ppermute | solution.py:307
  57.0 1.2 %collective-permute-done.11.own1.refs_1_ = bf16[32,4096]{1,0:T(8,128)(2,1)S(1)} collective-permute-done((bf16[32,4096]{1,0:T(8,128)(2,1)S(1)}, bf16[32,4096]{1,0:T(8,128)(2,1)S(1)}, u32[]{:S(2)}, u32[]{:S(2)}) %collective-permute-start.11) | collective-permute-done | bytes 262176 | tf_op jit(solution)/shard_map/ppermute | solution.py:307
  58.2 3.2 %collective-permute-start.15 = (bf16[128,4096]{1,0:T(8,128)(2,1)S(1)}, bf16[128,4096]{1,0:T(8,128)(2,1)S(1)}, u32[]{:S(2)}, u32[]{:S(2)}) collective-permute-start(bf16[128,4096]{1,0:T(8,128)(2,1)S(1)} %shard_map.83), channel_id=1, source_target_pairs={{0,96},{1,13},{2,98},{3,15},{4,100},{5,1},{6,102},{7,3},{8,104},{9... | collective-permute-start | bytes 3145736 | tf_op jit(solution)/shard_map/ppermute | solution.py:307
  61.4 5.7 %shard_map.79 = (bf16[4096,1024]{1,0:T(8,128)(2,1)S(1)}, f32[8,128]{1,0:T(8,128)}) custom-call(s32[5]{0:T(128)S(1)} %stack.23.place_ref, bf16[32,4096]{1,0:T(8,128)(2,1)S(1)} %collective-permute-done.8.refs_8_.own0, bf16[32,4096]{1,0:T(8,128)(2,1)S(1)} %collective-permute-done.11.own1.refs_1_, f32[144,128]{1,0:T(8,128)S(1)} %get-tuple-element.22.small_ref), custom_call_target="tpu_custom_call" | custom-call | flops 1024 | bytes 1024 | tf_op jit(solution)/shard_map/pallas_call | solution.py:209
  67.1 6.6 %shard_map.80 = (f32[64,16,2048]{2,1,0:T(8,128)}, f32[8,128]{1,0:T(8,128)S(1)}) custom-call(s32[5]{0:T(128)S(1)} %stack.23.place_ref, bf16[128,4096]{1,0:T(8,128)(2,1)S(1)} %get-tuple-element.24.refs_0_, bf16[128,4096]{1,0:T(8,128)(2,1)S(1)} %collective-permute-done.10.refs_1_, bf16[4096,1024]{1,0:T(8,128)(2,1)S(1)} %get-tuple-element.26.refs_2_, ...), custom_call_target="tpu_custom_call" | custom-call | flops 1024 | bytes 1024 | tf_op jit(solution)/shard_map/pallas_call | solution.py:283
  73.8 2.2 %collective-permute-start.14 = (bf16[128,4096]{1,0:T(8,128)(2,1)S(1)}, bf16[128,4096]{1,0:T(8,128)(2,1)S(1)}, u32[]{:S(2)}, u32[]{:S(2)}) collective-permute-start(bf16[128,4096]{1,0:T(8,128)(2,1)S(1)} %shard_map.82.refs_1_), channel_id=1, source_target_pairs={{0,12},{1,97},{2,14},{3,99},{4,0},{5,101},{6,2},{7,103},{8,4},{9,1... | collective-permute-start | bytes 3145736 | tf_op jit(solution)/shard_map/ppermute | solution.py:307
  76.0 7.2 %shard_map.85 = (f32[64,16,2048]{2,1,0:T(8,128)}, f32[8,128]{1,0:T(8,128)}) custom-call(s32[5]{0:T(128)S(1)} %stack.23.place_ref, bf16[128,4096]{1,0:T(8,128)(2,1)S(1)} %shard_map.81.refs_0_, bf16[128,4096]{1,0:T(8,128)(2,1)S(1)} %shard_map.82.refs_1_, bf16[4096,1024]{1,0:T(8,128)(2,1)S(1)} %get-tuple-element.26.refs_2_, ...), custom_call_target="tpu_custom_call", output_to_operand_aliasing={{0}: (5, {})} | custom-call | flops 1024 | bytes 1024 | tf_op jit(solution)/shard_map/pallas_call | solution.py:283
  83.9 7.2 %shard_map.86 = (f32[64,16,2048]{2,1,0:T(8,128)}, f32[8,128]{1,0:T(8,128)}) custom-call(s32[5]{0:T(128)S(1)} %stack.23.place_ref, bf16[128,4096]{1,0:T(8,128)(2,1)S(1)} %collective-permute-done.15.refs_0_, bf16[128,4096]{1,0:T(8,128)(2,1)S(1)} %collective-permute-done.16.refs_1_, ...), custom_call_target="tpu_custom_call", output_to_operand_aliasing={{0}: (5, {})} | custom-call | flops 1024 | bytes 1024 | tf_op jit(solution)/shard_map/pallas_call | solution.py:283
  91.0 1.3 %collective-permute-done.12.refs_0_ = bf16[128,4096]{1,0:T(8,128)(2,1)S(1)} collective-permute-done((bf16[128,4096]{1,0:T(8,128)(2,1)S(1)}, bf16[128,4096]{1,0:T(8,128)(2,1)S(1)}, u32[]{:S(2)}, u32[]{:S(2)}) %collective-permute-start.12) | collective-permute-done | bytes 1048608 | tf_op jit(solution)/shard_map/ppermute | solution.py:307
  92.4 7.2 %shard_map.87 = (f32[64,16,2048]{2,1,0:T(8,128)}, f32[8,128]{1,0:T(8,128)}) custom-call(s32[5]{0:T(128)S(1)} %stack.23.place_ref, bf16[128,4096]{1,0:T(8,128)(2,1)S(1)} %collective-permute-done.12.refs_0_, bf16[128,4096]{1,0:T(8,128)(2,1)S(1)} %collective-permute-done.14.refs_1_, ...), custom_call_target="tpu_custom_call", output_to_operand_aliasing={{0}: (5, {})} | custom-call | flops 1024 | bytes 1024 | tf_op jit(solution)/shard_map/pallas_call | solution.py:283
  (42 shorter events, 7.2 us)
Async XLA Ops:
  1.4 1.0 %copy-start.1 = (bf16[256,1024]{1,0:T(8,128)(2,1)S(1)}, bf16[256,1024]{1,0:T(8,128)(2,1)}, u32[]{:S(2)}) copy-start(bf16[256,1024]{1,0:T(8,128)(2,1)} %raw_ref.1) | copy-start | bytes 1572868
  3.9 25.4 %all-to-all-start = ((bf16[128,2,1152]{2,1,0:T(2,128)(2,1)}), bf16[128,2,1152]{2,1,0:T(2,128)(2,1)S(1)}, u32[]{:S(2)}, u32[]{:S(2)}) async-start(bf16[128,2,1152]{2,1,0:T(2,128)(2,1)} %reshape.13), calls=%async_computation | async-start | bytes 1179648 | tf_op jit(solution)/shard_map/all_to_all | solution.py:343
  15.0 1.6 %copy-start = (bf16[1024,1024]{1,0:T(8,128)(2,1)S(1)}, bf16[1024,1024]{1,0:T(8,128)(2,1)}, u32[]{:S(2)}) copy-start(bf16[1024,1024]{1,0:T(8,128)(2,1)} %constant.72.clone.basis_hbm) | copy-start | bytes 6291460
  16.6 0.9 copy-start.2
  17.5 0.7 copy-start.3
  31.2 1.6 %collective-permute-start = (bf16[32,4096]{1,0:T(8,128)(2,1)S(1)}, bf16[32,4096]{1,0:T(8,128)(2,1)S(1)}, u32[]{:S(2)}, u32[]{:S(2)}) collective-permute-start(bf16[32,4096]{1,0:T(8,128)(2,1)S(1)} %shard_map.75.own0), channel_id=1, source_target_pairs={{0,1},{1,0},{2,3},{3,2},{4,5},{5,4},{6,7},{7,6},{8,9},{9,8},{10,11... | collective-permute-start | bytes 786440 | tf_op jit(solution)/shard_map/ppermute | solution.py:307
  32.9 9.9 %collective-permute-start.4 = (bf16[32,4096]{1,0:T(8,128)(2,1)S(1)}, bf16[32,4096]{1,0:T(8,128)(2,1)S(1)}, u32[]{:S(2)}, u32[]{:S(2)}) collective-permute-start(bf16[32,4096]{1,0:T(8,128)(2,1)S(1)} %pad_maximum_fusion.refs_0_), channel_id=1, source_target_pairs={{0,16},{1,17},{2,18},{3,19},{4,20},{5,21},{6,22},{7,23},{8,24},{9,... | collective-permute-start | bytes 786440 | tf_op jit(solution)/shard_map/ppermute | solution.py:307
  34.1 11.5 %collective-permute-start.3 = (bf16[32,4096]{1,0:T(8,128)(2,1)S(1)}, bf16[32,4096]{1,0:T(8,128)(2,1)S(1)}, u32[]{:S(2)}, u32[]{:S(2)}) collective-permute-start(bf16[32,4096]{1,0:T(8,128)(2,1)S(1)} %pad_maximum_fusion.refs_0_), channel_id=1, source_target_pairs={{0,8},{1,65},{2,10},{3,67},{4,12},{5,69},{6,14},{7,71},{8,0},{9,73... | collective-permute-start | bytes 786440 | tf_op jit(solution)/shard_map/ppermute | solution.py:307
  34.9 10.7 %collective-permute-start.2 = (bf16[32,4096]{1,0:T(8,128)(2,1)S(1)}, bf16[32,4096]{1,0:T(8,128)(2,1)S(1)}, u32[]{:S(2)}, u32[]{:S(2)}) collective-permute-start(bf16[32,4096]{1,0:T(8,128)(2,1)S(1)} %pad_maximum_fusion.refs_0_), channel_id=1, source_target_pairs={{0,12},{1,97},{2,14},{3,99},{4,0},{5,101},{6,2},{7,103},{8,4},{9,1... | collective-permute-start | bytes 786440 | tf_op jit(solution)/shard_map/ppermute | solution.py:307
  37.4 8.2 %collective-permute-start.1 = (bf16[32,4096]{1,0:T(8,128)(2,1)S(1)}, bf16[32,4096]{1,0:T(8,128)(2,1)S(1)}, u32[]{:S(2)}, u32[]{:S(2)}) collective-permute-start(bf16[32,4096]{1,0:T(8,128)(2,1)S(1)} %pad_maximum_fusion.refs_0_), channel_id=1, source_target_pairs={{0,4},{1,33},{2,6},{3,35},{4,8},{5,37},{6,10},{7,39},{8,12},{9,41}... | collective-permute-start | bytes 786440 | tf_op jit(solution)/shard_map/ppermute | solution.py:307
  42.8 9.5 %collective-permute-start.7 = (bf16[32,4096]{1,0:T(8,128)(2,1)S(1)}, bf16[32,4096]{1,0:T(8,128)(2,1)S(1)}, u32[]{:S(2)}, u32[]{:S(2)}) collective-permute-start(bf16[32,4096]{1,0:T(8,128)(2,1)S(1)} %collective-permute-done.4.refs_4_), channel_id=1, source_target_pairs={{0,8},{1,65},{2,10},{3,67},{4,12},{5,69},{6,14},{7,71},{8,0},{9,73... | collective-permute-start | bytes 786440 | tf_op jit(solution)/shard_map/ppermute | solution.py:307
  43.6 8.8 %collective-permute-start.6 = (bf16[32,4096]{1,0:T(8,128)(2,1)S(1)}, bf16[32,4096]{1,0:T(8,128)(2,1)S(1)}, u32[]{:S(2)}, u32[]{:S(2)}) collective-permute-start(bf16[32,4096]{1,0:T(8,128)(2,1)S(1)} %collective-permute-done.4.refs_4_), channel_id=1, source_target_pairs={{0,12},{1,97},{2,14},{3,99},{4,0},{5,101},{6,2},{7,103},{8,4},{9,1... | collective-permute-start | bytes 786440 | tf_op jit(solution)/shard_map/ppermute | solution.py:307
  45.6 7.9 %collective-permute-start.5 = (bf16[32,4096]{1,0:T(8,128)(2,1)S(1)}, bf16[32,4096]{1,0:T(8,128)(2,1)S(1)}, u32[]{:S(2)}, u32[]{:S(2)}) collective-permute-start(bf16[32,4096]{1,0:T(8,128)(2,1)S(1)} %collective-permute-done.4.refs_4_), channel_id=1, source_target_pairs={{0,4},{1,33},{2,6},{3,35},{4,8},{5,37},{6,10},{7,39},{8,12},{9,41}... | collective-permute-start | bytes 786440 | tf_op jit(solution)/shard_map/ppermute | solution.py:307
  45.6 7.8 %collective-permute-start.8 = (bf16[32,4096]{1,0:T(8,128)(2,1)S(1)}, bf16[32,4096]{1,0:T(8,128)(2,1)S(1)}, u32[]{:S(2)}, u32[]{:S(2)}) collective-permute-start(bf16[32,4096]{1,0:T(8,128)(2,1)S(1)} %shard_map.76), channel_id=1, source_target_pairs={{0,2},{1,3},{2,0},{3,1},{4,6},{5,7},{6,4},{7,5},{8,10},{9,11},{10,... | collective-permute-start | bytes 786440 | tf_op jit(solution)/shard_map/ppermute | solution.py:307
  53.7 13.3 %collective-permute-start.10 = (bf16[128,4096]{1,0:T(8,128)(2,1)S(1)}, bf16[128,4096]{1,0:T(8,128)(2,1)S(1)}, u32[]{:S(2)}, u32[]{:S(2)}) collective-permute-start(bf16[128,4096]{1,0:T(8,128)(2,1)S(1)} %get-tuple-element.25), channel_id=1, source_target_pairs={{0,1},{1,0},{2,3},{3,2},{4,5},{5,4},{6,7},{7,6},{8,9},{9,8},{10,11... | collective-permute-start | bytes 3145736 | tf_op jit(solution)/shard_map/ppermute | solution.py:307
  53.8 19.8 %collective-permute-start.9 = (bf16[128,4096]{1,0:T(8,128)(2,1)S(1)}, bf16[128,4096]{1,0:T(8,128)(2,1)S(1)}, u32[]{:S(2)}, u32[]{:S(2)}) collective-permute-start(bf16[128,4096]{1,0:T(8,128)(2,1)S(1)} %get-tuple-element.24.refs_0_), channel_id=1, source_target_pairs={{0,32},{1,5},{2,34},{3,7},{4,36},{5,9},{6,38},{7,11},{8,40},{9,13}... | collective-permute-start | bytes 3145736 | tf_op jit(solution)/shard_map/ppermute | solution.py:307
  54.4 19.3 %collective-permute-start.13 = (bf16[128,4096]{1,0:T(8,128)(2,1)S(1)}, bf16[128,4096]{1,0:T(8,128)(2,1)S(1)}, u32[]{:S(2)}, u32[]{:S(2)}) collective-permute-start(bf16[128,4096]{1,0:T(8,128)(2,1)S(1)} %get-tuple-element.25), channel_id=1, source_target_pairs={{0,97},{1,12},{2,99},{3,14},{4,101},{5,0},{6,103},{7,2},{8,105},{9... | collective-permute-start | bytes 3145736 | tf_op jit(solution)/shard_map/ppermute | solution.py:307
  56.5 1.6 %collective-permute-start.11 = (bf16[32,4096]{1,0:T(8,128)(2,1)S(1)}, bf16[32,4096]{1,0:T(8,128)(2,1)S(1)}, u32[]{:S(2)}, u32[]{:S(2)}) collective-permute-start(bf16[32,4096]{1,0:T(8,128)(2,1)S(1)} %collective-permute-done.8.refs_8_.own0), channel_id=1, source_target_pairs={{0,1},{1,0},{2,3},{3,2},{4,5},{5,4},{6,7},{7,6},{8,9},{9,8},{10,11... | collective-permute-start | bytes 786440 | tf_op jit(solution)/shard_map/ppermute | solution.py:307
  58.1 25.1 %collective-permute-start.16 = (bf16[128,4096]{1,0:T(8,128)(2,1)S(1)}, bf16[128,4096]{1,0:T(8,128)(2,1)S(1)}, u32[]{:S(2)}, u32[]{:S(2)}) collective-permute-start(bf16[128,4096]{1,0:T(8,128)(2,1)S(1)} %shard_map.84), channel_id=1, source_target_pairs={{0,33},{1,4},{2,35},{3,6},{4,37},{5,8},{6,39},{7,10},{8,41},{9,12}... | collective-permute-start | bytes 3145736 | tf_op jit(solution)/shard_map/ppermute | solution.py:307
  58.2 25.7 %collective-permute-start.15 = (bf16[128,4096]{1,0:T(8,128)(2,1)S(1)}, bf16[128,4096]{1,0:T(8,128)(2,1)S(1)}, u32[]{:S(2)}, u32[]{:S(2)}) collective-permute-start(bf16[128,4096]{1,0:T(8,128)(2,1)S(1)} %shard_map.83), channel_id=1, source_target_pairs={{0,96},{1,13},{2,98},{3,15},{4,100},{5,1},{6,102},{7,3},{8,104},{9... | collective-permute-start | bytes 3145736 | tf_op jit(solution)/shard_map/ppermute | solution.py:307
  73.7 18.7 %collective-permute-start.12 = (bf16[128,4096]{1,0:T(8,128)(2,1)S(1)}, bf16[128,4096]{1,0:T(8,128)(2,1)S(1)}, u32[]{:S(2)}, u32[]{:S(2)}) collective-permute-start(bf16[128,4096]{1,0:T(8,128)(2,1)S(1)} %shard_map.81.refs_0_), channel_id=1, source_target_pairs={{0,32},{1,5},{2,34},{3,7},{4,36},{5,9},{6,38},{7,11},{8,40},{9,13}... | collective-permute-start | bytes 3145736 | tf_op jit(solution)/shard_map/ppermute | solution.py:307
  73.8 18.6 %collective-permute-start.14 = (bf16[128,4096]{1,0:T(8,128)(2,1)S(1)}, bf16[128,4096]{1,0:T(8,128)(2,1)S(1)}, u32[]{:S(2)}, u32[]{:S(2)}) collective-permute-start(bf16[128,4096]{1,0:T(8,128)(2,1)S(1)} %shard_map.82.refs_1_), channel_id=1, source_target_pairs={{0,12},{1,97},{2,14},{3,99},{4,0},{5,101},{6,2},{7,103},{8,4},{9,1... | collective-permute-start | bytes 3145736 | tf_op jit(solution)/shard_map/ppermute | solution.py:307

commit v9 on v8

--- a/solution.py
+++ b/solution.py
@@ -110,7 +110,7 @@
     return total / count.astype(F32)
 
 
-def whiten_kernel(place_ref, recv_ref, basis_ref, taper_ref, out_ref):
+def whiten_kernel(place_ref, recv_ref, basis_ref, taper_ref, keep_ref, give_ref):
     place_col = recv_ref[:, SAMPLES : SAMPLES + 1].astype(F32)
     place = jnp.sum(jnp.where(diagonal(SLOTS), place_col, 0.0), axis=0, keepdims=True)
     row = lax.broadcasted_iota(jnp.int32, (SEG_DEV, SLOTS), 0)
@@ -124,9 +124,10 @@
     inverse = lax.rsqrt(band_mean(real * real + imag * imag) + EPSILON)
     real, imag = (real * inverse).astype(BF16), (imag * inverse).astype(BF16)
     for w in range(WIN):
-        rows = slice(w * QC, (w + 1) * QC)
-        out_ref[:, 2 * w * FREQS : (2 * w + 1) * FREQS] = real[rows]
-        out_ref[:, (2 * w + 1) * FREQS : (2 * w + 2) * FREQS] = imag[rows]
+        for h, out_ref in enumerate((keep_ref, give_ref)):
+            rows = slice(w * QC + h * HALF, w * QC + (h + 1) * HALF)
+            out_ref[:, 2 * w * FREQS : (2 * w + 1) * FREQS] = real[rows]
+            out_ref[:, (2 * w + 1) * FREQS : (2 * w + 2) * FREQS] = imag[rows]
 
 
 def group_kernel(moves, n_in, *refs):
@@ -356,20 +357,19 @@
         compiler_params=pltpu.CompilerParams(vmem_limit_bytes=MIB),
         cost_estimate=SMALL,
     )(packed, basis, taper, turn)
-    white = pl.pallas_call(
+    keep, give = pl.pallas_call(
         whiten_kernel,
         in_specs=[SMEM] + [VMEM] * 3,
-        out_specs=VMEM,
-        out_shape=jax.ShapeDtypeStruct((QC, SPEC), BF16),
+        out_specs=[VMEM] * 2,
+        out_shape=[jax.ShapeDtypeStruct((HALF, SPEC), BF16)] * 2,
         compiler_params=pltpu.CompilerParams(vmem_limit_bytes=8 * MIB),
     )(place, arrived, basis, taper)
 
-    sib = sibling(white)
-    unit = jnp.concatenate([white[:HALF], sib[HALF:]], axis=0)
+    unit = jnp.concatenate([keep, sibling(give)], axis=0)
     beyond = across(unit)
     ahead, behind = first(unit, 1), first(unit, -1)
     opposite = first(unit, 2)
-    near_side, token = rotate(place, [(0, 0), (0, 1), (1, 1), (1, 0)], white, sib, turn)
+    near_side, token = rotate(place, [(0, 0), (1, 0), (1, 1), (0, 1)], unit, sibling(unit), turn)
     beyond_ahead, beyond_behind, beyond_opposite = first(beyond, 1), first(beyond, -1), first(beyond, 2)
     (turned,) = grouped([(0, h, 0, h) for h in range(2)], [2], [unit], [ahead, behind, opposite])
     facing = neighbour(turned)

time: 101 us -> 100 us (0.990)
    ppermute x17 -> x18, waiting for transfers between devices: 11.2 us -> 11.1 us  [permuted(): return lax.ppermute(value, ('blk', 'freq'), pairs)]
    ppermute x17 -> x18, starting transfers between devices: 17 us -> 17.1 us  [permuted(): return lax.ppermute(value, ('blk', 'freq'), pairs)]
    unnamed x8 -> x9, local copies, waits for them, and re-layouts: 4.2 us -> 4.21 us
  transfers between devices with their start and end apart: 18 -> 19, of which waited for: 7 -> 7; matrix products, arithmetic and copies ran while one was open for 0% -> 0% of each run, Pallas kernels for 33% -> 33%
where the time goes in v9:
time: 100 us; the launch traced here: 99.5 us
  Pallas kernels  42.2 us (42%)
  starting transfers between devices  28.2 us (28%)
  waiting for transfers between devices  21.8 us (22%)
  local copies, waits for them, and re-layouts  5.56 us (6%)
  between operations  1.07 us (1%)
    pallas_call x4, Pallas kernels, matmul(): pl.pallas_call(functools.partial(matmul_kernel, sources, len(arrays)), in...  28.1 us
    ppermute x18, starting transfers between devices, permuted(): return lax.ppermute(value, ('blk', 'freq'), pairs)  17.1 us
    pallas_call x2, Pallas kernels, rotate(): pl.pallas_call(functools.partial(rotate_kernel, halves), in_specs=[SMEM,...  11.5 us
    all_to_all x1, starting transfers between devices, local(): lax.all_to_all(packed.reshape(DEVICES, SLOTS // DEVICES, SAMPLES + TAIL),...  11.2 us
    ppermute x18, waiting for transfers between devices, permuted(): return lax.ppermute(value, ('blk', 'freq'), pairs)  11.1 us
    all_to_all x1, waiting for transfers between devices, local(): lax.all_to_all(packed.reshape(DEVICES, SLOTS // DEVICES, SAMPLES + TAIL),...  10.7 us
    unnamed x9, local copies, waits for them, and re-layouts  4.21 us
  transfers between devices with their start and end apart: 19, of which 7 were waited for; matrix products, arithmetic and copies ran while one was open for 0% of the time, Pallas kernels for 33%

profile of v9, /device:TPU:0, one launch (start us, length us, event | category | flops | bytes accessed | tf_op | source)
XLA Modules:
  0.0 99.5 jit_solution(13322725643582229227)
XLA Ops:
  1.4 1.0 %copy-done.1 = bf16[256,1024]{1,0:T(8,128)(2,1)S(1)} copy-done((bf16[256,1024]{1,0:T(8,128)(2,1)S(1)}, bf16[256,1024]{1,0:T(8,128)(2,1)}, u32[]{:S(2)}) %copy-start.1) | copy-done | bytes 524312
  2.8 1.0 %reshape.13 = bf16[128,2,1152]{2,1,0:T(2,128)(2,1)} reshape(bf16[256,1152]{1,0:T(8,128)(2,1)S(1)} %shard_map.73.after_hbm) | data formatting | bytes 1179648 | tf_op jit(solution)/shard_map/reshape | solution.py:345
  3.9 11.2 %all-to-all-start = ((bf16[128,2,1152]{2,1,0:T(2,128)(2,1)}), bf16[128,2,1152]{2,1,0:T(2,128)(2,1)S(1)}, u32[]{:S(2)}, u32[]{:S(2)}) async-start(bf16[128,2,1152]{2,1,0:T(2,128)(2,1)} %reshape.13), calls=%async_computation | async-start | bytes 1179648 | tf_op jit(solution)/shard_map/all_to_all | solution.py:344
  15.0 1.6 %copy-done = bf16[1024,1024]{1,0:T(8,128)(2,1)S(1)} copy-done((bf16[1024,1024]{1,0:T(8,128)(2,1)S(1)}, bf16[1024,1024]{1,0:T(8,128)(2,1)}, u32[]{:S(2)}) %copy-start) | copy-done | bytes 2097176
  18.6 10.7 %all-to-all-done = bf16[128,2,1152]{2,1,0:T(2,128)(2,1)S(1)} async-done(((bf16[128,2,1152]{2,1,0:T(2,128)(2,1)}), bf16[128,2,1152]{2,1,0:T(2,128)(2,1)S(1)}, u32[]{:S(2)}, u32[]{:S(2)}) %all-to-all-start) | async-done | bytes 589856 | tf_op jit(solution)/shard_map/all_to_all | solution.py:344
  29.5 1.7 %shard_map.75 = (bf16[16,4096]{1,0:T(8,128)(2,1)S(1)}, bf16[16,4096]{1,0:T(8,128)(2,1)S(1)}) custom-call(s32[5]{0:T(128)S(1)} %stack.23.place_ref, bf16[256,1152]{1,0:T(8,128)(2,1)S(1)} %reshape.14.recv_ref, bf16[1024,1024]{1,0:T(8,128)(2,1)S(1)} %get-tuple-element.22.basis_ref, f32[1,1024]{1,0:T(1,128)S(1)} %get-tuple-element.23.taper_ref), custom_call_target="tpu_custom_call" | custom-call | tf_op jit(solution)/shard_map/pallas_call | solution.py:360
  31.3 1.3 %collective-permute-done = bf16[16,4096]{1,0:T(8,128)(2,1)S(1)} collective-permute-done((bf16[16,4096]{1,0:T(8,128)(2,1)S(1)}, bf16[16,4096]{1,0:T(8,128)(2,1)S(1)}, u32[]{:S(2)}, u32[]{:S(2)}) %collective-permute-start) | collective-permute-done | bytes 131104 | tf_op jit(solution)/shard_map/ppermute | solution.py:308
  32.6 1.2 %collective-permute-start.4 = (bf16[32,4096]{1,0:T(8,128)(2,1)S(1)}, bf16[32,4096]{1,0:T(8,128)(2,1)S(1)}, u32[]{:S(2)}, u32[]{:S(2)}) collective-permute-start(bf16[32,4096]{1,0:T(8,128)(2,1)S(1)} %constant_dynamic-update-slice_fusion.refs_0_.own0), channel_id=1, source_target_pairs={{0,16},{1,17},{2,18},{3,19},{4,20},{5,21},{6,22},{7,23},{8,24},{9,... | collective-permute-start | bytes 786440 | tf_op jit(solution)/shard_map/ppermute | solution.py:308
  34.7 2.5 %collective-permute-start.2 = (bf16[32,4096]{1,0:T(8,128)(2,1)S(1)}, bf16[32,4096]{1,0:T(8,128)(2,1)S(1)}, u32[]{:S(2)}, u32[]{:S(2)}) collective-permute-start(bf16[32,4096]{1,0:T(8,128)(2,1)S(1)} %constant_dynamic-update-slice_fusion.refs_0_.own0), channel_id=1, source_target_pairs={{0,12},{1,97},{2,14},{3,99},{4,0},{5,101},{6,2},{7,103},{8,4},{9,1... | collective-permute-start | bytes 786440 | tf_op jit(solution)/shard_map/ppermute | solution.py:308
  37.2 5.4 %collective-permute-done.4.refs_4_ = bf16[32,4096]{1,0:T(8,128)(2,1)S(1)} collective-permute-done((bf16[32,4096]{1,0:T(8,128)(2,1)S(1)}, bf16[32,4096]{1,0:T(8,128)(2,1)S(1)}, u32[]{:S(2)}, u32[]{:S(2)}) %collective-permute-start.4) | collective-permute-done | bytes 262176 | tf_op jit(solution)/shard_map/ppermute | solution.py:308
  43.4 2.0 %collective-permute-start.6 = (bf16[32,4096]{1,0:T(8,128)(2,1)S(1)}, bf16[32,4096]{1,0:T(8,128)(2,1)S(1)}, u32[]{:S(2)}, u32[]{:S(2)}) collective-permute-start(bf16[32,4096]{1,0:T(8,128)(2,1)S(1)} %collective-permute-done.4.refs_4_), channel_id=1, source_target_pairs={{0,12},{1,97},{2,14},{3,99},{4,0},{5,101},{6,2},{7,103},{8,4},{9,1... | collective-permute-start | bytes 786440 | tf_op jit(solution)/shard_map/ppermute | solution.py:308
  45.4 0.9 collective-permute-start.8
  46.3 5.8 %shard_map.77 = (bf16[4096,1024]{1,0:T(8,128)(2,1)S(1)}, f32[8,128]{1,0:T(8,128)S(1)}) custom-call(s32[5]{0:T(128)S(1)} %stack.23.place_ref, bf16[32,4096]{1,0:T(8,128)(2,1)S(1)} %constant_dynamic-update-slice_fusion.refs_0_.own0, bf16[32,4096]{1,0:T(8,128)(2,1)S(1)} %collective-permute-done.9.own1, f32[144,128]{1,0:T(8,128)S(1)} %get-tuple-element.26.small_ref), custom_call_target="tpu_custom_call" | custom-call | flops 1024 | bytes 1024 | tf_op jit(solution)/shard_map/pallas_call | solution.py:210
  52.1 1.1 %collective-permute-done.5.refs_5_ = bf16[32,4096]{1,0:T(8,128)(2,1)S(1)} collective-permute-done((bf16[32,4096]{1,0:T(8,128)(2,1)S(1)}, bf16[32,4096]{1,0:T(8,128)(2,1)S(1)}, u32[]{:S(2)}, u32[]{:S(2)}) %collective-permute-start.5) | collective-permute-done | bytes 262176 | tf_op jit(solution)/shard_map/ppermute | solution.py:308
  54.2 2.1 %collective-permute-start.14 = (bf16[128,4096]{1,0:T(8,128)(2,1)S(1)}, bf16[128,4096]{1,0:T(8,128)(2,1)S(1)}, u32[]{:S(2)}, u32[]{:S(2)}) collective-permute-start(bf16[128,4096]{1,0:T(8,128)(2,1)S(1)} %get-tuple-element.29), channel_id=1, source_target_pairs={{0,97},{1,12},{2,99},{3,14},{4,101},{5,0},{6,103},{7,2},{8,105},{9... | collective-permute-start | bytes 3145736 | tf_op jit(solution)/shard_map/ppermute | solution.py:308
  56.8 1.2 %collective-permute-done.12.own1.refs_1_ = bf16[32,4096]{1,0:T(8,128)(2,1)S(1)} collective-permute-done((bf16[32,4096]{1,0:T(8,128)(2,1)S(1)}, bf16[32,4096]{1,0:T(8,128)(2,1)S(1)}, u32[]{:S(2)}, u32[]{:S(2)}) %collective-permute-start.12) | collective-permute-done | bytes 262176 | tf_op jit(solution)/shard_map/ppermute | solution.py:308
  58.0 3.2 %collective-permute-start.16 = (bf16[128,4096]{1,0:T(8,128)(2,1)S(1)}, bf16[128,4096]{1,0:T(8,128)(2,1)S(1)}, u32[]{:S(2)}, u32[]{:S(2)}) collective-permute-start(bf16[128,4096]{1,0:T(8,128)(2,1)S(1)} %shard_map.83), channel_id=1, source_target_pairs={{0,96},{1,13},{2,98},{3,15},{4,100},{5,1},{6,102},{7,3},{8,104},{9... | collective-permute-start | bytes 3145736 | tf_op jit(solution)/shard_map/ppermute | solution.py:308
  61.2 5.7 %shard_map.79 = (bf16[4096,1024]{1,0:T(8,128)(2,1)S(1)}, f32[8,128]{1,0:T(8,128)}) custom-call(s32[5]{0:T(128)S(1)} %stack.23.place_ref, bf16[32,4096]{1,0:T(8,128)(2,1)S(1)} %collective-permute-done.8.refs_8_.own0, bf16[32,4096]{1,0:T(8,128)(2,1)S(1)} %collective-permute-done.12.own1.refs_1_, f32[144,128]{1,0:T(8,128)S(1)} %get-tuple-element.26.small_ref), custom_call_target="tpu_custom_call" | custom-call | flops 1024 | bytes 1024 | tf_op jit(solution)/shard_map/pallas_call | solution.py:210
  66.9 6.6 %shard_map.80 = (f32[64,16,2048]{2,1,0:T(8,128)}, f32[8,128]{1,0:T(8,128)S(1)}) custom-call(s32[5]{0:T(128)S(1)} %stack.23.place_ref, bf16[128,4096]{1,0:T(8,128)(2,1)S(1)} %get-tuple-element.28.refs_0_, bf16[128,4096]{1,0:T(8,128)(2,1)S(1)} %collective-permute-done.11.refs_1_, bf16[4096,1024]{1,0:T(8,128)(2,1)S(1)} %get-tuple-element.30.refs_2_, ...), custom_call_target="tpu_custom_call" | custom-call | flops 1024 | bytes 1024 | tf_op jit(solution)/shard_map/pallas_call | solution.py:284
  73.6 2.2 %collective-permute-start.15 = (bf16[128,4096]{1,0:T(8,128)(2,1)S(1)}, bf16[128,4096]{1,0:T(8,128)(2,1)S(1)}, u32[]{:S(2)}, u32[]{:S(2)}) collective-permute-start(bf16[128,4096]{1,0:T(8,128)(2,1)S(1)} %shard_map.82.refs_1_), channel_id=1, source_target_pairs={{0,12},{1,97},{2,14},{3,99},{4,0},{5,101},{6,2},{7,103},{8,4},{9,1... | collective-permute-start | bytes 3145736 | tf_op jit(solution)/shard_map/ppermute | solution.py:308
  75.8 7.2 %shard_map.85 = (f32[64,16,2048]{2,1,0:T(8,128)}, f32[8,128]{1,0:T(8,128)}) custom-call(s32[5]{0:T(128)S(1)} %stack.23.place_ref, bf16[128,4096]{1,0:T(8,128)(2,1)S(1)} %shard_map.81.refs_0_, bf16[128,4096]{1,0:T(8,128)(2,1)S(1)} %shard_map.82.refs_1_, bf16[4096,1024]{1,0:T(8,128)(2,1)S(1)} %get-tuple-element.30.refs_2_, ...), custom_call_target="tpu_custom_call", output_to_operand_aliasing={{0}: (5, {})} | custom-call | flops 1024 | bytes 1024 | tf_op jit(solution)/shard_map/pallas_call | solution.py:284
  83.7 7.2 %shard_map.86 = (f32[64,16,2048]{2,1,0:T(8,128)}, f32[8,128]{1,0:T(8,128)}) custom-call(s32[5]{0:T(128)S(1)} %stack.23.place_ref, bf16[128,4096]{1,0:T(8,128)(2,1)S(1)} %collective-permute-done.16.refs_0_, bf16[128,4096]{1,0:T(8,128)(2,1)S(1)} %collective-permute-done.17.refs_1_, ...), custom_call_target="tpu_custom_call", output_to_operand_aliasing={{0}: (5, {})} | custom-call | flops 1024 | bytes 1024 | tf_op jit(solution)/shard_map/pallas_call | solution.py:284
  90.8 1.3 %collective-permute-done.13.refs_0_ = bf16[128,4096]{1,0:T(8,128)(2,1)S(1)} collective-permute-done((bf16[128,4096]{1,0:T(8,128)(2,1)S(1)}, bf16[128,4096]{1,0:T(8,128)(2,1)S(1)}, u32[]{:S(2)}, u32[]{:S(2)}) %collective-permute-start.13) | collective-permute-done | bytes 1048608 | tf_op jit(solution)/shard_map/ppermute | solution.py:308
  92.2 7.2 %shard_map.87 = (f32[64,16,2048]{2,1,0:T(8,128)}, f32[8,128]{1,0:T(8,128)}) custom-call(s32[5]{0:T(128)S(1)} %stack.23.place_ref, bf16[128,4096]{1,0:T(8,128)(2,1)S(1)} %collective-permute-done.13.refs_0_, bf16[128,4096]{1,0:T(8,128)(2,1)S(1)} %collective-permute-done.15.refs_1_, ...), custom_call_target="tpu_custom_call", output_to_operand_aliasing={{0}: (5, {})} | custom-call | flops 1024 | bytes 1024 | tf_op jit(solution)/shard_map/pallas_call | solution.py:284
  (43 shorter events, 7.2 us)
Async XLA Ops:
  1.4 1.0 %copy-start.1 = (bf16[256,1024]{1,0:T(8,128)(2,1)S(1)}, bf16[256,1024]{1,0:T(8,128)(2,1)}, u32[]{:S(2)}) copy-start(bf16[256,1024]{1,0:T(8,128)(2,1)} %raw_ref.1) | copy-start | bytes 1572868
  3.9 25.4 %all-to-all-start = ((bf16[128,2,1152]{2,1,0:T(2,128)(2,1)}), bf16[128,2,1152]{2,1,0:T(2,128)(2,1)S(1)}, u32[]{:S(2)}, u32[]{:S(2)}) async-start(bf16[128,2,1152]{2,1,0:T(2,128)(2,1)} %reshape.13), calls=%async_computation | async-start | bytes 1179648 | tf_op jit(solution)/shard_map/all_to_all | solution.py:344
  15.0 1.6 %copy-start = (bf16[1024,1024]{1,0:T(8,128)(2,1)S(1)}, bf16[1024,1024]{1,0:T(8,128)(2,1)}, u32[]{:S(2)}) copy-start(bf16[1024,1024]{1,0:T(8,128)(2,1)} %constant.72.clone.basis_hbm) | copy-start | bytes 6291460
  16.6 0.9 copy-start.2
  17.5 0.7 copy-start.3
  31.2 1.4 %collective-permute-start = (bf16[16,4096]{1,0:T(8,128)(2,1)S(1)}, bf16[16,4096]{1,0:T(8,128)(2,1)S(1)}, u32[]{:S(2)}, u32[]{:S(2)}) collective-permute-start(bf16[16,4096]{1,0:T(8,128)(2,1)S(1)} %get-tuple-element.25), channel_id=1, source_target_pairs={{0,1},{1,0},{2,3},{3,2},{4,5},{5,4},{6,7},{7,6},{8,9},{9,8},{10,11... | collective-permute-start | bytes 393224 | tf_op jit(solution)/shard_map/ppermute | solution.py:308
  32.6 9.9 %collective-permute-start.4 = (bf16[32,4096]{1,0:T(8,128)(2,1)S(1)}, bf16[32,4096]{1,0:T(8,128)(2,1)S(1)}, u32[]{:S(2)}, u32[]{:S(2)}) collective-permute-start(bf16[32,4096]{1,0:T(8,128)(2,1)S(1)} %constant_dynamic-update-slice_fusion.refs_0_.own0), channel_id=1, source_target_pairs={{0,16},{1,17},{2,18},{3,19},{4,20},{5,21},{6,22},{7,23},{8,24},{9,... | collective-permute-start | bytes 786440 | tf_op jit(solution)/shard_map/ppermute | solution.py:308
  33.9 9.5 %collective-permute-start.3 = (bf16[32,4096]{1,0:T(8,128)(2,1)S(1)}, bf16[32,4096]{1,0:T(8,128)(2,1)S(1)}, u32[]{:S(2)}, u32[]{:S(2)}) collective-permute-start(bf16[32,4096]{1,0:T(8,128)(2,1)S(1)} %constant_dynamic-update-slice_fusion.refs_0_.own0), channel_id=1, source_target_pairs={{0,8},{1,65},{2,10},{3,67},{4,12},{5,69},{6,14},{7,71},{8,0},{9,73... | collective-permute-start | bytes 786440 | tf_op jit(solution)/shard_map/ppermute | solution.py:308
  34.7 10.7 %collective-permute-start.2 = (bf16[32,4096]{1,0:T(8,128)(2,1)S(1)}, bf16[32,4096]{1,0:T(8,128)(2,1)S(1)}, u32[]{:S(2)}, u32[]{:S(2)}) collective-permute-start(bf16[32,4096]{1,0:T(8,128)(2,1)S(1)} %constant_dynamic-update-slice_fusion.refs_0_.own0), channel_id=1, source_target_pairs={{0,12},{1,97},{2,14},{3,99},{4,0},{5,101},{6,2},{7,103},{8,4},{9,1... | collective-permute-start | bytes 786440 | tf_op jit(solution)/shard_map/ppermute | solution.py:308
  37.2 8.2 %collective-permute-start.1 = (bf16[32,4096]{1,0:T(8,128)(2,1)S(1)}, bf16[32,4096]{1,0:T(8,128)(2,1)S(1)}, u32[]{:S(2)}, u32[]{:S(2)}) collective-permute-start(bf16[32,4096]{1,0:T(8,128)(2,1)S(1)} %constant_dynamic-update-slice_fusion.refs_0_.own0), channel_id=1, source_target_pairs={{0,4},{1,33},{2,6},{3,35},{4,8},{5,37},{6,10},{7,39},{8,12},{9,41}... | collective-permute-start | bytes 786440 | tf_op jit(solution)/shard_map/ppermute | solution.py:308
  37.2 9.2 %collective-permute-start.9 = (bf16[32,4096]{1,0:T(8,128)(2,1)S(1)}, bf16[32,4096]{1,0:T(8,128)(2,1)S(1)}, u32[]{:S(2)}, u32[]{:S(2)}) collective-permute-start(bf16[32,4096]{1,0:T(8,128)(2,1)S(1)} %constant_dynamic-update-slice_fusion.refs_0_.own0), channel_id=1, source_target_pairs={{0,1},{1,0},{2,3},{3,2},{4,5},{5,4},{6,7},{7,6},{8,9},{9,8},{10,11... | collective-permute-start | bytes 786440 | tf_op jit(solution)/shard_map/ppermute | solution.py:308
  42.6 9.6 %collective-permute-start.7 = (bf16[32,4096]{1,0:T(8,128)(2,1)S(1)}, bf16[32,4096]{1,0:T(8,128)(2,1)S(1)}, u32[]{:S(2)}, u32[]{:S(2)}) collective-permute-start(bf16[32,4096]{1,0:T(8,128)(2,1)S(1)} %collective-permute-done.4.refs_4_), channel_id=1, source_target_pairs={{0,8},{1,65},{2,10},{3,67},{4,12},{5,69},{6,14},{7,71},{8,0},{9,73... | collective-permute-start | bytes 786440 | tf_op jit(solution)/shard_map/ppermute | solution.py:308
  43.4 8.8 %collective-permute-start.6 = (bf16[32,4096]{1,0:T(8,128)(2,1)S(1)}, bf16[32,4096]{1,0:T(8,128)(2,1)S(1)}, u32[]{:S(2)}, u32[]{:S(2)}) collective-permute-start(bf16[32,4096]{1,0:T(8,128)(2,1)S(1)} %collective-permute-done.4.refs_4_), channel_id=1, source_target_pairs={{0,12},{1,97},{2,14},{3,99},{4,0},{5,101},{6,2},{7,103},{8,4},{9,1... | collective-permute-start | bytes 786440 | tf_op jit(solution)/shard_map/ppermute | solution.py:308
  45.4 7.9 %collective-permute-start.5 = (bf16[32,4096]{1,0:T(8,128)(2,1)S(1)}, bf16[32,4096]{1,0:T(8,128)(2,1)S(1)}, u32[]{:S(2)}, u32[]{:S(2)}) collective-permute-start(bf16[32,4096]{1,0:T(8,128)(2,1)S(1)} %collective-permute-done.4.refs_4_), channel_id=1, source_target_pairs={{0,4},{1,33},{2,6},{3,35},{4,8},{5,37},{6,10},{7,39},{8,12},{9,41}... | collective-permute-start | bytes 786440 | tf_op jit(solution)/shard_map/ppermute | solution.py:308
  45.4 7.9 %collective-permute-start.8 = (bf16[32,4096]{1,0:T(8,128)(2,1)S(1)}, bf16[32,4096]{1,0:T(8,128)(2,1)S(1)}, u32[]{:S(2)}, u32[]{:S(2)}) collective-permute-start(bf16[32,4096]{1,0:T(8,128)(2,1)S(1)} %shard_map.76), channel_id=1, source_target_pairs={{0,2},{1,3},{2,0},{3,1},{4,6},{5,7},{6,4},{7,5},{8,10},{9,11},{10,... | collective-permute-start | bytes 786440 | tf_op jit(solution)/shard_map/ppermute | solution.py:308
  53.5 13.4 %collective-permute-start.11 = (bf16[128,4096]{1,0:T(8,128)(2,1)S(1)}, bf16[128,4096]{1,0:T(8,128)(2,1)S(1)}, u32[]{:S(2)}, u32[]{:S(2)}) collective-permute-start(bf16[128,4096]{1,0:T(8,128)(2,1)S(1)} %get-tuple-element.29), channel_id=1, source_target_pairs={{0,1},{1,0},{2,3},{3,2},{4,5},{5,4},{6,7},{7,6},{8,9},{9,8},{10,11... | collective-permute-start | bytes 3145736 | tf_op jit(solution)/shard_map/ppermute | solution.py:308
  53.6 19.9 %collective-permute-start.10 = (bf16[128,4096]{1,0:T(8,128)(2,1)S(1)}, bf16[128,4096]{1,0:T(8,128)(2,1)S(1)}, u32[]{:S(2)}, u32[]{:S(2)}) collective-permute-start(bf16[128,4096]{1,0:T(8,128)(2,1)S(1)} %get-tuple-element.28.refs_0_), channel_id=1, source_target_pairs={{0,32},{1,5},{2,34},{3,7},{4,36},{5,9},{6,38},{7,11},{8,40},{9,13}... | collective-permute-start | bytes 3145736 | tf_op jit(solution)/shard_map/ppermute | solution.py:308
  54.2 19.4 %collective-permute-start.14 = (bf16[128,4096]{1,0:T(8,128)(2,1)S(1)}, bf16[128,4096]{1,0:T(8,128)(2,1)S(1)}, u32[]{:S(2)}, u32[]{:S(2)}) collective-permute-start(bf16[128,4096]{1,0:T(8,128)(2,1)S(1)} %get-tuple-element.29), channel_id=1, source_target_pairs={{0,97},{1,12},{2,99},{3,14},{4,101},{5,0},{6,103},{7,2},{8,105},{9... | collective-permute-start | bytes 3145736 | tf_op jit(solution)/shard_map/ppermute | solution.py:308
  56.4 1.6 %collective-permute-start.12 = (bf16[32,4096]{1,0:T(8,128)(2,1)S(1)}, bf16[32,4096]{1,0:T(8,128)(2,1)S(1)}, u32[]{:S(2)}, u32[]{:S(2)}) collective-permute-start(bf16[32,4096]{1,0:T(8,128)(2,1)S(1)} %collective-permute-done.8.refs_8_.own0), channel_id=1, source_target_pairs={{0,1},{1,0},{2,3},{3,2},{4,5},{5,4},{6,7},{7,6},{8,9},{9,8},{10,11... | collective-permute-start | bytes 786440 | tf_op jit(solution)/shard_map/ppermute | solution.py:308
  58.0 25.0 %collective-permute-start.17 = (bf16[128,4096]{1,0:T(8,128)(2,1)S(1)}, bf16[128,4096]{1,0:T(8,128)(2,1)S(1)}, u32[]{:S(2)}, u32[]{:S(2)}) collective-permute-start(bf16[128,4096]{1,0:T(8,128)(2,1)S(1)} %shard_map.84), channel_id=1, source_target_pairs={{0,33},{1,4},{2,35},{3,6},{4,37},{5,8},{6,39},{7,10},{8,41},{9,12}... | collective-permute-start | bytes 3145736 | tf_op jit(solution)/shard_map/ppermute | solution.py:308
  58.0 25.7 %collective-permute-start.16 = (bf16[128,4096]{1,0:T(8,128)(2,1)S(1)}, bf16[128,4096]{1,0:T(8,128)(2,1)S(1)}, u32[]{:S(2)}, u32[]{:S(2)}) collective-permute-start(bf16[128,4096]{1,0:T(8,128)(2,1)S(1)} %shard_map.83), channel_id=1, source_target_pairs={{0,96},{1,13},{2,98},{3,15},{4,100},{5,1},{6,102},{7,3},{8,104},{9... | collective-permute-start | bytes 3145736 | tf_op jit(solution)/shard_map/ppermute | solution.py:308
  73.5 18.7 %collective-permute-start.13 = (bf16[128,4096]{1,0:T(8,128)(2,1)S(1)}, bf16[128,4096]{1,0:T(8,128)(2,1)S(1)}, u32[]{:S(2)}, u32[]{:S(2)}) collective-permute-start(bf16[128,4096]{1,0:T(8,128)(2,1)S(1)} %shard_map.81.refs_0_), channel_id=1, source_target_pairs={{0,32},{1,5},{2,34},{3,7},{4,36},{5,9},{6,38},{7,11},{8,40},{9,13}... | collective-permute-start | bytes 3145736 | tf_op jit(solution)/shard_map/ppermute | solution.py:308
  73.6 18.6 %collective-permute-start.15 = (bf16[128,4096]{1,0:T(8,128)(2,1)S(1)}, bf16[128,4096]{1,0:T(8,128)(2,1)S(1)}, u32[]{:S(2)}, u32[]{:S(2)}) collective-permute-start(bf16[128,4096]{1,0:T(8,128)(2,1)S(1)} %shard_map.82.refs_1_), channel_id=1, source_target_pairs={{0,12},{1,97},{2,14},{3,99},{4,0},{5,101},{6,2},{7,103},{8,4},{9,1... | collective-permute-start | bytes 3145736 | tf_op jit(solution)/shard_map/ppermute | solution.py:308

commit v10 on v9

--- a/solution.py
+++ b/solution.py
@@ -77,8 +77,10 @@
     pick = jnp.where(flat == row.astype(F32), 1.0, 0.0)
     place = (key % WIN * QC + chan % QC + 1).astype(F32)
     place_col = jnp.sum(pick * place, axis=1, keepdims=True)
-    out_ref[:, SAMPLES:] = jnp.broadcast_to(place_col, (SLOTS, TAIL)).astype(BF16)
-    out_ref[:, :SAMPLES] = jnp.dot(pick.astype(BF16), raw_ref[...], preferred_element_type=F32).astype(BF16)
+    place_all = jnp.broadcast_to(place_col, (SLOTS, TAIL)).astype(BF16)
+    out_ref[:, :, SAMPLES:] = place_all.reshape(DEVICES, SLOTS // DEVICES, TAIL)
+    sent = jnp.dot(pick.astype(BF16), raw_ref[...], preferred_element_type=F32).astype(BF16)
+    out_ref[:, :, :SAMPLES] = sent.reshape(DEVICES, SLOTS // DEVICES, SAMPLES)
 
 
 def fetch_kernel(after_hbm, basis_hbm, taper_hbm, turn_hbm, basis_ref, taper_ref, turn_ref, sem):
@@ -338,11 +340,11 @@
         pack_kernel,
         in_specs=[SMEM, VMEM, VMEM],
         out_specs=VMEM,
-        out_shape=jax.ShapeDtypeStruct((SLOTS, SAMPLES + TAIL), BF16),
+        out_shape=jax.ShapeDtypeStruct((DEVICES, SLOTS // DEVICES, SAMPLES + TAIL), BF16),
         compiler_params=pltpu.CompilerParams(vmem_limit_bytes=8 * MIB),
     )(file_count, (seg_chan * WIN + seg_win).reshape(1, SLOTS), raw)
     arrived = lax.all_to_all(
-        packed.reshape(DEVICES, SLOTS // DEVICES, SAMPLES + TAIL),
+        packed,
         ("blk", "freq"),
         split_axis=0,
         concat_axis=0,

time: 100 us -> 100 us (level)
  local copies, waits for them, and re-layouts: 5.56 us -> 4.52 us
    reshape x2 -> x1, local copies, waits for them, and re-layouts: 1.26 us -> 0.22 us  [local(): arrived = lax.all_to_all(packed, ('blk', 'freq'), split_axis=0, concat_ax...]
where the time goes in v10:
time: 100 us; the launch traced here: 99.3 us
  Pallas kernels  43 us (43%)
  starting transfers between devices  28.2 us (28%)
  waiting for transfers between devices  21.8 us (22%)
  local copies, waits for them, and re-layouts  4.52 us (5%)
  between operations  1.06 us (1%)
    pallas_call x4, Pallas kernels, matmul(): pl.pallas_call(functools.partial(matmul_kernel, sources, len(arrays)), in...  28.1 us
    ppermute x18, starting transfers between devices, permuted(): return lax.ppermute(value, ('blk', 'freq'), pairs)  17 us
    pallas_call x2, Pallas kernels, rotate(): pl.pallas_call(functools.partial(rotate_kernel, halves), in_specs=[SMEM,...  11.5 us
    all_to_all x1, starting transfers between devices, local(): lax.all_to_all(packed, ('blk', 'freq'), split_axis=0, concat_axis=0, tile...  11.2 us
    ppermute x18, waiting for transfers between devices, permuted(): return lax.ppermute(value, ('blk', 'freq'), pairs)  11.1 us
    all_to_all x1, waiting for transfers between devices, local(): lax.all_to_all(packed, ('blk', 'freq'), split_axis=0, concat_axis=0, tile...  10.7 us
    unnamed x9, local copies, waits for them, and re-layouts  4.21 us
  transfers between devices with their start and end apart: 19, of which 7 were waited for; matrix products, arithmetic and copies ran while one was open for 0% of the time, Pallas kernels for 33%

profile of v10, /device:TPU:0, one launch (start us, length us, event | category | flops | bytes accessed | tf_op | source)
XLA Modules:
  0.0 99.3 jit_solution(11484791018049475806)
XLA Ops:
  1.4 1.0 %copy-done.1 = bf16[256,1024]{1,0:T(8,128)(2,1)S(1)} copy-done((bf16[256,1024]{1,0:T(8,128)(2,1)S(1)}, bf16[256,1024]{1,0:T(8,128)(2,1)}, u32[]{:S(2)}) %copy-start.1) | copy-done | bytes 524312
  2.4 1.2 %shard_map.73.after_hbm = bf16[128,2,1152]{2,1,0:T(2,128)(2,1)} custom-call(s32[1]{0:T(128)S(6)} %copy.23.count_ref, s32[1,256]{1,0:T(1,128)S(1)} %bitcast.7, bf16[256,1024]{1,0:T(8,128)(2,1)S(1)} %copy-done.1), custom_call_target="tpu_custom_call" | custom-call | tf_op jit(solution)/shard_map/pallas_call | solution.py:339
  3.6 11.2 %all-to-all-start = ((bf16[128,2,1152]{2,1,0:T(2,128)(2,1)}), bf16[128,2,1152]{2,1,0:T(2,128)(2,1)S(1)}, u32[]{:S(2)}, u32[]{:S(2)}) async-start(bf16[128,2,1152]{2,1,0:T(2,128)(2,1)} %shard_map.73.after_hbm), calls=%async_computation | async-start | bytes 1179648 | tf_op jit(solution)/shard_map/all_to_all | solution.py:346
  14.8 1.6 %copy-done = bf16[1024,1024]{1,0:T(8,128)(2,1)S(1)} copy-done((bf16[1024,1024]{1,0:T(8,128)(2,1)S(1)}, bf16[1024,1024]{1,0:T(8,128)(2,1)}, u32[]{:S(2)}) %copy-start) | copy-done | bytes 2097176
  18.4 10.7 %all-to-all-done = bf16[128,2,1152]{2,1,0:T(2,128)(2,1)S(1)} async-done(((bf16[128,2,1152]{2,1,0:T(2,128)(2,1)}), bf16[128,2,1152]{2,1,0:T(2,128)(2,1)S(1)}, u32[]{:S(2)}, u32[]{:S(2)}) %all-to-all-start) | async-done | bytes 589856 | tf_op jit(solution)/shard_map/all_to_all | solution.py:346
  29.3 1.7 %shard_map.75 = (bf16[16,4096]{1,0:T(8,128)(2,1)S(1)}, bf16[16,4096]{1,0:T(8,128)(2,1)S(1)}) custom-call(s32[5]{0:T(128)S(1)} %stack.23.place_ref, bf16[256,1152]{1,0:T(8,128)(2,1)S(1)} %reshape.10.recv_ref, bf16[1024,1024]{1,0:T(8,128)(2,1)S(1)} %get-tuple-element.22.basis_ref, f32[1,1024]{1,0:T(1,128)S(1)} %get-tuple-element.23.taper_ref), custom_call_target="tpu_custom_call" | custom-call | tf_op jit(solution)/shard_map/pallas_call | solution.py:362
  31.1 1.3 %collective-permute-done = bf16[16,4096]{1,0:T(8,128)(2,1)S(1)} collective-permute-done((bf16[16,4096]{1,0:T(8,128)(2,1)S(1)}, bf16[16,4096]{1,0:T(8,128)(2,1)S(1)}, u32[]{:S(2)}, u32[]{:S(2)}) %collective-permute-start) | collective-permute-done | bytes 131104 | tf_op jit(solution)/shard_map/ppermute | solution.py:310
  32.4 1.2 %collective-permute-start.4 = (bf16[32,4096]{1,0:T(8,128)(2,1)S(1)}, bf16[32,4096]{1,0:T(8,128)(2,1)S(1)}, u32[]{:S(2)}, u32[]{:S(2)}) collective-permute-start(bf16[32,4096]{1,0:T(8,128)(2,1)S(1)} %constant_dynamic-update-slice_fusion.refs_0_.own0), channel_id=1, source_target_pairs={{0,16},{1,17},{2,18},{3,19},{4,20},{5,21},{6,22},{7,23},{8,24},{9,... | collective-permute-start | bytes 786440 | tf_op jit(solution)/shard_map/ppermute | solution.py:310
  34.5 2.5 %collective-permute-start.2 = (bf16[32,4096]{1,0:T(8,128)(2,1)S(1)}, bf16[32,4096]{1,0:T(8,128)(2,1)S(1)}, u32[]{:S(2)}, u32[]{:S(2)}) collective-permute-start(bf16[32,4096]{1,0:T(8,128)(2,1)S(1)} %constant_dynamic-update-slice_fusion.refs_0_.own0), channel_id=1, source_target_pairs={{0,12},{1,97},{2,14},{3,99},{4,0},{5,101},{6,2},{7,103},{8,4},{9,1... | collective-permute-start | bytes 786440 | tf_op jit(solution)/shard_map/ppermute | solution.py:310
  37.0 5.4 %collective-permute-done.4.refs_4_ = bf16[32,4096]{1,0:T(8,128)(2,1)S(1)} collective-permute-done((bf16[32,4096]{1,0:T(8,128)(2,1)S(1)}, bf16[32,4096]{1,0:T(8,128)(2,1)S(1)}, u32[]{:S(2)}, u32[]{:S(2)}) %collective-permute-start.4) | collective-permute-done | bytes 262176 | tf_op jit(solution)/shard_map/ppermute | solution.py:310
  43.1 2.0 %collective-permute-start.6 = (bf16[32,4096]{1,0:T(8,128)(2,1)S(1)}, bf16[32,4096]{1,0:T(8,128)(2,1)S(1)}, u32[]{:S(2)}, u32[]{:S(2)}) collective-permute-start(bf16[32,4096]{1,0:T(8,128)(2,1)S(1)} %collective-permute-done.4.refs_4_), channel_id=1, source_target_pairs={{0,12},{1,97},{2,14},{3,99},{4,0},{5,101},{6,2},{7,103},{8,4},{9,1... | collective-permute-start | bytes 786440 | tf_op jit(solution)/shard_map/ppermute | solution.py:310
  45.2 0.9 collective-permute-start.8
  46.1 5.8 %shard_map.77 = (bf16[4096,1024]{1,0:T(8,128)(2,1)S(1)}, f32[8,128]{1,0:T(8,128)S(1)}) custom-call(s32[5]{0:T(128)S(1)} %stack.23.place_ref, bf16[32,4096]{1,0:T(8,128)(2,1)S(1)} %constant_dynamic-update-slice_fusion.refs_0_.own0, bf16[32,4096]{1,0:T(8,128)(2,1)S(1)} %collective-permute-done.9.own1, f32[144,128]{1,0:T(8,128)S(1)} %get-tuple-element.26.small_ref), custom_call_target="tpu_custom_call" | custom-call | flops 1024 | bytes 1024 | tf_op jit(solution)/shard_map/pallas_call | solution.py:212
  51.9 1.1 %collective-permute-done.5.refs_5_ = bf16[32,4096]{1,0:T(8,128)(2,1)S(1)} collective-permute-done((bf16[32,4096]{1,0:T(8,128)(2,1)S(1)}, bf16[32,4096]{1,0:T(8,128)(2,1)S(1)}, u32[]{:S(2)}, u32[]{:S(2)}) %collective-permute-start.5) | collective-permute-done | bytes 262176 | tf_op jit(solution)/shard_map/ppermute | solution.py:310
  54.0 2.1 %collective-permute-start.14 = (bf16[128,4096]{1,0:T(8,128)(2,1)S(1)}, bf16[128,4096]{1,0:T(8,128)(2,1)S(1)}, u32[]{:S(2)}, u32[]{:S(2)}) collective-permute-start(bf16[128,4096]{1,0:T(8,128)(2,1)S(1)} %get-tuple-element.29), channel_id=1, source_target_pairs={{0,97},{1,12},{2,99},{3,14},{4,101},{5,0},{6,103},{7,2},{8,105},{9... | collective-permute-start | bytes 3145736 | tf_op jit(solution)/shard_map/ppermute | solution.py:310
  56.6 1.2 %collective-permute-done.12.own1.refs_1_ = bf16[32,4096]{1,0:T(8,128)(2,1)S(1)} collective-permute-done((bf16[32,4096]{1,0:T(8,128)(2,1)S(1)}, bf16[32,4096]{1,0:T(8,128)(2,1)S(1)}, u32[]{:S(2)}, u32[]{:S(2)}) %collective-permute-start.12) | collective-permute-done | bytes 262176 | tf_op jit(solution)/shard_map/ppermute | solution.py:310
  57.8 3.2 %collective-permute-start.16 = (bf16[128,4096]{1,0:T(8,128)(2,1)S(1)}, bf16[128,4096]{1,0:T(8,128)(2,1)S(1)}, u32[]{:S(2)}, u32[]{:S(2)}) collective-permute-start(bf16[128,4096]{1,0:T(8,128)(2,1)S(1)} %shard_map.83), channel_id=1, source_target_pairs={{0,96},{1,13},{2,98},{3,15},{4,100},{5,1},{6,102},{7,3},{8,104},{9... | collective-permute-start | bytes 3145736 | tf_op jit(solution)/shard_map/ppermute | solution.py:310
  61.0 5.7 %shard_map.79 = (bf16[4096,1024]{1,0:T(8,128)(2,1)S(1)}, f32[8,128]{1,0:T(8,128)}) custom-call(s32[5]{0:T(128)S(1)} %stack.23.place_ref, bf16[32,4096]{1,0:T(8,128)(2,1)S(1)} %collective-permute-done.8.refs_8_.own0, bf16[32,4096]{1,0:T(8,128)(2,1)S(1)} %collective-permute-done.12.own1.refs_1_, f32[144,128]{1,0:T(8,128)S(1)} %get-tuple-element.26.small_ref), custom_call_target="tpu_custom_call" | custom-call | flops 1024 | bytes 1024 | tf_op jit(solution)/shard_map/pallas_call | solution.py:212
  66.7 6.6 %shard_map.80 = (f32[64,16,2048]{2,1,0:T(8,128)}, f32[8,128]{1,0:T(8,128)S(1)}) custom-call(s32[5]{0:T(128)S(1)} %stack.23.place_ref, bf16[128,4096]{1,0:T(8,128)(2,1)S(1)} %get-tuple-element.28.refs_0_, bf16[128,4096]{1,0:T(8,128)(2,1)S(1)} %collective-permute-done.11.refs_1_, bf16[4096,1024]{1,0:T(8,128)(2,1)S(1)} %get-tuple-element.30.refs_2_, ...), custom_call_target="tpu_custom_call" | custom-call | flops 1024 | bytes 1024 | tf_op jit(solution)/shard_map/pallas_call | solution.py:286
  73.4 2.1 %collective-permute-start.15 = (bf16[128,4096]{1,0:T(8,128)(2,1)S(1)}, bf16[128,4096]{1,0:T(8,128)(2,1)S(1)}, u32[]{:S(2)}, u32[]{:S(2)}) collective-permute-start(bf16[128,4096]{1,0:T(8,128)(2,1)S(1)} %shard_map.82.refs_1_), channel_id=1, source_target_pairs={{0,12},{1,97},{2,14},{3,99},{4,0},{5,101},{6,2},{7,103},{8,4},{9,1... | collective-permute-start | bytes 3145736 | tf_op jit(solution)/shard_map/ppermute | solution.py:310
  75.5 7.2 %shard_map.85 = (f32[64,16,2048]{2,1,0:T(8,128)}, f32[8,128]{1,0:T(8,128)}) custom-call(s32[5]{0:T(128)S(1)} %stack.23.place_ref, bf16[128,4096]{1,0:T(8,128)(2,1)S(1)} %shard_map.81.refs_0_, bf16[128,4096]{1,0:T(8,128)(2,1)S(1)} %shard_map.82.refs_1_, bf16[4096,1024]{1,0:T(8,128)(2,1)S(1)} %get-tuple-element.30.refs_2_, ...), custom_call_target="tpu_custom_call", output_to_operand_aliasing={{0}: (5, {})} | custom-call | flops 1024 | bytes 1024 | tf_op jit(solution)/shard_map/pallas_call | solution.py:286
  83.4 7.2 %shard_map.86 = (f32[64,16,2048]{2,1,0:T(8,128)}, f32[8,128]{1,0:T(8,128)}) custom-call(s32[5]{0:T(128)S(1)} %stack.23.place_ref, bf16[128,4096]{1,0:T(8,128)(2,1)S(1)} %collective-permute-done.16.refs_0_, bf16[128,4096]{1,0:T(8,128)(2,1)S(1)} %collective-permute-done.17.refs_1_, ...), custom_call_target="tpu_custom_call", output_to_operand_aliasing={{0}: (5, {})} | custom-call | flops 1024 | bytes 1024 | tf_op jit(solution)/shard_map/pallas_call | solution.py:286
  90.6 1.4 %collective-permute-done.13.refs_0_ = bf16[128,4096]{1,0:T(8,128)(2,1)S(1)} collective-permute-done((bf16[128,4096]{1,0:T(8,128)(2,1)S(1)}, bf16[128,4096]{1,0:T(8,128)(2,1)S(1)}, u32[]{:S(2)}, u32[]{:S(2)}) %collective-permute-start.13) | collective-permute-done | bytes 1048608 | tf_op jit(solution)/shard_map/ppermute | solution.py:310
  92.0 7.2 %shard_map.87 = (f32[64,16,2048]{2,1,0:T(8,128)}, f32[8,128]{1,0:T(8,128)}) custom-call(s32[5]{0:T(128)S(1)} %stack.23.place_ref, bf16[128,4096]{1,0:T(8,128)(2,1)S(1)} %collective-permute-done.13.refs_0_, bf16[128,4096]{1,0:T(8,128)(2,1)S(1)} %collective-permute-done.15.refs_1_, ...), custom_call_target="tpu_custom_call", output_to_operand_aliasing={{0}: (5, {})} | custom-call | flops 1024 | bytes 1024 | tf_op jit(solution)/shard_map/pallas_call | solution.py:286
  (42 shorter events, 6.9 us)
Async XLA Ops:
  1.4 1.0 %copy-start.1 = (bf16[256,1024]{1,0:T(8,128)(2,1)S(1)}, bf16[256,1024]{1,0:T(8,128)(2,1)}, u32[]{:S(2)}) copy-start(bf16[256,1024]{1,0:T(8,128)(2,1)} %raw_ref.1) | copy-start | bytes 1572868
  3.6 25.4 %all-to-all-start = ((bf16[128,2,1152]{2,1,0:T(2,128)(2,1)}), bf16[128,2,1152]{2,1,0:T(2,128)(2,1)S(1)}, u32[]{:S(2)}, u32[]{:S(2)}) async-start(bf16[128,2,1152]{2,1,0:T(2,128)(2,1)} %shard_map.73.after_hbm), calls=%async_computation | async-start | bytes 1179648 | tf_op jit(solution)/shard_map/all_to_all | solution.py:346
  14.8 1.6 %copy-start = (bf16[1024,1024]{1,0:T(8,128)(2,1)S(1)}, bf16[1024,1024]{1,0:T(8,128)(2,1)}, u32[]{:S(2)}) copy-start(bf16[1024,1024]{1,0:T(8,128)(2,1)} %constant.72.clone.basis_hbm) | copy-start | bytes 6291460
  16.4 0.9 copy-start.2
  17.3 0.7 copy-start.3
  31.0 1.4 %collective-permute-start = (bf16[16,4096]{1,0:T(8,128)(2,1)S(1)}, bf16[16,4096]{1,0:T(8,128)(2,1)S(1)}, u32[]{:S(2)}, u32[]{:S(2)}) collective-permute-start(bf16[16,4096]{1,0:T(8,128)(2,1)S(1)} %get-tuple-element.25), channel_id=1, source_target_pairs={{0,1},{1,0},{2,3},{3,2},{4,5},{5,4},{6,7},{7,6},{8,9},{9,8},{10,11... | collective-permute-start | bytes 393224 | tf_op jit(solution)/shard_map/ppermute | solution.py:310
  32.4 9.9 %collective-permute-start.4 = (bf16[32,4096]{1,0:T(8,128)(2,1)S(1)}, bf16[32,4096]{1,0:T(8,128)(2,1)S(1)}, u32[]{:S(2)}, u32[]{:S(2)}) collective-permute-start(bf16[32,4096]{1,0:T(8,128)(2,1)S(1)} %constant_dynamic-update-slice_fusion.refs_0_.own0), channel_id=1, source_target_pairs={{0,16},{1,17},{2,18},{3,19},{4,20},{5,21},{6,22},{7,23},{8,24},{9,... | collective-permute-start | bytes 786440 | tf_op jit(solution)/shard_map/ppermute | solution.py:310
  33.7 9.5 %collective-permute-start.3 = (bf16[32,4096]{1,0:T(8,128)(2,1)S(1)}, bf16[32,4096]{1,0:T(8,128)(2,1)S(1)}, u32[]{:S(2)}, u32[]{:S(2)}) collective-permute-start(bf16[32,4096]{1,0:T(8,128)(2,1)S(1)} %constant_dynamic-update-slice_fusion.refs_0_.own0), channel_id=1, source_target_pairs={{0,8},{1,65},{2,10},{3,67},{4,12},{5,69},{6,14},{7,71},{8,0},{9,73... | collective-permute-start | bytes 786440 | tf_op jit(solution)/shard_map/ppermute | solution.py:310
  34.5 10.7 %collective-permute-start.2 = (bf16[32,4096]{1,0:T(8,128)(2,1)S(1)}, bf16[32,4096]{1,0:T(8,128)(2,1)S(1)}, u32[]{:S(2)}, u32[]{:S(2)}) collective-permute-start(bf16[32,4096]{1,0:T(8,128)(2,1)S(1)} %constant_dynamic-update-slice_fusion.refs_0_.own0), channel_id=1, source_target_pairs={{0,12},{1,97},{2,14},{3,99},{4,0},{5,101},{6,2},{7,103},{8,4},{9,1... | collective-permute-start | bytes 786440 | tf_op jit(solution)/shard_map/ppermute | solution.py:310
  37.0 8.2 %collective-permute-start.1 = (bf16[32,4096]{1,0:T(8,128)(2,1)S(1)}, bf16[32,4096]{1,0:T(8,128)(2,1)S(1)}, u32[]{:S(2)}, u32[]{:S(2)}) collective-permute-start(bf16[32,4096]{1,0:T(8,128)(2,1)S(1)} %constant_dynamic-update-slice_fusion.refs_0_.own0), channel_id=1, source_target_pairs={{0,4},{1,33},{2,6},{3,35},{4,8},{5,37},{6,10},{7,39},{8,12},{9,41}... | collective-permute-start | bytes 786440 | tf_op jit(solution)/shard_map/ppermute | solution.py:310
  37.0 9.2 %collective-permute-start.9 = (bf16[32,4096]{1,0:T(8,128)(2,1)S(1)}, bf16[32,4096]{1,0:T(8,128)(2,1)S(1)}, u32[]{:S(2)}, u32[]{:S(2)}) collective-permute-start(bf16[32,4096]{1,0:T(8,128)(2,1)S(1)} %constant_dynamic-update-slice_fusion.refs_0_.own0), channel_id=1, source_target_pairs={{0,1},{1,0},{2,3},{3,2},{4,5},{5,4},{6,7},{7,6},{8,9},{9,8},{10,11... | collective-permute-start | bytes 786440 | tf_op jit(solution)/shard_map/ppermute | solution.py:310
  42.4 9.6 %collective-permute-start.7 = (bf16[32,4096]{1,0:T(8,128)(2,1)S(1)}, bf16[32,4096]{1,0:T(8,128)(2,1)S(1)}, u32[]{:S(2)}, u32[]{:S(2)}) collective-permute-start(bf16[32,4096]{1,0:T(8,128)(2,1)S(1)} %collective-permute-done.4.refs_4_), channel_id=1, source_target_pairs={{0,8},{1,65},{2,10},{3,67},{4,12},{5,69},{6,14},{7,71},{8,0},{9,73... | collective-permute-start | bytes 786440 | tf_op jit(solution)/shard_map/ppermute | solution.py:310
  43.1 8.8 %collective-permute-start.6 = (bf16[32,4096]{1,0:T(8,128)(2,1)S(1)}, bf16[32,4096]{1,0:T(8,128)(2,1)S(1)}, u32[]{:S(2)}, u32[]{:S(2)}) collective-permute-start(bf16[32,4096]{1,0:T(8,128)(2,1)S(1)} %collective-permute-done.4.refs_4_), channel_id=1, source_target_pairs={{0,12},{1,97},{2,14},{3,99},{4,0},{5,101},{6,2},{7,103},{8,4},{9,1... | collective-permute-start | bytes 786440 | tf_op jit(solution)/shard_map/ppermute | solution.py:310
  45.2 7.9 %collective-permute-start.5 = (bf16[32,4096]{1,0:T(8,128)(2,1)S(1)}, bf16[32,4096]{1,0:T(8,128)(2,1)S(1)}, u32[]{:S(2)}, u32[]{:S(2)}) collective-permute-start(bf16[32,4096]{1,0:T(8,128)(2,1)S(1)} %collective-permute-done.4.refs_4_), channel_id=1, source_target_pairs={{0,4},{1,33},{2,6},{3,35},{4,8},{5,37},{6,10},{7,39},{8,12},{9,41}... | collective-permute-start | bytes 786440 | tf_op jit(solution)/shard_map/ppermute | solution.py:310
  45.2 7.8 %collective-permute-start.8 = (bf16[32,4096]{1,0:T(8,128)(2,1)S(1)}, bf16[32,4096]{1,0:T(8,128)(2,1)S(1)}, u32[]{:S(2)}, u32[]{:S(2)}) collective-permute-start(bf16[32,4096]{1,0:T(8,128)(2,1)S(1)} %shard_map.76), channel_id=1, source_target_pairs={{0,2},{1,3},{2,0},{3,1},{4,6},{5,7},{6,4},{7,5},{8,10},{9,11},{10,... | collective-permute-start | bytes 786440 | tf_op jit(solution)/shard_map/ppermute | solution.py:310
  53.3 13.3 %collective-permute-start.11 = (bf16[128,4096]{1,0:T(8,128)(2,1)S(1)}, bf16[128,4096]{1,0:T(8,128)(2,1)S(1)}, u32[]{:S(2)}, u32[]{:S(2)}) collective-permute-start(bf16[128,4096]{1,0:T(8,128)(2,1)S(1)} %get-tuple-element.29), channel_id=1, source_target_pairs={{0,1},{1,0},{2,3},{3,2},{4,5},{5,4},{6,7},{7,6},{8,9},{9,8},{10,11... | collective-permute-start | bytes 3145736 | tf_op jit(solution)/shard_map/ppermute | solution.py:310
  53.4 19.9 %collective-permute-start.10 = (bf16[128,4096]{1,0:T(8,128)(2,1)S(1)}, bf16[128,4096]{1,0:T(8,128)(2,1)S(1)}, u32[]{:S(2)}, u32[]{:S(2)}) collective-permute-start(bf16[128,4096]{1,0:T(8,128)(2,1)S(1)} %get-tuple-element.28.refs_0_), channel_id=1, source_target_pairs={{0,32},{1,5},{2,34},{3,7},{4,36},{5,9},{6,38},{7,11},{8,40},{9,13}... | collective-permute-start | bytes 3145736 | tf_op jit(solution)/shard_map/ppermute | solution.py:310
  54.0 19.4 %collective-permute-start.14 = (bf16[128,4096]{1,0:T(8,128)(2,1)S(1)}, bf16[128,4096]{1,0:T(8,128)(2,1)S(1)}, u32[]{:S(2)}, u32[]{:S(2)}) collective-permute-start(bf16[128,4096]{1,0:T(8,128)(2,1)S(1)} %get-tuple-element.29), channel_id=1, source_target_pairs={{0,97},{1,12},{2,99},{3,14},{4,101},{5,0},{6,103},{7,2},{8,105},{9... | collective-permute-start | bytes 3145736 | tf_op jit(solution)/shard_map/ppermute | solution.py:310
  56.1 1.6 %collective-permute-start.12 = (bf16[32,4096]{1,0:T(8,128)(2,1)S(1)}, bf16[32,4096]{1,0:T(8,128)(2,1)S(1)}, u32[]{:S(2)}, u32[]{:S(2)}) collective-permute-start(bf16[32,4096]{1,0:T(8,128)(2,1)S(1)} %collective-permute-done.8.refs_8_.own0), channel_id=1, source_target_pairs={{0,1},{1,0},{2,3},{3,2},{4,5},{5,4},{6,7},{7,6},{8,9},{9,8},{10,11... | collective-permute-start | bytes 786440 | tf_op jit(solution)/shard_map/ppermute | solution.py:310
  57.7 25.0 %collective-permute-start.17 = (bf16[128,4096]{1,0:T(8,128)(2,1)S(1)}, bf16[128,4096]{1,0:T(8,128)(2,1)S(1)}, u32[]{:S(2)}, u32[]{:S(2)}) collective-permute-start(bf16[128,4096]{1,0:T(8,128)(2,1)S(1)} %shard_map.84), channel_id=1, source_target_pairs={{0,33},{1,4},{2,35},{3,6},{4,37},{5,8},{6,39},{7,10},{8,41},{9,12}... | collective-permute-start | bytes 3145736 | tf_op jit(solution)/shard_map/ppermute | solution.py:310
  57.8 25.6 %collective-permute-start.16 = (bf16[128,4096]{1,0:T(8,128)(2,1)S(1)}, bf16[128,4096]{1,0:T(8,128)(2,1)S(1)}, u32[]{:S(2)}, u32[]{:S(2)}) collective-permute-start(bf16[128,4096]{1,0:T(8,128)(2,1)S(1)} %shard_map.83), channel_id=1, source_target_pairs={{0,96},{1,13},{2,98},{3,15},{4,100},{5,1},{6,102},{7,3},{8,104},{9... | collective-permute-start | bytes 3145736 | tf_op jit(solution)/shard_map/ppermute | solution.py:310
  73.3 18.7 %collective-permute-start.13 = (bf16[128,4096]{1,0:T(8,128)(2,1)S(1)}, bf16[128,4096]{1,0:T(8,128)(2,1)S(1)}, u32[]{:S(2)}, u32[]{:S(2)}) collective-permute-start(bf16[128,4096]{1,0:T(8,128)(2,1)S(1)} %shard_map.81.refs_0_), channel_id=1, source_target_pairs={{0,32},{1,5},{2,34},{3,7},{4,36},{5,9},{6,38},{7,11},{8,40},{9,13}... | collective-permute-start | bytes 3145736 | tf_op jit(solution)/shard_map/ppermute | solution.py:310
  73.4 18.6 %collective-permute-start.15 = (bf16[128,4096]{1,0:T(8,128)(2,1)S(1)}, bf16[128,4096]{1,0:T(8,128)(2,1)S(1)}, u32[]{:S(2)}, u32[]{:S(2)}) collective-permute-start(bf16[128,4096]{1,0:T(8,128)(2,1)S(1)} %shard_map.82.refs_1_), channel_id=1, source_target_pairs={{0,12},{1,97},{2,14},{3,99},{4,0},{5,101},{6,2},{7,103},{8,4},{9,1... | collective-permute-start | bytes 3145736 | tf_op jit(solution)/shard_map/ppermute | solution.py:310
